TPU v7x, 512 devices: a whole 4x4x16 slice. The times are simulated.
512 devices in a mesh: dp: 64 (over z, y), tensor: 8 (over x, core).
Axes of the slice: x: 4, y: 4, z: 16, core: 2. Of those that a mesh axis runs over, the one named last changes fastest.
Arguments:
- post_deter: bfloat16 [16384, 4096], P('dp', 'tensor'), may hold values from -1 to 1
- post_sample: int32 [16384, 32], P('dp'), may hold values from 0 to 31
- samples: int32 [2, 16384, 32], P(None, 'dp'), may hold values from 0 to 31
- actions: int32 [2, 16384], P(None, 'dp'), may hold values from 0 to 17
- counts: int32 [256], P('dp'), may hold values from 1 to 64, 8192 in all
- w_stoch: bfloat16 [1024, 1024], P(None, 'tensor'), may hold values from -1 to 1
- w_action: bfloat16 [18, 1024], P(None, 'tensor'), may hold values from -6 to 6
- w_gate: bfloat16 [1024, 12288], P('dp', 'tensor'), may hold values from -0.1875 to 0.1875
- w_rec: bfloat16 [8, 512, 1536], P('tensor'), may hold values from -0.25 to 0.25
- w_prior_in: bfloat16 [4096, 1024], P('tensor'), may hold values from -0.09375 to 0.09375
- w_prior_out: bfloat16 [1024, 1024], P(None, 'tensor'), may hold values from -8 to 8
Outputs:
- deter_out: bfloat16 [16384, 4096], P('dp', 'tensor')
- log_prob: float32 [2, 16384], P(None, 'dp')
Inputs may be any that keep to these rules, and one draw needn't show every extreme that they name: Every sequence has at least one valid start; the counts of all sequences sum to 8192 and the largest is 64.
All inputs are finite; a program needn't handle non-finite values. No bound on the sum of `counts` on one device may be relied on, other than what follows from the above.
Results may differ from a plain program's by a relative error of at most 0.0051.
Values may be sent and summed in bfloat16 or wider, within the bound.
No kernel may reach another device: no remote copies, remote signals or barrier semaphores. Data moves between devices by JAX's collectives and lax.ppermute only.
A program may use at most 64 MiB of HBM per device.

v0:
```python
import jax
import jax.numpy as jnp
from jax import lax
from jax.sharding import PartitionSpec as P

STOCH = 32
CLASSES = 32
ACTIONS = 18
STEPS = 64
IMAG = 2


epsilon = 1e-06


def body(
    post_deter,
    post_sample,
    samples,
    actions,
    counts,
    w_stoch,
    w_action,
    w_gate,
    w_rec,
    w_prior_in,
    w_prior_out,
):
    row_count = post_deter.shape[0]
    local_blocks = w_rec.shape[0]
    block_width = w_rec.shape[1]
    hidden_width = w_prior_in.shape[1]
    local_groups = w_prior_out.shape[1] // CLASSES
    positions = jnp.arange(STEPS, dtype=jnp.int32)
    valid_mask = (positions[None, :] < counts[:, None]).reshape(row_count)
    class_ids = jnp.arange(CLASSES, dtype=jnp.int32)
    action_ids = jnp.arange(ACTIONS, dtype=jnp.int32)
    group_start = lax.axis_index("tensor") * local_groups
    deter = post_deter
    latent = post_sample
    rows = deter.shape[0]
    log_list = []
    for imag_step in range(IMAG):
        latent_hot = (
            (latent[:, :, None] == class_ids).reshape(rows, STOCH * CLASSES).astype(jnp.bfloat16)
        )
        action_hot = (actions[imag_step][:, None] == action_ids).astype(jnp.bfloat16)
        embed_pre = jnp.dot(latent_hot, w_stoch, preferred_element_type=jnp.float32)
        embed_pre = embed_pre + jnp.dot(action_hot, w_action, preferred_element_type=jnp.float32)
        square_sum = lax.psum(jnp.sum(embed_pre * embed_pre, axis=1), "tensor")
        embed_part = jax.nn.silu(
            embed_pre * lax.rsqrt(square_sum / hidden_width + epsilon)[:, None]
        ).astype(jnp.bfloat16)
        features = lax.all_gather(embed_part, "tensor", axis=1, tiled=True)
        gate_sum = jnp.dot(
            features,
            lax.all_gather(w_gate, "dp", axis=0, tiled=True),
            preferred_element_type=jnp.float32,
        )
        gate_sum = gate_sum.reshape(rows, local_blocks, 3 * block_width)
        deter_blocks = deter.reshape(rows, local_blocks, block_width)
        gate_sum = gate_sum + jnp.einsum(
            "rbk,bkn->rbn", deter_blocks, w_rec, preferred_element_type=jnp.float32
        )
        reset_gate = jax.nn.sigmoid(gate_sum[..., :block_width])
        candidate = jnp.tanh(reset_gate * gate_sum[..., block_width : 2 * block_width])
        update = jax.nn.sigmoid(gate_sum[..., 2 * block_width :] - 1.0)
        fresh = update * candidate + (1.0 - update) * deter_blocks.astype(jnp.float32)
        deter = fresh.reshape(rows, local_blocks * block_width).astype(jnp.bfloat16)
        prior_pre = jnp.dot(deter, w_prior_in, preferred_element_type=jnp.float32)
        summed = lax.psum(prior_pre, "tensor")
        scale = lax.rsqrt(jnp.mean(summed * summed, axis=1, keepdims=True) + epsilon)
        prior_hidden = jax.nn.silu(summed * scale).astype(jnp.bfloat16)
        logits = jnp.dot(prior_hidden, w_prior_out, preferred_element_type=jnp.float32)
        logits = logits.reshape(rows, local_groups, CLASSES)
        softmax_probs = jax.nn.softmax(logits, axis=-1)
        mixture = 0.99 * softmax_probs + 0.01 / CLASSES
        picked = lax.dynamic_slice_in_dim(samples[imag_step], group_start, local_groups, 1)
        chosen = jnp.sum(jnp.where(picked[:, :, None] == class_ids, mixture, 0.0), axis=-1)
        log_terms = lax.psum(jnp.sum(jnp.log(chosen), axis=1), "tensor")
        log_list.append(log_terms)
        latent = samples[imag_step]
    deter, logs = (deter, jnp.stack(log_list))
    deter_out = jnp.where(valid_mask[:, None], deter, jnp.zeros_like(deter))
    log_prob = jnp.where(valid_mask[None, :], logs, 0.0)
    return (deter_out, log_prob)


def solution(mesh):
    in_specs = (
        P("dp", "tensor"),
        P("dp", None),
        P(None, "dp", None),
        P(None, "dp"),
        P("dp"),
        P(None, "tensor"),
        P(None, "tensor"),
        P("dp", "tensor"),
        P("tensor", None, None),
        P("tensor", None),
        P(None, "tensor"),
    )
    out_specs = (P("dp", "tensor"), P(None, "dp"))
    return jax.shard_map(body, mesh=mesh, in_specs=in_specs, out_specs=out_specs, check_vma=False)
```

profile of v0, /device:TPU:1, one launch (start us, length us, event | category | flops | bytes accessed | tf_op | source)
XLA Modules:
  0.0 268.9 jit_solution(4196766330366359730)
XLA Ops:
  7.2 0.7 all-gather.2.cloned.1.call-update
  8.1 0.7 iota_compare_fusion.6
  8.8 0.1 lt.31
  8.9 1.4 fusion.58
  10.3 1.1 bitcast_compare_fusion.1
  11.4 0.8 fusion.59
  12.2 0.9 fusion.50
  13.1 0.9 fusion.49
  14.1 1.3 multiply_reduce_fusion.2
  15.4 1.0 multiply_reduce_fusion.3
  16.3 18.6 %all-reduce.1 = (f32[256]{0:T(256)S(1)}, f32[256]{0:T(256)S(1)}) all-reduce(f32[256]{0:T(256)S(1)} %get-tuple-element.17, f32[256]{0:T(256)S(1)} %get-tuple-element.19), channel_id=1, replica_groups=mesh['dp'=64,'tensor'=8] {'tensor'}, use_global_device_ids=true, to_apply=%region_3.4 | all-reduce | flops 512 | bytes 4096 | tf_op jit(solution)/shard_map/psum | solution.py:50
  35.0 0.6 convolution_bitcast_fusion
  35.6 0.2 copy-done.8
  35.9 14.7 %all_gather.12 = bf16[256,1024]{0,1:T(8,128)(2,1)} all-gather(bf16[256,128]{0,1:T(8,128)(2,1)S(1)} %multiply_convert_fusion.4), channel_id=1, replica_groups=mesh['dp'=64,'tensor'=8] {'tensor'}, dimensions={1}, use_global_device_ids=true | all-gather | bytes 589824 | tf_op jit(solution)/shard_map/all_gather | solution.py:54
  50.6 14.2 %all_gather.10 = bf16[256,1024]{0,1:T(8,128)(2,1)} all-gather(bf16[256,128]{0,1:T(8,128)(2,1)S(1)} %multiply_convert_fusion.5), channel_id=1, replica_groups=mesh['dp'=64,'tensor'=8] {'tensor'}, dimensions={1}, use_global_device_ids=true | all-gather | bytes 589824 | tf_op jit(solution)/shard_map/all_gather | solution.py:54
  64.8 86.7 %all-gather.2.cloned.1.call-done = bf16[1024,1536]{1,0:T(8,128)(2,1)} async-done(((bf16[16,1536]{1,0:T(8,128)(2,1)}), bf16[1024,1536]{1,0:T(8,128)(2,1)}) %all-gather.2.cloned.1.call-update) | async-done | bytes 3145744 | tf_op jit(solution)/shard_map/all_gather | solution.py:57
  151.5 3.1 %fusion.5 = f32[256,1,1536]{2,0,1:T(8,128)S(1)} fusion(f32[256,1,1536]{2,0,1:T(8,128)S(1)} %convolution_bitcast_fusion, bf16[256,1024]{0,1:T(8,128)(2,1)} %all_gather.12, bf16[1024,1536]{1,0:T(8,128)(2,1)} %all-gather.2.cloned.1.call-done), kind=kOutput, calls=%fused_computation.9 | convolution fusion | flops 805699584 | bytes 6815744 | tf_op jit(solution)/shard_map/dot_general | solution.py:55
  154.6 0.4 fusion.34
  154.9 0.6 convolution_bitcast_fusion.1
  155.5 0.3 copy-done.2
  155.8 1.4 fusion.46
  157.2 1.0 fusion.4
  158.2 1.1 bitcast_select_fusion
  159.3 1.4 fusion.44
  160.8 0.8 dynamic-slice_bitcast_fusion
  161.5 82.0 %all-reduce.5.cloned.1.call-done = (f32[256,1024]{1,0:T(8,128)}, f32[256,1024]{1,0:T(8,128)}) async-done(((f32[256,1024]{1,0:T(8,128)}, f32[256,1024]{1,0:T(8,128)}), (f32[256,1024]{1,0:T(8,128)}, f32[256,1024]{1,0:T(8,128)})) %all-reduce.5.cloned.1.call-update) | async-done | bytes 2097168 | tf_op jit(solution)/shard_map/psum | solution.py:71
  243.5 1.8 multiply_reduce_fusion
  245.4 0.5 fusion.42
  246.1 0.6 copy-done.4
  246.6 0.5 fusion.43
  247.3 14.2 %all-reduce = (f32[1,256]{1,0:T(1,128)S(1)}, f32[1,256]{1,0:T(1,128)S(1)}) all-reduce(f32[1,256]{1,0:T(1,128)S(1)} %bitcast.73, f32[1,256]{1,0:T(1,128)S(1)} %bitcast.72), channel_id=1, replica_groups=mesh['dp'=64,'tensor'=8] {'tensor'}, use_global_device_ids=true, to_apply=%region_17.18 | all-reduce | flops 512 | bytes 4096 | tf_op jit(solution)/shard_map/psum | solution.py:80
  261.4 0.6 maximum_select_fusion
  (32 shorter events, 0.6 us)
Async XLA Ops:
  7.2 27.8 %copy-start = (bf16[1,512,1536]{2,1,0:T(8,128)(2,1)S(1)}, bf16[1,512,1536]{2,1,0:T(8,128)(2,1)}, u32[]{:S(2)}) copy-start(bf16[1,512,1536]{2,1,0:T(8,128)(2,1)} %param.19) | copy-start | bytes 4718596
  7.2 8.2 %copy-start.6 = (bf16[1024,128]{1,0:T(8,128)(2,1)S(1)}, bf16[1024,128]{1,0:T(8,128)(2,1)}, u32[]{:S(2)}) copy-start(bf16[1024,128]{1,0:T(8,128)(2,1)} %param.16) | copy-start | bytes 786436
  7.2 27.8 %copy-start.7 = (bf16[256,512]{1,0:T(8,128)(2,1)S(1)}, bf16[256,512]{1,0:T(8,128)(2,1)}, u32[]{:S(2)}) copy-start(bf16[256,512]{1,0:T(8,128)(2,1)} %param.11) | copy-start | bytes 786436
  7.2 144.3 %all-gather.2.cloned.1.call-start = ((), (), s32[]{:S(2)}) async-start(), calls=%async_computation | async-start | bytes 3194880 | tf_op jit(solution)/shard_map/all_gather | solution.py:57
  7.9 235.6 %all-reduce.5.cloned.1.call-start = ((), (), s32[]{:S(2)}) async-start(), calls=%async_computation.1 | async-start | bytes 4194304 | tf_op jit(solution)/shard_map/psum | solution.py:71
  35.0 0.9 copy-start.8
  154.6 1.2 copy-start.2
  154.9 2.3 copy-start.1
  155.8 1.4 copy-start.3
  160.8 84.6 %copy-start.9 = (bf16[1024,128]{1,0:T(8,128)(2,1)S(1)}, bf16[1024,128]{1,0:T(8,128)(2,1)}, u32[]{:S(2)}) copy-start(bf16[1024,128]{1,0:T(8,128)(2,1)} %param.21) | copy-start | bytes 786436
  243.5 1.9 copy-start.5
  245.4 1.2 copy-start.4
Sparse Core Ops, SparseCore 0:
  11.0 140.4 all-gather.1
  160.9 82.5 all-reduce.4
where the time goes:
time: 270 us; the launch traced here: 269 us
  waiting for transfers between devices  169 us (63%)
  blocking collectives  61.7 us (23%)
  between operations  14.2 us (5%)
  matrix products  13.2 us (5%)
  other arithmetic  6.06 us (2%)
  local copies, waits for them, and re-layouts  4.19 us (2%)
    all_gather x1, waiting for transfers between devices, body(): lax.all_gather(w_gate, 'dp', axis=0, tiled=True)  86.7 us
    psum x1, waiting for transfers between devices, body(): summed = lax.psum(prior_pre, 'tensor')  82 us
    all_gather x2, blocking collectives, body(): features = lax.all_gather(embed_part, 'tensor', axis=1, tiled=True)  28.8 us
    psum x1, blocking collectives, body(): square_sum = lax.psum(jnp.sum(embed_pre * embed_pre, axis=1), 'tensor')  18.6 us
    psum x1, blocking collectives, body(): log_terms = lax.psum(jnp.sum(jnp.log(chosen), axis=1), 'tensor')  14.2 us
  transfers between devices with their start and end apart: 2, of which 2 were waited for; matrix products, arithmetic and copies ran while one was open for 4% of the time, Pallas kernels for 0%

commit v1 on v0

v1 whole, which is shorter than its diff:
```python
import functools

import jax
import jax.numpy as jnp
from jax import lax
from jax.experimental import pallas as pl
from jax.experimental.pallas import tpu as pltpu
from jax.sharding import PartitionSpec as P

STOCH = 32
CLASSES = 32
LAT = STOCH * CLASSES
ACTIONS = 18
STEPS = 64
IMAG = 2
UNITS = 1024
NY = 4
NX = 4
NC = 2
LANES = 128
EPS = 1e-06
MIB = 1024 * 1024


def y_groups(n_dp):
    return [[start + y for y in range(NY)] for start in range(0, n_dp, NY)]


def z_groups(n_dp):
    return [list(range(y, n_dp, NY)) for y in range(NY)]


def x_groups():
    return [list(range(core, NX * NC, NC)) for core in range(NC)]


def spread_to(value, axis, groups, count):
    copies = jnp.broadcast_to(value[None], (count,) + value.shape)
    return lax.all_to_all(copies, axis, 0, 0, axis_index_groups=groups)


def core_swap(value):
    perm = [(i, i ^ 1) for i in range(NX * NC)]
    return lax.ppermute(value, "tensor", perm)


def features_kernel(core_ref, pack_ref, spread_ref, target_ref, mine_ref, other_ref, out_ref, w_ref):
    @pl.when(pl.program_id(0) == 0)
    def _():
        core = core_ref[0]
        for x in range(NX):
            base = x * NC * LANES
            w_ref[:, pl.ds(pl.multiple_of(base + core * LANES, LANES), LANES)] = mine_ref[x]
            w_ref[:, pl.ds(pl.multiple_of(base + (1 - core) * LANES, LANES), LANES)] = other_ref[x]

    spread = jnp.dot(pack_ref[...], spread_ref[...], preferred_element_type=jnp.float32)
    hot = jnp.where(spread == target_ref[...], 1.0, 0.0).astype(jnp.bfloat16)
    pre = jnp.dot(hot, w_ref[...], preferred_element_type=jnp.float32)
    scale = lax.rsqrt(jnp.mean(pre * pre, axis=1, keepdims=True) + EPS)
    normed = pre * scale
    out_ref[...] = (normed * jax.nn.sigmoid(normed)).astype(jnp.bfloat16)


def features_call(step, core, pack, mine, other):
    rows = pack.shape[1]
    width = mine.shape[1]
    lane = jnp.arange(width, dtype=jnp.int32)
    is_lat = lane < LAT
    target = jnp.where(is_lat, lane % CLASSES, lane - LAT).astype(jnp.float32)[None, :]
    source = jnp.where(is_lat, step * STOCH + lane // CLASSES, IMAG * STOCH + step)
    spread = (jnp.arange(LANES, dtype=jnp.int32)[:, None] == source[None, :]).astype(jnp.bfloat16)
    return pl.pallas_call(
        features_kernel,
        grid=(NY,),
        in_specs=[
            pl.BlockSpec(memory_space=pltpu.SMEM),
            pl.BlockSpec((None, rows, LANES), lambda b: (b, 0, 0)),
            pl.BlockSpec((LANES, width), lambda b: (0, 0)),
            pl.BlockSpec((1, width), lambda b: (0, 0)),
            pl.BlockSpec((NX, width, LANES), lambda b: (0, 0, 0)),
            pl.BlockSpec((NX, width, LANES), lambda b: (0, 0, 0)),
        ],
        out_specs=pl.BlockSpec((None, rows, UNITS), lambda b: (b, 0, 0)),
        out_shape=jax.ShapeDtypeStruct((NY, rows, UNITS), jnp.bfloat16),
        scratch_shapes=[pltpu.VMEM((width, UNITS), jnp.bfloat16)],
        compiler_params=pltpu.CompilerParams(vmem_limit_bytes=32 * MIB),
        cost_estimate=pl.CostEstimate(
            flops=2 * NY * rows * width * (UNITS + LANES),
            bytes_accessed=NY * rows * UNITS * 2 + width * UNITS * 2,
            transcendentals=NY * rows * UNITS,
        ),
        name="features",
    )(core, pack, spread, target, mine, other)


def gru_kernel(deter_ref, w_rec_ref, w_in_ref, f_ref, new_ref, prior_ref):
    bw = deter_ref.shape[1]
    part = bw // NY
    rec = jnp.dot(deter_ref[...], w_rec_ref[...], preferred_element_type=jnp.float32)
    for q in range(NY):

        def gate(which):
            mine = f_ref[q, :, which * part : (which + 1) * part].astype(jnp.float32)
            return rec[:, which * bw + q * part : which * bw + (q + 1) * part] + mine

        reset = jax.nn.sigmoid(gate(0))
        candidate = jnp.tanh(reset * gate(1))
        update = jax.nn.sigmoid(gate(2) - 1.0)
        old = deter_ref[:, q * part : (q + 1) * part].astype(jnp.float32)
        fresh = update * candidate + (1.0 - update) * old
        new_ref[:, q * part : (q + 1) * part] = fresh.astype(jnp.bfloat16)
    prior_ref[...] = jnp.dot(new_ref[...], w_in_ref[...], preferred_element_type=jnp.float32).astype(jnp.bfloat16)


def gru_call(deter, w_rec, w_in, sums):
    rows, bw = deter.shape
    vmem = pl.BlockSpec(memory_space=pltpu.VMEM)
    return pl.pallas_call(
        gru_kernel,
        in_specs=[vmem] * 4,
        out_specs=[vmem, vmem],
        out_shape=[
            jax.ShapeDtypeStruct((rows, bw), jnp.bfloat16),
            jax.ShapeDtypeStruct((rows, w_in.shape[1]), jnp.bfloat16),
        ],
        compiler_params=pltpu.CompilerParams(vmem_limit_bytes=32 * MIB),
        cost_estimate=pl.CostEstimate(
            flops=2 * rows * bw * (3 * bw + w_in.shape[1]),
            bytes_accessed=2 * (w_rec.size + w_in.size) + 12 * rows * bw,
            transcendentals=3 * rows * bw,
        ),
        name="gru",
    )(deter, w_rec, w_in, sums)


def tail_kernel(p0_ref, p1_ref, w_out_ref, picked_ref, var_ref, mask_ref, log_ref):
    def hidden_of(ref):
        pre = ref[0].astype(jnp.float32)
        for i in range(1, ref.shape[0]):
            pre = pre + ref[i].astype(jnp.float32)
        normed = pre * lax.rsqrt(jnp.mean(pre * pre, axis=1, keepdims=True) + EPS)
        return (normed * jax.nn.sigmoid(normed)).astype(jnp.bfloat16)

    hidden = jnp.concatenate([hidden_of(p0_ref), hidden_of(p1_ref)], axis=0)
    rows = hidden.shape[0]
    cls = lax.broadcasted_iota(jnp.int32, (rows, LANES), 1) % CLASSES

    def within(value, combine):
        step = 1
        while step < CLASSES:
            ahead = pltpu.roll(value, step, 1)
            wrapped = pltpu.roll(value, LANES - CLASSES + step, 1)
            value = combine(value, jnp.where(cls >= step, ahead, wrapped))
            step *= 2
        return value

    total = jnp.zeros((rows, LANES), jnp.float32)
    for j in range(w_out_ref.shape[0]):
        logits = jnp.dot(hidden, w_out_ref[j], preferred_element_type=jnp.float32)
        powers = jnp.exp(logits - within(logits, jnp.maximum))
        probs = 0.99 * (powers / within(powers, jnp.add)) + 0.01 / CLASSES
        want = jnp.dot(picked_ref[...], var_ref[:, j * LANES : (j + 1) * LANES], preferred_element_type=jnp.float32)
        total = total + jnp.where(cls.astype(jnp.float32) == want, jnp.log(probs), 0.0)
    summed = jnp.where(mask_ref[...] > 0, jnp.sum(total, axis=1, keepdims=True), 0.0)
    diagonal = lax.broadcasted_iota(jnp.int32, (rows, rows), 0) == lax.broadcasted_iota(jnp.int32, (rows, rows), 1)
    log_ref[...] = jnp.sum(jnp.where(diagonal, summed, 0.0), axis=0, keepdims=True)


def tail_call(parts, w_out, picked, mask):
    rows = picked.shape[0]
    lane = jnp.arange(LAT, dtype=jnp.int32)
    var_of = (jnp.arange(STOCH, dtype=jnp.int32)[:, None] == lane[None, :] // CLASSES).astype(jnp.bfloat16)
    vmem = pl.BlockSpec(memory_space=pltpu.VMEM)
    return pl.pallas_call(
        tail_kernel,
        in_specs=[vmem] * 6,
        out_specs=vmem,
        out_shape=jax.ShapeDtypeStruct((1, rows), jnp.float32),
        compiler_params=pltpu.CompilerParams(vmem_limit_bytes=32 * MIB),
        cost_estimate=pl.CostEstimate(
            flops=2 * rows * UNITS * LAT, bytes_accessed=4 * w_out.size, transcendentals=4 * rows * LAT
        ),
        name="tail",
    )(parts[0], parts[1], w_out, picked, var_of, mask)


def body(
    post_deter,
    post_sample,
    samples,
    actions,
    counts,
    w_stoch,
    w_action,
    w_gate,
    w_rec,
    w_prior_in,
    w_prior_out,
    n_dp,
):
    rows = post_deter.shape[0]
    bw = w_rec.shape[1]
    part = bw // NY
    depth = w_gate.shape[0]
    tensor_n = NX * NC
    share = rows // tensor_n
    me = lax.axis_index("tensor")
    core = (me % NC).reshape(1).astype(jnp.int32)

    quarters = w_gate.reshape(depth * 3, NY, part).transpose(1, 0, 2)
    columns = [post_sample, samples[0]] + [actions[k][:, None] for k in range(IMAG)]
    pack = jnp.concatenate(columns, axis=1).astype(jnp.bfloat16)
    pack = jnp.pad(pack, ((0, 0), (0, LANES - pack.shape[1])))
    sent = jnp.concatenate([quarters, jnp.broadcast_to(pack[None], (NY,) + pack.shape)], axis=1)
    came = lax.all_to_all(sent, "dp", 0, 0, axis_index_groups=y_groups(n_dp))
    pack = came[:, depth * 3 :]
    held = came[:, : depth * 3].reshape(NY * depth, 3 * part)
    gate = lax.all_gather(held, "dp", axis=0, tiled=True, axis_index_groups=z_groups(n_dp))

    action_rows = jnp.pad(w_action, ((0, LANES - ACTIONS), (0, 0)))
    embed, _ = lax.optimization_barrier((jnp.concatenate([w_stoch, action_rows], axis=0), came))
    mine = spread_to(embed, "tensor", x_groups(), NX)
    other = core_swap(mine)

    w_out_late, _ = lax.optimization_barrier((w_prior_out, gate))
    w_out = lax.all_gather(w_out_late, "tensor", axis=0)

    positions = jnp.arange(STEPS, dtype=jnp.int32)
    valid_mask = (positions[None, :] < counts[:, None]).reshape(rows)
    my_mask = lax.dynamic_slice_in_dim(valid_mask, me * share, share, 0).astype(jnp.float32)
    my_mask = jnp.concatenate([my_mask] * IMAG)[:, None]
    picked = lax.dynamic_slice_in_dim(samples, me * share, share, 1)
    picked = picked.reshape(IMAG * share, STOCH).astype(jnp.bfloat16)

    sums = []
    for k in range(IMAG):
        features = features_call(k, core, pack, mine, other)
        total = jnp.dot(features.reshape(NY * rows, UNITS), gate, preferred_element_type=jnp.float32)
        total = total.astype(jnp.bfloat16).reshape(NY, rows, 3 * part)
        sums.append(lax.all_to_all(total, "dp", 0, 0, axis_index_groups=y_groups(n_dp)))

    deter = post_deter
    parts = []
    for k in range(IMAG):
        deter, partial = gru_call(deter, w_rec[0], w_prior_in, sums[k])
        parts.append(lax.all_to_all(partial.reshape(tensor_n, share, UNITS), "tensor", 0, 0))
    logs = tail_call(parts, w_out, picked, my_mask)
    logs = spread_to(logs.reshape(IMAG, share), "tensor", None, tensor_n)
    log_prob = logs.transpose(1, 0, 2).reshape(IMAG, rows)
    deter_out = jnp.where(valid_mask[:, None], deter, jnp.zeros_like(deter))
    return (deter_out, log_prob)


def solution(mesh):
    in_specs = (
        P("dp", "tensor"),
        P("dp", None),
        P(None, "dp", None),
        P(None, "dp"),
        P("dp"),
        P(None, "tensor"),
        P(None, "tensor"),
        P("dp", "tensor"),
        P("tensor", None, None),
        P("tensor", None),
        P(None, "tensor"),
    )
    out_specs = (P("dp", "tensor"), P(None, "dp"))
    whole = functools.partial(body, n_dp=mesh.shape["dp"])
    return jax.shard_map(whole, mesh=mesh, in_specs=in_specs, out_specs=out_specs, check_vma=False)
```

time: 270 us -> 176 us (0.65)
  waiting for transfers between devices: 169 us -> 32.8 us
  starting transfers between devices: 0.08 us -> 41 us
  Pallas kernels: 0 us -> 18.2 us
  blocking collectives: 61.7 us -> 51 us
  matrix products: 13.2 us -> 4.28 us
  local copies, waits for them, and re-layouts: 4.19 us -> 8.93 us
    all_gather x1, waiting for transfers between devices: 86.7 us -> 0.01 us  [body(): w_out = lax.all_gather(w_out_late, 'tensor', axis=0)]
    psum x1 -> x0, waiting for transfers between devices: 82 us -> none  [body(): summed = lax.psum(prior_pre, 'tensor')]
    all_to_all x0 -> x6, starting transfers between devices: none -> 33 us  [the longest x2 16.1 us: body(): lax.all_to_all(partial.reshape(tensor_n, share, UNITS), 'tensor', 0, 0)]
    all_to_all x0 -> x6, waiting for transfers between devices: none -> 32.8 us  [the longest x2 18.4 us: body(): lax.all_to_all(partial.reshape(tensor_n, share, UNITS), 'tensor', 0, 0)]
    psum x2 -> x0, blocking collectives: 32.8 us -> none  [the longest x1 18.6 us: body(): square_sum = lax.psum(jnp.sum(embed_pre * embed_pre, axis=1), 'tensor')]
    pallas_call x0 -> x5, Pallas kernels: none -> 18.2 us  [the longest x2 11 us: features_call(): pl.pallas_call(features_kernel, grid=(NY,), in_specs=[pl.BlockSpec(memory...]
    all_to_all x0 -> x1, blocking collectives: none -> 15.4 us  [spread_to(): return lax.all_to_all(copies, axis, 0, 0, axis_index_groups=groups)]
    dot_general x12 -> x2, matrix products: 13.2 us -> 4.28 us  [body(): jnp.dot(features.reshape(NY * rows, UNITS), gate, preferred_element_type=...]
  transfers between devices with their start and end apart: 2 -> 8, of which waited for: 2 -> 5; matrix products, arithmetic and copies ran while one was open for 4% -> 3% of each run, Pallas kernels for 0% -> 9%
where the time goes in v1:
time: 176 us; the launch traced here: 175 us
  blocking collectives  51 us (29%)
  starting transfers between devices  41 us (23%)
  waiting for transfers between devices  32.8 us (19%)
  Pallas kernels  18.2 us (10%)
  between operations  14.3 us (8%)
  local copies, waits for them, and re-layouts  8.93 us (5%)
  other arithmetic  4.86 us (3%)
  matrix products  4.28 us (2%)
    all_gather x1, blocking collectives, body(): lax.all_gather(held, 'dp', axis=0, tiled=True, axis_index_groups=z_groups...  35.6 us
    all_to_all x2, waiting for transfers between devices, body(): lax.all_to_all(partial.reshape(tensor_n, share, UNITS), 'tensor', 0, 0)  18.4 us
    all_to_all x2, starting transfers between devices, body(): lax.all_to_all(partial.reshape(tensor_n, share, UNITS), 'tensor', 0, 0)  16.1 us
    all_to_all x1, blocking collectives, spread_to(): return lax.all_to_all(copies, axis, 0, 0, axis_index_groups=groups)  15.4 us
    pallas_call x2, Pallas kernels, features_call(): pl.pallas_call(features_kernel, grid=(NY,), in_specs=[pl.BlockSpec(memory...  11 us
    ppermute x1, starting transfers between devices, core_swap(): return lax.ppermute(value, 'tensor', perm)  7.96 us
    all_to_all x2, starting transfers between devices, body(): lax.all_to_all(total, 'dp', 0, 0, axis_index_groups=y_groups(n_dp))  7.82 us
    all_to_all x1, waiting for transfers between devices, body(): came = lax.all_to_all(sent, 'dp', 0, 0, axis_index_groups=y_groups(n_dp))  5.75 us
  transfers between devices with their start and end apart: 8, of which 5 were waited for; matrix products, arithmetic and copies ran while one was open for 3% of the time, Pallas kernels for 9%

profile of v1, /device:TPU:1, one launch (start us, length us, event | category | flops | bytes accessed | tf_op | source)
XLA Modules:
  0.0 175.3 jit_solution(4869863139075777066)
XLA Ops:
  7.2 0.7 convert.20
  7.9 0.8 convert.18
  8.7 0.8 fusion.5
  9.6 0.8 reshape.153
  10.5 0.7 pad_maximum_fusion
  11.2 5.0 %all-to-all-start = ((bf16[4,304,128]{2,1,0:T(8,128)(2,1)}), bf16[4,304,128]{2,1,0:T(8,128)(2,1)S(1)}, u32[]{:S(2)}, u32[]{:S(2)}) async-start(bf16[4,304,128]{2,1,0:T(8,128)(2,1)} %pad_maximum_fusion), calls=%async_computation | async-start | bytes 622592 | tf_op jit(solution)/shard_map/all_to_all | solution.py:215
  16.3 5.8 %all-to-all-done = bf16[4,304,128]{2,1,0:T(8,128)(2,1)S(1)} async-done(((bf16[4,304,128]{2,1,0:T(8,128)(2,1)}), bf16[4,304,128]{2,1,0:T(8,128)(2,1)S(1)}, u32[]{:S(2)}, u32[]{:S(2)}) %all-to-all-start) | async-done | bytes 311328 | tf_op jit(solution)/shard_map/all_to_all | solution.py:215
  22.2 15.4 %all_to_all.35.mine_ref = bf16[4,1152,128]{2,1,0:T(8,128)(2,1)S(1)} all-to-all(bf16[4,1152,128]{2,1,0:T(8,128)(2,1)S(1)} %broadcast_in_dim.55), channel_id=1, replica_groups={{0,2,4,6},{1,3,5,7},{8,10,12,14},{9,11,13,15},{16,18,20,22},{17,19,21,2..., dimensions={0} | all-to-all | bytes 2359296 | tf_op jit(solution)/shard_map/all_to_all | solution.py:39
  37.6 8.0 %collective-permute-start = (bf16[4,1152,128]{2,1,0:T(8,128)(2,1)S(1)}, bf16[4,1152,128]{2,1,0:T(8,128)(2,1)S(1)}, u32[]{:S(2)}, u32[]{:S(2)}) collective-permute-start(bf16[4,1152,128]{2,1,0:T(8,128)(2,1)S(1)} %all_to_all.35.mine_ref), channel_id=1, source_target_pairs={{0,1},{1,0},{2,3},{3,2},{4,5},{5,4},{6,7},{7,6},{8,9},{9,8},{10,11... | collective-permute-start | bytes 3538952 | tf_op jit(solution)/shard_map/ppermute | solution.py:44
  45.7 35.6 %all_gather.9 = bf16[1024,384]{1,0:T(8,128)(2,1)} all-gather(bf16[64,384]{1,0:T(8,128)(2,1)S(1)} %reshape.155), channel_id=1, replica_groups={{0,32,64,96,128,160,192,224,256,288,320,352,384,416,448,480},{8,40,72,1..., dimensions={0}, use_global_device_ids=true | all-gather | bytes 835584 | tf_op jit(solution)/shard_map/all_gather | solution.py:218
  81.4 5.5 %features.2 = bf16[4,256,1024]{2,1,0:T(8,128)(2,1)S(1)} custom-call(s32[1]{0:T(128)} %bitcast.1.core_ref, bf16[4,256,128]{2,1,0:T(8,128)(2,1)S(1)} %slice.26.pack_ref, bf16[128,1152]{1,0:T(8,128)(2,1)S(1)} %fusion.spread_ref, f32[1,1152]{1,0:T(1,128)S(1)} %fusion.12.target_ref, bf16[4,1152,128]{2,1,0:T(8,128)(2,1)S(1)} %all_to_all.35.mine_ref, ...), custom_call_target="tpu_custom_call" | custom-call | flops 2717908992 | bytes 4456448 | tf_op jit(solution)/shard_map/features/pallas_call | solution.py:72
  86.9 2.1 %convolution_convert_fusion.1 = bf16[1024,384]{1,0:T(8,128)(2,1)} fusion(bf16[1024,1024]{1,0:T(8,128)(2,1)S(1)} %bitcast.31, bf16[1024,384]{1,0:T(8,128)(2,1)S(1)} %copy-done.8), kind=kOutput, calls=%fused_computation.1 | convolution fusion | flops 805699584 | bytes 3670016 | tf_op jit(solution)/shard_map/dot_general | solution.py:238
  89.1 3.5 %all-to-all-start.2 = ((bf16[4,256,384]{2,1,0:T(8,128)(2,1)}), bf16[4,256,384]{2,1,0:T(8,128)(2,1)S(1)}, u32[]{:S(2)}, u32[]{:S(2)}) async-start(bf16[4,256,384]{2,1,0:T(8,128)(2,1)} %bitcast.7), calls=%async_computation.2 | async-start | bytes 1572864 | tf_op jit(solution)/shard_map/all_to_all | solution.py:240
  92.6 1.3 copy-done.7
  93.9 5.5 %features.3 = bf16[4,256,1024]{2,1,0:T(8,128)(2,1)S(1)} custom-call(s32[1]{0:T(128)} %bitcast.1.core_ref, bf16[4,256,128]{2,1,0:T(8,128)(2,1)S(1)} %slice.26.pack_ref, bf16[128,1152]{1,0:T(8,128)(2,1)S(1)} %fusion.1.spread_ref, f32[1,1152]{1,0:T(1,128)S(1)} %fusion.12.target_ref, bf16[4,1152,128]{2,1,0:T(8,128)(2,1)S(1)} %all_to_all.35.mine_ref, ...), custom_call_target="tpu_custom_call" | custom-call | flops 2717908992 | bytes 4456448 | tf_op jit(solution)/shard_map/features/pallas_call | solution.py:72
  99.4 2.1 %convolution_convert_fusion = bf16[1024,384]{1,0:T(8,128)(2,1)} fusion(bf16[1024,1024]{1,0:T(8,128)(2,1)S(1)} %bitcast.30, bf16[1024,384]{1,0:T(8,128)(2,1)S(1)} %copy-done.9), kind=kOutput, calls=%fused_computation | convolution fusion | flops 805699584 | bytes 3670016 | tf_op jit(solution)/shard_map/dot_general | solution.py:238
  101.6 4.3 %all-to-all-start.3 = ((bf16[4,256,384]{2,1,0:T(8,128)(2,1)}), bf16[4,256,384]{2,1,0:T(8,128)(2,1)}, u32[]{:S(2)}, u32[]{:S(2)}) async-start(bf16[4,256,384]{2,1,0:T(8,128)(2,1)} %bitcast.32), calls=%async_computation.3 | async-start | bytes 1572864 | tf_op jit(solution)/shard_map/all_to_all | solution.py:240
  105.9 0.9 copy-done.3
  106.9 1.9 %gru.2 = (bf16[256,512]{1,0:T(8,128)(2,1)S(1)}, bf16[256,1024]{1,0:T(8,128)(2,1)}) custom-call(bf16[256,512]{1,0:T(8,128)(2,1)S(1)} %copy-done.3, bf16[512,1536]{1,0:T(8,128)(2,1)S(1)} %bitcast.26, bf16[512,1024]{1,0:T(8,128)(2,1)S(1)} %copy-done.1, bf16[4,256,384]{2,1,0:T(8,128)(2,1)S(1)} %all-to-all-done.2.f_ref), custom_call_target="tpu_custom_call" | custom-call | flops 671088640 | bytes 4194304 | tf_op jit(solution)/shard_map/gru/pallas_call | solution.py:118
  108.8 0.7 copy-done.4
  109.5 4.9 %all-to-all-done.3.f_ref = bf16[4,256,384]{2,1,0:T(8,128)(2,1)} async-done(((bf16[4,256,384]{2,1,0:T(8,128)(2,1)}), bf16[4,256,384]{2,1,0:T(8,128)(2,1)}, u32[]{:S(2)}, u32[]{:S(2)}) %all-to-all-start.3) | async-done | bytes 786464 | tf_op jit(solution)/shard_map/all_to_all | solution.py:240
  114.4 0.9 copy-done.5
  115.3 3.1 %gru.3 = (bf16[256,512]{1,0:T(8,128)(2,1)S(1)}, bf16[256,1024]{1,0:T(8,128)(2,1)}) custom-call(bf16[256,512]{1,0:T(8,128)(2,1)S(1)} %copy-done.5, bf16[512,1536]{1,0:T(8,128)(2,1)S(1)} %bitcast.27, bf16[512,1024]{1,0:T(8,128)(2,1)S(1)} %copy-done.1, bf16[4,256,384]{2,1,0:T(8,128)(2,1)} %all-to-all-done.3.f_ref), custom_call_target="tpu_custom_call" | custom-call | flops 671088640 | bytes 4194304 | tf_op jit(solution)/shard_map/gru/pallas_call | solution.py:118
  118.4 11.8 %all-to-all-start.5 = ((bf16[8,32,1024]{2,1,0:T(8,128)(2,1)}), bf16[8,32,1024]{2,1,0:T(8,128)(2,1)S(1)}, u32[]{:S(2)}, u32[]{:S(2)}) async-start(bf16[8,32,1024]{2,1,0:T(8,128)(2,1)} %bitcast.11), calls=%async_computation.5 | async-start | bytes 1048576 | tf_op jit(solution)/shard_map/all_to_all | solution.py:246
  130.4 9.3 %all-to-all-done.5.p1_ref = bf16[8,32,1024]{2,1,0:T(8,128)(2,1)S(1)} async-done(((bf16[8,32,1024]{2,1,0:T(8,128)(2,1)}), bf16[8,32,1024]{2,1,0:T(8,128)(2,1)S(1)}, u32[]{:S(2)}, u32[]{:S(2)}) %all-to-all-start.5) | async-done | bytes 524320 | tf_op jit(solution)/shard_map/all_to_all | solution.py:246
  139.7 4.3 %all-to-all-start.4 = ((bf16[8,32,1024]{2,1,0:T(8,128)(2,1)}), bf16[8,32,1024]{2,1,0:T(8,128)(2,1)S(1)}, u32[]{:S(2)}, u32[]{:S(2)}) async-start(bf16[8,32,1024]{2,1,0:T(8,128)(2,1)} %bitcast.10), calls=%async_computation.4 | async-start | bytes 1048576 | tf_op jit(solution)/shard_map/all_to_all | solution.py:246
  144.3 9.1 %all-to-all-done.4.p0_ref = bf16[8,32,1024]{2,1,0:T(8,128)(2,1)S(1)} async-done(((bf16[8,32,1024]{2,1,0:T(8,128)(2,1)}), bf16[8,32,1024]{2,1,0:T(8,128)(2,1)S(1)}, u32[]{:S(2)}, u32[]{:S(2)}) %all-to-all-start.4) | async-done | bytes 524320 | tf_op jit(solution)/shard_map/all_to_all | solution.py:246
  153.5 1.6 copy-done.2
  155.1 2.2 %tail.1 = f32[1,64]{1,0:T(1,128)S(1)} custom-call(bf16[8,32,1024]{2,1,0:T(8,128)(2,1)S(1)} %all-to-all-done.4.p0_ref, bf16[8,32,1024]{2,1,0:T(8,128)(2,1)S(1)} %all-to-all-done.5.p1_ref, bf16[8,1024,128]{2,1,0:T(8,128)(2,1)S(1)} %bitcast.28, bf16[64,32]{1,0:T(8,128)(2,1)S(1)} %bitcast.29, bf16[32,1024]{1,0:T(8,128)(2,1)S(1)} %fusion.4.var_ref, ...), custom_call_target="tpu_custom_call" | custom-call | flops 134217728 | bytes 4194304 | tf_op jit(solution)/shard_map/tail/pallas_call | solution.py:174
  159.1 4.1 %all-to-all-start.6 = ((f32[8,2,32]{2,1,0:T(2,128)}), f32[8,2,32]{2,1,0:T(2,128)S(1)}, u32[]{:S(2)}, u32[]{:S(2)}) async-start(f32[8,2,32]{2,1,0:T(2,128)} %broadcast_in_dim.61), calls=%async_computation.6 | async-start | bytes 16384 | tf_op jit(solution)/shard_map/all_to_all | solution.py:39
  163.2 0.8 broadcast_select_fusion
  164.0 3.8 %all-to-all-done.6 = f32[8,2,32]{2,1,0:T(2,128)S(1)} async-done(((f32[8,2,32]{2,1,0:T(2,128)}), f32[8,2,32]{2,1,0:T(2,128)S(1)}, u32[]{:S(2)}, u32[]{:S(2)}) %all-to-all-start.6) | async-done | bytes 2080 | tf_op jit(solution)/shard_map/all_to_all | solution.py:39
  (59 shorter events, 3.8 us)
Async XLA Ops:
  7.2 9.1 %copy-start.10 = (bf16[1024,128]{1,0:T(8,128)(2,1)S(1)}, bf16[1024,128]{1,0:T(8,128)(2,1)}, u32[]{:S(2)}) copy-start(bf16[1024,128]{1,0:T(8,128)(2,1)} %param.16) | copy-start | bytes 786436
  7.2 9.1 %copy-start.12 = (bf16[18,128]{1,0:T(8,128)(2,1)S(1)}, bf16[18,128]{1,0:T(8,128)(2,1)}, u32[]{:S(2)}) copy-start(bf16[18,128]{1,0:T(8,128)(2,1)} %param.17) | copy-start | bytes 13828
  11.2 10.8 %all-to-all-start = ((bf16[4,304,128]{2,1,0:T(8,128)(2,1)}), bf16[4,304,128]{2,1,0:T(8,128)(2,1)S(1)}, u32[]{:S(2)}, u32[]{:S(2)}) async-start(bf16[4,304,128]{2,1,0:T(8,128)(2,1)} %pad_maximum_fusion), calls=%async_computation | async-start | bytes 622592 | tf_op jit(solution)/shard_map/all_to_all | solution.py:215
  16.2 137.2 %all-gather.3.cloned.1.call-start = ((), (), s32[]{:S(2)}) async-start(), calls=%async_computation.7 | async-start | bytes 2359296 | tf_op jit(solution)/shard_map/all_gather | solution.py:226
  37.6 43.8 %collective-permute-start = (bf16[4,1152,128]{2,1,0:T(8,128)(2,1)S(1)}, bf16[4,1152,128]{2,1,0:T(8,128)(2,1)S(1)}, u32[]{:S(2)}, u32[]{:S(2)}) collective-permute-start(bf16[4,1152,128]{2,1,0:T(8,128)(2,1)S(1)} %all_to_all.35.mine_ref), channel_id=1, source_target_pairs={{0,1},{1,0},{2,3},{3,2},{4,5},{5,4},{6,7},{7,6},{8,9},{9,8},{10,11... | collective-permute-start | bytes 3538952 | tf_op jit(solution)/shard_map/ppermute | solution.py:44
  81.4 5.5 %copy-start.6 = (bf16[4,1152,128]{2,1,0:T(8,128)(2,1)}, bf16[4,1152,128]{2,1,0:T(8,128)(2,1)S(1)}, u32[]{:S(2)}) copy-start(bf16[4,1152,128]{2,1,0:T(8,128)(2,1)S(1)} %collective-permute-done.other_ref) | copy-start | bytes 3538948
  81.4 5.5 %copy-start.8 = (bf16[1024,384]{1,0:T(8,128)(2,1)S(1)}, bf16[1024,384]{1,0:T(8,128)(2,1)}, u32[]{:S(2)}) copy-start(bf16[1024,384]{1,0:T(8,128)(2,1)} %all_gather.9) | copy-start | bytes 2359300
  89.1 12.5 %all-to-all-start.2 = ((bf16[4,256,384]{2,1,0:T(8,128)(2,1)}), bf16[4,256,384]{2,1,0:T(8,128)(2,1)S(1)}, u32[]{:S(2)}, u32[]{:S(2)}) async-start(bf16[4,256,384]{2,1,0:T(8,128)(2,1)} %bitcast.7), calls=%async_computation.2 | async-start | bytes 1572864 | tf_op jit(solution)/shard_map/all_to_all | solution.py:240
  92.6 1.3 copy-start.7
  93.9 5.5 %copy-start.9 = (bf16[1024,384]{1,0:T(8,128)(2,1)S(1)}, bf16[1024,384]{1,0:T(8,128)(2,1)}, u32[]{:S(2)}) copy-start(bf16[1024,384]{1,0:T(8,128)(2,1)} %all_gather.9) | copy-start | bytes 2359300
  99.4 6.5 %copy-start.1 = (bf16[512,1024]{1,0:T(8,128)(2,1)S(1)}, bf16[512,1024]{1,0:T(8,128)(2,1)}, u32[]{:S(2)}) copy-start(bf16[512,1024]{1,0:T(8,128)(2,1)} %w_in_ref.3) | copy-start | bytes 3145732
  101.6 4.3 %copy-start = (bf16[1,512,1536]{2,1,0:T(8,128)(2,1)S(1)}, bf16[1,512,1536]{2,1,0:T(8,128)(2,1)}, u32[]{:S(2)}) copy-start(bf16[1,512,1536]{2,1,0:T(8,128)(2,1)} %param.19) | copy-start | bytes 4718596
  101.6 12.8 %all-to-all-start.3 = ((bf16[4,256,384]{2,1,0:T(8,128)(2,1)}), bf16[4,256,384]{2,1,0:T(8,128)(2,1)}, u32[]{:S(2)}, u32[]{:S(2)}) async-start(bf16[4,256,384]{2,1,0:T(8,128)(2,1)} %bitcast.32), calls=%async_computation.3 | async-start | bytes 1572864 | tf_op jit(solution)/shard_map/all_to_all | solution.py:240
  105.9 1.0 copy-start.3
  108.8 0.7 copy-start.4
  114.3 1.0 copy-start.5
  115.3 14.9 %copy-start.13 = (s32[4]{0:T(128)S(1)}, s32[4]{0:T(128)}, u32[]{:S(2)}) copy-start(s32[4]{0:T(128)} %param.15) | copy-start | bytes 52
  115.3 28.8 %copy-start.11 = (s32[2,256,32]{1,2,0:T(8,128)S(1)}, s32[2,256,32]{1,2,0:T(8,128)}, u32[]{:S(2)}) copy-start(s32[2,256,32]{1,2,0:T(8,128)} %param.13) | copy-start | bytes 196612
  118.4 21.3 %all-to-all-start.5 = ((bf16[8,32,1024]{2,1,0:T(8,128)(2,1)}), bf16[8,32,1024]{2,1,0:T(8,128)(2,1)S(1)}, u32[]{:S(2)}, u32[]{:S(2)}) async-start(bf16[8,32,1024]{2,1,0:T(8,128)(2,1)} %bitcast.11), calls=%async_computation.5 | async-start | bytes 1048576 | tf_op jit(solution)/shard_map/all_to_all | solution.py:246
  139.7 13.8 %all-to-all-start.4 = ((bf16[8,32,1024]{2,1,0:T(8,128)(2,1)}), bf16[8,32,1024]{2,1,0:T(8,128)(2,1)S(1)}, u32[]{:S(2)}, u32[]{:S(2)}) async-start(bf16[8,32,1024]{2,1,0:T(8,128)(2,1)} %bitcast.10), calls=%async_computation.4 | async-start | bytes 1048576 | tf_op jit(solution)/shard_map/all_to_all | solution.py:246
  153.5 1.6 copy-start.2
  159.1 8.7 %all-to-all-start.6 = ((f32[8,2,32]{2,1,0:T(2,128)}), f32[8,2,32]{2,1,0:T(2,128)S(1)}, u32[]{:S(2)}, u32[]{:S(2)}) async-start(f32[8,2,32]{2,1,0:T(2,128)} %broadcast_in_dim.61), calls=%async_computation.6 | async-start | bytes 16384 | tf_op jit(solution)/shard_map/all_to_all | solution.py:39
Sparse Core Ops, SparseCore 0:
  81.4 31.4 all-gather.2

commit v2 on v1

v2 whole, which is shorter than its diff:
```python
import functools

import jax
import jax.numpy as jnp
from jax import lax
from jax.experimental import pallas as pl
from jax.experimental.pallas import tpu as pltpu
from jax.sharding import PartitionSpec as P

STOCH = 32
CLASSES = 32
LAT = STOCH * CLASSES
ACTIONS = 18
STEPS = 64
IMAG = 2
UNITS = 1024
NY = 4
NX = 4
NC = 2
LANES = 128
EPS = 1e-06
MIB = 1024 * 1024


def y_groups(n_dp):
    return [[start + y for y in range(NY)] for start in range(0, n_dp, NY)]


def y_shift(value, step, n_dp):
    perm = [(i, i // NY * NY + (i % NY + step) % NY) for i in range(n_dp)]
    return lax.ppermute(value, "dp", perm)


def x_shift(value, step):
    count = NX * NC
    perm = [(i, (i + step * NC) % count) for i in range(count)]
    return lax.ppermute(value, "tensor", perm)


def core_swap(value):
    perm = [(i, i ^ 1) for i in range(NX * NC)]
    return lax.ppermute(value, "tensor", perm)


def tensor_gather(value):
    mine = jnp.stack([value] + [x_shift(value, step) for step in range(1, NX)])
    return mine, core_swap(mine)


def split_kernel(w_ref, out_ref):
    part = w_ref.shape[1] // 3 // NY
    for y in range(NY):
        for which in range(3):
            columns = w_ref[:, (which * NY + y) * part : (which * NY + y + 1) * part]
            for z in range(out_ref.shape[0]):
                out_ref[z, y, :, which * part : (which + 1) * part] = columns


def split_call(w_gate, n_z):
    depth, width = w_gate.shape
    vmem = pl.BlockSpec(memory_space=pltpu.VMEM)
    return pl.pallas_call(
        split_kernel,
        in_specs=[vmem],
        out_specs=vmem,
        out_shape=jax.ShapeDtypeStruct((n_z, NY, depth, width // NY), w_gate.dtype),
        compiler_params=pltpu.CompilerParams(vmem_limit_bytes=16 * MIB),
        cost_estimate=pl.CostEstimate(flops=0, bytes_accessed=2 * n_z * depth * width, transcendentals=0),
        name="split",
    )(w_gate)


def features_kernel(me_ref, pack_ref, spread_ref, target_ref, mine_ref, other_ref, out_ref, w_ref):
    @pl.when(pl.program_id(0) == 0)
    def _():
        x, core = me_ref[0], me_ref[1]
        for i in range(NX):
            base = lax.rem(x + NX - i, NX) * NC
            w_ref[:, pl.ds(pl.multiple_of((base + core) * LANES, LANES), LANES)] = mine_ref[i]
            w_ref[:, pl.ds(pl.multiple_of((base + 1 - core) * LANES, LANES), LANES)] = other_ref[i]

    for k in range(IMAG):
        spread = jnp.dot(pack_ref[...], spread_ref[k], preferred_element_type=jnp.float32)
        hot = jnp.where(spread == target_ref[...], 1.0, 0.0).astype(jnp.bfloat16)
        pre = jnp.dot(hot, w_ref[...], preferred_element_type=jnp.float32)
        scale = lax.rsqrt(jnp.mean(pre * pre, axis=1, keepdims=True) + EPS)
        normed = pre * scale
        out_ref[k] = (normed * jax.nn.sigmoid(normed)).astype(jnp.bfloat16)


def features_call(place, pack, mine, other):
    rows = pack.shape[1]
    width = mine.shape[1]
    lane = jnp.arange(width, dtype=jnp.int32)
    is_lat = lane < LAT
    target = jnp.where(is_lat, lane % CLASSES, lane - LAT).astype(jnp.float32)[None, :]
    step = jnp.arange(IMAG, dtype=jnp.int32)[:, None]
    source = jnp.where(is_lat[None, :], step * STOCH + lane[None, :] // CLASSES, IMAG * STOCH + step)
    spread = (jnp.arange(LANES, dtype=jnp.int32)[None, :, None] == source[:, None, :]).astype(jnp.bfloat16)
    return pl.pallas_call(
        features_kernel,
        grid=(NY,),
        in_specs=[
            pl.BlockSpec(memory_space=pltpu.SMEM),
            pl.BlockSpec((None, rows, LANES), lambda b: (b, 0, 0)),
            pl.BlockSpec((IMAG, LANES, width), lambda b: (0, 0, 0)),
            pl.BlockSpec((1, width), lambda b: (0, 0)),
            pl.BlockSpec((NX, width, LANES), lambda b: (0, 0, 0)),
            pl.BlockSpec((NX, width, LANES), lambda b: (0, 0, 0)),
        ],
        out_specs=pl.BlockSpec((IMAG, None, rows, UNITS), lambda b: (0, b, 0, 0)),
        out_shape=jax.ShapeDtypeStruct((IMAG, NY, rows, UNITS), jnp.bfloat16),
        scratch_shapes=[pltpu.VMEM((width, UNITS), jnp.bfloat16)],
        compiler_params=pltpu.CompilerParams(vmem_limit_bytes=32 * MIB),
        cost_estimate=pl.CostEstimate(
            flops=2 * IMAG * NY * rows * width * (UNITS + LANES),
            bytes_accessed=IMAG * NY * rows * UNITS * 2 + width * UNITS * 2,
            transcendentals=IMAG * NY * rows * UNITS,
        ),
        name="features",
    )(place, pack, spread, target, mine, other)


def gate_kernel(features_ref, gate_ref, out_ref):
    for k in range(IMAG):
        out_ref[k] = jnp.dot(features_ref[k], gate_ref[...], preferred_element_type=jnp.float32).astype(jnp.bfloat16)


def gate_call(features, gate):
    rows = features.shape[2]
    width = gate.shape[1]
    return pl.pallas_call(
        gate_kernel,
        grid=(NY,),
        in_specs=[
            pl.BlockSpec((IMAG, None, rows, UNITS), lambda b: (0, b, 0, 0)),
            pl.BlockSpec((UNITS, width), lambda b: (0, 0)),
        ],
        out_specs=pl.BlockSpec((None, IMAG, rows, width), lambda b: (b, 0, 0, 0)),
        out_shape=jax.ShapeDtypeStruct((NY, IMAG, rows, width), jnp.bfloat16),
        compiler_params=pltpu.CompilerParams(vmem_limit_bytes=32 * MIB),
        cost_estimate=pl.CostEstimate(
            flops=2 * IMAG * NY * rows * UNITS * width,
            bytes_accessed=IMAG * NY * rows * (UNITS + width) * 2 + UNITS * width * 2,
            transcendentals=0,
        ),
        name="gate",
    )(features, gate)


def gru_kernel(deter_ref, w_rec_ref, w_in_ref, f_ref, new_ref, prior_ref, mid_ref):
    rows, bw = deter_ref.shape
    part = bw // NY
    for k in range(IMAG):
        old_ref = deter_ref if k == 0 else mid_ref
        next_ref = new_ref if k == IMAG - 1 else mid_ref
        old = old_ref[...]
        rec = jnp.dot(old, w_rec_ref[...], preferred_element_type=jnp.float32)
        for q in range(NY):

            def gate(which):
                mine = f_ref[q, k, :, which * part : (which + 1) * part].astype(jnp.float32)
                return rec[:, which * bw + q * part : which * bw + (q + 1) * part] + mine

            reset = jax.nn.sigmoid(gate(0))
            candidate = jnp.tanh(reset * gate(1))
            update = jax.nn.sigmoid(gate(2) - 1.0)
            before = old[:, q * part : (q + 1) * part].astype(jnp.float32)
            fresh = update * candidate + (1.0 - update) * before
            next_ref[:, q * part : (q + 1) * part] = fresh.astype(jnp.bfloat16)
        prior = jnp.dot(next_ref[...], w_in_ref[...], preferred_element_type=jnp.float32).astype(jnp.bfloat16)
        share = prior_ref.shape[2]
        for j in range(prior_ref.shape[0]):
            prior_ref[j, k] = prior[j * share : (j + 1) * share]


def gru_call(deter, w_rec, w_in, sums, tensor_n):
    rows, bw = deter.shape
    vmem = pl.BlockSpec(memory_space=pltpu.VMEM)
    return pl.pallas_call(
        gru_kernel,
        in_specs=[vmem] * 4,
        out_specs=[vmem, vmem],
        out_shape=[
            jax.ShapeDtypeStruct((rows, bw), jnp.bfloat16),
            jax.ShapeDtypeStruct((tensor_n, IMAG, rows // tensor_n, w_in.shape[1]), jnp.bfloat16),
        ],
        scratch_shapes=[pltpu.VMEM((rows, bw), jnp.bfloat16)],
        compiler_params=pltpu.CompilerParams(vmem_limit_bytes=32 * MIB),
        cost_estimate=pl.CostEstimate(
            flops=2 * IMAG * rows * bw * (3 * bw + w_in.shape[1]),
            bytes_accessed=2 * (w_rec.size + w_in.size) + 24 * rows * bw,
            transcendentals=6 * rows * bw,
        ),
        name="gru",
    )(deter, w_rec, w_in, sums)


def tail_kernel(me_ref, parts_ref, mine_ref, other_ref, picked_ref, var_ref, mask_ref, log_ref):
    pre = parts_ref[0].astype(jnp.float32)
    for i in range(1, parts_ref.shape[0]):
        pre = pre + parts_ref[i].astype(jnp.float32)
    normed = pre * lax.rsqrt(jnp.mean(pre * pre, axis=1, keepdims=True) + EPS)
    hidden = (normed * jax.nn.sigmoid(normed)).astype(jnp.bfloat16)
    rows = hidden.shape[0]
    cls = lax.broadcasted_iota(jnp.int32, (rows, LANES), 1) % CLASSES

    def within(value, combine):
        step = 1
        while step < CLASSES:
            ahead = pltpu.roll(value, step, 1)
            wrapped = pltpu.roll(value, LANES - CLASSES + step, 1)
            value = combine(value, jnp.where(cls >= step, ahead, wrapped))
            step *= 2
        return value

    total = jnp.zeros((rows, LANES), jnp.float32)
    x, core = me_ref[0], me_ref[1]
    for i in range(NX * NC):
        w_ref = mine_ref if i % NC == 0 else other_ref
        piece = lax.rem(x + NX - i // NC, NX) * NC + (core if i % NC == 0 else 1 - core)
        here = pl.ds(pl.multiple_of(piece * LANES, LANES), LANES)
        logits = jnp.dot(hidden, w_ref[i // NC], preferred_element_type=jnp.float32)
        powers = jnp.exp(logits - within(logits, jnp.maximum))
        probs = 0.99 * (powers / within(powers, jnp.add)) + 0.01 / CLASSES
        want = jnp.dot(picked_ref[...], var_ref[:, here], preferred_element_type=jnp.float32)
        total = total + jnp.where(cls.astype(jnp.float32) == want, jnp.log(probs), 0.0)
    summed = jnp.where(mask_ref[...] > 0, jnp.sum(total, axis=1, keepdims=True), 0.0)
    lanes = lax.broadcasted_iota(jnp.int32, (rows, LANES), 1)
    diagonal = lax.broadcasted_iota(jnp.int32, (rows, LANES), 0) == lanes
    line = jnp.sum(jnp.where(diagonal, summed, 0.0), axis=0, keepdims=True)
    log_ref[...] = jnp.broadcast_to(line[None], log_ref.shape)


def tail_call(place, parts, mine, other, picked, mask):
    tensor_n, rows = parts.shape[:2]
    lane = jnp.arange(LAT, dtype=jnp.int32)
    var_of = (jnp.arange(STOCH, dtype=jnp.int32)[:, None] == lane[None, :] // CLASSES).astype(jnp.bfloat16)
    vmem = pl.BlockSpec(memory_space=pltpu.VMEM)
    return pl.pallas_call(
        tail_kernel,
        in_specs=[pl.BlockSpec(memory_space=pltpu.SMEM)] + [vmem] * 6,
        out_specs=vmem,
        out_shape=jax.ShapeDtypeStruct((tensor_n, 8, LANES), jnp.float32),
        compiler_params=pltpu.CompilerParams(vmem_limit_bytes=32 * MIB),
        cost_estimate=pl.CostEstimate(
            flops=2 * rows * UNITS * LAT, bytes_accessed=8 * mine.size, transcendentals=4 * rows * LAT
        ),
        name="tail",
    )(place, parts, mine, other, picked, var_of, mask)


def body(
    post_deter,
    post_sample,
    samples,
    actions,
    counts,
    w_stoch,
    w_action,
    w_gate,
    w_rec,
    w_prior_in,
    w_prior_out,
    n_dp,
):
    rows = post_deter.shape[0]
    depth = w_gate.shape[0]
    tensor_n = NX * NC
    share = rows // tensor_n
    me = lax.axis_index("tensor")
    place = jnp.stack([me // NC, me % NC]).astype(jnp.int32)

    sent = split_call(w_gate, n_dp // NY)
    gate = lax.all_to_all(sent.reshape(n_dp, depth, -1), "dp", 0, 0).reshape(n_dp * depth, -1)

    action_rows = jnp.pad(w_action, ((0, LANES - ACTIONS), (0, 0)))
    mine, other = tensor_gather(jnp.concatenate([w_stoch, action_rows], axis=0))

    columns = [post_sample, samples[0]] + [actions[k][:, None] for k in range(IMAG)]
    pack = jnp.concatenate(columns, axis=1).astype(jnp.bfloat16)
    pack = jnp.pad(pack, ((0, 0), (0, LANES - pack.shape[1])))
    pack = jnp.stack([pack] + [y_shift(pack, b, n_dp) for b in range(1, NY)])
    y = lax.axis_index("dp") % NY
    pack = jnp.stack([lax.dynamic_index_in_dim(pack, (y - b + NY) % NY, 0, keepdims=False) for b in range(NY)])

    features = features_call(place, pack, mine, other)
    sums = lax.all_to_all(gate_call(features, gate), "dp", 0, 0, axis_index_groups=y_groups(n_dp))

    w_out_late, _ = lax.optimization_barrier((w_prior_out, features))
    out_mine, out_other = tensor_gather(w_out_late)

    positions = jnp.arange(STEPS, dtype=jnp.int32)
    valid_mask = (positions[None, :] < counts[:, None]).reshape(rows)
    my_mask = lax.dynamic_slice_in_dim(valid_mask, me * share, share, 0).astype(jnp.float32)
    my_mask = jnp.concatenate([my_mask] * IMAG)[:, None]
    picked = lax.dynamic_slice_in_dim(samples, me * share, share, 1)
    picked = picked.reshape(IMAG * share, STOCH).astype(jnp.bfloat16)

    deter, partial = gru_call(post_deter, w_rec[0], w_prior_in, sums, tensor_n)
    parts = lax.all_to_all(partial.reshape(tensor_n, IMAG * share, UNITS), "tensor", 0, 0)
    logs = tail_call(place, parts, out_mine, out_other, picked, my_mask)
    logs = lax.all_to_all(logs, "tensor", 0, 0)[:, 0, : IMAG * share]
    log_prob = logs.reshape(tensor_n, IMAG, share).transpose(1, 0, 2).reshape(IMAG, rows)
    deter_out = jnp.where(valid_mask[:, None], deter, jnp.zeros_like(deter))
    return (deter_out, log_prob)


def solution(mesh):
    in_specs = (
        P("dp", "tensor"),
        P("dp", None),
        P(None, "dp", None),
        P(None, "dp"),
        P("dp"),
        P(None, "tensor"),
        P(None, "tensor"),
        P("dp", "tensor"),
        P("tensor", None, None),
        P("tensor", None),
        P(None, "tensor"),
    )
    out_specs = (P("dp", "tensor"), P(None, "dp"))
    whole = functools.partial(body, n_dp=mesh.shape["dp"])
    return jax.shard_map(whole, mesh=mesh, in_specs=in_specs, out_specs=out_specs, check_vma=False)
```

time: 176 us -> 147 us (0.84)
  blocking collectives: 51 us -> 0 us
  starting transfers between devices: 41 us -> 68.3 us
  between operations: 14.3 us -> 1.07 us
  waiting for transfers between devices: 32.8 us -> 40 us
  matrix products: 4.28 us -> 0 us
  Pallas kernels: 18.2 us -> 21.2 us
    all_gather x1 -> x0, blocking collectives: 35.6 us -> none  [body(): lax.all_gather(held, 'dp', axis=0, tiled=True, axis_index_groups=z_groups...]
    ppermute x0 -> x9, starting transfers between devices: none -> 29 us  [the longest x6 18.8 us: x_shift(): return lax.ppermute(value, 'tensor', perm)]
    ppermute x0 -> x9, waiting for transfers between devices: none -> 20.7 us  [the longest x6 20.7 us: x_shift(): return lax.ppermute(value, 'tensor', perm)]
    all_to_all x1 -> x0, blocking collectives: 15.4 us -> none  [spread_to(): return lax.all_to_all(copies, axis, 0, 0, axis_index_groups=groups)]
    all_to_all x6 -> x4, waiting for transfers between devices: 32.8 us -> 18.4 us  [the longest x1 14.4 us: body(): lax.all_to_all(partial.reshape(tensor_n, IMAG * share, UNITS), 'tensor',...]
    pallas_call x1 -> x3, Pallas kernels: 2.21 us -> 8.99 us  [the longest x1 4.06 us: tail_call(): pl.pallas_call(tail_kernel, in_specs=[pl.BlockSpec(memory_space=pltpu.SME...]
    dot_general x2 -> x0, matrix products: 4.28 us -> none  [body(): jnp.dot(features.reshape(NY * rows, UNITS), gate, preferred_element_type=...]
    unnamed x29 -> x25, local copies, waits for them, and re-layouts: 5.62 us -> 8.67 us
  transfers between devices with their start and end apart: 8 -> 15, of which waited for: 5 -> 8; matrix products, arithmetic and copies ran while one was open for 3% -> 2% of each run, Pallas kernels for 9% -> 9%
where the time goes in v2:
time: 147 us; the launch traced here: 146 us
  starting transfers between devices  68.3 us (46%)
  waiting for transfers between devices  40 us (27%)
  Pallas kernels  21.2 us (14%)
  local copies, waits for them, and re-layouts  10.2 us (7%)
  other arithmetic  5.11 us (3%)
    ppermute x6, waiting for transfers between devices, x_shift(): return lax.ppermute(value, 'tensor', perm)  20.7 us
    ppermute x6, starting transfers between devices, x_shift(): return lax.ppermute(value, 'tensor', perm)  18.8 us
    all_to_all x1, starting transfers between devices, body(): lax.all_to_all(sent.reshape(n_dp, depth, -1), 'dp', 0, 0)  18.2 us
    all_to_all x1, waiting for transfers between devices, body(): lax.all_to_all(partial.reshape(tensor_n, IMAG * share, UNITS), 'tensor',...  14.4 us
    ppermute x3, starting transfers between devices, y_shift(): return lax.ppermute(value, 'dp', perm)  10.2 us
    pallas_call x1, Pallas kernels, features_call(): pl.pallas_call(features_kernel, grid=(NY,), in_specs=[pl.BlockSpec(memory...  10.2 us
    unnamed x25, local copies, waits for them, and re-layouts  8.67 us
    ppermute x2, starting transfers between devices, core_swap(): return lax.ppermute(value, 'tensor', perm)  7.5 us
  transfers between devices with their start and end apart: 15, of which 8 were waited for; matrix products, arithmetic and copies ran while one was open for 2% of the time, Pallas kernels for 9%

profile of v2, /device:TPU:1, one launch (start us, length us, event | category | flops | bytes accessed | tf_op | source)
XLA Modules:
  0.0 145.9 jit_solution(2899449070557727368)
XLA Ops:
  3.5 5.5 %collective-permute-start.2 = (bf16[256,128]{1,0:T(8,128)(2,1)S(1)}, bf16[256,128]{1,0:T(8,128)(2,1)}, u32[]{:S(2)}, u32[]{:S(2)}) collective-permute-start(bf16[256,128]{1,0:T(8,128)(2,1)S(1)} %fusion.10), channel_id=1, source_target_pairs={{0,24},{8,0},{16,8},{24,16},{32,56},{40,32},{48,40},{56,48},{64,88... | collective-permute-start | bytes 196616 | tf_op jit(solution)/shard_map/ppermute | solution.py:31
  9.0 2.3 %collective-permute-start.1 = (bf16[256,128]{1,0:T(8,128)(2,1)S(1)}, bf16[256,128]{1,0:T(8,128)(2,1)}, u32[]{:S(2)}, u32[]{:S(2)}) collective-permute-start(bf16[256,128]{1,0:T(8,128)(2,1)S(1)} %fusion.10), channel_id=1, source_target_pairs={{0,16},{8,24},{16,0},{24,8},{32,48},{40,56},{48,32},{56,40},{64,80... | collective-permute-start | bytes 196616 | tf_op jit(solution)/shard_map/ppermute | solution.py:31
  12.1 1.0 split.1
  13.1 18.2 %all-to-all-start = ((bf16[64,16,384]{2,1,0:T(8,128)(2,1)}), bf16[64,16,384]{2,1,0:T(8,128)(2,1)S(1)}, u32[]{:S(2)}, u32[]{:S(2)}) async-start(bf16[64,16,384]{2,1,0:T(8,128)(2,1)} %bitcast.14), calls=%async_computation | async-start | bytes 1572864 | tf_op jit(solution)/shard_map/all_to_all | solution.py:275
  31.4 4.4 %collective-permute-start.5 = (bf16[1152,128]{1,0:T(8,128)(2,1)S(1)}, bf16[1152,128]{1,0:T(8,128)(2,1)S(1)}, u32[]{:S(2)}, u32[]{:S(2)}) collective-permute-start(bf16[1152,128]{1,0:T(8,128)(2,1)S(1)} %get-tuple-element.9), channel_id=1, source_target_pairs={{0,6},{1,7},{2,0},{3,1},{4,2},{5,3},{6,4},{7,5},{8,14},{9,15},{10,... | collective-permute-start | bytes 884744 | tf_op jit(solution)/shard_map/ppermute | solution.py:37
  35.8 2.4 %collective-permute-start.4 = (bf16[1152,128]{1,0:T(8,128)(2,1)S(1)}, bf16[1152,128]{1,0:T(8,128)(2,1)S(1)}, u32[]{:S(2)}, u32[]{:S(2)}) collective-permute-start(bf16[1152,128]{1,0:T(8,128)(2,1)S(1)} %get-tuple-element.9), channel_id=1, source_target_pairs={{0,4},{1,5},{2,6},{3,7},{4,0},{5,1},{6,2},{7,3},{8,12},{9,13},{10,... | collective-permute-start | bytes 884744 | tf_op jit(solution)/shard_map/ppermute | solution.py:37
  38.2 2.5 %collective-permute-start.3 = (bf16[1152,128]{1,0:T(8,128)(2,1)S(1)}, bf16[1152,128]{1,0:T(8,128)(2,1)S(1)}, u32[]{:S(2)}, u32[]{:S(2)}) collective-permute-start(bf16[1152,128]{1,0:T(8,128)(2,1)S(1)} %get-tuple-element.9), channel_id=1, source_target_pairs={{0,2},{1,3},{2,4},{3,5},{4,6},{5,7},{6,0},{7,1},{8,10},{9,11},{10,... | collective-permute-start | bytes 884744 | tf_op jit(solution)/shard_map/ppermute | solution.py:37
  41.3 2.5 %collective-permute-start = (bf16[256,128]{1,0:T(8,128)(2,1)S(1)}, bf16[256,128]{1,0:T(8,128)(2,1)}, u32[]{:S(2)}, u32[]{:S(2)}) collective-permute-start(bf16[256,128]{1,0:T(8,128)(2,1)S(1)} %fusion.10), channel_id=1, source_target_pairs={{0,8},{8,16},{16,24},{24,0},{32,40},{40,48},{48,56},{56,32},{64,72... | collective-permute-start | bytes 196616 | tf_op jit(solution)/shard_map/ppermute | solution.py:31
  43.8 2.1 %collective-permute-done.4 = bf16[1152,128]{1,0:T(8,128)(2,1)S(1)} collective-permute-done((bf16[1152,128]{1,0:T(8,128)(2,1)S(1)}, bf16[1152,128]{1,0:T(8,128)(2,1)S(1)}, u32[]{:S(2)}, u32[]{:S(2)}) %collective-permute-start.4) | collective-permute-done | bytes 294944 | tf_op jit(solution)/shard_map/ppermute | solution.py:37
  45.9 8.2 %collective-permute-done.3 = bf16[1152,128]{1,0:T(8,128)(2,1)S(1)} collective-permute-done((bf16[1152,128]{1,0:T(8,128)(2,1)S(1)}, bf16[1152,128]{1,0:T(8,128)(2,1)S(1)}, u32[]{:S(2)}, u32[]{:S(2)}) %collective-permute-start.3) | collective-permute-done | bytes 294944 | tf_op jit(solution)/shard_map/ppermute | solution.py:37
  54.2 2.7 %collective-permute-start.6 = (bf16[4,1152,128]{2,1,0:T(8,128)(2,1)S(1)}, bf16[4,1152,128]{2,1,0:T(8,128)(2,1)S(1)}, u32[]{:S(2)}, u32[]{:S(2)}) collective-permute-start(bf16[4,1152,128]{2,1,0:T(8,128)(2,1)S(1)} %pad_maximum_fusion.mine_ref), channel_id=1, source_target_pairs={{0,1},{1,0},{2,3},{3,2},{4,5},{5,4},{6,7},{7,6},{8,9},{9,8},{10,11... | collective-permute-start | bytes 3538952 | tf_op jit(solution)/shard_map/ppermute | solution.py:42
  58.4 1.0 collective-permute-done.6.other_ref
  59.4 10.2 %features.1.features_ref = bf16[2,4,256,1024]{3,2,1,0:T(8,128)(2,1)S(1)} custom-call(s32[2]{0:T(128)S(1)} %pad_add_fusion.me_ref, bf16[4,256,128]{2,1,0:T(8,128)(2,1)S(1)} %pad_maximum_fusion.3.pack_ref, bf16[2,128,1152]{2,1,0:T(8,128)(2,1)S(1)} %fusion.spread_ref, f32[1,1152]{1,0:T(1,128)S(1)} %fusion.14.target_ref, ...), custom_call_target="tpu_custom_call" | custom-call | flops 5435817984 | bytes 6553600 | tf_op jit(solution)/shard_map/features/pallas_call | solution.py:100
  69.7 1.9 %copy-done = bf16[2,4,256,1024]{3,2,1,0:T(8,128)(2,1)} copy-done((bf16[2,4,256,1024]{3,2,1,0:T(8,128)(2,1)}, bf16[2,4,256,1024]{3,2,1,0:T(8,128)(2,1)S(1)}, u32[]{:S(2)}) %copy-start) | copy-done | bytes 4194328
  71.6 2.2 %copy-done.1 = bf16[2,4,256,1024]{3,2,1,0:T(8,128)(2,1)S(1)} copy-done((bf16[2,4,256,1024]{3,2,1,0:T(8,128)(2,1)S(1)}, bf16[2,4,256,1024]{3,2,1,0:T(8,128)(2,1)}, u32[]{:S(2)}) %copy-start.1) | copy-done | bytes 4194328
  73.8 3.9 %gate.1 = bf16[4,2,256,384]{3,2,1,0:T(8,128)(2,1)} custom-call(bf16[2,4,256,1024]{3,2,1,0:T(8,128)(2,1)S(1)} %copy-done.1, bf16[1024,384]{1,0:T(8,128)(2,1)S(1)} %bitcast.29), custom_call_target="tpu_custom_call" | custom-call | flops 1610612736 | bytes 6553600 | tf_op jit(solution)/shard_map/gate/pallas_call | solution.py:132
  77.7 5.9 %all-to-all-start.1 = ((bf16[4,2,256,384]{3,2,1,0:T(8,128)(2,1)}), bf16[4,2,256,384]{3,2,1,0:T(8,128)(2,1)S(1)}, u32[]{:S(2)}, u32[]{:S(2)}) async-start(bf16[4,2,256,384]{3,2,1,0:T(8,128)(2,1)} %gate.1), calls=%async_computation.1 | async-start | bytes 3145728 | tf_op jit(solution)/shard_map/all_to_all | solution.py:288
  83.6 4.5 %collective-permute-start.9 = (bf16[1024,128]{1,0:T(8,128)(2,1)S(1)}, bf16[1024,128]{1,0:T(8,128)(2,1)S(1)}, u32[]{:S(2)}, u32[]{:S(2)}) collective-permute-start(bf16[1024,128]{1,0:T(8,128)(2,1)S(1)} %copy-done.8), channel_id=1, source_target_pairs={{0,6},{1,7},{2,0},{3,1},{4,2},{5,3},{6,4},{7,5},{8,14},{9,15},{10,... | collective-permute-start | bytes 786440 | tf_op jit(solution)/shard_map/ppermute | solution.py:37
  88.1 2.4 %collective-permute-start.8 = (bf16[1024,128]{1,0:T(8,128)(2,1)S(1)}, bf16[1024,128]{1,0:T(8,128)(2,1)S(1)}, u32[]{:S(2)}, u32[]{:S(2)}) collective-permute-start(bf16[1024,128]{1,0:T(8,128)(2,1)S(1)} %copy-done.8), channel_id=1, source_target_pairs={{0,4},{1,5},{2,6},{3,7},{4,0},{5,1},{6,2},{7,3},{8,12},{9,13},{10,... | collective-permute-start | bytes 786440 | tf_op jit(solution)/shard_map/ppermute | solution.py:37
  90.5 2.5 %collective-permute-start.7 = (bf16[1024,128]{1,0:T(8,128)(2,1)S(1)}, bf16[1024,128]{1,0:T(8,128)(2,1)S(1)}, u32[]{:S(2)}, u32[]{:S(2)}) collective-permute-start(bf16[1024,128]{1,0:T(8,128)(2,1)S(1)} %copy-done.8), channel_id=1, source_target_pairs={{0,2},{1,3},{2,4},{3,5},{4,6},{5,7},{6,0},{7,1},{8,10},{9,11},{10,... | collective-permute-start | bytes 786440 | tf_op jit(solution)/shard_map/ppermute | solution.py:37
  93.0 3.7 %collective-permute-done.8 = bf16[1024,128]{1,0:T(8,128)(2,1)S(1)} collective-permute-done((bf16[1024,128]{1,0:T(8,128)(2,1)S(1)}, bf16[1024,128]{1,0:T(8,128)(2,1)S(1)}, u32[]{:S(2)}, u32[]{:S(2)}) %collective-permute-start.8) | collective-permute-done | bytes 262176 | tf_op jit(solution)/shard_map/ppermute | solution.py:37
  96.8 6.2 %collective-permute-done.7 = bf16[1024,128]{1,0:T(8,128)(2,1)S(1)} collective-permute-done((bf16[1024,128]{1,0:T(8,128)(2,1)S(1)}, bf16[1024,128]{1,0:T(8,128)(2,1)S(1)}, u32[]{:S(2)}, u32[]{:S(2)}) %collective-permute-start.7) | collective-permute-done | bytes 262176 | tf_op jit(solution)/shard_map/ppermute | solution.py:37
  103.1 4.8 %collective-permute-start.10 = (bf16[4,1024,128]{2,1,0:T(8,128)(2,1)S(1)}, bf16[4,1024,128]{2,1,0:T(8,128)(2,1)}, u32[]{:S(2)}, u32[]{:S(2)}) collective-permute-start(bf16[4,1024,128]{2,1,0:T(8,128)(2,1)S(1)} %pad_maximum_fusion.1.mine_ref), channel_id=1, source_target_pairs={{0,1},{1,0},{2,3},{3,2},{4,5},{5,4},{6,7},{7,6},{8,9},{9,8},{10,11... | collective-permute-start | bytes 3145736 | tf_op jit(solution)/shard_map/ppermute | solution.py:42
  107.9 1.4 copy-done.4
  109.3 1.2 copy-done.5
  110.5 2.0 %gru.1 = (bf16[256,512]{1,0:T(8,128)(2,1)S(1)}, bf16[8,2,32,1024]{3,2,1,0:T(8,128)(2,1)S(1)}) custom-call(bf16[256,512]{1,0:T(8,128)(2,1)S(1)} %copy-done.6, bf16[512,1536]{1,0:T(8,128)(2,1)S(1)} %bitcast.32, bf16[512,1024]{1,0:T(8,128)(2,1)S(1)} %copy-done.5, bf16[4,2,256,384]{3,2,1,0:T(8,128)(2,1)S(1)} %all-to-all-done.1.f_ref), custom_call_target="tpu_custom_call" | custom-call | flops 1342177280 | bytes 5767168 | tf_op jit(solution)/shard_map/gru/pallas_call | solution.py:180
  112.6 1.0 copy-done.2
  113.5 3.6 %all-to-all-start.2 = ((bf16[8,64,1024]{2,1,0:T(8,128)(2,1)}), bf16[8,64,1024]{2,1,0:T(8,128)(2,1)S(1)}, u32[]{:S(2)}, u32[]{:S(2)}) async-start(bf16[8,64,1024]{2,1,0:T(8,128)(2,1)} %bitcast.30), calls=%async_computation.2 | async-start | bytes 2097152 | tf_op jit(solution)/shard_map/all_to_all | solution.py:301
  117.8 14.4 %all-to-all-done.2.parts_ref = bf16[8,64,1024]{2,1,0:T(8,128)(2,1)S(1)} async-done(((bf16[8,64,1024]{2,1,0:T(8,128)(2,1)}), bf16[8,64,1024]{2,1,0:T(8,128)(2,1)S(1)}, u32[]{:S(2)}, u32[]{:S(2)}) %all-to-all-start.2) | async-done | bytes 1048608 | tf_op jit(solution)/shard_map/all_to_all | solution.py:301
  132.2 4.1 %tail.1 = f32[8,8,128]{2,1,0:T(8,128)} custom-call(s32[2]{0:T(128)S(1)} %pad_add_fusion.me_ref, bf16[8,64,1024]{2,1,0:T(8,128)(2,1)S(1)} %all-to-all-done.2.parts_ref, bf16[4,1024,128]{2,1,0:T(8,128)(2,1)S(1)} %pad_maximum_fusion.1.mine_ref, bf16[4,1024,128]{2,1,0:T(8,128)(2,1)} %collective-permute-done.10.other_ref, bf16[64,32]{1,0:T(8,128)(2,1)S(1)} %bitcast.31, ...), custom_call_target="tpu_custom_call" | custom-call | flops 134217728 | bytes 4194304 | tf_op jit(solution)/shard_map/tail/pallas_call | solution.py:240
  136.3 4.1 %all-to-all-start.3 = ((f32[8,8,128]{2,1,0:T(8,128)}), f32[8,8,128]{2,1,0:T(8,128)S(1)}, u32[]{:S(2)}, u32[]{:S(2)}) async-start(f32[8,8,128]{2,1,0:T(8,128)} %tail.1), calls=%async_computation.3 | async-start | bytes 65536 | tf_op jit(solution)/shard_map/all_to_all | solution.py:303
  141.2 3.9 %all-to-all-done.3 = f32[8,8,128]{2,1,0:T(8,128)S(1)} async-done(((f32[8,8,128]{2,1,0:T(8,128)}), f32[8,8,128]{2,1,0:T(8,128)S(1)}, u32[]{:S(2)}, u32[]{:S(2)}) %all-to-all-start.3) | async-done | bytes 32800 | tf_op jit(solution)/shard_map/all_to_all | solution.py:303
  (64 shorter events, 8.1 us)
Async XLA Ops:
  3.4 27.9 %copy-start.7 = (bf16[1024,128]{1,0:T(8,128)(2,1)S(1)}, bf16[1024,128]{1,0:T(8,128)(2,1)}, u32[]{:S(2)}) copy-start(bf16[1024,128]{1,0:T(8,128)(2,1)} %param.16) | copy-start | bytes 786436
  3.4 27.9 %copy-start.10 = (bf16[18,128]{1,0:T(8,128)(2,1)S(1)}, bf16[18,128]{1,0:T(8,128)(2,1)}, u32[]{:S(2)}) copy-start(bf16[18,128]{1,0:T(8,128)(2,1)} %param.17) | copy-start | bytes 13828
  3.5 53.9 %collective-permute-start.2 = (bf16[256,128]{1,0:T(8,128)(2,1)S(1)}, bf16[256,128]{1,0:T(8,128)(2,1)}, u32[]{:S(2)}, u32[]{:S(2)}) collective-permute-start(bf16[256,128]{1,0:T(8,128)(2,1)S(1)} %fusion.10), channel_id=1, source_target_pairs={{0,24},{8,0},{16,8},{24,16},{32,56},{40,32},{48,40},{56,48},{64,88... | collective-permute-start | bytes 196616 | tf_op jit(solution)/shard_map/ppermute | solution.py:31
  9.0 48.4 %collective-permute-start.1 = (bf16[256,128]{1,0:T(8,128)(2,1)S(1)}, bf16[256,128]{1,0:T(8,128)(2,1)}, u32[]{:S(2)}, u32[]{:S(2)}) collective-permute-start(bf16[256,128]{1,0:T(8,128)(2,1)S(1)} %fusion.10), channel_id=1, source_target_pairs={{0,16},{8,24},{16,0},{24,8},{32,48},{40,56},{48,32},{56,40},{64,80... | collective-permute-start | bytes 196616 | tf_op jit(solution)/shard_map/ppermute | solution.py:31
  11.3 0.8 copy-start.3
  13.1 58.5 %all-to-all-start = ((bf16[64,16,384]{2,1,0:T(8,128)(2,1)}), bf16[64,16,384]{2,1,0:T(8,128)(2,1)S(1)}, u32[]{:S(2)}, u32[]{:S(2)}) async-start(bf16[64,16,384]{2,1,0:T(8,128)(2,1)} %bitcast.14), calls=%async_computation | async-start | bytes 1572864 | tf_op jit(solution)/shard_map/all_to_all | solution.py:275
  31.4 9.9 %collective-permute-start.5 = (bf16[1152,128]{1,0:T(8,128)(2,1)S(1)}, bf16[1152,128]{1,0:T(8,128)(2,1)S(1)}, u32[]{:S(2)}, u32[]{:S(2)}) collective-permute-start(bf16[1152,128]{1,0:T(8,128)(2,1)S(1)} %get-tuple-element.9), channel_id=1, source_target_pairs={{0,6},{1,7},{2,0},{3,1},{4,2},{5,3},{6,4},{7,5},{8,14},{9,15},{10,... | collective-permute-start | bytes 884744 | tf_op jit(solution)/shard_map/ppermute | solution.py:37
  35.8 10.1 %collective-permute-start.4 = (bf16[1152,128]{1,0:T(8,128)(2,1)S(1)}, bf16[1152,128]{1,0:T(8,128)(2,1)S(1)}, u32[]{:S(2)}, u32[]{:S(2)}) collective-permute-start(bf16[1152,128]{1,0:T(8,128)(2,1)S(1)} %get-tuple-element.9), channel_id=1, source_target_pairs={{0,4},{1,5},{2,6},{3,7},{4,0},{5,1},{6,2},{7,3},{8,12},{9,13},{10,... | collective-permute-start | bytes 884744 | tf_op jit(solution)/shard_map/ppermute | solution.py:37
  38.2 15.9 %collective-permute-start.3 = (bf16[1152,128]{1,0:T(8,128)(2,1)S(1)}, bf16[1152,128]{1,0:T(8,128)(2,1)S(1)}, u32[]{:S(2)}, u32[]{:S(2)}) collective-permute-start(bf16[1152,128]{1,0:T(8,128)(2,1)S(1)} %get-tuple-element.9), channel_id=1, source_target_pairs={{0,2},{1,3},{2,4},{3,5},{4,6},{5,7},{6,0},{7,1},{8,10},{9,11},{10,... | collective-permute-start | bytes 884744 | tf_op jit(solution)/shard_map/ppermute | solution.py:37
  41.3 16.1 %collective-permute-start = (bf16[256,128]{1,0:T(8,128)(2,1)S(1)}, bf16[256,128]{1,0:T(8,128)(2,1)}, u32[]{:S(2)}, u32[]{:S(2)}) collective-permute-start(bf16[256,128]{1,0:T(8,128)(2,1)S(1)} %fusion.10), channel_id=1, source_target_pairs={{0,8},{8,16},{16,24},{24,0},{32,40},{40,48},{48,56},{56,32},{64,72... | collective-permute-start | bytes 196616 | tf_op jit(solution)/shard_map/ppermute | solution.py:31
  54.2 5.2 %collective-permute-start.6 = (bf16[4,1152,128]{2,1,0:T(8,128)(2,1)S(1)}, bf16[4,1152,128]{2,1,0:T(8,128)(2,1)S(1)}, u32[]{:S(2)}, u32[]{:S(2)}) collective-permute-start(bf16[4,1152,128]{2,1,0:T(8,128)(2,1)S(1)} %pad_maximum_fusion.mine_ref), channel_id=1, source_target_pairs={{0,1},{1,0},{2,3},{3,2},{4,5},{5,4},{6,7},{7,6},{8,9},{9,8},{10,11... | collective-permute-start | bytes 3538952 | tf_op jit(solution)/shard_map/ppermute | solution.py:42
  69.7 2.0 %copy-start = (bf16[2,4,256,1024]{3,2,1,0:T(8,128)(2,1)}, bf16[2,4,256,1024]{3,2,1,0:T(8,128)(2,1)S(1)}, u32[]{:S(2)}) copy-start(bf16[2,4,256,1024]{3,2,1,0:T(8,128)(2,1)S(1)} %features.1.features_ref) | copy-start | bytes 12582916
  71.6 2.2 %copy-start.1 = (bf16[2,4,256,1024]{3,2,1,0:T(8,128)(2,1)S(1)}, bf16[2,4,256,1024]{3,2,1,0:T(8,128)(2,1)}, u32[]{:S(2)}) copy-start(bf16[2,4,256,1024]{3,2,1,0:T(8,128)(2,1)} %copy-done) | copy-start | bytes 12582916
  77.7 5.9 %copy-start.8 = (bf16[1024,128]{1,0:T(8,128)(2,1)S(1)}, bf16[1024,128]{1,0:T(8,128)(2,1)}, u32[]{:S(2)}) copy-start(bf16[1024,128]{1,0:T(8,128)(2,1)} %param.21) | copy-start | bytes 786436
  77.7 30.2 %all-to-all-start.1 = ((bf16[4,2,256,384]{3,2,1,0:T(8,128)(2,1)}), bf16[4,2,256,384]{3,2,1,0:T(8,128)(2,1)S(1)}, u32[]{:S(2)}, u32[]{:S(2)}) async-start(bf16[4,2,256,384]{3,2,1,0:T(8,128)(2,1)} %gate.1), calls=%async_computation.1 | async-start | bytes 3145728 | tf_op jit(solution)/shard_map/all_to_all | solution.py:288
  83.6 24.3 %copy-start.6 = (bf16[256,512]{1,0:T(8,128)(2,1)S(1)}, bf16[256,512]{1,0:T(8,128)(2,1)}, u32[]{:S(2)}) copy-start(bf16[256,512]{1,0:T(8,128)(2,1)} %deter_ref.1) | copy-start | bytes 786436
  83.6 9.5 %collective-permute-start.9 = (bf16[1024,128]{1,0:T(8,128)(2,1)S(1)}, bf16[1024,128]{1,0:T(8,128)(2,1)S(1)}, u32[]{:S(2)}, u32[]{:S(2)}) collective-permute-start(bf16[1024,128]{1,0:T(8,128)(2,1)S(1)} %copy-done.8), channel_id=1, source_target_pairs={{0,6},{1,7},{2,0},{3,1},{4,2},{5,3},{6,4},{7,5},{8,14},{9,15},{10,... | collective-permute-start | bytes 786440 | tf_op jit(solution)/shard_map/ppermute | solution.py:37
  88.1 8.7 %collective-permute-start.8 = (bf16[1024,128]{1,0:T(8,128)(2,1)S(1)}, bf16[1024,128]{1,0:T(8,128)(2,1)S(1)}, u32[]{:S(2)}, u32[]{:S(2)}) collective-permute-start(bf16[1024,128]{1,0:T(8,128)(2,1)S(1)} %copy-done.8), channel_id=1, source_target_pairs={{0,4},{1,5},{2,6},{3,7},{4,0},{5,1},{6,2},{7,3},{8,12},{9,13},{10,... | collective-permute-start | bytes 786440 | tf_op jit(solution)/shard_map/ppermute | solution.py:37
  90.5 12.4 %collective-permute-start.7 = (bf16[1024,128]{1,0:T(8,128)(2,1)S(1)}, bf16[1024,128]{1,0:T(8,128)(2,1)S(1)}, u32[]{:S(2)}, u32[]{:S(2)}) collective-permute-start(bf16[1024,128]{1,0:T(8,128)(2,1)S(1)} %copy-done.8), channel_id=1, source_target_pairs={{0,2},{1,3},{2,4},{3,5},{4,6},{5,7},{6,0},{7,1},{8,10},{9,11},{10,... | collective-permute-start | bytes 786440 | tf_op jit(solution)/shard_map/ppermute | solution.py:37
  103.1 14.7 %collective-permute-start.10 = (bf16[4,1024,128]{2,1,0:T(8,128)(2,1)S(1)}, bf16[4,1024,128]{2,1,0:T(8,128)(2,1)}, u32[]{:S(2)}, u32[]{:S(2)}) collective-permute-start(bf16[4,1024,128]{2,1,0:T(8,128)(2,1)S(1)} %pad_maximum_fusion.1.mine_ref), channel_id=1, source_target_pairs={{0,1},{1,0},{2,3},{3,2},{4,5},{5,4},{6,7},{7,6},{8,9},{9,8},{10,11... | collective-permute-start | bytes 3145736 | tf_op jit(solution)/shard_map/ppermute | solution.py:42
  107.9 1.4 copy-start.4
  109.3 1.2 copy-start.5
  112.5 1.0 copy-start.2
  113.5 3.7 %copy-start.11 = (s32[4]{0:T(128)S(1)}, s32[4]{0:T(128)}, u32[]{:S(2)}) copy-start(s32[4]{0:T(128)} %param.15) | copy-start | bytes 52
  113.5 3.8 %copy-start.9 = (s32[2,256,32]{1,2,0:T(8,128)S(1)}, s32[2,256,32]{1,2,0:T(8,128)}, u32[]{:S(2)}) copy-start(s32[2,256,32]{1,2,0:T(8,128)} %param.13) | copy-start | bytes 196612
  113.5 18.7 %all-to-all-start.2 = ((bf16[8,64,1024]{2,1,0:T(8,128)(2,1)}), bf16[8,64,1024]{2,1,0:T(8,128)(2,1)S(1)}, u32[]{:S(2)}, u32[]{:S(2)}) async-start(bf16[8,64,1024]{2,1,0:T(8,128)(2,1)} %bitcast.30), calls=%async_computation.2 | async-start | bytes 2097152 | tf_op jit(solution)/shard_map/all_to_all | solution.py:301
  136.3 8.9 %all-to-all-start.3 = ((f32[8,8,128]{2,1,0:T(8,128)}), f32[8,8,128]{2,1,0:T(8,128)S(1)}, u32[]{:S(2)}, u32[]{:S(2)}) async-start(f32[8,8,128]{2,1,0:T(8,128)} %tail.1), calls=%async_computation.3 | async-start | bytes 65536 | tf_op jit(solution)/shard_map/all_to_all | solution.py:303

commit v3 on v2

--- a/solution.py
+++ b/solution.py
@@ -17,13 +17,29 @@
 NY = 4
 NX = 4
 NC = 2
+NEAR = 4
 LANES = 128
 EPS = 1e-06
 MIB = 1024 * 1024
+GRANT = 60 * MIB
 
 
 def y_groups(n_dp):
     return [[start + y for y in range(NY)] for start in range(0, n_dp, NY)]
+
+
+def far_groups(n_dp):
+    n_far = n_dp // NY // NEAR
+    return [[(far * NEAR + near) * NY + y for far in range(n_far) for y in range(NY)] for near in range(NEAR)]
+
+
+def near_groups(n_dp):
+    n_far = n_dp // NY // NEAR
+    return [[(far * NEAR + near) * NY + y for near in range(NEAR)] for far in range(n_far) for y in range(NY)]
+
+
+def x_groups():
+    return [list(range(core, NX * NC, NC)) for core in range(NC)]
 
 
 def y_shift(value, step, n_dp):
@@ -42,9 +58,17 @@
     return lax.ppermute(value, "tensor", perm)
 
 
-def tensor_gather(value):
-    mine = jnp.stack([value] + [x_shift(value, step) for step in range(1, NX)])
-    return mine, core_swap(mine)
+def x_gather(value):
+    return jnp.stack([value] + [x_shift(value, step) for step in range(1, NX)])
+
+
+def silu(value):
+    half = 0.5 * value
+    return half + half * jnp.tanh(half)
+
+
+def sigmoid(value):
+    return 0.5 + 0.5 * jnp.tanh(0.5 * value)
 
 
 def split_kernel(w_ref, out_ref):
@@ -85,7 +109,7 @@
         pre = jnp.dot(hot, w_ref[...], preferred_element_type=jnp.float32)
         scale = lax.rsqrt(jnp.mean(pre * pre, axis=1, keepdims=True) + EPS)
         normed = pre * scale
-        out_ref[k] = (normed * jax.nn.sigmoid(normed)).astype(jnp.bfloat16)
+        out_ref[k] = silu(normed).astype(jnp.bfloat16)
 
 
 def features_call(place, pack, mine, other):
@@ -109,7 +133,7 @@
             pl.BlockSpec((NX, width, LANES), lambda b: (0, 0, 0)),
         ],
         out_specs=pl.BlockSpec((IMAG, None, rows, UNITS), lambda b: (0, b, 0, 0)),
-        out_shape=jax.ShapeDtypeStruct((IMAG, NY, rows, UNITS), jnp.bfloat16),
+        out_shape=pltpu.HBM((IMAG, NY, rows, UNITS), jnp.bfloat16),
         scratch_shapes=[pltpu.VMEM((width, UNITS), jnp.bfloat16)],
         compiler_params=pltpu.CompilerParams(vmem_limit_bytes=32 * MIB),
         cost_estimate=pl.CostEstimate(
@@ -121,24 +145,34 @@
     )(place, pack, spread, target, mine, other)
 
 
-def gate_kernel(features_ref, gate_ref, out_ref):
+def gate_kernel(n_far, features_ref, gate_ref, out_ref, w_ref):
+    near, held = gate_ref.shape[:2]
+    depth = held // n_far
+
+    @pl.when(pl.program_id(0) == 0)
+    def _():
+        for i in range(near):
+            for far in range(n_far):
+                w_ref[(far * near + i) * depth : (far * near + i + 1) * depth] = gate_ref[i, far * depth : (far + 1) * depth]
+
     for k in range(IMAG):
-        out_ref[k] = jnp.dot(features_ref[k], gate_ref[...], preferred_element_type=jnp.float32).astype(jnp.bfloat16)
-
-
-def gate_call(features, gate):
+        out_ref[k] = jnp.dot(features_ref[k], w_ref[...], preferred_element_type=jnp.float32).astype(jnp.bfloat16)
+
+
+def gate_call(features, gate, n_far):
     rows = features.shape[2]
-    width = gate.shape[1]
+    width = gate.shape[2]
     return pl.pallas_call(
-        gate_kernel,
+        functools.partial(gate_kernel, n_far),
         grid=(NY,),
         in_specs=[
             pl.BlockSpec((IMAG, None, rows, UNITS), lambda b: (0, b, 0, 0)),
-            pl.BlockSpec((UNITS, width), lambda b: (0, 0)),
+            pl.BlockSpec(gate.shape, lambda b: (0, 0, 0)),
         ],
         out_specs=pl.BlockSpec((None, IMAG, rows, width), lambda b: (b, 0, 0, 0)),
-        out_shape=jax.ShapeDtypeStruct((NY, IMAG, rows, width), jnp.bfloat16),
-        compiler_params=pltpu.CompilerParams(vmem_limit_bytes=32 * MIB),
+        out_shape=pltpu.HBM((NY, IMAG, rows, width), jnp.bfloat16),
+        scratch_shapes=[pltpu.VMEM((UNITS, width), jnp.bfloat16)],
+        compiler_params=pltpu.CompilerParams(vmem_limit_bytes=GRANT),
         cost_estimate=pl.CostEstimate(
             flops=2 * IMAG * NY * rows * UNITS * width,
             bytes_accessed=IMAG * NY * rows * (UNITS + width) * 2 + UNITS * width * 2,
@@ -148,52 +182,100 @@
     )(features, gate)
 
 
-def gru_kernel(deter_ref, w_rec_ref, w_in_ref, f_ref, new_ref, prior_ref, mid_ref):
+def gru_kernel(
+    core_ref,
+    deter_hbm,
+    w_rec_hbm,
+    w_in_hbm,
+    f_hbm,
+    new_ref,
+    keep_ref,
+    send_ref,
+    deter_ref,
+    w_rec_ref,
+    w_in_ref,
+    f_ref,
+    mid_ref,
+    prior_ref,
+    sems,
+):
     rows, bw = deter_ref.shape
     part = bw // NY
+    half = bw // 2
+    core = core_ref[1]
+    pairs = [(deter_hbm, deter_ref)]
+    pairs += [(w_rec_hbm.at[pl.ds(i * half, half)], w_rec_ref.at[pl.ds(i * half, half)]) for i in range(2)]
+    pairs += [(f_hbm.at[:, k], f_ref.at[:, k]) for k in range(IMAG)]
+    pairs += [(w_in_hbm, w_in_ref)]
+    copies = [pltpu.make_async_copy(src, dst, sems.at[i]) for i, (src, dst) in enumerate(pairs)]
+    for copy in copies:
+        copy.start()
+    copies[0].wait()
     for k in range(IMAG):
         old_ref = deter_ref if k == 0 else mid_ref
         next_ref = new_ref if k == IMAG - 1 else mid_ref
         old = old_ref[...]
-        rec = jnp.dot(old, w_rec_ref[...], preferred_element_type=jnp.float32)
+        rec = None
+        for i in range(2):
+            if k == 0:
+                copies[1 + i].wait()
+            term = jnp.dot(
+                old[:, i * half : (i + 1) * half],
+                w_rec_ref[i * half : (i + 1) * half],
+                preferred_element_type=jnp.float32,
+            )
+            rec = term if rec is None else rec + term
+        copies[3 + k].wait()
         for q in range(NY):
 
             def gate(which):
                 mine = f_ref[q, k, :, which * part : (which + 1) * part].astype(jnp.float32)
                 return rec[:, which * bw + q * part : which * bw + (q + 1) * part] + mine
 
-            reset = jax.nn.sigmoid(gate(0))
+            reset = sigmoid(gate(0))
             candidate = jnp.tanh(reset * gate(1))
-            update = jax.nn.sigmoid(gate(2) - 1.0)
+            update = sigmoid(gate(2) - 1.0)
             before = old[:, q * part : (q + 1) * part].astype(jnp.float32)
             fresh = update * candidate + (1.0 - update) * before
             next_ref[:, q * part : (q + 1) * part] = fresh.astype(jnp.bfloat16)
-        prior = jnp.dot(next_ref[...], w_in_ref[...], preferred_element_type=jnp.float32).astype(jnp.bfloat16)
-        share = prior_ref.shape[2]
-        for j in range(prior_ref.shape[0]):
-            prior_ref[j, k] = prior[j * share : (j + 1) * share]
-
-
-def gru_call(deter, w_rec, w_in, sums, tensor_n):
+        if k == 0:
+            copies[3 + IMAG].wait()
+        prior_ref[...] = jnp.dot(next_ref[...], w_in_ref[...], preferred_element_type=jnp.float32)
+        share = keep_ref.shape[2]
+        for x in range(NX):
+            for out_ref, owner in ((keep_ref, core), (send_ref, 1 - core)):
+                here = pl.ds(pl.multiple_of((x * NC + owner) * share, share), share)
+                out_ref[x, k] = prior_ref[here].astype(jnp.bfloat16)
+
+
+def gru_call(place, deter, w_rec, w_in, sums):
     rows, bw = deter.shape
+    width = w_in.shape[1]
     vmem = pl.BlockSpec(memory_space=pltpu.VMEM)
+    hbm = pl.BlockSpec(memory_space=pl.ANY)
+    prior = jax.ShapeDtypeStruct((NX, IMAG, rows // (NX * NC), width), jnp.bfloat16)
     return pl.pallas_call(
         gru_kernel,
-        in_specs=[vmem] * 4,
-        out_specs=[vmem, vmem],
-        out_shape=[
-            jax.ShapeDtypeStruct((rows, bw), jnp.bfloat16),
-            jax.ShapeDtypeStruct((tensor_n, IMAG, rows // tensor_n, w_in.shape[1]), jnp.bfloat16),
+        in_specs=[pl.BlockSpec(memory_space=pltpu.SMEM)] + [hbm] * 4,
+        out_specs=[vmem, vmem, vmem],
+        out_shape=[jax.ShapeDtypeStruct((rows, bw), jnp.bfloat16), prior, prior],
+        scratch_shapes=[
+            pltpu.VMEM(deter.shape, jnp.bfloat16),
+            pltpu.VMEM(w_rec.shape, jnp.bfloat16),
+            pltpu.VMEM(w_in.shape, jnp.bfloat16),
+            pltpu.VMEM(sums.shape, jnp.bfloat16),
+            pltpu.VMEM((rows, bw), jnp.bfloat16),
+            pltpu.VMEM((rows, width), jnp.float32),
+            pltpu.SemaphoreType.DMA((4 + IMAG,)),
         ],
-        scratch_shapes=[pltpu.VMEM((rows, bw), jnp.bfloat16)],
-        compiler_params=pltpu.CompilerParams(vmem_limit_bytes=32 * MIB),
+        compiler_params=pltpu.CompilerParams(vmem_limit_bytes=GRANT),
         cost_estimate=pl.CostEstimate(
-            flops=2 * IMAG * rows * bw * (3 * bw + w_in.shape[1]),
+            flops=2 * IMAG * rows * bw * (3 * bw + width),
             bytes_accessed=2 * (w_rec.size + w_in.size) + 24 * rows * bw,
             transcendentals=6 * rows * bw,
         ),
         name="gru",
-    )(deter, w_rec, w_in, sums)
+    )(place, deter, w_rec, w_in, sums)
 
 
 def tail_kernel(me_ref, parts_ref, mine_ref, other_ref, picked_ref, var_ref, mask_ref, log_ref):
@@ -201,7 +283,7 @@
     for i in range(1, parts_ref.shape[0]):
         pre = pre + parts_ref[i].astype(jnp.float32)
     normed = pre * lax.rsqrt(jnp.mean(pre * pre, axis=1, keepdims=True) + EPS)
-    hidden = (normed * jax.nn.sigmoid(normed)).astype(jnp.bfloat16)
+    hidden = silu(normed).astype(jnp.bfloat16)
     rows = hidden.shape[0]
     cls = lax.broadcasted_iota(jnp.int32, (rows, LANES), 1) % CLASSES
 
@@ -233,7 +315,7 @@
 
 
 def tail_call(place, parts, mine, other, picked, mask):
-    tensor_n, rows = parts.shape[:2]
+    rows = parts.shape[1]
     lane = jnp.arange(LAT, dtype=jnp.int32)
     var_of = (jnp.arange(STOCH, dtype=jnp.int32)[:, None] == lane[None, :] // CLASSES).astype(jnp.bfloat16)
     vmem = pl.BlockSpec(memory_space=pltpu.VMEM)
@@ -241,7 +323,7 @@
         tail_kernel,
         in_specs=[pl.BlockSpec(memory_space=pltpu.SMEM)] + [vmem] * 6,
         out_specs=vmem,
-        out_shape=jax.ShapeDtypeStruct((tensor_n, 8, LANES), jnp.float32),
+        out_shape=jax.ShapeDtypeStruct((NX * NC, 8, LANES), jnp.float32),
         compiler_params=pltpu.CompilerParams(vmem_limit_bytes=32 * MIB),
         cost_estimate=pl.CostEstimate(
             flops=2 * rows * UNITS * LAT, bytes_accessed=8 * mine.size, transcendentals=4 * rows * LAT
@@ -271,13 +353,18 @@
     me = lax.axis_index("tensor")
     place = jnp.stack([me // NC, me % NC]).astype(jnp.int32)
 
-    sent = split_call(w_gate, n_dp // NY)
-    gate = lax.all_to_all(sent.reshape(n_dp, depth, -1), "dp", 0, 0).reshape(n_dp * depth, -1)
+    n_far = n_dp // NY // NEAR
+    sent = split_call(w_gate, n_far).reshape(n_far * NY, depth, -1)
+    held = lax.all_to_all(sent, "dp", 0, 0, axis_index_groups=far_groups(n_dp)).reshape(n_far * NY * depth, -1)
+    gate = jnp.broadcast_to(held[None], (NEAR,) + held.shape)
+    gate = lax.all_to_all(gate, "dp", 0, 0, axis_index_groups=near_groups(n_dp))
 
     action_rows = jnp.pad(w_action, ((0, LANES - ACTIONS), (0, 0)))
-    mine, other = tensor_gather(jnp.concatenate([w_stoch, action_rows], axis=0))
-
-    columns = [post_sample, samples[0]] + [actions[k][:, None] for k in range(IMAG)]
+    mine = x_gather(jnp.concatenate([w_stoch, action_rows], axis=0))
+    other = core_swap(mine)
+
+    first_latent, first_samples, late_actions, _ = lax.optimization_barrier((post_sample, samples[0], actions, held))
+    columns = [first_latent, first_samples] + [late_actions[k][:, None] for k in range(IMAG)]
     pack = jnp.concatenate(columns, axis=1).astype(jnp.bfloat16)
     pack = jnp.pad(pack, ((0, 0), (0, LANES - pack.shape[1])))
     pack = jnp.stack([pack] + [y_shift(pack, b, n_dp) for b in range(1, NY)])
@@ -285,10 +372,10 @@
     pack = jnp.stack([lax.dynamic_index_in_dim(pack, (y - b + NY) % NY, 0, keepdims=False) for b in range(NY)])
 
     features = features_call(place, pack, mine, other)
-    sums = lax.all_to_all(gate_call(features, gate), "dp", 0, 0, axis_index_groups=y_groups(n_dp))
+    sums = lax.all_to_all(gate_call(features, gate, n_far), "dp", 0, 0, axis_index_groups=y_groups(n_dp))
 
     w_out_late, _ = lax.optimization_barrier((w_prior_out, features))
-    out_mine, out_other = tensor_gather(w_out_late)
+    out_mine = x_gather(w_out_late)
 
     positions = jnp.arange(STEPS, dtype=jnp.int32)
     valid_mask = (positions[None, :] < counts[:, None]).reshape(rows)
@@ -297,8 +384,11 @@
     picked = lax.dynamic_slice_in_dim(samples, me * share, share, 1)
     picked = picked.reshape(IMAG * share, STOCH).astype(jnp.bfloat16)
 
-    deter, partial = gru_call(post_deter, w_rec[0], w_prior_in, sums, tensor_n)
-    parts = lax.all_to_all(partial.reshape(tensor_n, IMAG * share, UNITS), "tensor", 0, 0)
+    deter, keep, send = gru_call(place, post_deter, w_rec[0], w_prior_in, sums)
+    pair = (keep.astype(jnp.float32) + core_swap(send).astype(jnp.float32)).astype(jnp.bfloat16)
+    parts = lax.all_to_all(pair.reshape(NX, IMAG * share, UNITS), "tensor", 0, 0, axis_index_groups=x_groups())
+    out_mine, _ = lax.optimization_barrier((out_mine, pair))
+    out_other = core_swap(out_mine)
     logs = tail_call(place, parts, out_mine, out_other, picked, my_mask)
     logs = lax.all_to_all(logs, "tensor", 0, 0)[:, 0, : IMAG * share]
     log_prob = logs.reshape(tensor_n, IMAG, share).transpose(1, 0, 2).reshape(IMAG, rows)

time: 147 us -> 161 us (1.095)
  blocking collectives: 0 us -> 24.9 us
  waiting for transfers between devices: 40 us -> 32.8 us
  Pallas kernels: 21.2 us -> 27.5 us
  local copies, waits for them, and re-layouts: 10.2 us -> 5.09 us
  starting transfers between devices: 68.3 us -> 64 us
    all_to_all x0 -> x1, blocking collectives: none -> 24.9 us  [body(): lax.all_to_all(gate_call(features, gate, n_far), 'dp', 0, 0, axis_index_g...]
    unnamed x25, local copies, waits for them, and re-layouts: 8.67 us -> 1.81 us
    pallas_call x2, Pallas kernels: 5.9 us -> 11.8 us  [the longest x1 5.92 us: gru_call(): pl.pallas_call(gru_kernel, in_specs=[pl.BlockSpec(memory_space=pltpu.SMEM...]
    all_to_all x3, waiting for transfers between devices: 14.4 us -> 9.28 us  [the longest x1 9.28 us: body(): lax.all_to_all(pair.reshape(NX, IMAG * share, UNITS), 'tensor', 0, 0, axi...]
    all_to_all x3, starting transfers between devices: 27.7 us -> 25.3 us  [the longest x1 18.4 us: body(): lax.all_to_all(sent, 'dp', 0, 0, axis_index_groups=far_groups(n_dp))]
    ppermute x6, starting transfers between devices: 18.8 us -> 16.5 us  [x_shift(): return lax.ppermute(value, 'tensor', perm)]
    ppermute x6, waiting for transfers between devices: 20.7 us -> 18.6 us  [x_shift(): return lax.ppermute(value, 'tensor', perm)]
    ppermute x2 -> x3, starting transfers between devices: 7.5 us -> 8.6 us  [core_swap(): return lax.ppermute(value, 'tensor', perm)]
  transfers between devices with their start and end apart: 15 -> 16, of which waited for: 8 -> 7; matrix products, arithmetic and copies ran while one was open for 2% -> 4% of each run, Pallas kernels for 9% -> 7%
where the time goes in v3:
time: 161 us; the launch traced here: 160 us
  starting transfers between devices  64 us (40%)
  waiting for transfers between devices  32.8 us (20%)
  Pallas kernels  27.5 us (17%)
  blocking collectives  24.9 us (15%)
  local copies, waits for them, and re-layouts  5.09 us (3%)
  other arithmetic  4.59 us (3%)
    all_to_all x1, blocking collectives, body(): lax.all_to_all(gate_call(features, gate, n_far), 'dp', 0, 0, axis_index_g...  24.9 us
    ppermute x6, waiting for transfers between devices, x_shift(): return lax.ppermute(value, 'tensor', perm)  18.6 us
    all_to_all x1, starting transfers between devices, body(): lax.all_to_all(sent, 'dp', 0, 0, axis_index_groups=far_groups(n_dp))  18.4 us
    ppermute x6, starting transfers between devices, x_shift(): return lax.ppermute(value, 'tensor', perm)  16.5 us
    pallas_call x1, Pallas kernels, features_call(): pl.pallas_call(features_kernel, grid=(NY,), in_specs=[pl.BlockSpec(memory...  11.6 us
    ppermute x3, starting transfers between devices, y_shift(): return lax.ppermute(value, 'dp', perm)  9.45 us
    all_to_all x1, waiting for transfers between devices, body(): lax.all_to_all(pair.reshape(NX, IMAG * share, UNITS), 'tensor', 0, 0, axi...  9.28 us
    ppermute x3, starting transfers between devices, core_swap(): return lax.ppermute(value, 'tensor', perm)  8.6 us
  transfers between devices with their start and end apart: 16, of which 7 were waited for; matrix products, arithmetic and copies ran while one was open for 4% of the time, Pallas kernels for 7%

profile of v3, /device:TPU:1, one launch (start us, length us, event | category | flops | bytes accessed | tf_op | source)
XLA Modules:
  0.0 159.8 jit_solution(2161304643298180752)
XLA Ops:
  2.1 18.4 %all-to-all-start = ((bf16[16,16,384]{2,1,0:T(8,128)(2,1)}), bf16[16,16,384]{2,1,0:T(8,128)(2,1)S(1)}, u32[]{:S(2)}, u32[]{:S(2)}) async-start(bf16[16,16,384]{2,1,0:T(8,128)(2,1)} %bitcast.14), calls=%async_computation | async-start | bytes 393216 | tf_op jit(solution)/shard_map/all_to_all | solution.py:358
  22.7 4.5 %collective-permute-start.2 = (bf16[256,128]{1,0:T(8,128)(2,1)S(1)}, bf16[256,128]{1,0:T(8,128)(2,1)}, u32[]{:S(2)}, u32[]{:S(2)}) collective-permute-start(bf16[256,128]{1,0:T(8,128)(2,1)S(1)} %fusion.10), channel_id=1, source_target_pairs={{0,24},{8,0},{16,8},{24,16},{32,56},{40,32},{48,40},{56,48},{64,88... | collective-permute-start | bytes 196616 | tf_op jit(solution)/shard_map/ppermute | solution.py:47
  27.2 2.5 %collective-permute-start.1 = (bf16[256,128]{1,0:T(8,128)(2,1)S(1)}, bf16[256,128]{1,0:T(8,128)(2,1)}, u32[]{:S(2)}, u32[]{:S(2)}) collective-permute-start(bf16[256,128]{1,0:T(8,128)(2,1)S(1)} %fusion.10), channel_id=1, source_target_pairs={{0,16},{8,24},{16,0},{24,8},{32,48},{40,56},{48,32},{56,40},{64,80... | collective-permute-start | bytes 196616 | tf_op jit(solution)/shard_map/ppermute | solution.py:47
  29.7 4.4 %collective-permute-start.5 = (bf16[1152,128]{1,0:T(8,128)(2,1)S(1)}, bf16[1152,128]{1,0:T(8,128)(2,1)S(1)}, u32[]{:S(2)}, u32[]{:S(2)}) collective-permute-start(bf16[1152,128]{1,0:T(8,128)(2,1)S(1)} %get-tuple-element.19), channel_id=1, source_target_pairs={{0,6},{1,7},{2,0},{3,1},{4,2},{5,3},{6,4},{7,5},{8,14},{9,15},{10,... | collective-permute-start | bytes 884744 | tf_op jit(solution)/shard_map/ppermute | solution.py:53
  34.1 2.4 %collective-permute-start.4 = (bf16[1152,128]{1,0:T(8,128)(2,1)S(1)}, bf16[1152,128]{1,0:T(8,128)(2,1)S(1)}, u32[]{:S(2)}, u32[]{:S(2)}) collective-permute-start(bf16[1152,128]{1,0:T(8,128)(2,1)S(1)} %get-tuple-element.19), channel_id=1, source_target_pairs={{0,4},{1,5},{2,6},{3,7},{4,0},{5,1},{6,2},{7,3},{8,12},{9,13},{10,... | collective-permute-start | bytes 884744 | tf_op jit(solution)/shard_map/ppermute | solution.py:53
  36.6 2.5 %collective-permute-start.3 = (bf16[1152,128]{1,0:T(8,128)(2,1)S(1)}, bf16[1152,128]{1,0:T(8,128)(2,1)S(1)}, u32[]{:S(2)}, u32[]{:S(2)}) collective-permute-start(bf16[1152,128]{1,0:T(8,128)(2,1)S(1)} %get-tuple-element.19), channel_id=1, source_target_pairs={{0,2},{1,3},{2,4},{3,5},{4,6},{5,7},{6,0},{7,1},{8,10},{9,11},{10,... | collective-permute-start | bytes 884744 | tf_op jit(solution)/shard_map/ppermute | solution.py:53
  39.1 1.0 broadcast_in_dim.53
  40.1 3.5 %all-to-all-start.1 = ((bf16[4,256,384]{2,1,0:T(8,128)(2,1)}), bf16[4,256,384]{2,1,0:T(8,128)(2,1)S(1)}, u32[]{:S(2)}, u32[]{:S(2)}) async-start(bf16[4,256,384]{2,1,0:T(8,128)(2,1)} %broadcast_in_dim.53), calls=%async_computation.1 | async-start | bytes 1572864 | tf_op jit(solution)/shard_map/all_to_all | solution.py:360
  43.7 2.5 %collective-permute-start = (bf16[256,128]{1,0:T(8,128)(2,1)S(1)}, bf16[256,128]{1,0:T(8,128)(2,1)}, u32[]{:S(2)}, u32[]{:S(2)}) collective-permute-start(bf16[256,128]{1,0:T(8,128)(2,1)S(1)} %fusion.10), channel_id=1, source_target_pairs={{0,8},{8,16},{16,24},{24,0},{32,40},{40,48},{48,56},{56,32},{64,72... | collective-permute-start | bytes 196616 | tf_op jit(solution)/shard_map/ppermute | solution.py:47
  46.2 6.0 %collective-permute-done.3 = bf16[1152,128]{1,0:T(8,128)(2,1)S(1)} collective-permute-done((bf16[1152,128]{1,0:T(8,128)(2,1)S(1)}, bf16[1152,128]{1,0:T(8,128)(2,1)S(1)}, u32[]{:S(2)}, u32[]{:S(2)}) %collective-permute-start.3) | collective-permute-done | bytes 294944 | tf_op jit(solution)/shard_map/ppermute | solution.py:53
  52.3 3.0 %collective-permute-start.6 = (bf16[4,1152,128]{2,1,0:T(8,128)(2,1)S(1)}, bf16[4,1152,128]{2,1,0:T(8,128)(2,1)S(1)}, u32[]{:S(2)}, u32[]{:S(2)}) collective-permute-start(bf16[4,1152,128]{2,1,0:T(8,128)(2,1)S(1)} %pad_maximum_fusion.mine_ref), channel_id=1, source_target_pairs={{0,1},{1,0},{2,3},{3,2},{4,5},{5,4},{6,7},{7,6},{8,9},{9,8},{10,11... | collective-permute-start | bytes 3538952 | tf_op jit(solution)/shard_map/ppermute | solution.py:58
  55.8 0.9 pad_maximum_fusion.2
  56.8 1.0 collective-permute-done.6.other_ref
  57.8 11.6 %features.1.features_ref = bf16[2,4,256,1024]{3,2,1,0:T(8,128)(2,1)} custom-call(s32[2]{0:T(128)S(1)} %pad_add_fusion.me_ref.core_ref, bf16[4,256,128]{2,1,0:T(8,128)(2,1)S(1)} %pad_maximum_fusion.3.pack_ref, bf16[2,128,1152]{2,1,0:T(8,128)(2,1)S(1)} %fusion.spread_ref, f32[1,1152]{1,0:T(1,128)S(1)} %fusion.14.target_ref, ...), custom_call_target="tpu_custom_call" | custom-call | flops 5435817984 | bytes 6553600 | tf_op jit(solution)/shard_map/features/pallas_call | solution.py:124
  69.4 0.9 copy-done.3
  70.3 5.9 %gate.1 = bf16[4,2,256,384]{3,2,1,0:T(8,128)(2,1)} custom-call(bf16[2,4,256,1024]{3,2,1,0:T(8,128)(2,1)} %features.1.features_ref, bf16[4,256,384]{2,1,0:T(8,128)(2,1)} %copy-done.3), custom_call_target="tpu_custom_call" | custom-call | flops 1610612736 | bytes 6553600 | tf_op jit(solution)/shard_map/gate/pallas_call | solution.py:165
  76.2 24.9 %all_to_all.25.f_hbm = bf16[4,2,256,384]{3,2,1,0:T(8,128)(2,1)} all-to-all(bf16[4,2,256,384]{3,2,1,0:T(8,128)(2,1)} %gate.1), channel_id=1, replica_groups={{0,8,16,24},{32,40,48,56},{64,72,80,88},{96,104,112,120},{128,136,144,1..., dimensions={0} | all-to-all | bytes 3145728 | tf_op jit(solution)/shard_map/all_to_all | solution.py:375
  101.0 5.9 %gru.1 = (bf16[256,512]{1,0:T(8,128)(2,1)}, bf16[4,2,32,1024]{3,2,1,0:T(8,128)(2,1)}, bf16[4,2,32,1024]{3,2,1,0:T(8,128)(2,1)}) custom-call(s32[2]{0:T(128)} %copy-done.1, bf16[256,512]{1,0:T(8,128)(2,1)} %deter_hbm.1, bf16[512,1536]{1,0:T(8,128)(2,1)} %bitcast.40, bf16[512,1024]{1,0:T(8,128)(2,1)} %w_in_hbm.1, bf16[4,2,256,384]{3,2,1,0:T(8,128)(2,1)} %all_to_all.25.f_hbm), custom_call_target="tpu_custom_call" | custom-call | flops 1342177280 | bytes 5767168 | tf_op jit(solution)/shard_map/gru/pallas_call | solution.py:257
  107.0 3.2 %collective-permute-start.7 = (bf16[4,2,32,1024]{3,2,1,0:T(8,128)(2,1)}, bf16[4,2,32,1024]{3,2,1,0:T(8,128)(2,1)S(1)}, u32[]{:S(2)}, u32[]{:S(2)}) collective-permute-start(bf16[4,2,32,1024]{3,2,1,0:T(8,128)(2,1)} %get-tuple-element.15), channel_id=1, source_target_pairs={{0,1},{1,0},{2,3},{3,2},{4,5},{5,4},{6,7},{7,6},{8,9},{9,8},{10,11... | collective-permute-start | bytes 1572872 | tf_op jit(solution)/shard_map/ppermute | solution.py:58
  110.2 2.5 %collective-permute-start.10 = (bf16[1024,128]{1,0:T(8,128)(2,1)S(1)}, bf16[1024,128]{1,0:T(8,128)(2,1)S(1)}, u32[]{:S(2)}, u32[]{:S(2)}) collective-permute-start(bf16[1024,128]{1,0:T(8,128)(2,1)S(1)} %copy-done.7), channel_id=1, source_target_pairs={{0,6},{1,7},{2,0},{3,1},{4,2},{5,3},{6,4},{7,5},{8,14},{9,15},{10,... | collective-permute-start | bytes 786440 | tf_op jit(solution)/shard_map/ppermute | solution.py:53
  112.7 2.1 %collective-permute-start.9 = (bf16[1024,128]{1,0:T(8,128)(2,1)S(1)}, bf16[1024,128]{1,0:T(8,128)(2,1)S(1)}, u32[]{:S(2)}, u32[]{:S(2)}) collective-permute-start(bf16[1024,128]{1,0:T(8,128)(2,1)S(1)} %copy-done.7), channel_id=1, source_target_pairs={{0,4},{1,5},{2,6},{3,7},{4,0},{5,1},{6,2},{7,3},{8,12},{9,13},{10,... | collective-permute-start | bytes 786440 | tf_op jit(solution)/shard_map/ppermute | solution.py:53
  114.9 2.6 %collective-permute-start.8 = (bf16[1024,128]{1,0:T(8,128)(2,1)S(1)}, bf16[1024,128]{1,0:T(8,128)(2,1)S(1)}, u32[]{:S(2)}, u32[]{:S(2)}) collective-permute-start(bf16[1024,128]{1,0:T(8,128)(2,1)S(1)} %copy-done.7), channel_id=1, source_target_pairs={{0,2},{1,3},{2,4},{3,5},{4,6},{5,7},{6,0},{7,1},{8,10},{9,11},{10,... | collective-permute-start | bytes 786440 | tf_op jit(solution)/shard_map/ppermute | solution.py:53
  117.5 2.6 %collective-permute-done.10 = bf16[1024,128]{1,0:T(8,128)(2,1)S(1)} collective-permute-done((bf16[1024,128]{1,0:T(8,128)(2,1)S(1)}, bf16[1024,128]{1,0:T(8,128)(2,1)S(1)}, u32[]{:S(2)}, u32[]{:S(2)}) %collective-permute-start.10) | collective-permute-done | bytes 262176 | tf_op jit(solution)/shard_map/ppermute | solution.py:53
  120.0 3.7 %collective-permute-done.9 = bf16[1024,128]{1,0:T(8,128)(2,1)S(1)} collective-permute-done((bf16[1024,128]{1,0:T(8,128)(2,1)S(1)}, bf16[1024,128]{1,0:T(8,128)(2,1)S(1)}, u32[]{:S(2)}, u32[]{:S(2)}) %collective-permute-start.9) | collective-permute-done | bytes 262176 | tf_op jit(solution)/shard_map/ppermute | solution.py:53
  123.8 6.2 %collective-permute-done.8 = bf16[1024,128]{1,0:T(8,128)(2,1)S(1)} collective-permute-done((bf16[1024,128]{1,0:T(8,128)(2,1)S(1)}, bf16[1024,128]{1,0:T(8,128)(2,1)S(1)}, u32[]{:S(2)}, u32[]{:S(2)}) %collective-permute-start.8) | collective-permute-done | bytes 262176 | tf_op jit(solution)/shard_map/ppermute | solution.py:53
  130.2 1.0 add_convert_fusion
  131.2 2.4 %collective-permute-start.11 = (bf16[4,1024,128]{2,1,0:T(8,128)(2,1)S(1)}, bf16[4,1024,128]{2,1,0:T(8,128)(2,1)S(1)}, u32[]{:S(2)}, u32[]{:S(2)}) collective-permute-start(bf16[4,1024,128]{2,1,0:T(8,128)(2,1)S(1)} %pad_maximum_fusion.1.mine_ref), channel_id=1, source_target_pairs={{0,1},{1,0},{2,3},{3,2},{4,5},{5,4},{6,7},{7,6},{8,9},{9,8},{10,11... | collective-permute-start | bytes 3145736 | tf_op jit(solution)/shard_map/ppermute | solution.py:58
  133.9 3.5 %all-to-all-start.3 = ((bf16[4,64,1024]{2,1,0:T(8,128)(2,1)}), bf16[4,64,1024]{2,1,0:T(8,128)(2,1)S(1)}, u32[]{:S(2)}, u32[]{:S(2)}) async-start(bf16[4,64,1024]{2,1,0:T(8,128)(2,1)} %bitcast.16), calls=%async_computation.3 | async-start | bytes 1048576 | tf_op jit(solution)/shard_map/all_to_all | solution.py:389
  137.6 9.3 %all-to-all-done.3.parts_ref = bf16[4,64,1024]{2,1,0:T(8,128)(2,1)S(1)} async-done(((bf16[4,64,1024]{2,1,0:T(8,128)(2,1)}), bf16[4,64,1024]{2,1,0:T(8,128)(2,1)S(1)}, u32[]{:S(2)}, u32[]{:S(2)}) %all-to-all-start.3) | async-done | bytes 524320 | tf_op jit(solution)/shard_map/all_to_all | solution.py:389
  146.9 3.3 %tail.1 = f32[8,8,128]{2,1,0:T(8,128)} custom-call(s32[2]{0:T(128)S(1)} %copy-done.2, bf16[4,64,1024]{2,1,0:T(8,128)(2,1)S(1)} %all-to-all-done.3.parts_ref, bf16[4,1024,128]{2,1,0:T(8,128)(2,1)S(1)} %pad_maximum_fusion.1.mine_ref, bf16[4,1024,128]{2,1,0:T(8,128)(2,1)S(1)} %collective-permute-done.11.other_ref, bf16[64,32]{1,0:T(8,128)(2,1)S(1)} %bitcast.29, ...), custom_call_target="tpu_custom_call" | custom-call | flops 134217728 | bytes 4194304 | tf_op jit(solution)/shard_map/tail/pallas_call | solution.py:322
  150.3 4.0 %all-to-all-start.4 = ((f32[8,8,128]{2,1,0:T(8,128)}), f32[8,8,128]{2,1,0:T(8,128)S(1)}, u32[]{:S(2)}, u32[]{:S(2)}) async-start(f32[8,8,128]{2,1,0:T(8,128)} %tail.1), calls=%async_computation.4 | async-start | bytes 65536 | tf_op jit(solution)/shard_map/all_to_all | solution.py:393
  155.1 3.9 %all-to-all-done.4 = f32[8,8,128]{2,1,0:T(8,128)S(1)} async-done(((f32[8,8,128]{2,1,0:T(8,128)}), f32[8,8,128]{2,1,0:T(8,128)S(1)}, u32[]{:S(2)}, u32[]{:S(2)}) %all-to-all-start.4) | async-done | bytes 32800 | tf_op jit(solution)/shard_map/all_to_all | solution.py:393
  (70 shorter events, 6.6 us)
Async XLA Ops:
  0.6 0.8 copy-start
  1.4 21.0 %copy-start.9 = (s32[256,32]{0,1:T(8,128)S(1)}, s32[256,32]{0,1:T(8,128)}, u32[]{:S(2)}) copy-start(s32[256,32]{0,1:T(8,128)} %param.12) | copy-start | bytes 98308
  1.4 28.2 %copy-start.6 = (bf16[1024,128]{1,0:T(8,128)(2,1)S(1)}, bf16[1024,128]{1,0:T(8,128)(2,1)}, u32[]{:S(2)}) copy-start(bf16[1024,128]{1,0:T(8,128)(2,1)} %param.16) | copy-start | bytes 786436
  1.4 28.2 %copy-start.10 = (bf16[18,128]{1,0:T(8,128)(2,1)S(1)}, bf16[18,128]{1,0:T(8,128)(2,1)}, u32[]{:S(2)}) copy-start(bf16[18,128]{1,0:T(8,128)(2,1)} %param.17) | copy-start | bytes 13828
  2.1 37.0 %all-to-all-start = ((bf16[16,16,384]{2,1,0:T(8,128)(2,1)}), bf16[16,16,384]{2,1,0:T(8,128)(2,1)S(1)}, u32[]{:S(2)}, u32[]{:S(2)}) async-start(bf16[16,16,384]{2,1,0:T(8,128)(2,1)} %bitcast.14), calls=%async_computation | async-start | bytes 393216 | tf_op jit(solution)/shard_map/all_to_all | solution.py:358
  22.7 33.1 %collective-permute-start.2 = (bf16[256,128]{1,0:T(8,128)(2,1)S(1)}, bf16[256,128]{1,0:T(8,128)(2,1)}, u32[]{:S(2)}, u32[]{:S(2)}) collective-permute-start(bf16[256,128]{1,0:T(8,128)(2,1)S(1)} %fusion.10), channel_id=1, source_target_pairs={{0,24},{8,0},{16,8},{24,16},{32,56},{40,32},{48,40},{56,48},{64,88... | collective-permute-start | bytes 196616 | tf_op jit(solution)/shard_map/ppermute | solution.py:47
  27.2 28.6 %collective-permute-start.1 = (bf16[256,128]{1,0:T(8,128)(2,1)S(1)}, bf16[256,128]{1,0:T(8,128)(2,1)}, u32[]{:S(2)}, u32[]{:S(2)}) collective-permute-start(bf16[256,128]{1,0:T(8,128)(2,1)S(1)} %fusion.10), channel_id=1, source_target_pairs={{0,16},{8,24},{16,0},{24,8},{32,48},{40,56},{48,32},{56,40},{64,80... | collective-permute-start | bytes 196616 | tf_op jit(solution)/shard_map/ppermute | solution.py:47
  29.7 13.9 %collective-permute-start.5 = (bf16[1152,128]{1,0:T(8,128)(2,1)S(1)}, bf16[1152,128]{1,0:T(8,128)(2,1)S(1)}, u32[]{:S(2)}, u32[]{:S(2)}) collective-permute-start(bf16[1152,128]{1,0:T(8,128)(2,1)S(1)} %get-tuple-element.19), channel_id=1, source_target_pairs={{0,6},{1,7},{2,0},{3,1},{4,2},{5,3},{6,4},{7,5},{8,14},{9,15},{10,... | collective-permute-start | bytes 884744 | tf_op jit(solution)/shard_map/ppermute | solution.py:53
  34.1 12.0 %collective-permute-start.4 = (bf16[1152,128]{1,0:T(8,128)(2,1)S(1)}, bf16[1152,128]{1,0:T(8,128)(2,1)S(1)}, u32[]{:S(2)}, u32[]{:S(2)}) collective-permute-start(bf16[1152,128]{1,0:T(8,128)(2,1)S(1)} %get-tuple-element.19), channel_id=1, source_target_pairs={{0,4},{1,5},{2,6},{3,7},{4,0},{5,1},{6,2},{7,3},{8,12},{9,13},{10,... | collective-permute-start | bytes 884744 | tf_op jit(solution)/shard_map/ppermute | solution.py:53
  36.6 15.6 %collective-permute-start.3 = (bf16[1152,128]{1,0:T(8,128)(2,1)S(1)}, bf16[1152,128]{1,0:T(8,128)(2,1)S(1)}, u32[]{:S(2)}, u32[]{:S(2)}) collective-permute-start(bf16[1152,128]{1,0:T(8,128)(2,1)S(1)} %get-tuple-element.19), channel_id=1, source_target_pairs={{0,2},{1,3},{2,4},{3,5},{4,6},{5,7},{6,0},{7,1},{8,10},{9,11},{10,... | collective-permute-start | bytes 884744 | tf_op jit(solution)/shard_map/ppermute | solution.py:53
  40.1 29.3 %all-to-all-start.1 = ((bf16[4,256,384]{2,1,0:T(8,128)(2,1)}), bf16[4,256,384]{2,1,0:T(8,128)(2,1)S(1)}, u32[]{:S(2)}, u32[]{:S(2)}) async-start(bf16[4,256,384]{2,1,0:T(8,128)(2,1)} %broadcast_in_dim.53), calls=%async_computation.1 | async-start | bytes 1572864 | tf_op jit(solution)/shard_map/all_to_all | solution.py:360
  43.7 12.1 %collective-permute-start = (bf16[256,128]{1,0:T(8,128)(2,1)S(1)}, bf16[256,128]{1,0:T(8,128)(2,1)}, u32[]{:S(2)}, u32[]{:S(2)}) collective-permute-start(bf16[256,128]{1,0:T(8,128)(2,1)S(1)} %fusion.10), channel_id=1, source_target_pairs={{0,8},{8,16},{16,24},{24,0},{32,40},{40,48},{48,56},{56,32},{64,72... | collective-permute-start | bytes 196616 | tf_op jit(solution)/shard_map/ppermute | solution.py:47
  52.3 5.5 %collective-permute-start.6 = (bf16[4,1152,128]{2,1,0:T(8,128)(2,1)S(1)}, bf16[4,1152,128]{2,1,0:T(8,128)(2,1)S(1)}, u32[]{:S(2)}, u32[]{:S(2)}) collective-permute-start(bf16[4,1152,128]{2,1,0:T(8,128)(2,1)S(1)} %pad_maximum_fusion.mine_ref), channel_id=1, source_target_pairs={{0,1},{1,0},{2,3},{3,2},{4,5},{5,4},{6,7},{7,6},{8,9},{9,8},{10,11... | collective-permute-start | bytes 3538952 | tf_op jit(solution)/shard_map/ppermute | solution.py:58
  55.8 13.6 %copy-start.1 = (s32[2]{0:T(128)}, s32[2]{0:T(128)S(1)}, u32[]{:S(2)}) copy-start(s32[2]{0:T(128)S(1)} %pad_add_fusion.me_ref.core_ref) | copy-start | bytes 28
  69.4 0.9 copy-start.3
  101.0 9.2 %copy-start.7 = (bf16[1024,128]{1,0:T(8,128)(2,1)S(1)}, bf16[1024,128]{1,0:T(8,128)(2,1)}, u32[]{:S(2)}) copy-start(bf16[1024,128]{1,0:T(8,128)(2,1)} %param.21) | copy-start | bytes 786436
  107.0 23.2 %copy-start.4 = (bf16[4,2,32,1024]{3,2,1,0:T(8,128)(2,1)S(1)}, bf16[4,2,32,1024]{3,2,1,0:T(8,128)(2,1)}, u32[]{:S(2)}) copy-start(bf16[4,2,32,1024]{3,2,1,0:T(8,128)(2,1)} %get-tuple-element.14) | copy-start | bytes 1572868
  107.0 23.2 %collective-permute-start.7 = (bf16[4,2,32,1024]{3,2,1,0:T(8,128)(2,1)}, bf16[4,2,32,1024]{3,2,1,0:T(8,128)(2,1)S(1)}, u32[]{:S(2)}, u32[]{:S(2)}) collective-permute-start(bf16[4,2,32,1024]{3,2,1,0:T(8,128)(2,1)} %get-tuple-element.15), channel_id=1, source_target_pairs={{0,1},{1,0},{2,3},{3,2},{4,5},{5,4},{6,7},{7,6},{8,9},{9,8},{10,11... | collective-permute-start | bytes 1572872 | tf_op jit(solution)/shard_map/ppermute | solution.py:58
  110.2 9.8 %collective-permute-start.10 = (bf16[1024,128]{1,0:T(8,128)(2,1)S(1)}, bf16[1024,128]{1,0:T(8,128)(2,1)S(1)}, u32[]{:S(2)}, u32[]{:S(2)}) collective-permute-start(bf16[1024,128]{1,0:T(8,128)(2,1)S(1)} %copy-done.7), channel_id=1, source_target_pairs={{0,6},{1,7},{2,0},{3,1},{4,2},{5,3},{6,4},{7,5},{8,14},{9,15},{10,... | collective-permute-start | bytes 786440 | tf_op jit(solution)/shard_map/ppermute | solution.py:53
  112.7 11.0 %collective-permute-start.9 = (bf16[1024,128]{1,0:T(8,128)(2,1)S(1)}, bf16[1024,128]{1,0:T(8,128)(2,1)S(1)}, u32[]{:S(2)}, u32[]{:S(2)}) collective-permute-start(bf16[1024,128]{1,0:T(8,128)(2,1)S(1)} %copy-done.7), channel_id=1, source_target_pairs={{0,4},{1,5},{2,6},{3,7},{4,0},{5,1},{6,2},{7,3},{8,12},{9,13},{10,... | collective-permute-start | bytes 786440 | tf_op jit(solution)/shard_map/ppermute | solution.py:53
  114.9 15.1 %collective-permute-start.8 = (bf16[1024,128]{1,0:T(8,128)(2,1)S(1)}, bf16[1024,128]{1,0:T(8,128)(2,1)S(1)}, u32[]{:S(2)}, u32[]{:S(2)}) collective-permute-start(bf16[1024,128]{1,0:T(8,128)(2,1)S(1)} %copy-done.7), channel_id=1, source_target_pairs={{0,2},{1,3},{2,4},{3,5},{4,6},{5,7},{6,0},{7,1},{8,10},{9,11},{10,... | collective-permute-start | bytes 786440 | tf_op jit(solution)/shard_map/ppermute | solution.py:53
  130.1 3.4 %copy-start.11 = (s32[4]{0:T(128)S(1)}, s32[4]{0:T(128)}, u32[]{:S(2)}) copy-start(s32[4]{0:T(128)} %param.15) | copy-start | bytes 52
  130.1 3.7 %copy-start.8 = (s32[2,256,32]{1,2,0:T(8,128)S(1)}, s32[2,256,32]{1,2,0:T(8,128)}, u32[]{:S(2)}) copy-start(s32[2,256,32]{1,2,0:T(8,128)} %param.13) | copy-start | bytes 196612
  130.2 16.8 %copy-start.2 = (s32[2]{0:T(128)S(1)}, s32[2]{0:T(128)}, u32[]{:S(2)}) copy-start(s32[2]{0:T(128)} %copy-done.1) | copy-start | bytes 28
  131.2 15.8 %collective-permute-start.11 = (bf16[4,1024,128]{2,1,0:T(8,128)(2,1)S(1)}, bf16[4,1024,128]{2,1,0:T(8,128)(2,1)S(1)}, u32[]{:S(2)}, u32[]{:S(2)}) collective-permute-start(bf16[4,1024,128]{2,1,0:T(8,128)(2,1)S(1)} %pad_maximum_fusion.1.mine_ref), channel_id=1, source_target_pairs={{0,1},{1,0},{2,3},{3,2},{4,5},{5,4},{6,7},{7,6},{8,9},{9,8},{10,11... | collective-permute-start | bytes 3145736 | tf_op jit(solution)/shard_map/ppermute | solution.py:58
  133.9 13.1 %all-to-all-start.3 = ((bf16[4,64,1024]{2,1,0:T(8,128)(2,1)}), bf16[4,64,1024]{2,1,0:T(8,128)(2,1)S(1)}, u32[]{:S(2)}, u32[]{:S(2)}) async-start(bf16[4,64,1024]{2,1,0:T(8,128)(2,1)} %bitcast.16), calls=%async_computation.3 | async-start | bytes 1048576 | tf_op jit(solution)/shard_map/all_to_all | solution.py:389
  146.9 7.4 %copy-start.5 = (bf16[256,512]{1,0:T(8,128)(2,1)S(1)}, bf16[256,512]{1,0:T(8,128)(2,1)}, u32[]{:S(2)}) copy-start(bf16[256,512]{1,0:T(8,128)(2,1)} %get-tuple-element.13) | copy-start | bytes 786436
  150.3 8.8 %all-to-all-start.4 = ((f32[8,8,128]{2,1,0:T(8,128)}), f32[8,8,128]{2,1,0:T(8,128)S(1)}, u32[]{:S(2)}, u32[]{:S(2)}) async-start(f32[8,8,128]{2,1,0:T(8,128)} %tail.1), calls=%async_computation.4 | async-start | bytes 65536 | tf_op jit(solution)/shard_map/all_to_all | solution.py:393

commit v4 on v2

v4 whole, which is shorter than its diff:
```python
import functools

import jax
import jax.numpy as jnp
from jax import lax
from jax.experimental import pallas as pl
from jax.experimental.pallas import tpu as pltpu
from jax.sharding import PartitionSpec as P

STOCH = 32
CLASSES = 32
LAT = STOCH * CLASSES
ACTIONS = 18
STEPS = 64
IMAG = 2
UNITS = 1024
NY = 4
NX = 4
NC = 2
NEAR = 4
LANES = 128
CODES = 80
EPS = 1e-06
MIB = 1024 * 1024


def y_groups(n_dp):
    return [[start + y for y in range(NY)] for start in range(0, n_dp, NY)]


def far_groups(n_dp):
    n_far = n_dp // NY // NEAR
    return [[(far * NEAR + near) * NY + y for far in range(n_far)] for near in range(NEAR) for y in range(NY)]


def y_shift(value, step, n_dp):
    perm = [(i, i // NY * NY + (i % NY + step) % NY) for i in range(n_dp)]
    return lax.ppermute(value, "dp", perm)


def z_shift(value, step, n_dp):
    return lax.ppermute(value, "dp", [(i, (i + step * NY) % n_dp) for i in range(n_dp)])


def x_shift(value, step):
    count = NX * NC
    perm = [(i, (i + step * NC) % count) for i in range(count)]
    return lax.ppermute(value, "tensor", perm)


def core_swap(value):
    perm = [(i, i ^ 1) for i in range(NX * NC)]
    return lax.ppermute(value, "tensor", perm)


def x_gather(value):
    return jnp.stack([value] + [x_shift(value, step) for step in range(1, NX)])


def silu(value):
    half = 0.5 * value
    return half + half * jnp.tanh(half)


def sigmoid(value):
    return 0.5 + 0.5 * jnp.tanh(0.5 * value)


def prep_kernel(w_ref, latent_ref, samples_ref, actions_ref, out_ref):
    depth = w_ref.shape[0]
    part = w_ref.shape[1] // 3 // NY
    rows = out_ref.shape[2]
    line = lax.broadcasted_iota(jnp.int32, (CODES - IMAG * STOCH, rows), 0)
    acts = jnp.zeros((CODES - IMAG * STOCH, rows), jnp.float32)
    for k in range(IMAG):
        acts = jnp.where(line == k, actions_ref[k : k + 1].astype(jnp.float32), acts)
    codes = [latent_ref[...].astype(jnp.float32), samples_ref[0].astype(jnp.float32), acts]
    codes = jnp.concatenate(codes, axis=0).astype(jnp.bfloat16)
    for y in range(NY):
        for which in range(3):
            columns = w_ref[:, (which * NY + y) * part : (which * NY + y + 1) * part]
            out_ref[y, which // 2 * depth : (which // 2 + 1) * depth, which % 2 * part : (which % 2 + 1) * part] = columns
        out_ref[y, depth : 2 * depth, part:] = jnp.zeros((depth, rows - part), jnp.bfloat16)
        out_ref[y, 2 * depth :] = codes


def prep_call(w_gate, latent, samples, actions):
    depth = w_gate.shape[0]
    rows = latent.shape[1]
    vmem = pl.BlockSpec(memory_space=pltpu.VMEM)
    return pl.pallas_call(
        prep_kernel,
        in_specs=[vmem] * 4,
        out_specs=vmem,
        out_shape=jax.ShapeDtypeStruct((NY, 2 * depth + CODES, rows), jnp.bfloat16),
        compiler_params=pltpu.CompilerParams(vmem_limit_bytes=16 * MIB),
        cost_estimate=pl.CostEstimate(flops=0, bytes_accessed=NY * rows * 512, transcendentals=0),
        name="prep",
    )(w_gate, latent, samples, actions)


def copies_kernel(came_ref, out_ref):
    depth = out_ref.shape[1] // NY
    part = out_ref.shape[2] // 3
    for y in range(NY):
        for far in range(out_ref.shape[0]):
            here = slice(y * depth, (y + 1) * depth)
            out_ref[far, here, : 2 * part] = came_ref[y, :depth, : 2 * part]
            out_ref[far, here, 2 * part :] = came_ref[y, depth : 2 * depth, :part]


def copies_call(came, n_far, depth, width):
    vmem = pl.BlockSpec(memory_space=pltpu.VMEM)
    return pl.pallas_call(
        copies_kernel,
        in_specs=[vmem],
        out_specs=vmem,
        out_shape=jax.ShapeDtypeStruct((n_far, NY * depth, width), jnp.bfloat16),
        compiler_params=pltpu.CompilerParams(vmem_limit_bytes=16 * MIB),
        cost_estimate=pl.CostEstimate(flops=0, bytes_accessed=4 * n_far * depth * width, transcendentals=0),
        name="copies",
    )(came)


def features_kernel(place_ref, came_ref, spread_ref, target_ref, mine_ref, other_ref, out0_ref, out1_ref, w_ref):
    x, core, y = place_ref[0], place_ref[1], place_ref[2]
    width = w_ref.shape[0]
    rows = out0_ref.shape[0]

    @pl.when(pl.program_id(0) == 0)
    def _():
        for i in range(NX):
            base = lax.rem(x + NX - i, NX) * NC
            w_ref[:, pl.ds(pl.multiple_of((base + core) * LANES, LANES), LANES)] = mine_ref[i]
            w_ref[:, pl.ds(pl.multiple_of((base + 1 - core) * LANES, LANES), LANES)] = other_ref[i]

    codes = came_ref[lax.rem(y + pl.program_id(0), NY)][came_ref.shape[1] - CODES :]
    spread = lax.dot_general(codes, spread_ref[...], (((0,), (0,)), ((), ())), preferred_element_type=jnp.float32)
    spread = jnp.concatenate([spread[:, :width], spread[:, width:]], axis=0)
    hot = jnp.where(spread == target_ref[...], 1.0, 0.0).astype(jnp.bfloat16)
    pre = jnp.dot(hot, w_ref[...], preferred_element_type=jnp.float32)
    scale = lax.rsqrt(jnp.mean(pre * pre, axis=1, keepdims=True) + EPS)
    features = silu(pre * scale).astype(jnp.bfloat16)
    out0_ref[...] = features[:rows]
    out1_ref[...] = features[rows:]


def features_call(place, came, mine, other):
    rows = came.shape[2]
    width = mine.shape[1]
    lane = jnp.arange(width, dtype=jnp.int32)
    is_lat = lane < LAT
    target = jnp.where(is_lat, lane % CLASSES, lane - LAT).astype(jnp.float32)[None, :]
    source = [jnp.where(is_lat, k * STOCH + lane // CLASSES, IMAG * STOCH + k) for k in range(IMAG)]
    source = jnp.concatenate(source)
    spread = (jnp.arange(CODES, dtype=jnp.int32)[:, None] == source[None, :]).astype(jnp.bfloat16)
    out = pltpu.HBM((NY, rows, UNITS), jnp.bfloat16)
    return pl.pallas_call(
        features_kernel,
        grid=(NY,),
        in_specs=[
            pl.BlockSpec(memory_space=pltpu.SMEM),
            pl.BlockSpec(came.shape, lambda b: (0, 0, 0)),
            pl.BlockSpec(spread.shape, lambda b: (0, 0)),
            pl.BlockSpec((1, width), lambda b: (0, 0)),
            pl.BlockSpec((NX, width, LANES), lambda b: (0, 0, 0)),
            pl.BlockSpec((NX, width, LANES), lambda b: (0, 0, 0)),
        ],
        out_specs=[pl.BlockSpec((None, rows, UNITS), lambda b: (b, 0, 0))] * IMAG,
        out_shape=[out] * IMAG,
        scratch_shapes=[pltpu.VMEM((width, UNITS), jnp.bfloat16)],
        compiler_params=pltpu.CompilerParams(vmem_limit_bytes=32 * MIB),
        cost_estimate=pl.CostEstimate(
            flops=2 * IMAG * NY * rows * width * (UNITS + LANES),
            bytes_accessed=IMAG * NY * rows * UNITS * 2 + width * UNITS * 2,
            transcendentals=IMAG * NY * rows * UNITS,
        ),
        name="features",
    )(place, came, spread, target, mine, other)


def gate_kernel(n_far, place_ref, features_ref, g0_ref, g1_ref, g2_ref, g3_ref, o0_ref, o1_ref, o2_ref, o3_ref, w_ref):
    outs = (o0_ref, o1_ref, o2_ref, o3_ref)
    depth = g0_ref.shape[0] // n_far
    near = place_ref[3]
    each, rows = features_ref.shape[:2]

    @pl.when(pl.program_id(0) == 0)
    def _():
        for i, g_ref in enumerate((g0_ref, g1_ref, g2_ref, g3_ref)):
            from_near = lax.rem(near + NEAR - i, NEAR)
            for far in range(n_far):
                start = pl.multiple_of((far * NEAR + from_near) * depth, depth)
                w_ref[pl.ds(start, depth)] = g_ref[far * depth : (far + 1) * depth]

    flat = features_ref[...].reshape(each * rows, UNITS)
    total = jnp.dot(flat, w_ref[...], preferred_element_type=jnp.float32).astype(jnp.bfloat16)
    for step in range(NY // each):

        @pl.when(pl.program_id(0) == step)
        def _():
            for i in range(each):
                outs[step * each + i][...] = total[i * rows : (i + 1) * rows]


def gate_call(place, features, held, n_far):
    rows = features.shape[1]
    width = held[0].shape[1]
    each = 2
    whole = pl.BlockSpec(held[0].shape, lambda b: (0, 0))
    return pl.pallas_call(
        functools.partial(gate_kernel, n_far),
        grid=(NY // each,),
        in_specs=[
            pl.BlockSpec(memory_space=pltpu.SMEM),
            pl.BlockSpec((each, rows, UNITS), lambda b: (b, 0, 0)),
        ]
        + [whole] * NEAR,
        out_specs=[pl.BlockSpec((rows, width), lambda b: (0, 0))] * NY,
        out_shape=[jax.ShapeDtypeStruct((rows, width), jnp.bfloat16)] * NY,
        scratch_shapes=[pltpu.VMEM((UNITS, width), jnp.bfloat16)],
        compiler_params=pltpu.CompilerParams(vmem_limit_bytes=24 * MIB),
        cost_estimate=pl.CostEstimate(
            flops=2 * NY * rows * UNITS * width,
            bytes_accessed=NY * rows * (UNITS + width) * 2 + UNITS * width * 2,
            transcendentals=0,
        ),
        name="gate",
    )(place, features, *held)


def gru_kernel(place_ref, deter_ref, w_rec_ref, w_in_ref, f0_ref, f1_ref, f2_ref, f3_ref, new_ref, prior_ref, rec_ref):
    y = place_ref[2]
    bw = deter_ref.shape[1]
    part = bw // NY
    rec_ref[...] = jnp.dot(deter_ref[...], w_rec_ref[...], preferred_element_type=jnp.float32)
    for i, f_ref in enumerate((f0_ref, f1_ref, f2_ref, f3_ref)):
        off = pl.multiple_of(lax.rem(y + NY - i, NY) * part, part)

        def gate(which):
            mine = f_ref[:, which * part : (which + 1) * part].astype(jnp.float32)
            return rec_ref[:, pl.ds(pl.multiple_of(which * bw + off, part), part)] + mine

        reset = sigmoid(gate(0))
        candidate = jnp.tanh(reset * gate(1))
        update = sigmoid(gate(2) - 1.0)
        old = deter_ref[:, pl.ds(off, part)].astype(jnp.float32)
        fresh = update * candidate + (1.0 - update) * old
        new_ref[:, pl.ds(off, part)] = fresh.astype(jnp.bfloat16)
    prior_ref[...] = jnp.dot(new_ref[...], w_in_ref[...], preferred_element_type=jnp.float32).astype(jnp.bfloat16)


def gru_call(place, deter, w_rec, w_in, sums):
    rows, bw = deter.shape
    vmem = pl.BlockSpec(memory_space=pltpu.VMEM)
    return pl.pallas_call(
        gru_kernel,
        in_specs=[pl.BlockSpec(memory_space=pltpu.SMEM)] + [vmem] * 7,
        out_specs=[vmem, vmem],
        out_shape=[
            jax.ShapeDtypeStruct((rows, bw), jnp.bfloat16),
            jax.ShapeDtypeStruct((rows, w_in.shape[1]), jnp.bfloat16),
        ],
        scratch_shapes=[pltpu.VMEM((rows, 3 * bw), jnp.float32)],
        compiler_params=pltpu.CompilerParams(vmem_limit_bytes=24 * MIB),
        cost_estimate=pl.CostEstimate(
            flops=2 * rows * bw * (3 * bw + w_in.shape[1]),
            bytes_accessed=2 * (w_rec.size + w_in.size) + 12 * rows * bw,
            transcendentals=3 * rows * bw,
        ),
        name="gru",
    )(place, deter, w_rec, w_in, *sums)


def tail_kernel(step, place_ref, parts_ref, mine_ref, other_ref, picked_ref, var_ref, mask_ref, prev_ref, log_ref):
    pre = parts_ref[0].astype(jnp.float32)
    for i in range(1, parts_ref.shape[0]):
        pre = pre + parts_ref[i].astype(jnp.float32)
    normed = pre * lax.rsqrt(jnp.mean(pre * pre, axis=1, keepdims=True) + EPS)
    hidden = silu(normed).astype(jnp.bfloat16)
    rows = hidden.shape[0]
    cls = lax.broadcasted_iota(jnp.int32, (rows, LANES), 1) % CLASSES

    def within(value, combine):
        step = 1
        while step < CLASSES:
            ahead = pltpu.roll(value, step, 1)
            wrapped = pltpu.roll(value, LANES - CLASSES + step, 1)
            value = combine(value, jnp.where(cls >= step, ahead, wrapped))
            step *= 2
        return value

    total = jnp.zeros((rows, LANES), jnp.float32)
    x, core = place_ref[0], place_ref[1]
    for i in range(NX * NC):
        w_ref = mine_ref if i % NC == 0 else other_ref
        piece = lax.rem(x + NX - i // NC, NX) * NC + (core if i % NC == 0 else 1 - core)
        here = pl.ds(pl.multiple_of(piece * LANES, LANES), LANES)
        logits = jnp.dot(hidden, w_ref[i // NC], preferred_element_type=jnp.float32)
        powers = jnp.exp(logits - within(logits, jnp.maximum))
        probs = 0.99 * (powers / within(powers, jnp.add)) + 0.01 / CLASSES
        want = jnp.dot(picked_ref[...], var_ref[:, here], preferred_element_type=jnp.float32)
        total = total + jnp.where(cls.astype(jnp.float32) == want, jnp.log(probs), 0.0)
    summed = jnp.where(mask_ref[...] > 0, jnp.sum(total, axis=1, keepdims=True), 0.0)
    lanes = lax.broadcasted_iota(jnp.int32, (rows, LANES), 1)
    diagonal = lax.broadcasted_iota(jnp.int32, (rows, LANES), 0) == lanes
    line = jnp.sum(jnp.where(diagonal, summed, 0.0), axis=0, keepdims=True)
    here = lax.broadcasted_iota(jnp.int32, log_ref.shape, 1) == step
    log_ref[...] = jnp.where(here, line[None], prev_ref[...])


def tail_call(step, place, parts, mine, other, picked, mask, prev):
    rows = parts.shape[1]
    lane = jnp.arange(LAT, dtype=jnp.int32)
    var_of = (jnp.arange(STOCH, dtype=jnp.int32)[:, None] == lane[None, :] // CLASSES).astype(jnp.bfloat16)
    vmem = pl.BlockSpec(memory_space=pltpu.VMEM)
    return pl.pallas_call(
        functools.partial(tail_kernel, step),
        in_specs=[pl.BlockSpec(memory_space=pltpu.SMEM)] + [vmem] * 7,
        out_specs=vmem,
        out_shape=jax.ShapeDtypeStruct(prev.shape, jnp.float32),
        compiler_params=pltpu.CompilerParams(vmem_limit_bytes=24 * MIB),
        cost_estimate=pl.CostEstimate(
            flops=2 * rows * UNITS * LAT, bytes_accessed=8 * mine.size, transcendentals=4 * rows * LAT
        ),
        name="tail",
    )(place, parts, mine, other, picked, var_of, mask, prev)


def body(
    post_deter,
    post_sample,
    samples,
    actions,
    counts,
    w_stoch,
    w_action,
    w_gate,
    w_rec,
    w_prior_in,
    w_prior_out,
    n_dp,
):
    rows = post_deter.shape[0]
    depth = w_gate.shape[0]
    tensor_n = NX * NC
    share = rows // tensor_n
    n_far = n_dp // NY // NEAR
    me, dp_index = lax.axis_index("tensor"), lax.axis_index("dp")
    place = jnp.stack([me // NC, me % NC, dp_index % NY, dp_index // NY % NEAR]).astype(jnp.int32)

    sent = prep_call(w_gate, post_sample.T, samples.transpose(0, 2, 1), actions)
    came = lax.all_to_all(sent, "dp", 0, 0, axis_index_groups=y_groups(n_dp))
    held = copies_call(came, n_far, depth, w_gate.shape[1] // NY)
    held = lax.all_to_all(held, "dp", 0, 0, axis_index_groups=far_groups(n_dp)).reshape(n_far * NY * depth, -1)
    held = [held] + [z_shift(held, step, n_dp) for step in range(1, NEAR)]

    action_rows = jnp.pad(w_action, ((0, LANES - ACTIONS), (0, 0)))
    mine = x_gather(jnp.concatenate([w_stoch, action_rows], axis=0))
    other = core_swap(mine)
    features = features_call(place, came, mine, other)

    out_mine = x_gather(w_prior_out)
    out_other = core_swap(out_mine)

    positions = jnp.arange(STEPS, dtype=jnp.int32)
    valid_mask = (positions[None, :] < counts[:, None]).reshape(rows)
    my_mask = lax.dynamic_slice_in_dim(valid_mask, me * share, share, 0).astype(jnp.float32)[:, None]
    picked = lax.dynamic_slice_in_dim(samples, me * share, share, 1).astype(jnp.bfloat16)

    sums = []
    for k in range(IMAG):
        pieces = gate_call(place, features[k], held, n_far)
        sums.append([pieces[0]] + [y_shift(pieces[i], i, n_dp) for i in range(1, NY)])

    deter = post_deter
    logs = jnp.zeros((tensor_n, 8, LANES), jnp.float32)
    for k in range(IMAG):
        deter, partial = gru_call(place, deter, w_rec[0], w_prior_in, sums[k])
        parts = lax.all_to_all(partial.reshape(tensor_n, share, UNITS), "tensor", 0, 0)
        logs = tail_call(k, place, parts, out_mine, out_other, picked[k], my_mask, logs)
    logs = lax.all_to_all(logs, "tensor", 0, 0)[:, :IMAG, :share]
    log_prob = logs.transpose(1, 0, 2).reshape(IMAG, rows)
    deter_out = jnp.where(valid_mask[:, None], deter, jnp.zeros_like(deter))
    return (deter_out, log_prob)


def solution(mesh):
    in_specs = (
        P("dp", "tensor"),
        P("dp", None),
        P(None, "dp", None),
        P(None, "dp"),
        P("dp"),
        P(None, "tensor"),
        P(None, "tensor"),
        P("dp", "tensor"),
        P("tensor", None, None),
        P("tensor", None),
        P(None, "tensor"),
    )
    out_specs = (P("dp", "tensor"), P(None, "dp"))
    whole = functools.partial(body, n_dp=mesh.shape["dp"])
    return jax.shard_map(whole, mesh=mesh, in_specs=in_specs, out_specs=out_specs, check_vma=False)
```

time: 147 us -> 183 us (1.24)
  starting transfers between devices: 68.3 us -> 104 us
  waiting for transfers between devices: 40 us -> 33.3 us
  Pallas kernels: 21.2 us -> 26.9 us
  local copies, waits for them, and re-layouts: 10.2 us -> 12.4 us
    ppermute x6, waiting for transfers between devices: 20.7 us -> 0.02 us  [x_shift(): return lax.ppermute(value, 'tensor', perm)]
    ppermute x0 -> x3, starting transfers between devices: none -> 15.7 us  [z_shift(): lax.ppermute(value, 'dp', [(i, (i + step * NY) % n_dp) for i in range(n_d...]
    ppermute x3 -> x6, starting transfers between devices: 10.2 us -> 21.1 us  [y_shift(): return lax.ppermute(value, 'dp', perm)]
    ppermute x2, starting transfers between devices: 7.5 us -> 17.1 us  [core_swap(): return lax.ppermute(value, 'tensor', perm)]
    ppermute x3 -> x6, waiting for transfers between devices: 0.01 us -> 6.7 us  [y_shift(): return lax.ppermute(value, 'dp', perm)]
    all_to_all x4 -> x5, waiting for transfers between devices: 18.4 us -> 23.3 us  [the longest x1 13 us: body(): lax.all_to_all(held, 'dp', 0, 0, axis_index_groups=far_groups(n_dp))]
    pallas_call x4 -> x8, Pallas kernels: 11 us -> 15.6 us  [the longest x2 6.13 us: tail_call(): pl.pallas_call(functools.partial(tail_kernel, step), in_specs=[pl.BlockSp...]
    ppermute x0 -> x3, waiting for transfers between devices: none -> 3.24 us  [z_shift(): lax.ppermute(value, 'dp', [(i, (i + step * NY) % n_dp) for i in range(n_d...]
  transfers between devices with their start and end apart: 15 -> 22, of which waited for: 8 -> 8; matrix products, arithmetic and copies ran while one was open for 2% -> 2% of each run, Pallas kernels for 9% -> 13%
where the time goes in v4:
time: 183 us; the launch traced here: 182 us
  starting transfers between devices  104 us (57%)
  waiting for transfers between devices  33.3 us (18%)
  Pallas kernels  26.9 us (15%)
  local copies, waits for them, and re-layouts  12.4 us (7%)
  other arithmetic  3.66 us (2%)
    ppermute x6, starting transfers between devices, y_shift(): return lax.ppermute(value, 'dp', perm)  21.1 us
    ppermute x6, starting transfers between devices, x_shift(): return lax.ppermute(value, 'tensor', perm)  20.4 us
    ppermute x2, starting transfers between devices, core_swap(): return lax.ppermute(value, 'tensor', perm)  17.1 us
    ppermute x3, starting transfers between devices, z_shift(): lax.ppermute(value, 'dp', [(i, (i + step * NY) % n_dp) for i in range(n_d...  15.7 us
    all_to_all x1, waiting for transfers between devices, body(): lax.all_to_all(held, 'dp', 0, 0, axis_index_groups=far_groups(n_dp))  13 us
    all_to_all x1, starting transfers between devices, body(): lax.all_to_all(held, 'dp', 0, 0, axis_index_groups=far_groups(n_dp))  11.8 us
    unnamed x45, local copies, waits for them, and re-layouts  11.5 us
    pallas_call x1, Pallas kernels, features_call(): pl.pallas_call(features_kernel, grid=(NY,), in_specs=[pl.BlockSpec(memory...  11.4 us
  transfers between devices with their start and end apart: 22, of which 8 were waited for; matrix products, arithmetic and copies ran while one was open for 2% of the time, Pallas kernels for 13%

profile of v4, /device:TPU:1, one launch (start us, length us, event | category | flops | bytes accessed | tf_op | source)
XLA Modules:
  0.0 181.5 jit_solution(7597760762906542959)
XLA Ops:
  1.7 5.2 %collective-permute-start.2 = (bf16[1152,128]{1,0:T(8,128)(2,1)S(1)}, bf16[1152,128]{1,0:T(8,128)(2,1)S(1)}, u32[]{:S(2)}, u32[]{:S(2)}) collective-permute-start(bf16[1152,128]{1,0:T(8,128)(2,1)S(1)} %get-tuple-element.31), channel_id=1, source_target_pairs={{0,6},{1,7},{2,0},{3,1},{4,2},{5,3},{6,4},{7,5},{8,14},{9,15},{10,... | collective-permute-start | bytes 884744 | tf_op jit(solution)/shard_map/ppermute | solution.py:48
  6.9 1.9 %collective-permute-start = (bf16[1152,128]{1,0:T(8,128)(2,1)S(1)}, bf16[1152,128]{1,0:T(8,128)(2,1)S(1)}, u32[]{:S(2)}, u32[]{:S(2)}) collective-permute-start(bf16[1152,128]{1,0:T(8,128)(2,1)S(1)} %get-tuple-element.31), channel_id=1, source_target_pairs={{0,2},{1,3},{2,4},{3,5},{4,6},{5,7},{6,0},{7,1},{8,10},{9,11},{10,... | collective-permute-start | bytes 884744 | tf_op jit(solution)/shard_map/ppermute | solution.py:48
  8.8 3.6 %collective-permute-start.1 = (bf16[1152,128]{1,0:T(8,128)(2,1)S(1)}, bf16[1152,128]{1,0:T(8,128)(2,1)S(1)}, u32[]{:S(2)}, u32[]{:S(2)}) collective-permute-start(bf16[1152,128]{1,0:T(8,128)(2,1)S(1)} %get-tuple-element.31), channel_id=1, source_target_pairs={{0,4},{1,5},{2,6},{3,7},{4,0},{5,1},{6,2},{7,3},{8,12},{9,13},{10,... | collective-permute-start | bytes 884744 | tf_op jit(solution)/shard_map/ppermute | solution.py:48
  12.5 3.4 %collective-permute-start.13 = (bf16[1024,128]{1,0:T(8,128)(2,1)}, bf16[1024,128]{1,0:T(8,128)(2,1)}, u32[]{:S(2)}, u32[]{:S(2)}) collective-permute-start(bf16[1024,128]{1,0:T(8,128)(2,1)} %param.21), channel_id=1, source_target_pairs={{0,2},{1,3},{2,4},{3,5},{4,6},{5,7},{6,0},{7,1},{8,10},{9,11},{10,... | collective-permute-start | bytes 786440 | tf_op jit(solution)/shard_map/ppermute | solution.py:48
  15.9 2.5 %collective-permute-start.14 = (bf16[1024,128]{1,0:T(8,128)(2,1)}, bf16[1024,128]{1,0:T(8,128)(2,1)}, u32[]{:S(2)}, u32[]{:S(2)}) collective-permute-start(bf16[1024,128]{1,0:T(8,128)(2,1)} %param.21), channel_id=1, source_target_pairs={{0,4},{1,5},{2,6},{3,7},{4,0},{5,1},{6,2},{7,3},{8,12},{9,13},{10,... | collective-permute-start | bytes 786440 | tf_op jit(solution)/shard_map/ppermute | solution.py:48
  22.2 4.2 %all-to-all-start = ((bf16[4,112,256]{2,1,0:T(8,128)(2,1)}), bf16[4,112,256]{2,1,0:T(8,128)(2,1)S(1)}, u32[]{:S(2)}, u32[]{:S(2)}) async-start(bf16[4,112,256]{2,1,0:T(8,128)(2,1)} %prep.1), calls=%async_computation | async-start | bytes 458752 | tf_op jit(solution)/shard_map/all_to_all | solution.py:353
  26.4 3.7 %collective-permute-start.15 = (bf16[1024,128]{1,0:T(8,128)(2,1)}, bf16[1024,128]{1,0:T(8,128)(2,1)}, u32[]{:S(2)}, u32[]{:S(2)}) collective-permute-start(bf16[1024,128]{1,0:T(8,128)(2,1)} %param.21), channel_id=1, source_target_pairs={{0,6},{1,7},{2,0},{3,1},{4,2},{5,3},{6,4},{7,5},{8,14},{9,15},{10,... | collective-permute-start | bytes 786440 | tf_op jit(solution)/shard_map/ppermute | solution.py:48
  30.3 7.2 %collective-permute-start.3 = (bf16[4,1152,128]{2,1,0:T(8,128)(2,1)S(1)}, bf16[4,1152,128]{2,1,0:T(8,128)(2,1)S(1)}, u32[]{:S(2)}, u32[]{:S(2)}) collective-permute-start(bf16[4,1152,128]{2,1,0:T(8,128)(2,1)S(1)} %pad_maximum_fusion.mine_ref), channel_id=1, source_target_pairs={{0,1},{1,0},{2,3},{3,2},{4,5},{5,4},{6,7},{7,6},{8,9},{9,8},{10,11... | collective-permute-start | bytes 3538952 | tf_op jit(solution)/shard_map/ppermute | solution.py:53
  38.4 11.8 %all-to-all-start.1 = ((bf16[4,64,384]{2,1,0:T(8,128)(2,1)}), bf16[4,64,384]{2,1,0:T(8,128)(2,1)S(1)}, u32[]{:S(2)}, u32[]{:S(2)}) async-start(bf16[4,64,384]{2,1,0:T(8,128)(2,1)} %copies.1), calls=%async_computation.1 | async-start | bytes 393216 | tf_op jit(solution)/shard_map/all_to_all | solution.py:355
  50.3 13.0 %all-to-all-done.1 = bf16[4,64,384]{2,1,0:T(8,128)(2,1)S(1)} async-done(((bf16[4,64,384]{2,1,0:T(8,128)(2,1)}), bf16[4,64,384]{2,1,0:T(8,128)(2,1)S(1)}, u32[]{:S(2)}, u32[]{:S(2)}) %all-to-all-start.1) | async-done | bytes 196640 | tf_op jit(solution)/shard_map/all_to_all | solution.py:355
  63.3 6.7 %collective-permute-start.4 = (bf16[256,384]{1,0:T(8,128)(2,1)S(1)}, bf16[256,384]{1,0:T(8,128)(2,1)S(1)}, u32[]{:S(2)}, u32[]{:S(2)}) collective-permute-start(bf16[256,384]{1,0:T(8,128)(2,1)S(1)} %bitcast.31), channel_id=1, source_target_pairs={{0,32},{8,40},{16,48},{24,56},{32,64},{40,72},{48,80},{56,88},{64,... | collective-permute-start | bytes 589832 | tf_op jit(solution)/shard_map/ppermute | solution.py:42
  70.0 2.6 %collective-permute-done.4.g1_ref = bf16[256,384]{1,0:T(8,128)(2,1)S(1)} collective-permute-done((bf16[256,384]{1,0:T(8,128)(2,1)S(1)}, bf16[256,384]{1,0:T(8,128)(2,1)S(1)}, u32[]{:S(2)}, u32[]{:S(2)}) %collective-permute-start.4) | collective-permute-done | bytes 196640 | tf_op jit(solution)/shard_map/ppermute | solution.py:42
  72.6 4.3 %collective-permute-start.5 = (bf16[256,384]{1,0:T(8,128)(2,1)S(1)}, bf16[256,384]{1,0:T(8,128)(2,1)S(1)}, u32[]{:S(2)}, u32[]{:S(2)}) collective-permute-start(bf16[256,384]{1,0:T(8,128)(2,1)S(1)} %bitcast.32), channel_id=1, source_target_pairs={{0,64},{8,72},{16,80},{24,88},{32,96},{40,104},{48,112},{56,120},{... | collective-permute-start | bytes 589832 | tf_op jit(solution)/shard_map/ppermute | solution.py:42
  76.9 4.7 %collective-permute-start.6 = (bf16[256,384]{1,0:T(8,128)(2,1)S(1)}, bf16[256,384]{1,0:T(8,128)(2,1)S(1)}, u32[]{:S(2)}, u32[]{:S(2)}) collective-permute-start(bf16[256,384]{1,0:T(8,128)(2,1)S(1)} %bitcast.33), channel_id=1, source_target_pairs={{0,96},{8,104},{16,112},{24,120},{32,128},{40,136},{48,144},{56,15... | collective-permute-start | bytes 589832 | tf_op jit(solution)/shard_map/ppermute | solution.py:42
  81.6 11.4 %features.1 = (bf16[4,256,1024]{2,1,0:T(8,128)(2,1)}, bf16[4,256,1024]{2,1,0:T(8,128)(2,1)}) custom-call(s32[4]{0:T(128)S(1)} %pad_add_fusion.1.place_ref, bf16[4,112,256]{2,1,0:T(8,128)(2,1)S(1)} %all-to-all-done.came_ref, bf16[80,2304]{1,0:T(8,128)(2,1)S(1)} %fusion.spread_ref, f32[1,1152]{1,0:T(1,128)S(1)} %fusion.10.target_ref, ...), custom_call_target="tpu_custom_call" | custom-call | flops 5435817984 | bytes 6553600 | tf_op jit(solution)/shard_map/features/pallas_call | solution.py:158
  95.3 2.1 %gate.2 = (bf16[256,384]{1,0:T(8,128)(2,1)S(1)}, bf16[256,384]{1,0:T(8,128)(2,1)S(1)}, bf16[256,384]{1,0:T(8,128)(2,1)S(1)}, bf16[256,384]{1,0:T(8,128)(2,1)S(1)}) custom-call(s32[4]{0:T(128)S(1)} %pad_add_fusion.1.place_ref, bf16[4,256,1024]{2,1,0:T(8,128)(2,1)S(1)} %copy-done.20, bf16[256,384]{1,0:T(8,128)(2,1)S(1)} %bitcast.34, ...), custom_call_target="tpu_custom_call" | custom-call | flops 805306368 | bytes 3670016 | tf_op jit(solution)/shard_map/gate/pallas_call | solution.py:211
  97.5 4.4 %collective-permute-start.7 = (bf16[256,384]{1,0:T(8,128)(2,1)S(1)}, bf16[256,384]{1,0:T(8,128)(2,1)S(1)}, u32[]{:S(2)}, u32[]{:S(2)}) collective-permute-start(bf16[256,384]{1,0:T(8,128)(2,1)S(1)} %get-tuple-element.18), channel_id=1, source_target_pairs={{0,8},{8,16},{16,24},{24,0},{32,40},{40,48},{48,56},{56,32},{64,72... | collective-permute-start | bytes 589832 | tf_op jit(solution)/shard_map/ppermute | solution.py:38
  101.9 4.3 %collective-permute-start.8 = (bf16[256,384]{1,0:T(8,128)(2,1)S(1)}, bf16[256,384]{1,0:T(8,128)(2,1)S(1)}, u32[]{:S(2)}, u32[]{:S(2)}) collective-permute-start(bf16[256,384]{1,0:T(8,128)(2,1)S(1)} %get-tuple-element.19), channel_id=1, source_target_pairs={{0,16},{8,24},{16,0},{24,8},{32,48},{40,56},{48,32},{56,40},{64,80... | collective-permute-start | bytes 589832 | tf_op jit(solution)/shard_map/ppermute | solution.py:38
  106.2 3.1 %collective-permute-start.9 = (bf16[256,384]{1,0:T(8,128)(2,1)S(1)}, bf16[256,384]{1,0:T(8,128)(2,1)S(1)}, u32[]{:S(2)}, u32[]{:S(2)}) collective-permute-start(bf16[256,384]{1,0:T(8,128)(2,1)S(1)} %get-tuple-element.20), channel_id=1, source_target_pairs={{0,24},{8,0},{16,8},{24,16},{32,56},{40,32},{48,40},{56,48},{64,88... | collective-permute-start | bytes 589832 | tf_op jit(solution)/shard_map/ppermute | solution.py:38
  110.6 9.8 %collective-permute-start.16 = (bf16[4,1024,128]{2,1,0:T(8,128)(2,1)S(1)}, bf16[4,1024,128]{2,1,0:T(8,128)(2,1)}, u32[]{:S(2)}, u32[]{:S(2)}) collective-permute-start(bf16[4,1024,128]{2,1,0:T(8,128)(2,1)S(1)} %pad_maximum_fusion.1.mine_ref), channel_id=1, source_target_pairs={{0,1},{1,0},{2,3},{3,2},{4,5},{5,4},{6,7},{7,6},{8,9},{9,8},{10,11... | collective-permute-start | bytes 3145736 | tf_op jit(solution)/shard_map/ppermute | solution.py:53
  123.9 4.3 %all-to-all-start.3 = ((bf16[8,32,1024]{2,1,0:T(8,128)(2,1)}), bf16[8,32,1024]{2,1,0:T(8,128)(2,1)S(1)}, u32[]{:S(2)}, u32[]{:S(2)}) async-start(bf16[8,32,1024]{2,1,0:T(8,128)(2,1)} %bitcast.29), calls=%async_computation.3 | async-start | bytes 1048576 | tf_op jit(solution)/shard_map/all_to_all | solution.py:380
  132.7 2.1 %gate.3 = (bf16[256,384]{1,0:T(8,128)(2,1)S(1)}, bf16[256,384]{1,0:T(8,128)(2,1)S(1)}, bf16[256,384]{1,0:T(8,128)(2,1)S(1)}, bf16[256,384]{1,0:T(8,128)(2,1)S(1)}) custom-call(s32[4]{0:T(128)S(1)} %pad_add_fusion.1.place_ref, bf16[4,256,1024]{2,1,0:T(8,128)(2,1)S(1)} %copy-done.19, bf16[256,384]{1,0:T(8,128)(2,1)S(1)} %bitcast.35, ...), custom_call_target="tpu_custom_call" | custom-call | flops 805306368 | bytes 3670016 | tf_op jit(solution)/shard_map/gate/pallas_call | solution.py:211
  134.9 2.1 %collective-permute-start.10 = (bf16[256,384]{1,0:T(8,128)(2,1)S(1)}, bf16[256,384]{1,0:T(8,128)(2,1)S(1)}, u32[]{:S(2)}, u32[]{:S(2)}) collective-permute-start(bf16[256,384]{1,0:T(8,128)(2,1)S(1)} %get-tuple-element.24), channel_id=1, source_target_pairs={{0,8},{8,16},{16,24},{24,0},{32,40},{40,48},{48,56},{56,32},{64,72... | collective-permute-start | bytes 589832 | tf_op jit(solution)/shard_map/ppermute | solution.py:38
  137.0 5.3 %collective-permute-start.11 = (bf16[256,384]{1,0:T(8,128)(2,1)S(1)}, bf16[256,384]{1,0:T(8,128)(2,1)S(1)}, u32[]{:S(2)}, u32[]{:S(2)}) collective-permute-start(bf16[256,384]{1,0:T(8,128)(2,1)S(1)} %get-tuple-element.25), channel_id=1, source_target_pairs={{0,16},{8,24},{16,0},{24,8},{32,48},{40,56},{48,32},{56,40},{64,80... | collective-permute-start | bytes 589832 | tf_op jit(solution)/shard_map/ppermute | solution.py:38
  142.3 1.9 %collective-permute-start.12 = (bf16[256,384]{1,0:T(8,128)(2,1)S(1)}, bf16[256,384]{1,0:T(8,128)(2,1)S(1)}, u32[]{:S(2)}, u32[]{:S(2)}) collective-permute-start(bf16[256,384]{1,0:T(8,128)(2,1)S(1)} %get-tuple-element.26), channel_id=1, source_target_pairs={{0,24},{8,0},{16,8},{24,16},{32,56},{40,32},{48,40},{56,48},{64,88... | collective-permute-start | bytes 589832 | tf_op jit(solution)/shard_map/ppermute | solution.py:38
  144.5 5.1 %collective-permute-done.11.f2_ref = bf16[256,384]{1,0:T(8,128)(2,1)S(1)} collective-permute-done((bf16[256,384]{1,0:T(8,128)(2,1)S(1)}, bf16[256,384]{1,0:T(8,128)(2,1)S(1)}, u32[]{:S(2)}, u32[]{:S(2)}) %collective-permute-start.11) | collective-permute-done | bytes 196640 | tf_op jit(solution)/shard_map/ppermute | solution.py:38
  153.8 5.4 %all-to-all-start.2 = ((bf16[8,32,1024]{2,1,0:T(8,128)(2,1)}), bf16[8,32,1024]{2,1,0:T(8,128)(2,1)S(1)}, u32[]{:S(2)}, u32[]{:S(2)}) async-start(bf16[8,32,1024]{2,1,0:T(8,128)(2,1)} %bitcast.30), calls=%async_computation.2 | async-start | bytes 1048576 | tf_op jit(solution)/shard_map/all_to_all | solution.py:380
  159.5 2.8 %tail.2.prev_ref = f32[8,8,128]{2,1,0:T(8,128)S(1)} custom-call(s32[4]{0:T(128)S(1)} %pad_add_fusion.1.place_ref, bf16[8,32,1024]{2,1,0:T(8,128)(2,1)S(1)} %all-to-all-done.3.parts_ref, bf16[4,1024,128]{2,1,0:T(8,128)(2,1)S(1)} %pad_maximum_fusion.1.mine_ref, bf16[4,1024,128]{2,1,0:T(8,128)(2,1)} %collective-permute-done.16.other_ref, ...), custom_call_target="tpu_custom_call" | custom-call | flops 67108864 | bytes 4194304 | tf_op jit(solution)/shard_map/tail/pallas_call | solution.py:317
  162.3 6.4 %all-to-all-done.2.parts_ref = bf16[8,32,1024]{2,1,0:T(8,128)(2,1)S(1)} async-done(((bf16[8,32,1024]{2,1,0:T(8,128)(2,1)}), bf16[8,32,1024]{2,1,0:T(8,128)(2,1)S(1)}, u32[]{:S(2)}, u32[]{:S(2)}) %all-to-all-start.2) | async-done | bytes 524320 | tf_op jit(solution)/shard_map/all_to_all | solution.py:380
  168.7 3.4 %tail.3 = f32[8,8,128]{2,1,0:T(8,128)} custom-call(s32[4]{0:T(128)S(1)} %pad_add_fusion.1.place_ref, bf16[8,32,1024]{2,1,0:T(8,128)(2,1)S(1)} %all-to-all-done.2.parts_ref, bf16[4,1024,128]{2,1,0:T(8,128)(2,1)S(1)} %pad_maximum_fusion.1.mine_ref, bf16[4,1024,128]{2,1,0:T(8,128)(2,1)} %collective-permute-done.16.other_ref, ...), custom_call_target="tpu_custom_call" | custom-call | flops 67108864 | bytes 4194304 | tf_op jit(solution)/shard_map/tail/pallas_call | solution.py:317
  172.0 4.1 %all-to-all-start.4 = ((f32[8,8,128]{2,1,0:T(8,128)}), f32[8,8,128]{2,1,0:T(8,128)S(1)}, u32[]{:S(2)}, u32[]{:S(2)}) async-start(f32[8,8,128]{2,1,0:T(8,128)} %tail.3), calls=%async_computation.4 | async-start | bytes 65536 | tf_op jit(solution)/shard_map/all_to_all | solution.py:382
  176.9 3.9 %all-to-all-done.4 = f32[8,8,128]{2,1,0:T(8,128)S(1)} async-done(((f32[8,8,128]{2,1,0:T(8,128)}), f32[8,8,128]{2,1,0:T(8,128)S(1)}, u32[]{:S(2)}, u32[]{:S(2)}) %all-to-all-start.4) | async-done | bytes 32800 | tf_op jit(solution)/shard_map/all_to_all | solution.py:382
  (88 shorter events, 23.5 us)
Async XLA Ops:
  1.7 24.7 %collective-permute-start.2 = (bf16[1152,128]{1,0:T(8,128)(2,1)S(1)}, bf16[1152,128]{1,0:T(8,128)(2,1)S(1)}, u32[]{:S(2)}, u32[]{:S(2)}) collective-permute-start(bf16[1152,128]{1,0:T(8,128)(2,1)S(1)} %get-tuple-element.31), channel_id=1, source_target_pairs={{0,6},{1,7},{2,0},{3,1},{4,2},{5,3},{6,4},{7,5},{8,14},{9,15},{10,... | collective-permute-start | bytes 884744 | tf_op jit(solution)/shard_map/ppermute | solution.py:48
  6.9 23.2 %collective-permute-start = (bf16[1152,128]{1,0:T(8,128)(2,1)S(1)}, bf16[1152,128]{1,0:T(8,128)(2,1)S(1)}, u32[]{:S(2)}, u32[]{:S(2)}) collective-permute-start(bf16[1152,128]{1,0:T(8,128)(2,1)S(1)} %get-tuple-element.31), channel_id=1, source_target_pairs={{0,2},{1,3},{2,4},{3,5},{4,6},{5,7},{6,0},{7,1},{8,10},{9,11},{10,... | collective-permute-start | bytes 884744 | tf_op jit(solution)/shard_map/ppermute | solution.py:48
  8.8 21.3 %collective-permute-start.1 = (bf16[1152,128]{1,0:T(8,128)(2,1)S(1)}, bf16[1152,128]{1,0:T(8,128)(2,1)S(1)}, u32[]{:S(2)}, u32[]{:S(2)}) collective-permute-start(bf16[1152,128]{1,0:T(8,128)(2,1)S(1)} %get-tuple-element.31), channel_id=1, source_target_pairs={{0,4},{1,5},{2,6},{3,7},{4,0},{5,1},{6,2},{7,3},{8,12},{9,13},{10,... | collective-permute-start | bytes 884744 | tf_op jit(solution)/shard_map/ppermute | solution.py:48
  12.5 93.7 %collective-permute-start.13 = (bf16[1024,128]{1,0:T(8,128)(2,1)}, bf16[1024,128]{1,0:T(8,128)(2,1)}, u32[]{:S(2)}, u32[]{:S(2)}) collective-permute-start(bf16[1024,128]{1,0:T(8,128)(2,1)} %param.21), channel_id=1, source_target_pairs={{0,2},{1,3},{2,4},{3,5},{4,6},{5,7},{6,0},{7,1},{8,10},{9,11},{10,... | collective-permute-start | bytes 786440 | tf_op jit(solution)/shard_map/ppermute | solution.py:48
  15.9 93.4 %collective-permute-start.14 = (bf16[1024,128]{1,0:T(8,128)(2,1)}, bf16[1024,128]{1,0:T(8,128)(2,1)}, u32[]{:S(2)}, u32[]{:S(2)}) collective-permute-start(bf16[1024,128]{1,0:T(8,128)(2,1)} %param.21), channel_id=1, source_target_pairs={{0,4},{1,5},{2,6},{3,7},{4,0},{5,1},{6,2},{7,3},{8,12},{9,13},{10,... | collective-permute-start | bytes 786440 | tf_op jit(solution)/shard_map/ppermute | solution.py:48
  22.2 15.5 %all-to-all-start = ((bf16[4,112,256]{2,1,0:T(8,128)(2,1)}), bf16[4,112,256]{2,1,0:T(8,128)(2,1)S(1)}, u32[]{:S(2)}, u32[]{:S(2)}) async-start(bf16[4,112,256]{2,1,0:T(8,128)(2,1)} %prep.1), calls=%async_computation | async-start | bytes 458752 | tf_op jit(solution)/shard_map/all_to_all | solution.py:353
  26.4 82.9 %collective-permute-start.15 = (bf16[1024,128]{1,0:T(8,128)(2,1)}, bf16[1024,128]{1,0:T(8,128)(2,1)}, u32[]{:S(2)}, u32[]{:S(2)}) collective-permute-start(bf16[1024,128]{1,0:T(8,128)(2,1)} %param.21), channel_id=1, source_target_pairs={{0,6},{1,7},{2,0},{3,1},{4,2},{5,3},{6,4},{7,5},{8,14},{9,15},{10,... | collective-permute-start | bytes 786440 | tf_op jit(solution)/shard_map/ppermute | solution.py:48
  30.3 46.6 %collective-permute-start.3 = (bf16[4,1152,128]{2,1,0:T(8,128)(2,1)S(1)}, bf16[4,1152,128]{2,1,0:T(8,128)(2,1)S(1)}, u32[]{:S(2)}, u32[]{:S(2)}) collective-permute-start(bf16[4,1152,128]{2,1,0:T(8,128)(2,1)S(1)} %pad_maximum_fusion.mine_ref), channel_id=1, source_target_pairs={{0,1},{1,0},{2,3},{3,2},{4,5},{5,4},{6,7},{7,6},{8,9},{9,8},{10,11... | collective-permute-start | bytes 3538952 | tf_op jit(solution)/shard_map/ppermute | solution.py:53
  38.4 24.9 %all-to-all-start.1 = ((bf16[4,64,384]{2,1,0:T(8,128)(2,1)}), bf16[4,64,384]{2,1,0:T(8,128)(2,1)S(1)}, u32[]{:S(2)}, u32[]{:S(2)}) async-start(bf16[4,64,384]{2,1,0:T(8,128)(2,1)} %copies.1), calls=%async_computation.1 | async-start | bytes 393216 | tf_op jit(solution)/shard_map/all_to_all | solution.py:355
  63.3 9.3 %collective-permute-start.4 = (bf16[256,384]{1,0:T(8,128)(2,1)S(1)}, bf16[256,384]{1,0:T(8,128)(2,1)S(1)}, u32[]{:S(2)}, u32[]{:S(2)}) collective-permute-start(bf16[256,384]{1,0:T(8,128)(2,1)S(1)} %bitcast.31), channel_id=1, source_target_pairs={{0,32},{8,40},{16,48},{24,56},{32,64},{40,72},{48,80},{56,88},{64,... | collective-permute-start | bytes 589832 | tf_op jit(solution)/shard_map/ppermute | solution.py:42
  72.6 21.1 %copy-start.13 = (bf16[256,384]{1,0:T(8,128)(2,1)}, bf16[256,384]{1,0:T(8,128)(2,1)S(1)}, u32[]{:S(2)}) copy-start(bf16[256,384]{1,0:T(8,128)(2,1)S(1)} %collective-permute-done.4.g1_ref) | copy-start | bytes 589828
  72.6 20.4 %collective-permute-start.5 = (bf16[256,384]{1,0:T(8,128)(2,1)S(1)}, bf16[256,384]{1,0:T(8,128)(2,1)S(1)}, u32[]{:S(2)}, u32[]{:S(2)}) collective-permute-start(bf16[256,384]{1,0:T(8,128)(2,1)S(1)} %bitcast.32), channel_id=1, source_target_pairs={{0,64},{8,72},{16,80},{24,88},{32,96},{40,104},{48,112},{56,120},{... | collective-permute-start | bytes 589832 | tf_op jit(solution)/shard_map/ppermute | solution.py:42
  76.9 16.7 %collective-permute-start.6 = (bf16[256,384]{1,0:T(8,128)(2,1)S(1)}, bf16[256,384]{1,0:T(8,128)(2,1)S(1)}, u32[]{:S(2)}, u32[]{:S(2)}) collective-permute-start(bf16[256,384]{1,0:T(8,128)(2,1)S(1)} %bitcast.33), channel_id=1, source_target_pairs={{0,96},{8,104},{16,112},{24,120},{32,128},{40,136},{48,144},{56,15... | collective-permute-start | bytes 589832 | tf_op jit(solution)/shard_map/ppermute | solution.py:42
  93.0 4.5 %copy-start.15 = (bf16[256,384]{1,0:T(8,128)(2,1)}, bf16[256,384]{1,0:T(8,128)(2,1)S(1)}, u32[]{:S(2)}) copy-start(bf16[256,384]{1,0:T(8,128)(2,1)S(1)} %collective-permute-done.5.g2_ref) | copy-start | bytes 589828
  93.6 3.8 %copy-start.17 = (bf16[256,384]{1,0:T(8,128)(2,1)}, bf16[256,384]{1,0:T(8,128)(2,1)S(1)}, u32[]{:S(2)}) copy-start(bf16[256,384]{1,0:T(8,128)(2,1)S(1)} %collective-permute-done.6.g3_ref) | copy-start | bytes 589828
  95.3 25.2 %copy-start.1 = (bf16[512,1024]{1,0:T(8,128)(2,1)S(1)}, bf16[512,1024]{1,0:T(8,128)(2,1)}, u32[]{:S(2)}) copy-start(bf16[512,1024]{1,0:T(8,128)(2,1)} %w_in_ref.3) | copy-start | bytes 3145732
  97.5 23.0 %copy-start = (bf16[1,512,1536]{2,1,0:T(8,128)(2,1)S(1)}, bf16[1,512,1536]{2,1,0:T(8,128)(2,1)}, u32[]{:S(2)}) copy-start(bf16[1,512,1536]{2,1,0:T(8,128)(2,1)} %param.19) | copy-start | bytes 4718596
  97.5 23.0 %copy-start.5 = (bf16[256,512]{1,0:T(8,128)(2,1)S(1)}, bf16[256,512]{1,0:T(8,128)(2,1)}, u32[]{:S(2)}) copy-start(bf16[256,512]{1,0:T(8,128)(2,1)} %deter_ref.1) | copy-start | bytes 786436
  97.5 23.0 %collective-permute-start.7 = (bf16[256,384]{1,0:T(8,128)(2,1)S(1)}, bf16[256,384]{1,0:T(8,128)(2,1)S(1)}, u32[]{:S(2)}, u32[]{:S(2)}) collective-permute-start(bf16[256,384]{1,0:T(8,128)(2,1)S(1)} %get-tuple-element.18), channel_id=1, source_target_pairs={{0,8},{8,16},{16,24},{24,0},{32,40},{40,48},{48,56},{56,32},{64,72... | collective-permute-start | bytes 589832 | tf_op jit(solution)/shard_map/ppermute | solution.py:38
  101.9 18.6 %collective-permute-start.8 = (bf16[256,384]{1,0:T(8,128)(2,1)S(1)}, bf16[256,384]{1,0:T(8,128)(2,1)S(1)}, u32[]{:S(2)}, u32[]{:S(2)}) collective-permute-start(bf16[256,384]{1,0:T(8,128)(2,1)S(1)} %get-tuple-element.19), channel_id=1, source_target_pairs={{0,16},{8,24},{16,0},{24,8},{32,48},{40,56},{48,32},{56,40},{64,80... | collective-permute-start | bytes 589832 | tf_op jit(solution)/shard_map/ppermute | solution.py:38
  106.2 14.3 %collective-permute-start.9 = (bf16[256,384]{1,0:T(8,128)(2,1)S(1)}, bf16[256,384]{1,0:T(8,128)(2,1)S(1)}, u32[]{:S(2)}, u32[]{:S(2)}) collective-permute-start(bf16[256,384]{1,0:T(8,128)(2,1)S(1)} %get-tuple-element.20), channel_id=1, source_target_pairs={{0,24},{8,0},{16,8},{24,16},{32,56},{40,32},{48,40},{56,48},{64,88... | collective-permute-start | bytes 589832 | tf_op jit(solution)/shard_map/ppermute | solution.py:38
  110.6 48.8 %collective-permute-start.16 = (bf16[4,1024,128]{2,1,0:T(8,128)(2,1)S(1)}, bf16[4,1024,128]{2,1,0:T(8,128)(2,1)}, u32[]{:S(2)}, u32[]{:S(2)}) collective-permute-start(bf16[4,1024,128]{2,1,0:T(8,128)(2,1)S(1)} %pad_maximum_fusion.1.mine_ref), channel_id=1, source_target_pairs={{0,1},{1,0},{2,3},{3,2},{4,5},{5,4},{6,7},{7,6},{8,9},{9,8},{10,11... | collective-permute-start | bytes 3145736 | tf_op jit(solution)/shard_map/ppermute | solution.py:53
  120.5 7.6 %copy-start.21 = (s32[4]{0:T(128)S(1)}, s32[4]{0:T(128)}, u32[]{:S(2)}) copy-start(s32[4]{0:T(128)} %param.15) | copy-start | bytes 52
  123.9 29.8 %all-to-all-start.3 = ((bf16[8,32,1024]{2,1,0:T(8,128)(2,1)}), bf16[8,32,1024]{2,1,0:T(8,128)(2,1)S(1)}, u32[]{:S(2)}, u32[]{:S(2)}) async-start(bf16[8,32,1024]{2,1,0:T(8,128)(2,1)} %bitcast.29), calls=%async_computation.3 | async-start | bytes 1048576 | tf_op jit(solution)/shard_map/all_to_all | solution.py:380
  132.7 11.5 %copy-start.9 = (s32[2,256,32]{1,2,0:T(8,128)S(1)}, s32[2,256,32]{1,2,0:T(8,128)}, u32[]{:S(2)}) copy-start(s32[2,256,32]{1,2,0:T(8,128)} %param.13) | copy-start | bytes 196612
  132.7 18.3 %copy-start.2 = (bf16[512,1024]{1,0:T(8,128)(2,1)S(1)}, bf16[512,1024]{1,0:T(8,128)(2,1)}, u32[]{:S(2)}) copy-start(bf16[512,1024]{1,0:T(8,128)(2,1)} %w_in_ref.3) | copy-start | bytes 3145732
  132.7 18.3 %copy-start.7 = (bf16[256,512]{1,0:T(8,128)(2,1)S(1)}, bf16[256,512]{1,0:T(8,128)(2,1)}, u32[]{:S(2)}) copy-start(bf16[256,512]{1,0:T(8,128)(2,1)} %copy-done.6) | copy-start | bytes 786436
  134.9 9.6 %collective-permute-start.10 = (bf16[256,384]{1,0:T(8,128)(2,1)S(1)}, bf16[256,384]{1,0:T(8,128)(2,1)S(1)}, u32[]{:S(2)}, u32[]{:S(2)}) collective-permute-start(bf16[256,384]{1,0:T(8,128)(2,1)S(1)} %get-tuple-element.24), channel_id=1, source_target_pairs={{0,8},{8,16},{16,24},{24,0},{32,40},{40,48},{48,56},{56,32},{64,72... | collective-permute-start | bytes 589832 | tf_op jit(solution)/shard_map/ppermute | solution.py:38
  137.0 12.6 %collective-permute-start.11 = (bf16[256,384]{1,0:T(8,128)(2,1)S(1)}, bf16[256,384]{1,0:T(8,128)(2,1)S(1)}, u32[]{:S(2)}, u32[]{:S(2)}) collective-permute-start(bf16[256,384]{1,0:T(8,128)(2,1)S(1)} %get-tuple-element.25), channel_id=1, source_target_pairs={{0,16},{8,24},{16,0},{24,8},{32,48},{40,56},{48,32},{56,40},{64,80... | collective-permute-start | bytes 589832 | tf_op jit(solution)/shard_map/ppermute | solution.py:38
  142.3 8.7 %collective-permute-start.12 = (bf16[256,384]{1,0:T(8,128)(2,1)S(1)}, bf16[256,384]{1,0:T(8,128)(2,1)S(1)}, u32[]{:S(2)}, u32[]{:S(2)}) collective-permute-start(bf16[256,384]{1,0:T(8,128)(2,1)S(1)} %get-tuple-element.26), channel_id=1, source_target_pairs={{0,24},{8,0},{16,8},{24,16},{32,56},{40,32},{48,40},{56,48},{64,88... | collective-permute-start | bytes 589832 | tf_op jit(solution)/shard_map/ppermute | solution.py:38
  153.8 14.9 %all-to-all-start.2 = ((bf16[8,32,1024]{2,1,0:T(8,128)(2,1)}), bf16[8,32,1024]{2,1,0:T(8,128)(2,1)S(1)}, u32[]{:S(2)}, u32[]{:S(2)}) async-start(bf16[8,32,1024]{2,1,0:T(8,128)(2,1)} %bitcast.30), calls=%async_computation.2 | async-start | bytes 1048576 | tf_op jit(solution)/shard_map/all_to_all | solution.py:380
  172.0 8.8 %all-to-all-start.4 = ((f32[8,8,128]{2,1,0:T(8,128)}), f32[8,8,128]{2,1,0:T(8,128)S(1)}, u32[]{:S(2)}, u32[]{:S(2)}) async-start(f32[8,8,128]{2,1,0:T(8,128)} %tail.3), calls=%async_computation.4 | async-start | bytes 65536 | tf_op jit(solution)/shard_map/all_to_all | solution.py:382
  (12 other events, 11.4 us)

commit v5 on v2

--- a/solution.py
+++ b/solution.py
@@ -18,6 +18,7 @@
 NX = 4
 NC = 2
 LANES = 128
+CODES = 80
 EPS = 1e-06
 MIB = 1024 * 1024
 
@@ -26,9 +27,8 @@
     return [[start + y for y in range(NY)] for start in range(0, n_dp, NY)]
 
 
-def y_shift(value, step, n_dp):
-    perm = [(i, i // NY * NY + (i % NY + step) % NY) for i in range(n_dp)]
-    return lax.ppermute(value, "dp", perm)
+def z_groups(n_dp):
+    return [list(range(y, n_dp, NY)) for y in range(NY)]
 
 
 def x_shift(value, step):
@@ -47,69 +47,116 @@
     return mine, core_swap(mine)
 
 
-def split_kernel(w_ref, out_ref):
+def silu(value):
+    half = 0.5 * value
+    return half + half * jnp.tanh(half)
+
+
+def sigmoid(value):
+    return 0.5 + 0.5 * jnp.tanh(0.5 * value)
+
+
+def prep_kernel(w_ref, latent_ref, samples_ref, actions_ref, out_ref):
+    depth = w_ref.shape[0]
     part = w_ref.shape[1] // 3 // NY
+    rows = out_ref.shape[2]
+    line = lax.broadcasted_iota(jnp.int32, (CODES - IMAG * STOCH, rows), 0)
+    acts = jnp.zeros((CODES - IMAG * STOCH, rows), jnp.float32)
+    for k in range(IMAG):
+        acts = jnp.where(line == k, actions_ref[k : k + 1].astype(jnp.float32), acts)
+    codes = [latent_ref[...].astype(jnp.float32), samples_ref[0].astype(jnp.float32), acts]
+    codes = jnp.concatenate(codes, axis=0).astype(jnp.bfloat16)
     for y in range(NY):
         for which in range(3):
             columns = w_ref[:, (which * NY + y) * part : (which * NY + y + 1) * part]
-            for z in range(out_ref.shape[0]):
-                out_ref[z, y, :, which * part : (which + 1) * part] = columns
-
-
-def split_call(w_gate, n_z):
-    depth, width = w_gate.shape
+            out_ref[y, which // 2 * depth : (which // 2 + 1) * depth, which % 2 * part : (which % 2 + 1) * part] = columns
+        out_ref[y, depth : 2 * depth, part:] = jnp.zeros((depth, rows - part), jnp.bfloat16)
+        out_ref[y, 2 * depth :] = codes
+
+
+def prep_call(w_gate, latent, samples, actions):
+    depth = w_gate.shape[0]
+    rows = latent.shape[1]
     vmem = pl.BlockSpec(memory_space=pltpu.VMEM)
     return pl.pallas_call(
-        split_kernel,
+        prep_kernel,
+        in_specs=[vmem] * 4,
+        out_specs=vmem,
+        out_shape=jax.ShapeDtypeStruct((NY, 2 * depth + CODES, rows), jnp.bfloat16),
+        compiler_params=pltpu.CompilerParams(vmem_limit_bytes=60 * MIB),
+        cost_estimate=pl.CostEstimate(flops=0, bytes_accessed=NY * rows * 512, transcendentals=0),
+        name="prep",
+    )(w_gate, latent, samples, actions)
+
+
+def copies_kernel(came_ref, out_ref):
+    depth = out_ref.shape[1] // NY
+    part = out_ref.shape[2] // 3
+    for y in range(NY):
+        for z in range(out_ref.shape[0]):
+            here = slice(y * depth, (y + 1) * depth)
+            out_ref[z, here, : 2 * part] = came_ref[y, :depth, : 2 * part]
+            out_ref[z, here, 2 * part :] = came_ref[y, depth : 2 * depth, :part]
+
+
+def copies_call(came, n_z, depth, width):
+    vmem = pl.BlockSpec(memory_space=pltpu.VMEM)
+    return pl.pallas_call(
+        copies_kernel,
         in_specs=[vmem],
         out_specs=vmem,
-        out_shape=jax.ShapeDtypeStruct((n_z, NY, depth, width // NY), w_gate.dtype),
-        compiler_params=pltpu.CompilerParams(vmem_limit_bytes=16 * MIB),
-        cost_estimate=pl.CostEstimate(flops=0, bytes_accessed=2 * n_z * depth * width, transcendentals=0),
-        name="split",
-    )(w_gate)
-
-
-def features_kernel(me_ref, pack_ref, spread_ref, target_ref, mine_ref, other_ref, out_ref, w_ref):
+        out_shape=jax.ShapeDtypeStruct((n_z, NY * depth, width), jnp.bfloat16),
+        compiler_params=pltpu.CompilerParams(vmem_limit_bytes=60 * MIB),
+        cost_estimate=pl.CostEstimate(flops=0, bytes_accessed=4 * n_z * depth * width, transcendentals=0),
+        name="copies",
+    )(came)
+
+
+def features_kernel(place_ref, came_ref, spread_ref, target_ref, mine_ref, other_ref, out_ref, w_ref):
+    x, core = place_ref[0], place_ref[1]
+    width = w_ref.shape[0]
+    rows = out_ref.shape[1]
+
     @pl.when(pl.program_id(0) == 0)
     def _():
-        x, core = me_ref[0], me_ref[1]
         for i in range(NX):
             base = lax.rem(x + NX - i, NX) * NC
             w_ref[:, pl.ds(pl.multiple_of((base + core) * LANES, LANES), LANES)] = mine_ref[i]
             w_ref[:, pl.ds(pl.multiple_of((base + 1 - core) * LANES, LANES), LANES)] = other_ref[i]
 
+    codes = came_ref[came_ref.shape[0] - CODES :]
+    spread = lax.dot_general(codes, spread_ref[...], (((0,), (0,)), ((), ())), preferred_element_type=jnp.float32)
+    spread = jnp.concatenate([spread[:, :width], spread[:, width:]], axis=0)
+    hot = jnp.where(spread == target_ref[...], 1.0, 0.0).astype(jnp.bfloat16)
+    pre = jnp.dot(hot, w_ref[...], preferred_element_type=jnp.float32)
+    scale = lax.rsqrt(jnp.mean(pre * pre, axis=1, keepdims=True) + EPS)
+    features = silu(pre * scale).astype(jnp.bfloat16)
     for k in range(IMAG):
-        spread = jnp.dot(pack_ref[...], spread_ref[k], preferred_element_type=jnp.float32)
-        hot = jnp.where(spread == target_ref[...], 1.0, 0.0).astype(jnp.bfloat16)
-        pre = jnp.dot(hot, w_ref[...], preferred_element_type=jnp.float32)
-        scale = lax.rsqrt(jnp.mean(pre * pre, axis=1, keepdims=True) + EPS)
-        normed = pre * scale
-        out_ref[k] = (normed * jax.nn.sigmoid(normed)).astype(jnp.bfloat16)
-
-
-def features_call(place, pack, mine, other):
-    rows = pack.shape[1]
+        out_ref[k] = features[k * rows : (k + 1) * rows]
+
+
+def features_call(place, came, mine, other):
+    rows = came.shape[2]
     width = mine.shape[1]
     lane = jnp.arange(width, dtype=jnp.int32)
     is_lat = lane < LAT
     target = jnp.where(is_lat, lane % CLASSES, lane - LAT).astype(jnp.float32)[None, :]
-    step = jnp.arange(IMAG, dtype=jnp.int32)[:, None]
-    source = jnp.where(is_lat[None, :], step * STOCH + lane[None, :] // CLASSES, IMAG * STOCH + step)
-    spread = (jnp.arange(LANES, dtype=jnp.int32)[None, :, None] == source[:, None, :]).astype(jnp.bfloat16)
+    source = [jnp.where(is_lat, k * STOCH + lane // CLASSES, IMAG * STOCH + k) for k in range(IMAG)]
+    source = jnp.concatenate(source)
+    spread = (jnp.arange(CODES, dtype=jnp.int32)[:, None] == source[None, :]).astype(jnp.bfloat16)
     return pl.pallas_call(
         features_kernel,
         grid=(NY,),
         in_specs=[
             pl.BlockSpec(memory_space=pltpu.SMEM),
-            pl.BlockSpec((None, rows, LANES), lambda b: (b, 0, 0)),
-            pl.BlockSpec((IMAG, LANES, width), lambda b: (0, 0, 0)),
+            pl.BlockSpec((None,) + came.shape[1:], lambda b: (b, 0, 0)),
+            pl.BlockSpec(spread.shape, lambda b: (0, 0)),
             pl.BlockSpec((1, width), lambda b: (0, 0)),
             pl.BlockSpec((NX, width, LANES), lambda b: (0, 0, 0)),
             pl.BlockSpec((NX, width, LANES), lambda b: (0, 0, 0)),
         ],
         out_specs=pl.BlockSpec((IMAG, None, rows, UNITS), lambda b: (0, b, 0, 0)),
-        out_shape=jax.ShapeDtypeStruct((IMAG, NY, rows, UNITS), jnp.bfloat16),
+        out_shape=pltpu.HBM((IMAG, NY, rows, UNITS), jnp.bfloat16),
         scratch_shapes=[pltpu.VMEM((width, UNITS), jnp.bfloat16)],
         compiler_params=pltpu.CompilerParams(vmem_limit_bytes=32 * MIB),
         cost_estimate=pl.CostEstimate(
@@ -118,7 +165,7 @@
             transcendentals=IMAG * NY * rows * UNITS,
         ),
         name="features",
-    )(place, pack, spread, target, mine, other)
+    )(place, came, spread, target, mine, other)
 
 
 def gate_kernel(features_ref, gate_ref, out_ref):
@@ -162,9 +209,9 @@
                 mine = f_ref[q, k, :, which * part : (which + 1) * part].astype(jnp.float32)
                 return rec[:, which * bw + q * part : which * bw + (q + 1) * part] + mine
 
-            reset = jax.nn.sigmoid(gate(0))
+            reset = sigmoid(gate(0))
             candidate = jnp.tanh(reset * gate(1))
-            update = jax.nn.sigmoid(gate(2) - 1.0)
+            update = sigmoid(gate(2) - 1.0)
             before = old[:, q * part : (q + 1) * part].astype(jnp.float32)
             fresh = update * candidate + (1.0 - update) * before
             next_ref[:, q * part : (q + 1) * part] = fresh.astype(jnp.bfloat16)
@@ -201,7 +248,7 @@
     for i in range(1, parts_ref.shape[0]):
         pre = pre + parts_ref[i].astype(jnp.float32)
     normed = pre * lax.rsqrt(jnp.mean(pre * pre, axis=1, keepdims=True) + EPS)
-    hidden = (normed * jax.nn.sigmoid(normed)).astype(jnp.bfloat16)
+    hidden = (silu(normed)).astype(jnp.bfloat16)
     rows = hidden.shape[0]
     cls = lax.broadcasted_iota(jnp.int32, (rows, LANES), 1) % CLASSES
 
@@ -271,20 +318,15 @@
     me = lax.axis_index("tensor")
     place = jnp.stack([me // NC, me % NC]).astype(jnp.int32)
 
-    sent = split_call(w_gate, n_dp // NY)
-    gate = lax.all_to_all(sent.reshape(n_dp, depth, -1), "dp", 0, 0).reshape(n_dp * depth, -1)
+    sent = prep_call(w_gate, post_sample.T, samples.transpose(0, 2, 1), actions)
+    came = lax.all_to_all(sent, "dp", 0, 0, axis_index_groups=y_groups(n_dp))
+    held = copies_call(came, n_dp // NY, depth, w_gate.shape[1] // NY)
+    gate = lax.all_to_all(held, "dp", 0, 0, axis_index_groups=z_groups(n_dp)).reshape(n_dp * depth, -1)
 
     action_rows = jnp.pad(w_action, ((0, LANES - ACTIONS), (0, 0)))
     mine, other = tensor_gather(jnp.concatenate([w_stoch, action_rows], axis=0))
 
-    columns = [post_sample, samples[0]] + [actions[k][:, None] for k in range(IMAG)]
-    pack = jnp.concatenate(columns, axis=1).astype(jnp.bfloat16)
-    pack = jnp.pad(pack, ((0, 0), (0, LANES - pack.shape[1])))
-    pack = jnp.stack([pack] + [y_shift(pack, b, n_dp) for b in range(1, NY)])
-    y = lax.axis_index("dp") % NY
-    pack = jnp.stack([lax.dynamic_index_in_dim(pack, (y - b + NY) % NY, 0, keepdims=False) for b in range(NY)])
-
-    features = features_call(place, pack, mine, other)
+    features = features_call(place, came, mine, other)
     sums = lax.all_to_all(gate_call(features, gate), "dp", 0, 0, axis_index_groups=y_groups(n_dp))
 
     w_out_late, _ = lax.optimization_barrier((w_prior_out, features))

time: 147 us -> 140 us (0.952)
  starting transfers between devices: 68.3 us -> 49.8 us
  blocking collectives: 0 us -> 10.5 us
  waiting for transfers between devices: 40 us -> 44.5 us
  Pallas kernels: 21.2 us -> 25.1 us
  other arithmetic: 5.11 us -> 1.54 us
  local copies, waits for them, and re-layouts: 10.2 us -> 6.96 us
    all_to_all x0 -> x1, blocking collectives: none -> 10.5 us  [body(): came = lax.all_to_all(sent, 'dp', 0, 0, axis_index_groups=y_groups(n_dp))]
    ppermute x3 -> x0, starting transfers between devices: 10.2 us -> none  [y_shift(): return lax.ppermute(value, 'dp', perm)]
    another operation x6 -> x0, other arithmetic: 3.32 us -> none
    all_to_all x1, starting transfers between devices: 18.2 us -> 14.9 us  [body(): lax.all_to_all(held, 'dp', 0, 0, axis_index_groups=z_groups(n_dp))]
    ppermute x6, waiting for transfers between devices: 20.7 us -> 23.9 us  [x_shift(): return lax.ppermute(value, 'tensor', perm)]
    unnamed x25 -> x22, local copies, waits for them, and re-layouts: 8.67 us -> 5.85 us
    pallas_call x1 -> x2, Pallas kernels: 1.04 us -> 3.54 us  [the longest x1 1.95 us: copies_call(): pl.pallas_call(copies_kernel, in_specs=[vmem], out_specs=vmem, out_shape=...]
    all_to_all x1, starting transfers between devices: 5.86 us -> 3.69 us  [body(): lax.all_to_all(gate_call(features, gate), 'dp', 0, 0, axis_index_groups=y...]
  transfers between devices with their start and end apart: 15 -> 12, of which waited for: 8 -> 8; matrix products, arithmetic and copies ran while one was open for 2% -> 1% of each run, Pallas kernels for 9% -> 10%
where the time goes in v5:
time: 140 us; the launch traced here: 139 us
  starting transfers between devices  49.8 us (36%)
  waiting for transfers between devices  44.5 us (32%)
  Pallas kernels  25.1 us (18%)
  blocking collectives  10.5 us (8%)
  local copies, waits for them, and re-layouts  6.96 us (5%)
  other arithmetic  1.54 us (1%)
    ppermute x6, waiting for transfers between devices, x_shift(): return lax.ppermute(value, 'tensor', perm)  23.9 us
    ppermute x6, starting transfers between devices, x_shift(): return lax.ppermute(value, 'tensor', perm)  16.7 us
    all_to_all x1, starting transfers between devices, body(): lax.all_to_all(held, 'dp', 0, 0, axis_index_groups=z_groups(n_dp))  14.9 us
    all_to_all x1, waiting for transfers between devices, body(): lax.all_to_all(partial.reshape(tensor_n, IMAG * share, UNITS), 'tensor',...  14.4 us
    pallas_call x1, Pallas kernels, features_call(): pl.pallas_call(features_kernel, grid=(NY,), in_specs=[pl.BlockSpec(memory...  11.5 us
    all_to_all x1, blocking collectives, body(): came = lax.all_to_all(sent, 'dp', 0, 0, axis_index_groups=y_groups(n_dp))  10.5 us
    ppermute x2, starting transfers between devices, core_swap(): return lax.ppermute(value, 'tensor', perm)  6.82 us
    unnamed x22, local copies, waits for them, and re-layouts  5.85 us
  transfers between devices with their start and end apart: 12, of which 8 were waited for; matrix products, arithmetic and copies ran while one was open for 1% of the time, Pallas kernels for 10%

profile of v5, /device:TPU:1, one launch (start us, length us, event | category | flops | bytes accessed | tf_op | source)
XLA Modules:
  0.0 139.3 jit_solution(10162476865416459785)
XLA Ops:
  0.6 1.6 %prep.1 = bf16[4,112,256]{2,1,0:T(8,128)(2,1)} custom-call(bf16[16,1536]{1,0:T(8,128)(2,1)} %w_ref.1, s32[32,256]{1,0:T(8,128)} %bitcast.32, s32[2,32,256]{2,1,0:T(8,128)} %bitcast.31, s32[2,256]{1,0:T(2,128)} %actions_ref.1), custom_call_target="tpu_custom_call" | custom-call | bytes 524288 | tf_op jit(solution)/shard_map/prep/pallas_call | solution.py:81
  2.2 10.5 %all_to_all.25.came_ref = bf16[4,112,256]{2,1,0:T(8,128)(2,1)} all-to-all(bf16[4,112,256]{2,1,0:T(8,128)(2,1)} %prep.1), channel_id=1, replica_groups={{0,8,16,24},{32,40,48,56},{64,72,80,88},{96,104,112,120},{128,136,144,1..., dimensions={0} | all-to-all | bytes 458752 | tf_op jit(solution)/shard_map/all_to_all | solution.py:322
  12.7 1.9 %copies.1 = bf16[16,64,384]{2,1,0:T(8,128)(2,1)} custom-call(bf16[4,112,256]{2,1,0:T(8,128)(2,1)} %all_to_all.25.came_ref), custom_call_target="tpu_custom_call" | custom-call | bytes 393216 | tf_op jit(solution)/shard_map/copies/pallas_call | solution.py:104
  14.7 14.9 %all-to-all-start.1 = ((bf16[16,64,384]{2,1,0:T(8,128)(2,1)}), bf16[16,64,384]{2,1,0:T(8,128)(2,1)S(1)}, u32[]{:S(2)}, u32[]{:S(2)}) async-start(bf16[16,64,384]{2,1,0:T(8,128)(2,1)} %copies.1), calls=%async_computation.1 | async-start | bytes 1572864 | tf_op jit(solution)/shard_map/all_to_all | solution.py:324
  29.6 4.4 %collective-permute-start.2 = (bf16[1152,128]{1,0:T(8,128)(2,1)S(1)}, bf16[1152,128]{1,0:T(8,128)(2,1)S(1)}, u32[]{:S(2)}, u32[]{:S(2)}) collective-permute-start(bf16[1152,128]{1,0:T(8,128)(2,1)S(1)} %get-tuple-element.9), channel_id=1, source_target_pairs={{0,6},{1,7},{2,0},{3,1},{4,2},{5,3},{6,4},{7,5},{8,14},{9,15},{10,... | collective-permute-start | bytes 884744 | tf_op jit(solution)/shard_map/ppermute | solution.py:37
  34.0 2.4 %collective-permute-start.1 = (bf16[1152,128]{1,0:T(8,128)(2,1)S(1)}, bf16[1152,128]{1,0:T(8,128)(2,1)S(1)}, u32[]{:S(2)}, u32[]{:S(2)}) collective-permute-start(bf16[1152,128]{1,0:T(8,128)(2,1)S(1)} %get-tuple-element.9), channel_id=1, source_target_pairs={{0,4},{1,5},{2,6},{3,7},{4,0},{5,1},{6,2},{7,3},{8,12},{9,13},{10,... | collective-permute-start | bytes 884744 | tf_op jit(solution)/shard_map/ppermute | solution.py:37
  36.5 2.5 %collective-permute-start = (bf16[1152,128]{1,0:T(8,128)(2,1)S(1)}, bf16[1152,128]{1,0:T(8,128)(2,1)S(1)}, u32[]{:S(2)}, u32[]{:S(2)}) collective-permute-start(bf16[1152,128]{1,0:T(8,128)(2,1)S(1)} %get-tuple-element.9), channel_id=1, source_target_pairs={{0,2},{1,3},{2,4},{3,5},{4,6},{5,7},{6,0},{7,1},{8,10},{9,11},{10,... | collective-permute-start | bytes 884744 | tf_op jit(solution)/shard_map/ppermute | solution.py:37
  39.0 4.3 %collective-permute-done.1 = bf16[1152,128]{1,0:T(8,128)(2,1)S(1)} collective-permute-done((bf16[1152,128]{1,0:T(8,128)(2,1)S(1)}, bf16[1152,128]{1,0:T(8,128)(2,1)S(1)}, u32[]{:S(2)}, u32[]{:S(2)}) %collective-permute-start.1) | collective-permute-done | bytes 294944 | tf_op jit(solution)/shard_map/ppermute | solution.py:37
  43.3 8.2 %collective-permute-done = bf16[1152,128]{1,0:T(8,128)(2,1)S(1)} collective-permute-done((bf16[1152,128]{1,0:T(8,128)(2,1)S(1)}, bf16[1152,128]{1,0:T(8,128)(2,1)S(1)}, u32[]{:S(2)}, u32[]{:S(2)}) %collective-permute-start) | collective-permute-done | bytes 294944 | tf_op jit(solution)/shard_map/ppermute | solution.py:37
  51.7 3.6 %collective-permute-start.3 = (bf16[4,1152,128]{2,1,0:T(8,128)(2,1)S(1)}, bf16[4,1152,128]{2,1,0:T(8,128)(2,1)S(1)}, u32[]{:S(2)}, u32[]{:S(2)}) collective-permute-start(bf16[4,1152,128]{2,1,0:T(8,128)(2,1)S(1)} %pad_maximum_fusion.mine_ref), channel_id=1, source_target_pairs={{0,1},{1,0},{2,3},{3,2},{4,5},{5,4},{6,7},{7,6},{8,9},{9,8},{10,11... | collective-permute-start | bytes 3538952 | tf_op jit(solution)/shard_map/ppermute | solution.py:42
  55.4 2.3 %collective-permute-done.3.other_ref = bf16[4,1152,128]{2,1,0:T(8,128)(2,1)S(1)} collective-permute-done((bf16[4,1152,128]{2,1,0:T(8,128)(2,1)S(1)}, bf16[4,1152,128]{2,1,0:T(8,128)(2,1)S(1)}, u32[]{:S(2)}, u32[]{:S(2)}) %collective-permute-start.3) | collective-permute-done | bytes 1179680 | tf_op jit(solution)/shard_map/ppermute | solution.py:42
  57.7 11.5 %features.1.features_ref = bf16[2,4,256,1024]{3,2,1,0:T(8,128)(2,1)} custom-call(s32[2]{0:T(128)S(1)} %pad_add_fusion.1.place_ref.me_ref, bf16[4,112,256]{2,1,0:T(8,128)(2,1)S(1)} %copy-done.2, bf16[80,2304]{1,0:T(8,128)(2,1)S(1)} %fusion.spread_ref, f32[1,1152]{1,0:T(1,128)S(1)} %fusion.10.target_ref, bf16[4,1152,128]{2,1,0:T(8,128)(2,1)S(1)} %pad_maximum_fusion.mine_ref, ...), custom_call_target="tpu_custom_call" | custom-call | flops 5435817984 | bytes 6553600 | tf_op jit(solution)/shard_map/features/pallas_call | solution.py:147
  69.2 2.2 %copy-done = bf16[2,4,256,1024]{3,2,1,0:T(8,128)(2,1)S(1)} copy-done((bf16[2,4,256,1024]{3,2,1,0:T(8,128)(2,1)S(1)}, bf16[2,4,256,1024]{3,2,1,0:T(8,128)(2,1)}, u32[]{:S(2)}) %copy-start) | copy-done | bytes 4194328
  71.4 3.9 %gate.1 = bf16[4,2,256,384]{3,2,1,0:T(8,128)(2,1)} custom-call(bf16[2,4,256,1024]{3,2,1,0:T(8,128)(2,1)S(1)} %copy-done, bf16[1024,384]{1,0:T(8,128)(2,1)S(1)} %bitcast.20), custom_call_target="tpu_custom_call" | custom-call | flops 1610612736 | bytes 6553600 | tf_op jit(solution)/shard_map/gate/pallas_call | solution.py:179
  75.3 3.7 %all-to-all-start.2 = ((bf16[4,2,256,384]{3,2,1,0:T(8,128)(2,1)}), bf16[4,2,256,384]{3,2,1,0:T(8,128)(2,1)S(1)}, u32[]{:S(2)}, u32[]{:S(2)}) async-start(bf16[4,2,256,384]{3,2,1,0:T(8,128)(2,1)} %gate.1), calls=%async_computation.2 | async-start | bytes 3145728 | tf_op jit(solution)/shard_map/all_to_all | solution.py:330
  79.0 2.3 %collective-permute-start.6 = (bf16[1024,128]{1,0:T(8,128)(2,1)S(1)}, bf16[1024,128]{1,0:T(8,128)(2,1)S(1)}, u32[]{:S(2)}, u32[]{:S(2)}) collective-permute-start(bf16[1024,128]{1,0:T(8,128)(2,1)S(1)} %copy-done.7), channel_id=1, source_target_pairs={{0,6},{1,7},{2,0},{3,1},{4,2},{5,3},{6,4},{7,5},{8,14},{9,15},{10,... | collective-permute-start | bytes 786440 | tf_op jit(solution)/shard_map/ppermute | solution.py:37
  81.3 2.4 %collective-permute-start.5 = (bf16[1024,128]{1,0:T(8,128)(2,1)S(1)}, bf16[1024,128]{1,0:T(8,128)(2,1)S(1)}, u32[]{:S(2)}, u32[]{:S(2)}) collective-permute-start(bf16[1024,128]{1,0:T(8,128)(2,1)S(1)} %copy-done.7), channel_id=1, source_target_pairs={{0,4},{1,5},{2,6},{3,7},{4,0},{5,1},{6,2},{7,3},{8,12},{9,13},{10,... | collective-permute-start | bytes 786440 | tf_op jit(solution)/shard_map/ppermute | solution.py:37
  83.8 2.6 %collective-permute-start.4 = (bf16[1024,128]{1,0:T(8,128)(2,1)S(1)}, bf16[1024,128]{1,0:T(8,128)(2,1)S(1)}, u32[]{:S(2)}, u32[]{:S(2)}) collective-permute-start(bf16[1024,128]{1,0:T(8,128)(2,1)S(1)} %copy-done.7), channel_id=1, source_target_pairs={{0,2},{1,3},{2,4},{3,5},{4,6},{5,7},{6,0},{7,1},{8,10},{9,11},{10,... | collective-permute-start | bytes 786440 | tf_op jit(solution)/shard_map/ppermute | solution.py:37
  86.4 2.2 %collective-permute-done.6 = bf16[1024,128]{1,0:T(8,128)(2,1)S(1)} collective-permute-done((bf16[1024,128]{1,0:T(8,128)(2,1)S(1)}, bf16[1024,128]{1,0:T(8,128)(2,1)S(1)}, u32[]{:S(2)}, u32[]{:S(2)}) %collective-permute-start.6) | collective-permute-done | bytes 262176 | tf_op jit(solution)/shard_map/ppermute | solution.py:37
  88.5 1.4 %collective-permute-done.5 = bf16[1024,128]{1,0:T(8,128)(2,1)S(1)} collective-permute-done((bf16[1024,128]{1,0:T(8,128)(2,1)S(1)}, bf16[1024,128]{1,0:T(8,128)(2,1)S(1)}, u32[]{:S(2)}, u32[]{:S(2)}) %collective-permute-start.5) | collective-permute-done | bytes 262176 | tf_op jit(solution)/shard_map/ppermute | solution.py:37
  90.0 7.8 %collective-permute-done.4 = bf16[1024,128]{1,0:T(8,128)(2,1)S(1)} collective-permute-done((bf16[1024,128]{1,0:T(8,128)(2,1)S(1)}, bf16[1024,128]{1,0:T(8,128)(2,1)S(1)}, u32[]{:S(2)}, u32[]{:S(2)}) %collective-permute-start.4) | collective-permute-done | bytes 262176 | tf_op jit(solution)/shard_map/ppermute | solution.py:37
  97.9 3.2 %collective-permute-start.7 = (bf16[4,1024,128]{2,1,0:T(8,128)(2,1)S(1)}, bf16[4,1024,128]{2,1,0:T(8,128)(2,1)}, u32[]{:S(2)}, u32[]{:S(2)}) collective-permute-start(bf16[4,1024,128]{2,1,0:T(8,128)(2,1)S(1)} %pad_maximum_fusion.1.mine_ref), channel_id=1, source_target_pairs={{0,1},{1,0},{2,3},{3,2},{4,5},{5,4},{6,7},{7,6},{8,9},{9,8},{10,11... | collective-permute-start | bytes 3145736 | tf_op jit(solution)/shard_map/ppermute | solution.py:42
  101.2 1.4 %copy-done.3 = bf16[1,512,1536]{2,1,0:T(8,128)(2,1)S(1)} copy-done((bf16[1,512,1536]{2,1,0:T(8,128)(2,1)S(1)}, bf16[1,512,1536]{2,1,0:T(8,128)(2,1)}, u32[]{:S(2)}) %copy-start.3) | copy-done | bytes 1572888
  102.6 1.2 copy-done.4
  103.8 2.2 %gru.1 = (bf16[256,512]{1,0:T(8,128)(2,1)S(1)}, bf16[8,2,32,1024]{3,2,1,0:T(8,128)(2,1)S(1)}) custom-call(bf16[256,512]{1,0:T(8,128)(2,1)S(1)} %copy-done.5, bf16[512,1536]{1,0:T(8,128)(2,1)S(1)} %bitcast.23, bf16[512,1024]{1,0:T(8,128)(2,1)S(1)} %copy-done.4, bf16[4,2,256,384]{3,2,1,0:T(8,128)(2,1)S(1)} %all-to-all-done.2.f_ref), custom_call_target="tpu_custom_call" | custom-call | flops 1342177280 | bytes 5767168 | tf_op jit(solution)/shard_map/gru/pallas_call | solution.py:227
  106.0 1.0 copy-done.1
  107.0 3.6 %all-to-all-start.3 = ((bf16[8,64,1024]{2,1,0:T(8,128)(2,1)}), bf16[8,64,1024]{2,1,0:T(8,128)(2,1)S(1)}, u32[]{:S(2)}, u32[]{:S(2)}) async-start(bf16[8,64,1024]{2,1,0:T(8,128)(2,1)} %bitcast.21), calls=%async_computation.3 | async-start | bytes 2097152 | tf_op jit(solution)/shard_map/all_to_all | solution.py:343
  111.3 14.4 %all-to-all-done.3.parts_ref = bf16[8,64,1024]{2,1,0:T(8,128)(2,1)S(1)} async-done(((bf16[8,64,1024]{2,1,0:T(8,128)(2,1)}), bf16[8,64,1024]{2,1,0:T(8,128)(2,1)S(1)}, u32[]{:S(2)}, u32[]{:S(2)}) %all-to-all-start.3) | async-done | bytes 1048608 | tf_op jit(solution)/shard_map/all_to_all | solution.py:343
  125.7 4.1 %tail.1 = f32[8,8,128]{2,1,0:T(8,128)} custom-call(s32[2]{0:T(128)S(1)} %pad_add_fusion.1.place_ref.me_ref, bf16[8,64,1024]{2,1,0:T(8,128)(2,1)S(1)} %all-to-all-done.3.parts_ref, bf16[4,1024,128]{2,1,0:T(8,128)(2,1)S(1)} %pad_maximum_fusion.1.mine_ref, bf16[4,1024,128]{2,1,0:T(8,128)(2,1)} %collective-permute-done.7.other_ref, bf16[64,32]{1,0:T(8,128)(2,1)S(1)} %bitcast.22, ...), custom_call_target="tpu_custom_call" | custom-call | flops 134217728 | bytes 4194304 | tf_op jit(solution)/shard_map/tail/pallas_call | solution.py:287
  129.7 4.1 %all-to-all-start.4 = ((f32[8,8,128]{2,1,0:T(8,128)}), f32[8,8,128]{2,1,0:T(8,128)S(1)}, u32[]{:S(2)}, u32[]{:S(2)}) async-start(f32[8,8,128]{2,1,0:T(8,128)} %tail.1), calls=%async_computation.4 | async-start | bytes 65536 | tf_op jit(solution)/shard_map/all_to_all | solution.py:345
  133.8 0.8 broadcast_select_fusion
  134.6 3.9 %all-to-all-done.4 = f32[8,8,128]{2,1,0:T(8,128)S(1)} async-done(((f32[8,8,128]{2,1,0:T(8,128)}), f32[8,8,128]{2,1,0:T(8,128)S(1)}, u32[]{:S(2)}, u32[]{:S(2)}) %all-to-all-start.4) | async-done | bytes 32800 | tf_op jit(solution)/shard_map/all_to_all | solution.py:345
  (43 shorter events, 1.9 us)
Async XLA Ops:
  12.7 16.9 %copy-start.6 = (bf16[1024,128]{1,0:T(8,128)(2,1)S(1)}, bf16[1024,128]{1,0:T(8,128)(2,1)}, u32[]{:S(2)}) copy-start(bf16[1024,128]{1,0:T(8,128)(2,1)} %param.16) | copy-start | bytes 786436
  12.7 16.9 %copy-start.9 = (bf16[18,128]{1,0:T(8,128)(2,1)S(1)}, bf16[18,128]{1,0:T(8,128)(2,1)}, u32[]{:S(2)}) copy-start(bf16[18,128]{1,0:T(8,128)(2,1)} %param.17) | copy-start | bytes 13828
  14.7 54.5 %all-to-all-start.1 = ((bf16[16,64,384]{2,1,0:T(8,128)(2,1)}), bf16[16,64,384]{2,1,0:T(8,128)(2,1)S(1)}, u32[]{:S(2)}, u32[]{:S(2)}) async-start(bf16[16,64,384]{2,1,0:T(8,128)(2,1)} %copies.1), calls=%async_computation.1 | async-start | bytes 1572864 | tf_op jit(solution)/shard_map/all_to_all | solution.py:324
  29.6 9.4 %collective-permute-start.2 = (bf16[1152,128]{1,0:T(8,128)(2,1)S(1)}, bf16[1152,128]{1,0:T(8,128)(2,1)S(1)}, u32[]{:S(2)}, u32[]{:S(2)}) collective-permute-start(bf16[1152,128]{1,0:T(8,128)(2,1)S(1)} %get-tuple-element.9), channel_id=1, source_target_pairs={{0,6},{1,7},{2,0},{3,1},{4,2},{5,3},{6,4},{7,5},{8,14},{9,15},{10,... | collective-permute-start | bytes 884744 | tf_op jit(solution)/shard_map/ppermute | solution.py:37
  34.0 9.3 %collective-permute-start.1 = (bf16[1152,128]{1,0:T(8,128)(2,1)S(1)}, bf16[1152,128]{1,0:T(8,128)(2,1)S(1)}, u32[]{:S(2)}, u32[]{:S(2)}) collective-permute-start(bf16[1152,128]{1,0:T(8,128)(2,1)S(1)} %get-tuple-element.9), channel_id=1, source_target_pairs={{0,4},{1,5},{2,6},{3,7},{4,0},{5,1},{6,2},{7,3},{8,12},{9,13},{10,... | collective-permute-start | bytes 884744 | tf_op jit(solution)/shard_map/ppermute | solution.py:37
  36.5 15.0 %collective-permute-start = (bf16[1152,128]{1,0:T(8,128)(2,1)S(1)}, bf16[1152,128]{1,0:T(8,128)(2,1)S(1)}, u32[]{:S(2)}, u32[]{:S(2)}) collective-permute-start(bf16[1152,128]{1,0:T(8,128)(2,1)S(1)} %get-tuple-element.9), channel_id=1, source_target_pairs={{0,2},{1,3},{2,4},{3,5},{4,6},{5,7},{6,0},{7,1},{8,10},{9,11},{10,... | collective-permute-start | bytes 884744 | tf_op jit(solution)/shard_map/ppermute | solution.py:37
  51.5 6.2 %copy-start.2 = (bf16[4,112,256]{2,1,0:T(8,128)(2,1)S(1)}, bf16[4,112,256]{2,1,0:T(8,128)(2,1)}, u32[]{:S(2)}) copy-start(bf16[4,112,256]{2,1,0:T(8,128)(2,1)} %all_to_all.25.came_ref) | copy-start | bytes 688132
  51.7 6.0 %collective-permute-start.3 = (bf16[4,1152,128]{2,1,0:T(8,128)(2,1)S(1)}, bf16[4,1152,128]{2,1,0:T(8,128)(2,1)S(1)}, u32[]{:S(2)}, u32[]{:S(2)}) collective-permute-start(bf16[4,1152,128]{2,1,0:T(8,128)(2,1)S(1)} %pad_maximum_fusion.mine_ref), channel_id=1, source_target_pairs={{0,1},{1,0},{2,3},{3,2},{4,5},{5,4},{6,7},{7,6},{8,9},{9,8},{10,11... | collective-permute-start | bytes 3538952 | tf_op jit(solution)/shard_map/ppermute | solution.py:42
  69.2 2.2 %copy-start = (bf16[2,4,256,1024]{3,2,1,0:T(8,128)(2,1)S(1)}, bf16[2,4,256,1024]{3,2,1,0:T(8,128)(2,1)}, u32[]{:S(2)}) copy-start(bf16[2,4,256,1024]{3,2,1,0:T(8,128)(2,1)} %features.1.features_ref) | copy-start | bytes 12582916
  75.3 3.7 %copy-start.7 = (bf16[1024,128]{1,0:T(8,128)(2,1)S(1)}, bf16[1024,128]{1,0:T(8,128)(2,1)}, u32[]{:S(2)}) copy-start(bf16[1024,128]{1,0:T(8,128)(2,1)} %param.21) | copy-start | bytes 786436
  75.3 25.8 %all-to-all-start.2 = ((bf16[4,2,256,384]{3,2,1,0:T(8,128)(2,1)}), bf16[4,2,256,384]{3,2,1,0:T(8,128)(2,1)S(1)}, u32[]{:S(2)}, u32[]{:S(2)}) async-start(bf16[4,2,256,384]{3,2,1,0:T(8,128)(2,1)} %gate.1), calls=%async_computation.2 | async-start | bytes 3145728 | tf_op jit(solution)/shard_map/all_to_all | solution.py:330
  79.0 22.1 %copy-start.5 = (bf16[256,512]{1,0:T(8,128)(2,1)S(1)}, bf16[256,512]{1,0:T(8,128)(2,1)}, u32[]{:S(2)}) copy-start(bf16[256,512]{1,0:T(8,128)(2,1)} %deter_ref.1) | copy-start | bytes 786436
  79.0 9.5 %collective-permute-start.6 = (bf16[1024,128]{1,0:T(8,128)(2,1)S(1)}, bf16[1024,128]{1,0:T(8,128)(2,1)S(1)}, u32[]{:S(2)}, u32[]{:S(2)}) collective-permute-start(bf16[1024,128]{1,0:T(8,128)(2,1)S(1)} %copy-done.7), channel_id=1, source_target_pairs={{0,6},{1,7},{2,0},{3,1},{4,2},{5,3},{6,4},{7,5},{8,14},{9,15},{10,... | collective-permute-start | bytes 786440 | tf_op jit(solution)/shard_map/ppermute | solution.py:37
  81.3 8.6 %collective-permute-start.5 = (bf16[1024,128]{1,0:T(8,128)(2,1)S(1)}, bf16[1024,128]{1,0:T(8,128)(2,1)S(1)}, u32[]{:S(2)}, u32[]{:S(2)}) collective-permute-start(bf16[1024,128]{1,0:T(8,128)(2,1)S(1)} %copy-done.7), channel_id=1, source_target_pairs={{0,4},{1,5},{2,6},{3,7},{4,0},{5,1},{6,2},{7,3},{8,12},{9,13},{10,... | collective-permute-start | bytes 786440 | tf_op jit(solution)/shard_map/ppermute | solution.py:37
  83.8 14.0 %collective-permute-start.4 = (bf16[1024,128]{1,0:T(8,128)(2,1)S(1)}, bf16[1024,128]{1,0:T(8,128)(2,1)S(1)}, u32[]{:S(2)}, u32[]{:S(2)}) collective-permute-start(bf16[1024,128]{1,0:T(8,128)(2,1)S(1)} %copy-done.7), channel_id=1, source_target_pairs={{0,2},{1,3},{2,4},{3,5},{4,6},{5,7},{6,0},{7,1},{8,10},{9,11},{10,... | collective-permute-start | bytes 786440 | tf_op jit(solution)/shard_map/ppermute | solution.py:37
  97.9 13.4 %collective-permute-start.7 = (bf16[4,1024,128]{2,1,0:T(8,128)(2,1)S(1)}, bf16[4,1024,128]{2,1,0:T(8,128)(2,1)}, u32[]{:S(2)}, u32[]{:S(2)}) collective-permute-start(bf16[4,1024,128]{2,1,0:T(8,128)(2,1)S(1)} %pad_maximum_fusion.1.mine_ref), channel_id=1, source_target_pairs={{0,1},{1,0},{2,3},{3,2},{4,5},{5,4},{6,7},{7,6},{8,9},{9,8},{10,11... | collective-permute-start | bytes 3145736 | tf_op jit(solution)/shard_map/ppermute | solution.py:42
  101.1 1.4 %copy-start.3 = (bf16[1,512,1536]{2,1,0:T(8,128)(2,1)S(1)}, bf16[1,512,1536]{2,1,0:T(8,128)(2,1)}, u32[]{:S(2)}) copy-start(bf16[1,512,1536]{2,1,0:T(8,128)(2,1)} %param.19) | copy-start | bytes 4718596
  102.6 1.2 copy-start.4
  106.0 1.0 copy-start.1
  107.0 3.7 %copy-start.10 = (s32[4]{0:T(128)S(1)}, s32[4]{0:T(128)}, u32[]{:S(2)}) copy-start(s32[4]{0:T(128)} %param.15) | copy-start | bytes 52
  107.0 3.8 %copy-start.8 = (s32[2,256,32]{1,2,0:T(8,128)S(1)}, s32[2,256,32]{1,2,0:T(8,128)}, u32[]{:S(2)}) copy-start(s32[2,256,32]{1,2,0:T(8,128)} %param.13) | copy-start | bytes 196612
  107.0 18.7 %all-to-all-start.3 = ((bf16[8,64,1024]{2,1,0:T(8,128)(2,1)}), bf16[8,64,1024]{2,1,0:T(8,128)(2,1)S(1)}, u32[]{:S(2)}, u32[]{:S(2)}) async-start(bf16[8,64,1024]{2,1,0:T(8,128)(2,1)} %bitcast.21), calls=%async_computation.3 | async-start | bytes 2097152 | tf_op jit(solution)/shard_map/all_to_all | solution.py:343
  129.7 8.8 %all-to-all-start.4 = ((f32[8,8,128]{2,1,0:T(8,128)}), f32[8,8,128]{2,1,0:T(8,128)S(1)}, u32[]{:S(2)}, u32[]{:S(2)}) async-start(f32[8,8,128]{2,1,0:T(8,128)} %tail.1), calls=%async_computation.4 | async-start | bytes 65536 | tf_op jit(solution)/shard_map/all_to_all | solution.py:345

commit v6 on v2

v6 whole, which is shorter than its diff:
```python
import functools

import jax
import jax.numpy as jnp
from jax import lax
from jax.experimental import pallas as pl
from jax.experimental.pallas import tpu as pltpu
from jax.sharding import PartitionSpec as P

STOCH = 32
CLASSES = 32
LAT = STOCH * CLASSES
ACTIONS = 18
STEPS = 64
IMAG = 2
UNITS = 1024
NY = 4
NX = 4
NC = 2
LANES = 128
EMBED = LAT + LANES
NEAR = 4
CODES = 80
EPS = 1e-06
MIB = 1024 * 1024
FEATURES_WEIGHT = 12


def y_groups(n_dp):
    return [[start + y for y in range(NY)] for start in range(0, n_dp, NY)]


def far_groups(n_dp):
    n_far = n_dp // NY // NEAR
    return [[(far * NEAR + near) * NY + y for far in range(n_far) for y in range(NY)] for near in range(NEAR)]


def near_groups(n_dp):
    n_far = n_dp // NY // NEAR
    return [[(far * NEAR + near) * NY + y for near in range(NEAR)] for far in range(n_far) for y in range(NY)]


def diagonal_gather(value, n_dp):
    places = [(z, y, x, core) for z in range(n_dp // NY) for y in range(NY) for x in range(NX) for core in range(NC)]

    def index(z, y, x, core):
        return ((z * NY + y) * NX + x) * NC + core

    pieces = [value]
    for step in range(1, NX):
        perm = [(index(*p), index(p[0], (p[1] + step) % NY, (p[2] + step) % NX, p[3])) for p in places]
        pieces.append(lax.ppermute(value, ("dp", "tensor"), perm))
    return jnp.stack(pieces)


def x_gather(value):
    pieces = [value]
    for step in range(1, NX):
        perm = [(i, (i + step * NC) % (NX * NC)) for i in range(NX * NC)]
        pieces.append(lax.ppermute(value, "tensor", perm))
    return jnp.stack(pieces)


def core_swap(value):
    perm = [(i, i ^ 1) for i in range(NX * NC)]
    return lax.ppermute(value, "tensor", perm)


def silu(value):
    half = 0.5 * value
    return half + half * jnp.tanh(half)


def sigmoid(value):
    return 0.5 + 0.5 * jnp.tanh(0.5 * value)


def split_kernel(w_ref, out_ref):
    part = w_ref.shape[1] // 3 // NY
    for y in range(NY):
        for which in range(3):
            columns = w_ref[:, (which * NY + y) * part : (which * NY + y + 1) * part]
            for z in range(out_ref.shape[0]):
                out_ref[z, y, :, which * part : (which + 1) * part] = columns


def split_call(w_gate, n_z):
    depth, width = w_gate.shape
    vmem = pl.BlockSpec(memory_space=pltpu.VMEM)
    return pl.pallas_call(
        split_kernel,
        in_specs=[vmem],
        out_specs=vmem,
        out_shape=jax.ShapeDtypeStruct((n_z, NY, depth, width // NY), w_gate.dtype),
        compiler_params=pltpu.CompilerParams(vmem_limit_bytes=60 * MIB),
        cost_estimate=pl.CostEstimate(flops=0, bytes_accessed=2 * n_z * depth * width, transcendentals=0),
        name="split",
    )(w_gate)


def prep_kernel(w_stoch_ref, w_action_ref, latent_ref, samples_ref, actions_ref, out_ref):
    rows = latent_ref.shape[1]
    out_ref[:LAT] = w_stoch_ref[...]
    out_ref[LAT:EMBED] = jnp.zeros((EMBED - LAT, LANES), jnp.bfloat16)
    out_ref[LAT : LAT + ACTIONS] = w_action_ref[...]
    line = lax.broadcasted_iota(jnp.int32, (CODES - IMAG * STOCH, rows), 0)
    acts = jnp.zeros((CODES - IMAG * STOCH, rows), jnp.float32)
    for k in range(IMAG):
        acts = jnp.where(line == k, actions_ref[k : k + 1].astype(jnp.float32), acts)
    codes = [latent_ref[...].astype(jnp.float32), samples_ref[0].astype(jnp.float32), acts]
    codes = jnp.concatenate(codes, axis=0).astype(jnp.bfloat16)
    for i in range(rows // LANES):
        out_ref[EMBED + i * CODES : EMBED + (i + 1) * CODES] = codes[:, i * LANES : (i + 1) * LANES]


def prep_call(w_stoch, w_action, latent, samples, actions):
    rows = latent.shape[1]
    vmem = pl.BlockSpec(memory_space=pltpu.VMEM)
    return pl.pallas_call(
        prep_kernel,
        in_specs=[vmem] * 5,
        out_specs=vmem,
        out_shape=jax.ShapeDtypeStruct((EMBED + rows // LANES * CODES, LANES), jnp.bfloat16),
        compiler_params=pltpu.CompilerParams(vmem_limit_bytes=60 * MIB),
        cost_estimate=pl.CostEstimate(flops=0, bytes_accessed=2 * EMBED * LANES * 2, transcendentals=0),
        name="prep",
    )(w_stoch, w_action, latent, samples, actions)


def features_kernel(place_ref, spread_ref, target_ref, mine_ref, other_ref, out_ref, w_ref):
    x, core, y = place_ref[0], place_ref[1], place_ref[2]
    rows = out_ref.shape[1]

    @pl.when(pl.program_id(0) == 0)
    def _():
        for i in range(NX):
            base = lax.rem(x + NX - i, NX) * NC
            w_ref[:, pl.ds(pl.multiple_of((base + core) * LANES, LANES), LANES)] = mine_ref[i, :EMBED]
            w_ref[:, pl.ds(pl.multiple_of((base + 1 - core) * LANES, LANES), LANES)] = other_ref[i, :EMBED]

    source = lax.rem(y + NY - pl.program_id(0), NY)
    spread = []
    for k in range(IMAG):
        for half in range(rows // LANES):
            codes = mine_ref[source, EMBED + half * CODES : EMBED + (half + 1) * CODES]
            wide = spread_ref[:, k * EMBED : (k + 1) * EMBED]
            spread.append(
                lax.dot_general(codes, wide, (((0,), (0,)), ((), ())), preferred_element_type=jnp.float32)
            )
    spread = jnp.concatenate(spread, axis=0)
    hot = jnp.where(spread == target_ref[...], 1.0, 0.0).astype(jnp.bfloat16)
    pre = jnp.dot(hot, w_ref[...], preferred_element_type=jnp.float32)
    scale = lax.rsqrt(jnp.mean(pre * pre, axis=1, keepdims=True) + EPS)
    features = silu(pre * scale).astype(jnp.bfloat16)
    for k in range(IMAG):
        out_ref[k] = features[k * rows : (k + 1) * rows]


def features_call(rows, place, mine, other):
    lane = jnp.arange(EMBED, dtype=jnp.int32)
    is_lat = lane < LAT
    target = jnp.where(is_lat, lane % CLASSES, lane - LAT).astype(jnp.float32)[None, :]
    source = [jnp.where(is_lat, k * STOCH + lane // CLASSES, IMAG * STOCH + k) for k in range(IMAG)]
    source = jnp.concatenate(source)
    spread = (jnp.arange(CODES, dtype=jnp.int32)[:, None] == source[None, :]).astype(jnp.bfloat16)
    return pl.pallas_call(
        features_kernel,
        grid=(NY,),
        in_specs=[
            pl.BlockSpec(memory_space=pltpu.SMEM),
            pl.BlockSpec(spread.shape, lambda b: (0, 0)),
            pl.BlockSpec((1, EMBED), lambda b: (0, 0)),
            pl.BlockSpec(mine.shape, lambda b: (0, 0, 0)),
            pl.BlockSpec(other.shape, lambda b: (0, 0, 0)),
        ],
        out_specs=pl.BlockSpec((IMAG, None, rows, UNITS), lambda b: (0, b, 0, 0)),
        out_shape=pltpu.HBM((IMAG, NY, rows, UNITS), jnp.bfloat16),
        scratch_shapes=[pltpu.VMEM((EMBED, UNITS), jnp.bfloat16)],
        compiler_params=pltpu.CompilerParams(vmem_limit_bytes=32 * MIB),
        cost_estimate=pl.CostEstimate(
            flops=FEATURES_WEIGHT * IMAG * NY * rows * EMBED * (UNITS + LANES) // 5,
            bytes_accessed=IMAG * NY * rows * UNITS * 2 + EMBED * UNITS * 2,
            transcendentals=IMAG * NY * rows * UNITS,
        ),
        name="features",
    )(place, spread, target, mine, other)


def gate_kernel(n_far, features_ref, gate_ref, out_ref, w_ref):
    near, held = gate_ref.shape[:2]
    depth = held // n_far

    @pl.when(pl.program_id(0) == 0)
    def _():
        for i in range(near):
            for far in range(n_far):
                w_ref[(far * near + i) * depth : (far * near + i + 1) * depth] = gate_ref[i, far * depth : (far + 1) * depth]

    for k in range(IMAG):
        out_ref[k] = jnp.dot(features_ref[k], w_ref[...], preferred_element_type=jnp.float32).astype(jnp.bfloat16)


def gate_call(features, gate, n_far):
    rows = features.shape[2]
    width = gate.shape[2]
    return pl.pallas_call(
        functools.partial(gate_kernel, n_far),
        grid=(NY,),
        in_specs=[
            pl.BlockSpec((IMAG, None, rows, UNITS), lambda b: (0, b, 0, 0)),
            pl.BlockSpec(gate.shape, lambda b: (0, 0, 0)),
        ],
        out_specs=pl.BlockSpec((None, IMAG, rows, width), lambda b: (b, 0, 0, 0)),
        out_shape=jax.ShapeDtypeStruct((NY, IMAG, rows, width), jnp.bfloat16),
        scratch_shapes=[pltpu.VMEM((UNITS, width), jnp.bfloat16)],
        compiler_params=pltpu.CompilerParams(vmem_limit_bytes=32 * MIB),
        cost_estimate=pl.CostEstimate(
            flops=2 * IMAG * NY * rows * UNITS * width,
            bytes_accessed=IMAG * NY * rows * (UNITS + width) * 2 + UNITS * width * 2,
            transcendentals=0,
        ),
        name="gate",
    )(features, gate)


def gru_kernel(
    deter_hbm, w_rec_hbm, w_in_hbm, f_hbm, new_ref, prior_hbm, deter_ref, w_rec_ref, w_in_ref, f_ref, mid_ref, prior_ref, sems
):
    rows, bw = deter_ref.shape
    part = bw // NY
    pairs = [(deter_hbm, deter_ref), (w_rec_hbm, w_rec_ref)]
    pairs += [(f_hbm.at[:, k], f_ref.at[:, k]) for k in range(IMAG)]
    pairs += [(w_in_hbm, w_in_ref)]
    pairs += [(prior_ref.at[:, k], prior_hbm.at[:, k]) for k in range(IMAG)]
    copies = [pltpu.make_async_copy(src, dst, sems.at[i]) for i, (src, dst) in enumerate(pairs)]
    for copy in copies[: 3 + IMAG]:
        copy.start()
    copies[0].wait()
    copies[1].wait()
    for k in range(IMAG):
        old_ref = deter_ref if k == 0 else mid_ref
        next_ref = new_ref if k == IMAG - 1 else mid_ref
        old = old_ref[...]
        rec = jnp.dot(old, w_rec_ref[...], preferred_element_type=jnp.float32)
        copies[2 + k].wait()
        for q in range(NY):

            def gate(which):
                mine = f_ref[q, k, :, which * part : (which + 1) * part].astype(jnp.float32)
                return rec[:, which * bw + q * part : which * bw + (q + 1) * part] + mine

            reset = sigmoid(gate(0))
            candidate = jnp.tanh(reset * gate(1))
            update = sigmoid(gate(2) - 1.0)
            before = old[:, q * part : (q + 1) * part].astype(jnp.float32)
            fresh = update * candidate + (1.0 - update) * before
            next_ref[:, q * part : (q + 1) * part] = fresh.astype(jnp.bfloat16)
        if k == 0:
            copies[2 + IMAG].wait()
        prior = jnp.dot(next_ref[...], w_in_ref[...], preferred_element_type=jnp.float32).astype(jnp.bfloat16)
        share = prior_ref.shape[2]
        for j in range(prior_ref.shape[0]):
            prior_ref[j, k] = prior[j * share : (j + 1) * share]
        copies[3 + IMAG + k].start()
    for k in range(IMAG):
        copies[3 + IMAG + k].wait()


def gru_call(deter, w_rec, w_in, sums, tensor_n):
    rows, bw = deter.shape
    hbm = pl.BlockSpec(memory_space=pl.ANY)
    prior = (tensor_n, IMAG, rows // tensor_n, w_in.shape[1])
    return pl.pallas_call(
        gru_kernel,
        in_specs=[hbm] * 4,
        out_specs=[pl.BlockSpec(memory_space=pltpu.VMEM), hbm],
        out_shape=[jax.ShapeDtypeStruct((rows, bw), jnp.bfloat16), jax.ShapeDtypeStruct(prior, jnp.bfloat16)],
        scratch_shapes=[
            pltpu.VMEM(deter.shape, jnp.bfloat16),
            pltpu.VMEM(w_rec.shape, jnp.bfloat16),
            pltpu.VMEM(w_in.shape, jnp.bfloat16),
            pltpu.VMEM(sums.shape, jnp.bfloat16),
            pltpu.VMEM((rows, bw), jnp.bfloat16),
            pltpu.VMEM(prior, jnp.bfloat16),
            pltpu.SemaphoreType.DMA((3 + 2 * IMAG,)),
        ],
        compiler_params=pltpu.CompilerParams(vmem_limit_bytes=60 * MIB),
        cost_estimate=pl.CostEstimate(
            flops=2 * IMAG * rows * bw * (3 * bw + w_in.shape[1]),
            bytes_accessed=2 * (w_rec.size + w_in.size) + 24 * rows * bw,
            transcendentals=6 * rows * bw,
        ),
        name="gru",
    )(deter, w_rec, w_in, sums)


def assemble_kernel(place_ref, mine_ref, other_ref, out_ref):
    x, core = place_ref[0], place_ref[1]
    for i in range(NX):
        base = lax.rem(x + NX - i, NX) * NC
        out_ref[:, pl.ds(pl.multiple_of((base + core) * LANES, LANES), LANES)] = mine_ref[i]
        out_ref[:, pl.ds(pl.multiple_of((base + 1 - core) * LANES, LANES), LANES)] = other_ref[i]


def assemble_call(place, mine, other):
    vmem = pl.BlockSpec(memory_space=pltpu.VMEM)
    return pl.pallas_call(
        assemble_kernel,
        in_specs=[pl.BlockSpec(memory_space=pltpu.SMEM), vmem, vmem],
        out_specs=vmem,
        out_shape=jax.ShapeDtypeStruct((mine.shape[1], NX * NC * LANES), jnp.bfloat16),
        compiler_params=pltpu.CompilerParams(vmem_limit_bytes=16 * MIB),
        cost_estimate=pl.CostEstimate(flops=0, bytes_accessed=8 * mine.size, transcendentals=0),
        name="assemble",
    )(place, mine, other)


def tail_kernel(parts_ref, w_out_ref, picked_ref, var_ref, mask_ref, log_ref):
    pre = parts_ref[0].astype(jnp.float32)
    for i in range(1, parts_ref.shape[0]):
        pre = pre + parts_ref[i].astype(jnp.float32)
    normed = pre * lax.rsqrt(jnp.mean(pre * pre, axis=1, keepdims=True) + EPS)
    hidden = (silu(normed)).astype(jnp.bfloat16)
    rows = hidden.shape[0]
    cls = lax.broadcasted_iota(jnp.int32, (rows, LANES), 1) % CLASSES

    def within(value, combine):
        step = 1
        while step < CLASSES:
            ahead = pltpu.roll(value, step, 1)
            wrapped = pltpu.roll(value, LANES - CLASSES + step, 1)
            value = combine(value, jnp.where(cls >= step, ahead, wrapped))
            step *= 2
        return value

    total = jnp.zeros((rows, LANES), jnp.float32)
    every = jnp.dot(hidden, w_out_ref[...], preferred_element_type=jnp.float32)
    wants = jnp.dot(picked_ref[...], var_ref[...], preferred_element_type=jnp.float32)
    for start in range(0, LAT, LANES):
        logits = every[:, start : start + LANES]
        powers = jnp.exp(logits - within(logits, jnp.maximum))
        probs = 0.99 * (powers / within(powers, jnp.add)) + 0.01 / CLASSES
        want = wants[:, start : start + LANES]
        total = total + jnp.where(cls.astype(jnp.float32) == want, jnp.log(probs), 0.0)
    summed = jnp.where(mask_ref[...] > 0, jnp.sum(total, axis=1, keepdims=True), 0.0)
    lanes = lax.broadcasted_iota(jnp.int32, (rows, LANES), 1)
    diagonal = lax.broadcasted_iota(jnp.int32, (rows, LANES), 0) == lanes
    line = jnp.sum(jnp.where(diagonal, summed, 0.0), axis=0, keepdims=True)
    log_ref[...] = jnp.broadcast_to(line[None], log_ref.shape)


def tail_call(parts, w_out, picked, mask):
    tensor_n, rows = parts.shape[:2]
    lane = jnp.arange(LAT, dtype=jnp.int32)
    var_of = (jnp.arange(STOCH, dtype=jnp.int32)[:, None] == lane[None, :] // CLASSES).astype(jnp.bfloat16)
    vmem = pl.BlockSpec(memory_space=pltpu.VMEM)
    return pl.pallas_call(
        tail_kernel,
        in_specs=[vmem] * 5,
        out_specs=vmem,
        out_shape=jax.ShapeDtypeStruct((tensor_n, 8, LANES), jnp.float32),
        compiler_params=pltpu.CompilerParams(vmem_limit_bytes=32 * MIB),
        cost_estimate=pl.CostEstimate(
            flops=2 * rows * UNITS * LAT, bytes_accessed=2 * w_out.size, transcendentals=4 * rows * LAT
        ),
        name="tail",
    )(parts, w_out, picked, var_of, mask)


def body(
    post_deter,
    post_sample,
    samples,
    actions,
    counts,
    w_stoch,
    w_action,
    w_gate,
    w_rec,
    w_prior_in,
    w_prior_out,
    n_dp,
):
    rows = post_deter.shape[0]
    depth = w_gate.shape[0]
    tensor_n = NX * NC
    share = rows // tensor_n
    me = lax.axis_index("tensor")
    place = jnp.stack([me // NC, me % NC, lax.axis_index("dp") % NY]).astype(jnp.int32)
    n_far = n_dp // NY // NEAR

    sent = split_call(w_gate, n_far).reshape(n_far * NY, depth, -1)
    held = lax.all_to_all(sent, "dp", 0, 0, axis_index_groups=far_groups(n_dp)).reshape(n_far * NY * depth, -1)
    gate = jnp.broadcast_to(held[None], (NEAR,) + held.shape)
    gate = lax.all_to_all(gate, "dp", 0, 0, axis_index_groups=near_groups(n_dp))

    mine = diagonal_gather(prep_call(w_stoch, w_action, post_sample.T, samples.transpose(0, 2, 1), actions), n_dp)
    other = core_swap(mine)
    features = features_call(rows, place, mine, other)
    sums = lax.all_to_all(gate_call(features, gate, n_far), "dp", 0, 0, axis_index_groups=y_groups(n_dp))

    w_out_late, _ = lax.optimization_barrier((w_prior_out, features))
    out_mine = x_gather(w_out_late)
    out_other = core_swap(out_mine)

    positions = jnp.arange(STEPS, dtype=jnp.int32)
    valid_mask = (positions[None, :] < counts[:, None]).reshape(rows)
    my_mask = lax.dynamic_slice_in_dim(valid_mask, me * share, share, 0).astype(jnp.float32)
    my_mask = jnp.concatenate([my_mask] * IMAG)[:, None]
    picked = lax.dynamic_slice_in_dim(samples, me * share, share, 1)
    picked = picked.reshape(IMAG * share, STOCH).astype(jnp.bfloat16)

    deter, partial = gru_call(post_deter, w_rec[0], w_prior_in, sums, tensor_n)
    parts = lax.all_to_all(partial.reshape(tensor_n, IMAG * share, UNITS), "tensor", 0, 0)
    logs = tail_call(parts, assemble_call(place, out_mine, out_other), picked, my_mask)
    logs = lax.all_to_all(logs, "tensor", 0, 0)[:, 0, : IMAG * share]
    log_prob = logs.reshape(tensor_n, IMAG, share).transpose(1, 0, 2).reshape(IMAG, rows)
    deter_out = jnp.where(valid_mask[:, None], deter, jnp.zeros_like(deter))
    return (deter_out, log_prob)


def solution(mesh):
    in_specs = (
        P("dp", "tensor"),
        P("dp", None),
        P(None, "dp", None),
        P(None, "dp"),
        P("dp"),
        P(None, "tensor"),
        P(None, "tensor"),
        P("dp", "tensor"),
        P("tensor", None, None),
        P("tensor", None),
        P(None, "tensor"),
    )
    out_specs = (P("dp", "tensor"), P(None, "dp"))
    whole = functools.partial(body, n_dp=mesh.shape["dp"])
    return jax.shard_map(whole, mesh=mesh, in_specs=in_specs, out_specs=out_specs, check_vma=False)
```

time: 147 us -> 145 us (0.986)
  Pallas kernels: 21.2 us -> 30.6 us
  local copies, waits for them, and re-layouts: 10.2 us -> 6.48 us
  other arithmetic: 5.11 us -> 1.52 us
  waiting for transfers between devices: 40 us -> 37.5 us
    pallas_call x3 -> x5, Pallas kernels: 9.96 us -> 16.8 us  [the longest x1 5.7 us: gru_call(): pl.pallas_call(gru_kernel, in_specs=[hbm] * 4, out_specs=[pl.BlockSpec(me...]
    ppermute x9 -> x6, starting transfers between devices: 29 us -> 23.2 us  [the longest x3 12.3 us: diagonal_gather(): pieces.append(lax.ppermute(value, ('dp', 'tensor'), perm))]
    all_to_all x2 -> x3, starting transfers between devices: 24 us -> 29.4 us  [the longest x1 18.4 us: body(): lax.all_to_all(sent, 'dp', 0, 0, axis_index_groups=far_groups(n_dp))]
    unnamed x25 -> x16, local copies, waits for them, and re-layouts: 8.67 us -> 4.41 us
    another operation x10 -> x3, other arithmetic: 3.72 us -> 0.38 us  [the longest x1 0.17 us: diagonal_gather(): return jnp.stack(pieces)]
    all_to_all x1, waiting for transfers between devices: 14.4 us -> 11.2 us  [body(): lax.all_to_all(partial.reshape(tensor_n, IMAG * share, UNITS), 'tensor',...]
    pallas_call x1, Pallas kernels: 10.2 us -> 12.3 us  [features_call(): pl.pallas_call(features_kernel, grid=(NY,), in_specs=[pl.BlockSpec(memory...]
    ppermute x2, waiting for transfers between devices: 0.98 us -> 2.61 us  [core_swap(): return lax.ppermute(value, 'tensor', perm)]
  transfers between devices with their start and end apart: 15 -> 13, of which waited for: 8 -> 9; matrix products, arithmetic and copies ran while one was open for 2% -> 2% of each run, Pallas kernels for 9% -> 15%
where the time goes in v6:
time: 145 us; the launch traced here: 144 us
  starting transfers between devices  67.1 us (46%)
  waiting for transfers between devices  37.5 us (26%)
  Pallas kernels  30.6 us (21%)
  local copies, waits for them, and re-layouts  6.48 us (4%)
  other arithmetic  1.52 us (1%)
    all_to_all x1, starting transfers between devices, body(): lax.all_to_all(sent, 'dp', 0, 0, axis_index_groups=far_groups(n_dp))  18.4 us
    pallas_call x1, Pallas kernels, features_call(): pl.pallas_call(features_kernel, grid=(NY,), in_specs=[pl.BlockSpec(memory...  12.3 us
    ppermute x3, starting transfers between devices, diagonal_gather(): pieces.append(lax.ppermute(value, ('dp', 'tensor'), perm))  12.3 us
    all_to_all x1, waiting for transfers between devices, body(): lax.all_to_all(partial.reshape(tensor_n, IMAG * share, UNITS), 'tensor',...  11.2 us
    ppermute x3, starting transfers between devices, x_gather(): pieces.append(lax.ppermute(value, 'tensor', perm))  10.8 us
    ppermute x3, waiting for transfers between devices, x_gather(): pieces.append(lax.ppermute(value, 'tensor', perm))  10.4 us
    ppermute x3, waiting for transfers between devices, diagonal_gather(): pieces.append(lax.ppermute(value, ('dp', 'tensor'), perm))  8.75 us
    all_to_all x1, starting transfers between devices, body(): gate = lax.all_to_all(gate, 'dp', 0, 0, axis_index_groups=near_groups(n_dp))  6.53 us
  transfers between devices with their start and end apart: 13, of which 9 were waited for; matrix products, arithmetic and copies ran while one was open for 2% of the time, Pallas kernels for 15%

profile of v6, /device:TPU:1, one launch (start us, length us, event | category | flops | bytes accessed | tf_op | source)
XLA Modules:
  0.0 144.1 jit_solution(16309179174364002360)
XLA Ops:
  0.6 1.5 %split.1 = bf16[4,4,16,384]{3,2,1,0:T(8,128)(2,1)} custom-call(bf16[16,1536]{1,0:T(8,128)(2,1)} %w_ref.1), custom_call_target="tpu_custom_call" | custom-call | bytes 196608 | tf_op jit(solution)/shard_map/split/pallas_call | solution.py:90
  2.1 18.4 %all-to-all-start = ((bf16[16,16,384]{2,1,0:T(8,128)(2,1)}), bf16[16,16,384]{2,1,0:T(8,128)(2,1)S(1)}, u32[]{:S(2)}, u32[]{:S(2)}) async-start(bf16[16,16,384]{2,1,0:T(8,128)(2,1)} %bitcast.24), calls=%async_computation | async-start | bytes 393216 | tf_op jit(solution)/shard_map/all_to_all | solution.py:393
  20.5 1.8 %prep.1 = bf16[1312,128]{1,0:T(8,128)(2,1)} custom-call(bf16[1024,128]{1,0:T(8,128)(2,1)} %w_stoch_ref.1, bf16[18,128]{1,0:T(8,128)(2,1)} %w_action_ref.1, s32[32,256]{1,0:T(8,128)} %bitcast.34, s32[2,32,256]{2,1,0:T(8,128)} %bitcast.33, s32[2,256]{1,0:T(2,128)} %actions_ref.1), custom_call_target="tpu_custom_call" | custom-call | bytes 589824 | tf_op jit(solution)/shard_map/prep/pallas_call | solution.py:119
  22.3 6.8 %collective-permute-start.2 = (bf16[1312,128]{1,0:T(8,128)(2,1)}, bf16[1312,128]{1,0:T(8,128)(2,1)S(1)}, u32[]{:S(2)}, u32[]{:S(2)}) collective-permute-start(bf16[1312,128]{1,0:T(8,128)(2,1)} %prep.1), channel_id=1, source_target_pairs={{0,30},{1,31},{2,24},{3,25},{4,26},{5,27},{6,28},{7,29},{8,6},{9,7... | collective-permute-start | bytes 1007624 | tf_op jit(solution)/shard_map/ppermute | solution.py:52
  29.1 2.7 %collective-permute-start.1 = (bf16[1312,128]{1,0:T(8,128)(2,1)}, bf16[1312,128]{1,0:T(8,128)(2,1)S(1)}, u32[]{:S(2)}, u32[]{:S(2)}) collective-permute-start(bf16[1312,128]{1,0:T(8,128)(2,1)} %prep.1), channel_id=1, source_target_pairs={{0,20},{1,21},{2,22},{3,23},{4,16},{5,17},{6,18},{7,19},{8,28},{9,... | collective-permute-start | bytes 1007624 | tf_op jit(solution)/shard_map/ppermute | solution.py:52
  31.8 2.8 %collective-permute-start = (bf16[1312,128]{1,0:T(8,128)(2,1)}, bf16[1312,128]{1,0:T(8,128)(2,1)S(1)}, u32[]{:S(2)}, u32[]{:S(2)}) collective-permute-start(bf16[1312,128]{1,0:T(8,128)(2,1)} %prep.1), channel_id=1, source_target_pairs={{0,10},{1,11},{2,12},{3,13},{4,14},{5,15},{6,8},{7,9},{8,18},{9,19... | collective-permute-start | bytes 1007624 | tf_op jit(solution)/shard_map/ppermute | solution.py:52
  35.2 1.0 broadcast_in_dim.41
  36.2 6.5 %all-to-all-start.1 = ((bf16[4,256,384]{2,1,0:T(8,128)(2,1)}), bf16[4,256,384]{2,1,0:T(8,128)(2,1)S(1)}, u32[]{:S(2)}, u32[]{:S(2)}) async-start(bf16[4,256,384]{2,1,0:T(8,128)(2,1)} %broadcast_in_dim.41), calls=%async_computation.1 | async-start | bytes 1572864 | tf_op jit(solution)/shard_map/all_to_all | solution.py:395
  42.7 1.4 collective-permute-done.1
  44.1 7.3 %collective-permute-done = bf16[1312,128]{1,0:T(8,128)(2,1)S(1)} collective-permute-done((bf16[1312,128]{1,0:T(8,128)(2,1)}, bf16[1312,128]{1,0:T(8,128)(2,1)S(1)}, u32[]{:S(2)}, u32[]{:S(2)}) %collective-permute-start) | collective-permute-done | bytes 335904 | tf_op jit(solution)/shard_map/ppermute | solution.py:52
  51.6 3.2 %collective-permute-start.3 = (bf16[4,1312,128]{2,1,0:T(8,128)(2,1)S(1)}, bf16[4,1312,128]{2,1,0:T(8,128)(2,1)}, u32[]{:S(2)}, u32[]{:S(2)}) collective-permute-start(bf16[4,1312,128]{2,1,0:T(8,128)(2,1)S(1)} %pad_maximum_fusion.mine_ref), channel_id=1, source_target_pairs={{0,1},{1,0},{2,3},{3,2},{4,5},{5,4},{6,7},{7,6},{8,9},{9,8},{10,11... | collective-permute-start | bytes 4030472 | tf_op jit(solution)/shard_map/ppermute | solution.py:66
  55.1 2.6 %collective-permute-done.3.other_ref = bf16[4,1312,128]{2,1,0:T(8,128)(2,1)} collective-permute-done((bf16[4,1312,128]{2,1,0:T(8,128)(2,1)S(1)}, bf16[4,1312,128]{2,1,0:T(8,128)(2,1)}, u32[]{:S(2)}, u32[]{:S(2)}) %collective-permute-start.3) | collective-permute-done | bytes 1343520 | tf_op jit(solution)/shard_map/ppermute | solution.py:66
  57.7 12.3 %features.1.features_ref = bf16[2,4,256,1024]{3,2,1,0:T(8,128)(2,1)} custom-call(s32[3]{0:T(128)S(1)} %pad_add_fusion.1.place_ref, bf16[80,2304]{1,0:T(8,128)(2,1)S(1)} %fusion.spread_ref, f32[1,1152]{1,0:T(1,128)S(1)} %fusion.8.target_ref, bf16[4,1312,128]{2,1,0:T(8,128)(2,1)S(1)} %pad_maximum_fusion.mine_ref, ...), custom_call_target="tpu_custom_call" | custom-call | flops 6522981376 | bytes 6553600 | tf_op jit(solution)/shard_map/features/pallas_call | solution.py:166
  70.0 2.2 %copy-done = bf16[2,4,256,1024]{3,2,1,0:T(8,128)(2,1)S(1)} copy-done((bf16[2,4,256,1024]{3,2,1,0:T(8,128)(2,1)S(1)}, bf16[2,4,256,1024]{3,2,1,0:T(8,128)(2,1)}, u32[]{:S(2)}) %copy-start) | copy-done | bytes 4194328
  72.2 4.0 %gate.1 = bf16[4,2,256,384]{3,2,1,0:T(8,128)(2,1)} custom-call(bf16[2,4,256,1024]{3,2,1,0:T(8,128)(2,1)S(1)} %copy-done, bf16[4,256,384]{2,1,0:T(8,128)(2,1)S(1)} %all-to-all-done.1.gate_ref), custom_call_target="tpu_custom_call" | custom-call | flops 1610612736 | bytes 6553600 | tf_op jit(solution)/shard_map/gate/pallas_call | solution.py:206
  76.2 4.5 %all-to-all-start.2 = ((bf16[4,2,256,384]{3,2,1,0:T(8,128)(2,1)}), bf16[4,2,256,384]{3,2,1,0:T(8,128)(2,1)}, u32[]{:S(2)}, u32[]{:S(2)}) async-start(bf16[4,2,256,384]{3,2,1,0:T(8,128)(2,1)} %gate.1), calls=%async_computation.2 | async-start | bytes 3145728 | tf_op jit(solution)/shard_map/all_to_all | solution.py:400
  80.7 4.5 %collective-permute-start.6 = (bf16[1024,128]{1,0:T(8,128)(2,1)S(1)}, bf16[1024,128]{1,0:T(8,128)(2,1)S(1)}, u32[]{:S(2)}, u32[]{:S(2)}) collective-permute-start(bf16[1024,128]{1,0:T(8,128)(2,1)S(1)} %copy-done.5), channel_id=1, source_target_pairs={{0,6},{1,7},{2,0},{3,1},{4,2},{5,3},{6,4},{7,5},{8,14},{9,15},{10,... | collective-permute-start | bytes 786440 | tf_op jit(solution)/shard_map/ppermute | solution.py:60
  85.2 4.5 %collective-permute-start.5 = (bf16[1024,128]{1,0:T(8,128)(2,1)S(1)}, bf16[1024,128]{1,0:T(8,128)(2,1)S(1)}, u32[]{:S(2)}, u32[]{:S(2)}) collective-permute-start(bf16[1024,128]{1,0:T(8,128)(2,1)S(1)} %copy-done.5), channel_id=1, source_target_pairs={{0,4},{1,5},{2,6},{3,7},{4,0},{5,1},{6,2},{7,3},{8,12},{9,13},{10,... | collective-permute-start | bytes 786440 | tf_op jit(solution)/shard_map/ppermute | solution.py:60
  89.6 1.9 %collective-permute-start.4 = (bf16[1024,128]{1,0:T(8,128)(2,1)S(1)}, bf16[1024,128]{1,0:T(8,128)(2,1)S(1)}, u32[]{:S(2)}, u32[]{:S(2)}) collective-permute-start(bf16[1024,128]{1,0:T(8,128)(2,1)S(1)} %copy-done.5), channel_id=1, source_target_pairs={{0,2},{1,3},{2,4},{3,5},{4,6},{5,7},{6,0},{7,1},{8,10},{9,11},{10,... | collective-permute-start | bytes 786440 | tf_op jit(solution)/shard_map/ppermute | solution.py:60
  91.6 0.8 collective-permute-done.6
  92.4 3.5 %collective-permute-done.5 = bf16[1024,128]{1,0:T(8,128)(2,1)S(1)} collective-permute-done((bf16[1024,128]{1,0:T(8,128)(2,1)S(1)}, bf16[1024,128]{1,0:T(8,128)(2,1)S(1)}, u32[]{:S(2)}, u32[]{:S(2)}) %collective-permute-start.5) | collective-permute-done | bytes 262176 | tf_op jit(solution)/shard_map/ppermute | solution.py:60
  95.9 6.1 %collective-permute-done.4 = bf16[1024,128]{1,0:T(8,128)(2,1)S(1)} collective-permute-done((bf16[1024,128]{1,0:T(8,128)(2,1)S(1)}, bf16[1024,128]{1,0:T(8,128)(2,1)S(1)}, u32[]{:S(2)}, u32[]{:S(2)}) %collective-permute-start.4) | collective-permute-done | bytes 262176 | tf_op jit(solution)/shard_map/ppermute | solution.py:60
  102.2 2.8 %collective-permute-start.7 = (bf16[4,1024,128]{2,1,0:T(8,128)(2,1)S(1)}, bf16[4,1024,128]{2,1,0:T(8,128)(2,1)S(1)}, u32[]{:S(2)}, u32[]{:S(2)}) collective-permute-start(bf16[4,1024,128]{2,1,0:T(8,128)(2,1)S(1)} %pad_maximum_fusion.1.mine_ref), channel_id=1, source_target_pairs={{0,1},{1,0},{2,3},{3,2},{4,5},{5,4},{6,7},{7,6},{8,9},{9,8},{10,11... | collective-permute-start | bytes 3145736 | tf_op jit(solution)/shard_map/ppermute | solution.py:66
  105.0 5.7 %gru.1 = (bf16[256,512]{1,0:T(8,128)(2,1)}, bf16[8,2,32,1024]{3,2,1,0:T(8,128)(2,1)}) custom-call(bf16[256,512]{1,0:T(8,128)(2,1)} %deter_hbm.1, bf16[512,1536]{1,0:T(8,128)(2,1)} %bitcast.36, bf16[512,1024]{1,0:T(8,128)(2,1)} %w_in_hbm.1, bf16[4,2,256,384]{3,2,1,0:T(8,128)(2,1)} %all-to-all-done.2.f_hbm), custom_call_target="tpu_custom_call" | custom-call | flops 1342177280 | bytes 5767168 | tf_op jit(solution)/shard_map/gru/pallas_call | solution.py:273
  110.7 4.4 %all-to-all-start.3 = ((bf16[8,64,1024]{2,1,0:T(8,128)(2,1)}), bf16[8,64,1024]{2,1,0:T(8,128)(2,1)}, u32[]{:S(2)}, u32[]{:S(2)}) async-start(bf16[8,64,1024]{2,1,0:T(8,128)(2,1)} %bitcast.23), calls=%async_computation.3 | async-start | bytes 2097152 | tf_op jit(solution)/shard_map/all_to_all | solution.py:414
  115.7 1.0 copy-done.1
  116.7 1.2 copy-done.2
  117.9 1.1 assemble.1.w_out_ref
  119.1 11.2 %all-to-all-done.3.parts_ref = bf16[8,64,1024]{2,1,0:T(8,128)(2,1)} async-done(((bf16[8,64,1024]{2,1,0:T(8,128)(2,1)}), bf16[8,64,1024]{2,1,0:T(8,128)(2,1)}, u32[]{:S(2)}, u32[]{:S(2)}) %all-to-all-start.3) | async-done | bytes 1048608 | tf_op jit(solution)/shard_map/all_to_all | solution.py:414
  130.3 4.2 %tail.1 = f32[8,8,128]{2,1,0:T(8,128)} custom-call(bf16[8,64,1024]{2,1,0:T(8,128)(2,1)} %all-to-all-done.3.parts_ref, bf16[1024,1024]{1,0:T(8,128)(2,1)S(1)} %assemble.1.w_out_ref, bf16[64,32]{1,0:T(8,128)(2,1)S(1)} %bitcast.21, bf16[32,1024]{1,0:T(8,128)(2,1)S(1)} %fusion.1.var_ref, f32[64,1]{1,0:T(8,128)S(1)} %copy.14.mask_ref), custom_call_target="tpu_custom_call" | custom-call | flops 134217728 | bytes 2097152 | tf_op jit(solution)/shard_map/tail/pallas_call | solution.py:357
  134.5 4.1 %all-to-all-start.4 = ((f32[8,8,128]{2,1,0:T(8,128)}), f32[8,8,128]{2,1,0:T(8,128)S(1)}, u32[]{:S(2)}, u32[]{:S(2)}) async-start(f32[8,8,128]{2,1,0:T(8,128)} %tail.1), calls=%async_computation.4 | async-start | bytes 65536 | tf_op jit(solution)/shard_map/all_to_all | solution.py:416
  139.4 3.9 %all-to-all-done.4 = f32[8,8,128]{2,1,0:T(8,128)S(1)} async-done(((f32[8,8,128]{2,1,0:T(8,128)}), f32[8,8,128]{2,1,0:T(8,128)S(1)}, u32[]{:S(2)}, u32[]{:S(2)}) %all-to-all-start.4) | async-done | bytes 32800 | tf_op jit(solution)/shard_map/all_to_all | solution.py:416
  (39 shorter events, 3.3 us)
Async XLA Ops:
  2.1 33.1 %all-to-all-start = ((bf16[16,16,384]{2,1,0:T(8,128)(2,1)}), bf16[16,16,384]{2,1,0:T(8,128)(2,1)S(1)}, u32[]{:S(2)}, u32[]{:S(2)}) async-start(bf16[16,16,384]{2,1,0:T(8,128)(2,1)} %bitcast.24), calls=%async_computation | async-start | bytes 393216 | tf_op jit(solution)/shard_map/all_to_all | solution.py:393
  22.3 29.2 %copy-start.3 = (bf16[1312,128]{1,0:T(8,128)(2,1)S(1)}, bf16[1312,128]{1,0:T(8,128)(2,1)}, u32[]{:S(2)}) copy-start(bf16[1312,128]{1,0:T(8,128)(2,1)} %prep.1) | copy-start | bytes 1007620
  22.3 20.4 %collective-permute-start.2 = (bf16[1312,128]{1,0:T(8,128)(2,1)}, bf16[1312,128]{1,0:T(8,128)(2,1)S(1)}, u32[]{:S(2)}, u32[]{:S(2)}) collective-permute-start(bf16[1312,128]{1,0:T(8,128)(2,1)} %prep.1), channel_id=1, source_target_pairs={{0,30},{1,31},{2,24},{3,25},{4,26},{5,27},{6,28},{7,29},{8,6},{9,7... | collective-permute-start | bytes 1007624 | tf_op jit(solution)/shard_map/ppermute | solution.py:52
  29.1 15.0 %collective-permute-start.1 = (bf16[1312,128]{1,0:T(8,128)(2,1)}, bf16[1312,128]{1,0:T(8,128)(2,1)S(1)}, u32[]{:S(2)}, u32[]{:S(2)}) collective-permute-start(bf16[1312,128]{1,0:T(8,128)(2,1)} %prep.1), channel_id=1, source_target_pairs={{0,20},{1,21},{2,22},{3,23},{4,16},{5,17},{6,18},{7,19},{8,28},{9,... | collective-permute-start | bytes 1007624 | tf_op jit(solution)/shard_map/ppermute | solution.py:52
  31.8 19.6 %collective-permute-start = (bf16[1312,128]{1,0:T(8,128)(2,1)}, bf16[1312,128]{1,0:T(8,128)(2,1)S(1)}, u32[]{:S(2)}, u32[]{:S(2)}) collective-permute-start(bf16[1312,128]{1,0:T(8,128)(2,1)} %prep.1), channel_id=1, source_target_pairs={{0,10},{1,11},{2,12},{3,13},{4,14},{5,15},{6,8},{7,9},{8,18},{9,19... | collective-permute-start | bytes 1007624 | tf_op jit(solution)/shard_map/ppermute | solution.py:52
  36.2 33.9 %all-to-all-start.1 = ((bf16[4,256,384]{2,1,0:T(8,128)(2,1)}), bf16[4,256,384]{2,1,0:T(8,128)(2,1)S(1)}, u32[]{:S(2)}, u32[]{:S(2)}) async-start(bf16[4,256,384]{2,1,0:T(8,128)(2,1)} %broadcast_in_dim.41), calls=%async_computation.1 | async-start | bytes 1572864 | tf_op jit(solution)/shard_map/all_to_all | solution.py:395
  51.6 6.1 %collective-permute-start.3 = (bf16[4,1312,128]{2,1,0:T(8,128)(2,1)S(1)}, bf16[4,1312,128]{2,1,0:T(8,128)(2,1)}, u32[]{:S(2)}, u32[]{:S(2)}) collective-permute-start(bf16[4,1312,128]{2,1,0:T(8,128)(2,1)S(1)} %pad_maximum_fusion.mine_ref), channel_id=1, source_target_pairs={{0,1},{1,0},{2,3},{3,2},{4,5},{5,4},{6,7},{7,6},{8,9},{9,8},{10,11... | collective-permute-start | bytes 4030472 | tf_op jit(solution)/shard_map/ppermute | solution.py:66
  70.0 2.2 %copy-start = (bf16[2,4,256,1024]{3,2,1,0:T(8,128)(2,1)S(1)}, bf16[2,4,256,1024]{3,2,1,0:T(8,128)(2,1)}, u32[]{:S(2)}) copy-start(bf16[2,4,256,1024]{3,2,1,0:T(8,128)(2,1)} %features.1.features_ref) | copy-start | bytes 12582916
  76.2 4.5 %copy-start.5 = (bf16[1024,128]{1,0:T(8,128)(2,1)S(1)}, bf16[1024,128]{1,0:T(8,128)(2,1)}, u32[]{:S(2)}) copy-start(bf16[1024,128]{1,0:T(8,128)(2,1)} %param.21) | copy-start | bytes 786436
  76.2 28.8 %all-to-all-start.2 = ((bf16[4,2,256,384]{3,2,1,0:T(8,128)(2,1)}), bf16[4,2,256,384]{3,2,1,0:T(8,128)(2,1)}, u32[]{:S(2)}, u32[]{:S(2)}) async-start(bf16[4,2,256,384]{3,2,1,0:T(8,128)(2,1)} %gate.1), calls=%async_computation.2 | async-start | bytes 3145728 | tf_op jit(solution)/shard_map/all_to_all | solution.py:400
  80.7 11.7 %collective-permute-start.6 = (bf16[1024,128]{1,0:T(8,128)(2,1)S(1)}, bf16[1024,128]{1,0:T(8,128)(2,1)S(1)}, u32[]{:S(2)}, u32[]{:S(2)}) collective-permute-start(bf16[1024,128]{1,0:T(8,128)(2,1)S(1)} %copy-done.5), channel_id=1, source_target_pairs={{0,6},{1,7},{2,0},{3,1},{4,2},{5,3},{6,4},{7,5},{8,14},{9,15},{10,... | collective-permute-start | bytes 786440 | tf_op jit(solution)/shard_map/ppermute | solution.py:60
  85.2 10.7 %collective-permute-start.5 = (bf16[1024,128]{1,0:T(8,128)(2,1)S(1)}, bf16[1024,128]{1,0:T(8,128)(2,1)S(1)}, u32[]{:S(2)}, u32[]{:S(2)}) collective-permute-start(bf16[1024,128]{1,0:T(8,128)(2,1)S(1)} %copy-done.5), channel_id=1, source_target_pairs={{0,4},{1,5},{2,6},{3,7},{4,0},{5,1},{6,2},{7,3},{8,12},{9,13},{10,... | collective-permute-start | bytes 786440 | tf_op jit(solution)/shard_map/ppermute | solution.py:60
  89.6 12.4 %collective-permute-start.4 = (bf16[1024,128]{1,0:T(8,128)(2,1)S(1)}, bf16[1024,128]{1,0:T(8,128)(2,1)S(1)}, u32[]{:S(2)}, u32[]{:S(2)}) collective-permute-start(bf16[1024,128]{1,0:T(8,128)(2,1)S(1)} %copy-done.5), channel_id=1, source_target_pairs={{0,2},{1,3},{2,4},{3,5},{4,6},{5,7},{6,0},{7,1},{8,10},{9,11},{10,... | collective-permute-start | bytes 786440 | tf_op jit(solution)/shard_map/ppermute | solution.py:60
  102.2 13.5 %collective-permute-start.7 = (bf16[4,1024,128]{2,1,0:T(8,128)(2,1)S(1)}, bf16[4,1024,128]{2,1,0:T(8,128)(2,1)S(1)}, u32[]{:S(2)}, u32[]{:S(2)}) collective-permute-start(bf16[4,1024,128]{2,1,0:T(8,128)(2,1)S(1)} %pad_maximum_fusion.1.mine_ref), channel_id=1, source_target_pairs={{0,1},{1,0},{2,3},{3,2},{4,5},{5,4},{6,7},{7,6},{8,9},{9,8},{10,11... | collective-permute-start | bytes 3145736 | tf_op jit(solution)/shard_map/ppermute | solution.py:66
  110.7 4.4 %copy-start.7 = (s32[4]{0:T(128)S(1)}, s32[4]{0:T(128)}, u32[]{:S(2)}) copy-start(s32[4]{0:T(128)} %param.15) | copy-start | bytes 52
  110.7 4.5 %copy-start.6 = (s32[2,256,32]{1,2,0:T(8,128)S(1)}, s32[2,256,32]{1,2,0:T(8,128)}, u32[]{:S(2)}) copy-start(s32[2,256,32]{1,2,0:T(8,128)} %param.13) | copy-start | bytes 196612
  110.7 19.6 %all-to-all-start.3 = ((bf16[8,64,1024]{2,1,0:T(8,128)(2,1)}), bf16[8,64,1024]{2,1,0:T(8,128)(2,1)}, u32[]{:S(2)}, u32[]{:S(2)}) async-start(bf16[8,64,1024]{2,1,0:T(8,128)(2,1)} %bitcast.23), calls=%async_computation.3 | async-start | bytes 2097152 | tf_op jit(solution)/shard_map/all_to_all | solution.py:414
  115.7 1.0 copy-start.1
  116.7 1.2 copy-start.2
  130.3 8.3 %copy-start.4 = (bf16[256,512]{1,0:T(8,128)(2,1)S(1)}, bf16[256,512]{1,0:T(8,128)(2,1)}, u32[]{:S(2)}) copy-start(bf16[256,512]{1,0:T(8,128)(2,1)} %get-tuple-element.5) | copy-start | bytes 786436
  134.5 8.8 %all-to-all-start.4 = ((f32[8,8,128]{2,1,0:T(8,128)}), f32[8,8,128]{2,1,0:T(8,128)S(1)}, u32[]{:S(2)}, u32[]{:S(2)}) async-start(f32[8,8,128]{2,1,0:T(8,128)} %tail.1), calls=%async_computation.4 | async-start | bytes 65536 | tf_op jit(solution)/shard_map/all_to_all | solution.py:416

commit v7 on v5

--- a/solution.py
+++ b/solution.py
@@ -89,24 +89,28 @@
     )(w_gate, latent, samples, actions)
 
 
-def copies_kernel(came_ref, out_ref):
-    depth = out_ref.shape[1] // NY
-    part = out_ref.shape[2] // 3
+def copies_kernel(came_ref, out_hbm, one_ref, sems):
+    depth = one_ref.shape[0] // NY
+    part = one_ref.shape[1] // 3
     for y in range(NY):
-        for z in range(out_ref.shape[0]):
-            here = slice(y * depth, (y + 1) * depth)
-            out_ref[z, here, : 2 * part] = came_ref[y, :depth, : 2 * part]
-            out_ref[z, here, 2 * part :] = came_ref[y, depth : 2 * depth, :part]
+        here = slice(y * depth, (y + 1) * depth)
+        one_ref[here, : 2 * part] = came_ref[y, :depth, : 2 * part]
+        one_ref[here, 2 * part :] = came_ref[y, depth : 2 * depth, :part]
+    copies = [pltpu.make_async_copy(one_ref, out_hbm.at[z], sems.at[z]) for z in range(out_hbm.shape[0])]
+    for copy in copies:
+        copy.start()
+    for copy in copies:
+        copy.wait()
 
 
 def copies_call(came, n_z, depth, width):
-    vmem = pl.BlockSpec(memory_space=pltpu.VMEM)
     return pl.pallas_call(
         copies_kernel,
-        in_specs=[vmem],
-        out_specs=vmem,
-        out_shape=jax.ShapeDtypeStruct((n_z, NY * depth, width), jnp.bfloat16),
-        compiler_params=pltpu.CompilerParams(vmem_limit_bytes=60 * MIB),
+        in_specs=[pl.BlockSpec(memory_space=pltpu.VMEM)],
+        out_specs=pl.BlockSpec(memory_space=pltpu.HBM),
+        out_shape=pltpu.HBM((n_z, NY * depth, width), jnp.bfloat16),
+        scratch_shapes=[pltpu.VMEM((NY * depth, width), jnp.bfloat16), pltpu.SemaphoreType.DMA((n_z,))],
+        compiler_params=pltpu.CompilerParams(vmem_limit_bytes=16 * MIB),
         cost_estimate=pl.CostEstimate(flops=0, bytes_accessed=4 * n_z * depth * width, transcendentals=0),
         name="copies",
     )(came)
@@ -155,8 +159,8 @@
             pl.BlockSpec((NX, width, LANES), lambda b: (0, 0, 0)),
             pl.BlockSpec((NX, width, LANES), lambda b: (0, 0, 0)),
         ],
-        out_specs=pl.BlockSpec((IMAG, None, rows, UNITS), lambda b: (0, b, 0, 0)),
-        out_shape=pltpu.HBM((IMAG, NY, rows, UNITS), jnp.bfloat16),
+        out_specs=pl.BlockSpec((None, IMAG, rows, UNITS), lambda b: (b, 0, 0, 0)),
+        out_shape=pltpu.HBM((NY, IMAG, rows, UNITS), jnp.bfloat16),
         scratch_shapes=[pltpu.VMEM((width, UNITS), jnp.bfloat16)],
         compiler_params=pltpu.CompilerParams(vmem_limit_bytes=32 * MIB),
         cost_estimate=pl.CostEstimate(
@@ -168,36 +172,18 @@
     )(place, came, spread, target, mine, other)
 
 
-def gate_kernel(features_ref, gate_ref, out_ref):
-    for k in range(IMAG):
-        out_ref[k] = jnp.dot(features_ref[k], gate_ref[...], preferred_element_type=jnp.float32).astype(jnp.bfloat16)
-
-
-def gate_call(features, gate):
-    rows = features.shape[2]
-    width = gate.shape[1]
-    return pl.pallas_call(
-        gate_kernel,
-        grid=(NY,),
-        in_specs=[
-            pl.BlockSpec((IMAG, None, rows, UNITS), lambda b: (0, b, 0, 0)),
-            pl.BlockSpec((UNITS, width), lambda b: (0, 0)),
-        ],
-        out_specs=pl.BlockSpec((None, IMAG, rows, width), lambda b: (b, 0, 0, 0)),
-        out_shape=jax.ShapeDtypeStruct((NY, IMAG, rows, width), jnp.bfloat16),
-        compiler_params=pltpu.CompilerParams(vmem_limit_bytes=32 * MIB),
-        cost_estimate=pl.CostEstimate(
-            flops=2 * IMAG * NY * rows * UNITS * width,
-            bytes_accessed=IMAG * NY * rows * (UNITS + width) * 2 + UNITS * width * 2,
-            transcendentals=0,
-        ),
-        name="gate",
-    )(features, gate)
-
-
-def gru_kernel(deter_ref, w_rec_ref, w_in_ref, f_ref, new_ref, prior_ref, mid_ref):
+def gru_kernel(
+    deter_hbm, w_rec_hbm, w_in_hbm, f_ref, new_ref, prior_hbm, deter_ref, w_rec_ref, w_in_ref, mid_ref, prior_ref, sems
+):
     rows, bw = deter_ref.shape
     part = bw // NY
+    pairs = [(deter_hbm, deter_ref), (w_rec_hbm, w_rec_ref), (w_in_hbm, w_in_ref)]
+    pairs += [(prior_ref.at[:, k], prior_hbm.at[:, k]) for k in range(IMAG)]
+    copies = [pltpu.make_async_copy(src, dst, sems.at[i]) for i, (src, dst) in enumerate(pairs)]
+    for copy in copies[:3]:
+        copy.start()
+    copies[0].wait()
+    copies[1].wait()
     for k in range(IMAG):
         old_ref = deter_ref if k == 0 else mid_ref
         next_ref = new_ref if k == IMAG - 1 else mid_ref
@@ -215,32 +201,42 @@
             before = old[:, q * part : (q + 1) * part].astype(jnp.float32)
             fresh = update * candidate + (1.0 - update) * before
             next_ref[:, q * part : (q + 1) * part] = fresh.astype(jnp.bfloat16)
+        if k == 0:
+            copies[2].wait()
         prior = jnp.dot(next_ref[...], w_in_ref[...], preferred_element_type=jnp.float32).astype(jnp.bfloat16)
         share = prior_ref.shape[2]
         for j in range(prior_ref.shape[0]):
             prior_ref[j, k] = prior[j * share : (j + 1) * share]
+        copies[3 + k].start()
+    for k in range(IMAG):
+        copies[3 + k].wait()
 
 
 def gru_call(deter, w_rec, w_in, sums, tensor_n):
     rows, bw = deter.shape
-    vmem = pl.BlockSpec(memory_space=pltpu.VMEM)
+    hbm, vmem = pl.BlockSpec(memory_space=pltpu.HBM), pl.BlockSpec(memory_space=pltpu.VMEM)
+    prior = (tensor_n, IMAG, rows // tensor_n, w_in.shape[1])
     return pl.pallas_call(
         gru_kernel,
-        in_specs=[vmem] * 4,
-        out_specs=[vmem, vmem],
-        out_shape=[
-            jax.ShapeDtypeStruct((rows, bw), jnp.bfloat16),
-            jax.ShapeDtypeStruct((tensor_n, IMAG, rows // tensor_n, w_in.shape[1]), jnp.bfloat16),
+        in_specs=[hbm] * 3 + [vmem],
+        out_specs=[vmem, hbm],
+        out_shape=[jax.ShapeDtypeStruct((rows, bw), jnp.bfloat16), pltpu.HBM(prior, jnp.bfloat16)],
+        scratch_shapes=[
+            pltpu.VMEM(deter.shape, jnp.bfloat16),
+            pltpu.VMEM(w_rec.shape, jnp.bfloat16),
+            pltpu.VMEM(w_in.shape, jnp.bfloat16),
+            pltpu.VMEM((rows, bw), jnp.bfloat16),
+            pltpu.VMEM(prior, jnp.bfloat16),
+            pltpu.SemaphoreType.DMA((3 + IMAG,)),
         ],
-        scratch_shapes=[pltpu.VMEM((rows, bw), jnp.bfloat16)],
-        compiler_params=pltpu.CompilerParams(vmem_limit_bytes=32 * MIB),
+        compiler_params=pltpu.CompilerParams(vmem_limit_bytes=24 * MIB),
         cost_estimate=pl.CostEstimate(
             flops=2 * IMAG * rows * bw * (3 * bw + w_in.shape[1]),
             bytes_accessed=2 * (w_rec.size + w_in.size) + 24 * rows * bw,
             transcendentals=6 * rows * bw,
         ),
         name="gru",
-    )(deter, w_rec, w_in, sums)
+    )(*[pltpu.with_memory_space_constraint(value, pltpu.HBM) for value in (deter, w_rec, w_in)], sums)
 
 
 def tail_kernel(me_ref, parts_ref, mine_ref, other_ref, picked_ref, var_ref, mask_ref, log_ref):
@@ -250,7 +246,7 @@
     normed = pre * lax.rsqrt(jnp.mean(pre * pre, axis=1, keepdims=True) + EPS)
     hidden = (silu(normed)).astype(jnp.bfloat16)
     rows = hidden.shape[0]
-    cls = lax.broadcasted_iota(jnp.int32, (rows, LANES), 1) % CLASSES
+    cls = lax.broadcasted_iota(jnp.int32, (NX * NC * rows, LANES), 1) % CLASSES
 
     def within(value, combine):
         step = 1
@@ -261,17 +257,21 @@
             step *= 2
         return value
 
-    total = jnp.zeros((rows, LANES), jnp.float32)
     x, core = me_ref[0], me_ref[1]
+    logits, wants = [], []
     for i in range(NX * NC):
         w_ref = mine_ref if i % NC == 0 else other_ref
         piece = lax.rem(x + NX - i // NC, NX) * NC + (core if i % NC == 0 else 1 - core)
         here = pl.ds(pl.multiple_of(piece * LANES, LANES), LANES)
-        logits = jnp.dot(hidden, w_ref[i // NC], preferred_element_type=jnp.float32)
-        powers = jnp.exp(logits - within(logits, jnp.maximum))
-        probs = 0.99 * (powers / within(powers, jnp.add)) + 0.01 / CLASSES
-        want = jnp.dot(picked_ref[...], var_ref[:, here], preferred_element_type=jnp.float32)
-        total = total + jnp.where(cls.astype(jnp.float32) == want, jnp.log(probs), 0.0)
+        logits.append(jnp.dot(hidden, w_ref[i // NC], preferred_element_type=jnp.float32))
+        wants.append(jnp.dot(picked_ref[...], var_ref[:, here], preferred_element_type=jnp.float32))
+    logits, wants = jnp.concatenate(logits, axis=0), jnp.concatenate(wants, axis=0)
+    powers = jnp.exp(logits - within(logits, jnp.maximum))
+    probs = 0.99 * (powers / within(powers, jnp.add)) + 0.01 / CLASSES
+    terms = jnp.where(cls.astype(jnp.float32) == wants, jnp.log(probs), 0.0)
+    total = terms[:rows]
+    for i in range(1, NX * NC):
+        total = total + terms[i * rows : (i + 1) * rows]
     summed = jnp.where(mask_ref[...] > 0, jnp.sum(total, axis=1, keepdims=True), 0.0)
     lanes = lax.broadcasted_iota(jnp.int32, (rows, LANES), 1)
     diagonal = lax.broadcasted_iota(jnp.int32, (rows, LANES), 0) == lanes
@@ -327,7 +327,9 @@
     mine, other = tensor_gather(jnp.concatenate([w_stoch, action_rows], axis=0))
 
     features = features_call(place, came, mine, other)
-    sums = lax.all_to_all(gate_call(features, gate), "dp", 0, 0, axis_index_groups=y_groups(n_dp))
+    total = jnp.dot(features.reshape(-1, UNITS), gate, preferred_element_type=jnp.float32).astype(jnp.bfloat16)
+    total = total.reshape(NY, IMAG, rows, -1)
+    sums = lax.all_to_all(total, "dp", 0, 0, axis_index_groups=y_groups(n_dp))
 
     w_out_late, _ = lax.optimization_barrier((w_prior_out, features))
     out_mine, out_other = tensor_gather(w_out_late)

time: 140 us -> 137 us (0.979)
  local copies, waits for them, and re-layouts: 6.96 us -> 1.14 us
  matrix products: 0 us -> 5.74 us
  Pallas kernels: 25.1 us -> 22.6 us
    unnamed x22 -> x10, local copies, waits for them, and re-layouts: 5.85 us -> 0.02 us
    dot_general x0 -> x1, matrix products: none -> 5.74 us  [body(): jnp.dot(features.reshape(-1, UNITS), gate, preferred_element_type=jnp.flo...]
    pallas_call x3 -> x2, Pallas kernels: 8.03 us -> 5.57 us  [the longest x1 4.54 us: gru_call(): pl.pallas_call(gru_kernel, in_specs=[hbm] * 3 + [vmem], out_specs=[vmem,...]
  transfers between devices with their start and end apart: 12 -> 12, of which waited for: 8 -> 8; matrix products, arithmetic and copies ran while one was open for 1% -> 1% of each run, Pallas kernels for 10% -> 12%
where the time goes in v7:
time: 137 us
  starting transfers between devices  49.7 us (36%)
  waiting for transfers between devices  44.5 us (32%)
  Pallas kernels  22.6 us (16%)
  blocking collectives  10.5 us (8%)
  matrix products  5.74 us (4%)
  other arithmetic  1.54 us (1%)
    ppermute x6, waiting for transfers between devices, x_shift(): return lax.ppermute(value, 'tensor', perm)  23.9 us
    ppermute x6, starting transfers between devices, x_shift(): return lax.ppermute(value, 'tensor', perm)  16.5 us
    all_to_all x1, starting transfers between devices, body(): lax.all_to_all(held, 'dp', 0, 0, axis_index_groups=z_groups(n_dp))  14.9 us
    all_to_all x1, waiting for transfers between devices, body(): lax.all_to_all(partial.reshape(tensor_n, IMAG * share, UNITS), 'tensor',...  14.4 us
    pallas_call x1, Pallas kernels, features_call(): pl.pallas_call(features_kernel, grid=(NY,), in_specs=[pl.BlockSpec(memory...  11.5 us
    all_to_all x1, blocking collectives, body(): came = lax.all_to_all(sent, 'dp', 0, 0, axis_index_groups=y_groups(n_dp))  10.5 us
    ppermute x2, starting transfers between devices, core_swap(): return lax.ppermute(value, 'tensor', perm)  6.79 us
    dot_general x1, matrix products, body(): jnp.dot(features.reshape(-1, UNITS), gate, preferred_element_type=jnp.flo...  5.74 us
  transfers between devices with their start and end apart: 12, of which 8 were waited for; matrix products, arithmetic and copies ran while one was open for 1% of the time, Pallas kernels for 12%

profile of v7, /device:TPU:1, one launch (start us, length us, event | category | flops | bytes accessed | tf_op | source)
XLA Modules:
  0.0 136.6 jit_solution(824928774827009376)
XLA Ops:
  0.6 1.6 %prep.1 = bf16[4,112,256]{2,1,0:T(8,128)(2,1)} custom-call(bf16[16,1536]{1,0:T(8,128)(2,1)} %w_ref.1, s32[32,256]{1,0:T(8,128)} %bitcast.36, s32[2,32,256]{2,1,0:T(8,128)} %bitcast.35, s32[2,256]{1,0:T(2,128)} %actions_ref.1), custom_call_target="tpu_custom_call" | custom-call | bytes 524288 | tf_op jit(solution)/shard_map/prep/pallas_call | solution.py:81
  2.2 10.5 %all_to_all.25.came_ref = bf16[4,112,256]{2,1,0:T(8,128)(2,1)S(1)} all-to-all(bf16[4,112,256]{2,1,0:T(8,128)(2,1)} %prep.1), channel_id=1, replica_groups={{0,8,16,24},{32,40,48,56},{64,72,80,88},{96,104,112,120},{128,136,144,1..., dimensions={0} | all-to-all | bytes 458752 | tf_op jit(solution)/shard_map/all_to_all | solution.py:322
  12.7 1.0 copies.1
  13.8 14.9 %all-to-all-start.1 = ((bf16[16,64,384]{2,1,0:T(8,128)(2,1)}), bf16[16,64,384]{2,1,0:T(8,128)(2,1)S(1)}, u32[]{:S(2)}, u32[]{:S(2)}) async-start(bf16[16,64,384]{2,1,0:T(8,128)(2,1)} %copies.1), calls=%async_computation.1 | async-start | bytes 1572864 | tf_op jit(solution)/shard_map/all_to_all | solution.py:324
  28.8 4.4 %collective-permute-start.2 = (bf16[1152,128]{1,0:T(8,128)(2,1)S(1)}, bf16[1152,128]{1,0:T(8,128)(2,1)S(1)}, u32[]{:S(2)}, u32[]{:S(2)}) collective-permute-start(bf16[1152,128]{1,0:T(8,128)(2,1)S(1)} %get-tuple-element.9), channel_id=1, source_target_pairs={{0,6},{1,7},{2,0},{3,1},{4,2},{5,3},{6,4},{7,5},{8,14},{9,15},{10,... | collective-permute-start | bytes 884744 | tf_op jit(solution)/shard_map/ppermute | solution.py:37
  33.2 2.4 %collective-permute-start.1 = (bf16[1152,128]{1,0:T(8,128)(2,1)S(1)}, bf16[1152,128]{1,0:T(8,128)(2,1)S(1)}, u32[]{:S(2)}, u32[]{:S(2)}) collective-permute-start(bf16[1152,128]{1,0:T(8,128)(2,1)S(1)} %get-tuple-element.9), channel_id=1, source_target_pairs={{0,4},{1,5},{2,6},{3,7},{4,0},{5,1},{6,2},{7,3},{8,12},{9,13},{10,... | collective-permute-start | bytes 884744 | tf_op jit(solution)/shard_map/ppermute | solution.py:37
  35.6 2.5 %collective-permute-start = (bf16[1152,128]{1,0:T(8,128)(2,1)S(1)}, bf16[1152,128]{1,0:T(8,128)(2,1)S(1)}, u32[]{:S(2)}, u32[]{:S(2)}) collective-permute-start(bf16[1152,128]{1,0:T(8,128)(2,1)S(1)} %get-tuple-element.9), channel_id=1, source_target_pairs={{0,2},{1,3},{2,4},{3,5},{4,6},{5,7},{6,0},{7,1},{8,10},{9,11},{10,... | collective-permute-start | bytes 884744 | tf_op jit(solution)/shard_map/ppermute | solution.py:37
  38.2 4.3 %collective-permute-done.1 = bf16[1152,128]{1,0:T(8,128)(2,1)S(1)} collective-permute-done((bf16[1152,128]{1,0:T(8,128)(2,1)S(1)}, bf16[1152,128]{1,0:T(8,128)(2,1)S(1)}, u32[]{:S(2)}, u32[]{:S(2)}) %collective-permute-start.1) | collective-permute-done | bytes 294944 | tf_op jit(solution)/shard_map/ppermute | solution.py:37
  42.4 8.2 %collective-permute-done = bf16[1152,128]{1,0:T(8,128)(2,1)S(1)} collective-permute-done((bf16[1152,128]{1,0:T(8,128)(2,1)S(1)}, bf16[1152,128]{1,0:T(8,128)(2,1)S(1)}, u32[]{:S(2)}, u32[]{:S(2)}) %collective-permute-start) | collective-permute-done | bytes 294944 | tf_op jit(solution)/shard_map/ppermute | solution.py:37
  50.7 0.1 pad_maximum_fusion.mine_ref
  50.8 3.6 %collective-permute-start.3 = (bf16[4,1152,128]{2,1,0:T(8,128)(2,1)S(1)}, bf16[4,1152,128]{2,1,0:T(8,128)(2,1)S(1)}, u32[]{:S(2)}, u32[]{:S(2)}) collective-permute-start(bf16[4,1152,128]{2,1,0:T(8,128)(2,1)S(1)} %pad_maximum_fusion.mine_ref), channel_id=1, source_target_pairs={{0,1},{1,0},{2,3},{3,2},{4,5},{5,4},{6,7},{7,6},{8,9},{9,8},{10,11... | collective-permute-start | bytes 3538952 | tf_op jit(solution)/shard_map/ppermute | solution.py:42
  54.6 2.3 %collective-permute-done.3.other_ref = bf16[4,1152,128]{2,1,0:T(8,128)(2,1)S(1)} collective-permute-done((bf16[4,1152,128]{2,1,0:T(8,128)(2,1)S(1)}, bf16[4,1152,128]{2,1,0:T(8,128)(2,1)S(1)}, u32[]{:S(2)}, u32[]{:S(2)}) %collective-permute-start.3) | collective-permute-done | bytes 1179680 | tf_op jit(solution)/shard_map/ppermute | solution.py:42
  56.8 11.5 %features.1 = bf16[4,2,256,1024]{3,2,1,0:T(8,128)(2,1)} custom-call(s32[2]{0:T(128)S(1)} %pad_add_fusion.1.place_ref.me_ref, bf16[4,112,256]{2,1,0:T(8,128)(2,1)S(1)} %all_to_all.25.came_ref, bf16[80,2304]{1,0:T(8,128)(2,1)S(1)} %fusion.spread_ref, f32[1,1152]{1,0:T(1,128)S(1)} %fusion.10.target_ref, bf16[4,1152,128]{2,1,0:T(8,128)(2,1)S(1)} %pad_maximum_fusion.mine_ref, ...), custom_call_target="tpu_custom_call" | custom-call | flops 5435817984 | bytes 6553600 | tf_op jit(solution)/shard_map/features/pallas_call | solution.py:151
  68.3 5.7 %convolution_convert_fusion = bf16[2048,384]{1,0:T(8,128)(2,1)} fusion(bf16[2048,1024]{1,0:T(8,128)(2,1)} %bitcast.39, bf16[1024,384]{1,0:T(8,128)(2,1)S(1)} %bitcast.27), kind=kOutput, calls=%fused_computation | convolution fusion | flops 1611399168 | bytes 6553600 | tf_op jit(solution)/shard_map/dot_general | solution.py:330
  74.1 3.7 %all-to-all-start.2 = ((bf16[4,2,256,384]{3,2,1,0:T(8,128)(2,1)}), bf16[4,2,256,384]{3,2,1,0:T(8,128)(2,1)S(1)}, u32[]{:S(2)}, u32[]{:S(2)}) async-start(bf16[4,2,256,384]{3,2,1,0:T(8,128)(2,1)} %bitcast.25), calls=%async_computation.2 | async-start | bytes 3145728 | tf_op jit(solution)/shard_map/all_to_all | solution.py:332
  77.8 2.2 %collective-permute-start.6 = (bf16[1024,128]{1,0:T(8,128)(2,1)S(1)}, bf16[1024,128]{1,0:T(8,128)(2,1)S(1)}, u32[]{:S(2)}, u32[]{:S(2)}) collective-permute-start(bf16[1024,128]{1,0:T(8,128)(2,1)S(1)} %copy-done.1), channel_id=1, source_target_pairs={{0,6},{1,7},{2,0},{3,1},{4,2},{5,3},{6,4},{7,5},{8,14},{9,15},{10,... | collective-permute-start | bytes 786440 | tf_op jit(solution)/shard_map/ppermute | solution.py:37
  80.0 2.4 %collective-permute-start.5 = (bf16[1024,128]{1,0:T(8,128)(2,1)S(1)}, bf16[1024,128]{1,0:T(8,128)(2,1)S(1)}, u32[]{:S(2)}, u32[]{:S(2)}) collective-permute-start(bf16[1024,128]{1,0:T(8,128)(2,1)S(1)} %copy-done.1), channel_id=1, source_target_pairs={{0,4},{1,5},{2,6},{3,7},{4,0},{5,1},{6,2},{7,3},{8,12},{9,13},{10,... | collective-permute-start | bytes 786440 | tf_op jit(solution)/shard_map/ppermute | solution.py:37
  82.4 2.6 %collective-permute-start.4 = (bf16[1024,128]{1,0:T(8,128)(2,1)S(1)}, bf16[1024,128]{1,0:T(8,128)(2,1)S(1)}, u32[]{:S(2)}, u32[]{:S(2)}) collective-permute-start(bf16[1024,128]{1,0:T(8,128)(2,1)S(1)} %copy-done.1), channel_id=1, source_target_pairs={{0,2},{1,3},{2,4},{3,5},{4,6},{5,7},{6,0},{7,1},{8,10},{9,11},{10,... | collective-permute-start | bytes 786440 | tf_op jit(solution)/shard_map/ppermute | solution.py:37
  85.0 2.2 %collective-permute-done.6 = bf16[1024,128]{1,0:T(8,128)(2,1)S(1)} collective-permute-done((bf16[1024,128]{1,0:T(8,128)(2,1)S(1)}, bf16[1024,128]{1,0:T(8,128)(2,1)S(1)}, u32[]{:S(2)}, u32[]{:S(2)}) %collective-permute-start.6) | collective-permute-done | bytes 262176 | tf_op jit(solution)/shard_map/ppermute | solution.py:37
  87.2 1.4 %collective-permute-done.5 = bf16[1024,128]{1,0:T(8,128)(2,1)S(1)} collective-permute-done((bf16[1024,128]{1,0:T(8,128)(2,1)S(1)}, bf16[1024,128]{1,0:T(8,128)(2,1)S(1)}, u32[]{:S(2)}, u32[]{:S(2)}) %collective-permute-start.5) | collective-permute-done | bytes 262176 | tf_op jit(solution)/shard_map/ppermute | solution.py:37
  88.6 7.8 %collective-permute-done.4 = bf16[1024,128]{1,0:T(8,128)(2,1)S(1)} collective-permute-done((bf16[1024,128]{1,0:T(8,128)(2,1)S(1)}, bf16[1024,128]{1,0:T(8,128)(2,1)S(1)}, u32[]{:S(2)}, u32[]{:S(2)}) %collective-permute-start.4) | collective-permute-done | bytes 262176 | tf_op jit(solution)/shard_map/ppermute | solution.py:37
  96.4 0.1 pad_maximum_fusion.1.mine_ref
  96.5 3.2 %collective-permute-start.7 = (bf16[4,1024,128]{2,1,0:T(8,128)(2,1)S(1)}, bf16[4,1024,128]{2,1,0:T(8,128)(2,1)}, u32[]{:S(2)}, u32[]{:S(2)}) collective-permute-start(bf16[4,1024,128]{2,1,0:T(8,128)(2,1)S(1)} %pad_maximum_fusion.1.mine_ref), channel_id=1, source_target_pairs={{0,1},{1,0},{2,3},{3,2},{4,5},{5,4},{6,7},{7,6},{8,9},{9,8},{10,11... | collective-permute-start | bytes 3145736 | tf_op jit(solution)/shard_map/ppermute | solution.py:42
  99.8 4.5 %gru.1 = (bf16[256,512]{1,0:T(8,128)(2,1)S(1)}, bf16[8,2,32,1024]{3,2,1,0:T(8,128)(2,1)}) custom-call(bf16[256,512]{1,0:T(8,128)(2,1)} %deter_hbm.1, bf16[512,1536]{1,0:T(8,128)(2,1)} %bitcast.38, bf16[512,1024]{1,0:T(8,128)(2,1)} %w_in_hbm.1, bf16[4,2,256,384]{3,2,1,0:T(8,128)(2,1)S(1)} %all-to-all-done.2.f_ref), custom_call_target="tpu_custom_call" | custom-call | flops 1342177280 | bytes 5767168 | tf_op jit(solution)/shard_map/gru/pallas_call | solution.py:219
  104.3 3.7 %all-to-all-start.3 = ((bf16[8,64,1024]{2,1,0:T(8,128)(2,1)}), bf16[8,64,1024]{2,1,0:T(8,128)(2,1)S(1)}, u32[]{:S(2)}, u32[]{:S(2)}) async-start(bf16[8,64,1024]{2,1,0:T(8,128)(2,1)} %bitcast.26), calls=%async_computation.3 | async-start | bytes 2097152 | tf_op jit(solution)/shard_map/all_to_all | solution.py:345
  108.5 0.1 copy.14.mask_ref
  108.6 14.4 %all-to-all-done.3.parts_ref = bf16[8,64,1024]{2,1,0:T(8,128)(2,1)S(1)} async-done(((bf16[8,64,1024]{2,1,0:T(8,128)(2,1)}), bf16[8,64,1024]{2,1,0:T(8,128)(2,1)S(1)}, u32[]{:S(2)}, u32[]{:S(2)}) %all-to-all-start.3) | async-done | bytes 1048608 | tf_op jit(solution)/shard_map/all_to_all | solution.py:345
  123.1 3.9 %tail.1 = f32[8,8,128]{2,1,0:T(8,128)} custom-call(s32[2]{0:T(128)S(1)} %pad_add_fusion.1.place_ref.me_ref, bf16[8,64,1024]{2,1,0:T(8,128)(2,1)S(1)} %all-to-all-done.3.parts_ref, bf16[4,1024,128]{2,1,0:T(8,128)(2,1)S(1)} %pad_maximum_fusion.1.mine_ref, bf16[4,1024,128]{2,1,0:T(8,128)(2,1)} %collective-permute-done.7.other_ref, bf16[64,32]{1,0:T(8,128)(2,1)S(1)} %bitcast.24, ...), custom_call_target="tpu_custom_call" | custom-call | flops 134217728 | bytes 4194304 | tf_op jit(solution)/shard_map/tail/pallas_call | solution.py:287
  127.0 4.1 %all-to-all-start.4 = ((f32[8,8,128]{2,1,0:T(8,128)}), f32[8,8,128]{2,1,0:T(8,128)S(1)}, u32[]{:S(2)}, u32[]{:S(2)}) async-start(f32[8,8,128]{2,1,0:T(8,128)} %tail.1), calls=%async_computation.4 | async-start | bytes 65536 | tf_op jit(solution)/shard_map/all_to_all | solution.py:347
  131.1 0.8 broadcast_select_fusion
  131.9 3.9 %all-to-all-done.4 = f32[8,8,128]{2,1,0:T(8,128)S(1)} async-done(((f32[8,8,128]{2,1,0:T(8,128)}), f32[8,8,128]{2,1,0:T(8,128)S(1)}, u32[]{:S(2)}, u32[]{:S(2)}) %all-to-all-start.4) | async-done | bytes 32800 | tf_op jit(solution)/shard_map/all_to_all | solution.py:347
  135.9 0.7 reshape.121
  (31 shorter events, 0.8 us)
Async XLA Ops:
  2.2 26.5 %copy-start = (bf16[1024,128]{1,0:T(8,128)(2,1)S(1)}, bf16[1024,128]{1,0:T(8,128)(2,1)}, u32[]{:S(2)}) copy-start(bf16[1024,128]{1,0:T(8,128)(2,1)} %param.16) | copy-start | bytes 786436
  2.2 26.5 %copy-start.3 = (bf16[18,128]{1,0:T(8,128)(2,1)S(1)}, bf16[18,128]{1,0:T(8,128)(2,1)}, u32[]{:S(2)}) copy-start(bf16[18,128]{1,0:T(8,128)(2,1)} %param.17) | copy-start | bytes 13828
  13.8 54.5 %all-to-all-start.1 = ((bf16[16,64,384]{2,1,0:T(8,128)(2,1)}), bf16[16,64,384]{2,1,0:T(8,128)(2,1)S(1)}, u32[]{:S(2)}, u32[]{:S(2)}) async-start(bf16[16,64,384]{2,1,0:T(8,128)(2,1)} %copies.1), calls=%async_computation.1 | async-start | bytes 1572864 | tf_op jit(solution)/shard_map/all_to_all | solution.py:324
  28.8 9.4 %collective-permute-start.2 = (bf16[1152,128]{1,0:T(8,128)(2,1)S(1)}, bf16[1152,128]{1,0:T(8,128)(2,1)S(1)}, u32[]{:S(2)}, u32[]{:S(2)}) collective-permute-start(bf16[1152,128]{1,0:T(8,128)(2,1)S(1)} %get-tuple-element.9), channel_id=1, source_target_pairs={{0,6},{1,7},{2,0},{3,1},{4,2},{5,3},{6,4},{7,5},{8,14},{9,15},{10,... | collective-permute-start | bytes 884744 | tf_op jit(solution)/shard_map/ppermute | solution.py:37
  33.2 9.3 %collective-permute-start.1 = (bf16[1152,128]{1,0:T(8,128)(2,1)S(1)}, bf16[1152,128]{1,0:T(8,128)(2,1)S(1)}, u32[]{:S(2)}, u32[]{:S(2)}) collective-permute-start(bf16[1152,128]{1,0:T(8,128)(2,1)S(1)} %get-tuple-element.9), channel_id=1, source_target_pairs={{0,4},{1,5},{2,6},{3,7},{4,0},{5,1},{6,2},{7,3},{8,12},{9,13},{10,... | collective-permute-start | bytes 884744 | tf_op jit(solution)/shard_map/ppermute | solution.py:37
  35.6 15.0 %collective-permute-start = (bf16[1152,128]{1,0:T(8,128)(2,1)S(1)}, bf16[1152,128]{1,0:T(8,128)(2,1)S(1)}, u32[]{:S(2)}, u32[]{:S(2)}) collective-permute-start(bf16[1152,128]{1,0:T(8,128)(2,1)S(1)} %get-tuple-element.9), channel_id=1, source_target_pairs={{0,2},{1,3},{2,4},{3,5},{4,6},{5,7},{6,0},{7,1},{8,10},{9,11},{10,... | collective-permute-start | bytes 884744 | tf_op jit(solution)/shard_map/ppermute | solution.py:37
  50.8 6.0 %collective-permute-start.3 = (bf16[4,1152,128]{2,1,0:T(8,128)(2,1)S(1)}, bf16[4,1152,128]{2,1,0:T(8,128)(2,1)S(1)}, u32[]{:S(2)}, u32[]{:S(2)}) collective-permute-start(bf16[4,1152,128]{2,1,0:T(8,128)(2,1)S(1)} %pad_maximum_fusion.mine_ref), channel_id=1, source_target_pairs={{0,1},{1,0},{2,3},{3,2},{4,5},{5,4},{6,7},{7,6},{8,9},{9,8},{10,11... | collective-permute-start | bytes 3538952 | tf_op jit(solution)/shard_map/ppermute | solution.py:42
  74.1 3.7 %copy-start.1 = (bf16[1024,128]{1,0:T(8,128)(2,1)S(1)}, bf16[1024,128]{1,0:T(8,128)(2,1)}, u32[]{:S(2)}) copy-start(bf16[1024,128]{1,0:T(8,128)(2,1)} %param.21) | copy-start | bytes 786436
  74.1 25.7 %all-to-all-start.2 = ((bf16[4,2,256,384]{3,2,1,0:T(8,128)(2,1)}), bf16[4,2,256,384]{3,2,1,0:T(8,128)(2,1)S(1)}, u32[]{:S(2)}, u32[]{:S(2)}) async-start(bf16[4,2,256,384]{3,2,1,0:T(8,128)(2,1)} %bitcast.25), calls=%async_computation.2 | async-start | bytes 3145728 | tf_op jit(solution)/shard_map/all_to_all | solution.py:332
  77.8 9.4 %collective-permute-start.6 = (bf16[1024,128]{1,0:T(8,128)(2,1)S(1)}, bf16[1024,128]{1,0:T(8,128)(2,1)S(1)}, u32[]{:S(2)}, u32[]{:S(2)}) collective-permute-start(bf16[1024,128]{1,0:T(8,128)(2,1)S(1)} %copy-done.1), channel_id=1, source_target_pairs={{0,6},{1,7},{2,0},{3,1},{4,2},{5,3},{6,4},{7,5},{8,14},{9,15},{10,... | collective-permute-start | bytes 786440 | tf_op jit(solution)/shard_map/ppermute | solution.py:37
  80.0 8.6 %collective-permute-start.5 = (bf16[1024,128]{1,0:T(8,128)(2,1)S(1)}, bf16[1024,128]{1,0:T(8,128)(2,1)S(1)}, u32[]{:S(2)}, u32[]{:S(2)}) collective-permute-start(bf16[1024,128]{1,0:T(8,128)(2,1)S(1)} %copy-done.1), channel_id=1, source_target_pairs={{0,4},{1,5},{2,6},{3,7},{4,0},{5,1},{6,2},{7,3},{8,12},{9,13},{10,... | collective-permute-start | bytes 786440 | tf_op jit(solution)/shard_map/ppermute | solution.py:37
  82.4 14.0 %collective-permute-start.4 = (bf16[1024,128]{1,0:T(8,128)(2,1)S(1)}, bf16[1024,128]{1,0:T(8,128)(2,1)S(1)}, u32[]{:S(2)}, u32[]{:S(2)}) collective-permute-start(bf16[1024,128]{1,0:T(8,128)(2,1)S(1)} %copy-done.1), channel_id=1, source_target_pairs={{0,2},{1,3},{2,4},{3,5},{4,6},{5,7},{6,0},{7,1},{8,10},{9,11},{10,... | collective-permute-start | bytes 786440 | tf_op jit(solution)/shard_map/ppermute | solution.py:37
  96.5 12.1 %collective-permute-start.7 = (bf16[4,1024,128]{2,1,0:T(8,128)(2,1)S(1)}, bf16[4,1024,128]{2,1,0:T(8,128)(2,1)}, u32[]{:S(2)}, u32[]{:S(2)}) collective-permute-start(bf16[4,1024,128]{2,1,0:T(8,128)(2,1)S(1)} %pad_maximum_fusion.1.mine_ref), channel_id=1, source_target_pairs={{0,1},{1,0},{2,3},{3,2},{4,5},{5,4},{6,7},{7,6},{8,9},{9,8},{10,11... | collective-permute-start | bytes 3145736 | tf_op jit(solution)/shard_map/ppermute | solution.py:42
  104.3 3.7 %copy-start.4 = (s32[4]{0:T(128)S(1)}, s32[4]{0:T(128)}, u32[]{:S(2)}) copy-start(s32[4]{0:T(128)} %param.15) | copy-start | bytes 52
  104.3 3.8 %copy-start.2 = (s32[2,256,32]{1,2,0:T(8,128)S(1)}, s32[2,256,32]{1,2,0:T(8,128)}, u32[]{:S(2)}) copy-start(s32[2,256,32]{1,2,0:T(8,128)} %param.13) | copy-start | bytes 196612
  104.3 18.7 %all-to-all-start.3 = ((bf16[8,64,1024]{2,1,0:T(8,128)(2,1)}), bf16[8,64,1024]{2,1,0:T(8,128)(2,1)S(1)}, u32[]{:S(2)}, u32[]{:S(2)}) async-start(bf16[8,64,1024]{2,1,0:T(8,128)(2,1)} %bitcast.26), calls=%async_computation.3 | async-start | bytes 2097152 | tf_op jit(solution)/shard_map/all_to_all | solution.py:345
  127.0 8.8 %all-to-all-start.4 = ((f32[8,8,128]{2,1,0:T(8,128)}), f32[8,8,128]{2,1,0:T(8,128)S(1)}, u32[]{:S(2)}, u32[]{:S(2)}) async-start(f32[8,8,128]{2,1,0:T(8,128)} %tail.1), calls=%async_computation.4 | async-start | bytes 65536 | tf_op jit(solution)/shard_map/all_to_all | solution.py:347

commit v8 on v6

--- a/solution.py
+++ b/solution.py
@@ -40,25 +40,26 @@
     return [[(far * NEAR + near) * NY + y for near in range(NEAR)] for far in range(n_far) for y in range(NY)]
 
 
-def diagonal_gather(value, n_dp):
-    places = [(z, y, x, core) for z in range(n_dp // NY) for y in range(NY) for x in range(NX) for core in range(NC)]
-
+def step_perm(n_dp, along_y, steps):
     def index(z, y, x, core):
         return ((z * NY + y) * NX + x) * NC + core
 
-    pieces = [value]
-    for step in range(1, NX):
-        perm = [(index(*p), index(p[0], (p[1] + step) % NY, (p[2] + step) % NX, p[3])) for p in places]
-        pieces.append(lax.ppermute(value, ("dp", "tensor"), perm))
-    return jnp.stack(pieces)
-
-
-def x_gather(value):
-    pieces = [value]
-    for step in range(1, NX):
-        perm = [(i, (i + step * NC) % (NX * NC)) for i in range(NX * NC)]
-        pieces.append(lax.ppermute(value, "tensor", perm))
-    return jnp.stack(pieces)
+    return [
+        (index(z, y, x, core), index(z, (y + along_y * steps[core]) % NY, (x + steps[core]) % NX, core))
+        for z in range(n_dp // NY)
+        for y in range(NY)
+        for x in range(NX)
+        for core in range(NC)
+    ]
+
+
+def ring_gather(value, n_dp, along_y):
+    axes = ("dp", "tensor")
+    behind = lax.ppermute(value, axes, step_perm(n_dp, along_y, (1, 1)))
+    ahead = lax.ppermute(value, axes, step_perm(n_dp, along_y, (-1, -1)))
+    passed = jnp.where(lax.axis_index("tensor") % NC == 0, behind, ahead)
+    across = lax.ppermute(passed, axes, step_perm(n_dp, along_y, (1, -1)))
+    return jnp.stack([value, behind, across, ahead])
 
 
 def core_swap(value):
@@ -224,16 +225,14 @@
 
 
 def gru_kernel(
-    deter_hbm, w_rec_hbm, w_in_hbm, f_hbm, new_ref, prior_hbm, deter_ref, w_rec_ref, w_in_ref, f_ref, mid_ref, prior_ref, sems
+    deter_hbm, w_rec_hbm, w_in_hbm, f_ref, new_ref, prior_hbm, deter_ref, w_rec_ref, w_in_ref, mid_ref, prior_ref, sems
 ):
     rows, bw = deter_ref.shape
     part = bw // NY
-    pairs = [(deter_hbm, deter_ref), (w_rec_hbm, w_rec_ref)]
-    pairs += [(f_hbm.at[:, k], f_ref.at[:, k]) for k in range(IMAG)]
-    pairs += [(w_in_hbm, w_in_ref)]
+    pairs = [(deter_hbm, deter_ref), (w_rec_hbm, w_rec_ref), (w_in_hbm, w_in_ref)]
     pairs += [(prior_ref.at[:, k], prior_hbm.at[:, k]) for k in range(IMAG)]
     copies = [pltpu.make_async_copy(src, dst, sems.at[i]) for i, (src, dst) in enumerate(pairs)]
-    for copy in copies[: 3 + IMAG]:
+    for copy in copies[:3]:
         copy.start()
     copies[0].wait()
     copies[1].wait()
@@ -242,7 +241,6 @@
         next_ref = new_ref if k == IMAG - 1 else mid_ref
         old = old_ref[...]
         rec = jnp.dot(old, w_rec_ref[...], preferred_element_type=jnp.float32)
-        copies[2 + k].wait()
         for q in range(NY):
 
             def gate(which):
@@ -256,73 +254,56 @@
             fresh = update * candidate + (1.0 - update) * before
             next_ref[:, q * part : (q + 1) * part] = fresh.astype(jnp.bfloat16)
         if k == 0:
-            copies[2 + IMAG].wait()
+            copies[2].wait()
         prior = jnp.dot(next_ref[...], w_in_ref[...], preferred_element_type=jnp.float32).astype(jnp.bfloat16)
         share = prior_ref.shape[2]
         for j in range(prior_ref.shape[0]):
             prior_ref[j, k] = prior[j * share : (j + 1) * share]
-        copies[3 + IMAG + k].start()
-    for k in range(IMAG):
-        copies[3 + IMAG + k].wait()
+        copies[3 + k].start()
+    for k in range(IMAG):
+        copies[3 + k].wait()
 
 
 def gru_call(deter, w_rec, w_in, sums, tensor_n):
     rows, bw = deter.shape
-    hbm = pl.BlockSpec(memory_space=pl.ANY)
+    hbm, vmem = pl.BlockSpec(memory_space=pltpu.HBM), pl.BlockSpec(memory_space=pltpu.VMEM)
     prior = (tensor_n, IMAG, rows // tensor_n, w_in.shape[1])
     return pl.pallas_call(
         gru_kernel,
-        in_specs=[hbm] * 4,
-        out_specs=[pl.BlockSpec(memory_space=pltpu.VMEM), hbm],
-        out_shape=[jax.ShapeDtypeStruct((rows, bw), jnp.bfloat16), jax.ShapeDtypeStruct(prior, jnp.bfloat16)],
+        in_specs=[hbm] * 3 + [vmem],
+        out_specs=[vmem, hbm],
+        out_shape=[jax.ShapeDtypeStruct((rows, bw), jnp.bfloat16), pltpu.HBM(prior, jnp.bfloat16)],
         scratch_shapes=[
             pltpu.VMEM(deter.shape, jnp.bfloat16),
             pltpu.VMEM(w_rec.shape, jnp.bfloat16),
             pltpu.VMEM(w_in.shape, jnp.bfloat16),
-            pltpu.VMEM(sums.shape, jnp.bfloat16),
             pltpu.VMEM((rows, bw), jnp.bfloat16),
             pltpu.VMEM(prior, jnp.bfloat16),
-            pltpu.SemaphoreType.DMA((3 + 2 * IMAG,)),
+            pltpu.SemaphoreType.DMA((3 + IMAG,)),
         ],
-        compiler_params=pltpu.CompilerParams(vmem_limit_bytes=60 * MIB),
+        compiler_params=pltpu.CompilerParams(vmem_limit_bytes=24 * MIB),
         cost_estimate=pl.CostEstimate(
             flops=2 * IMAG * rows * bw * (3 * bw + w_in.shape[1]),
             bytes_accessed=2 * (w_rec.size + w_in.size) + 24 * rows * bw,
             transcendentals=6 * rows * bw,
         ),
         name="gru",
-    )(deter, w_rec, w_in, sums)
-
-
-def assemble_kernel(place_ref, mine_ref, other_ref, out_ref):
-    x, core = place_ref[0], place_ref[1]
-    for i in range(NX):
-        base = lax.rem(x + NX - i, NX) * NC
-        out_ref[:, pl.ds(pl.multiple_of((base + core) * LANES, LANES), LANES)] = mine_ref[i]
-        out_ref[:, pl.ds(pl.multiple_of((base + 1 - core) * LANES, LANES), LANES)] = other_ref[i]
-
-
-def assemble_call(place, mine, other):
-    vmem = pl.BlockSpec(memory_space=pltpu.VMEM)
-    return pl.pallas_call(
-        assemble_kernel,
-        in_specs=[pl.BlockSpec(memory_space=pltpu.SMEM), vmem, vmem],
-        out_specs=vmem,
-        out_shape=jax.ShapeDtypeStruct((mine.shape[1], NX * NC * LANES), jnp.bfloat16),
-        compiler_params=pltpu.CompilerParams(vmem_limit_bytes=16 * MIB),
-        cost_estimate=pl.CostEstimate(flops=0, bytes_accessed=8 * mine.size, transcendentals=0),
-        name="assemble",
-    )(place, mine, other)
-
-
-def tail_kernel(parts_ref, w_out_ref, picked_ref, var_ref, mask_ref, log_ref):
+    )(*[pltpu.with_memory_space_constraint(value, pltpu.HBM) for value in (deter, w_rec, w_in)], sums)
+
+
+def tail_kernel(me_ref, parts_ref, mine_hbm, other_hbm, picked_ref, var_ref, mask_ref, log_ref, w_ref, sems):
+    copies = []
+    for i in range(NX * NC):
+        source = mine_hbm if i % NC == 0 else other_hbm
+        copies.append(pltpu.make_async_copy(source.at[i // NC], w_ref.at[i], sems.at[i]))
+        copies[i].start()
     pre = parts_ref[0].astype(jnp.float32)
     for i in range(1, parts_ref.shape[0]):
         pre = pre + parts_ref[i].astype(jnp.float32)
     normed = pre * lax.rsqrt(jnp.mean(pre * pre, axis=1, keepdims=True) + EPS)
     hidden = (silu(normed)).astype(jnp.bfloat16)
     rows = hidden.shape[0]
-    cls = lax.broadcasted_iota(jnp.int32, (rows, LANES), 1) % CLASSES
+    cls = lax.broadcasted_iota(jnp.int32, (NX * NC * rows, LANES), 1) % CLASSES
 
     def within(value, combine):
         step = 1
@@ -333,15 +314,21 @@
             step *= 2
         return value
 
-    total = jnp.zeros((rows, LANES), jnp.float32)
-    every = jnp.dot(hidden, w_out_ref[...], preferred_element_type=jnp.float32)
-    wants = jnp.dot(picked_ref[...], var_ref[...], preferred_element_type=jnp.float32)
-    for start in range(0, LAT, LANES):
-        logits = every[:, start : start + LANES]
-        powers = jnp.exp(logits - within(logits, jnp.maximum))
-        probs = 0.99 * (powers / within(powers, jnp.add)) + 0.01 / CLASSES
-        want = wants[:, start : start + LANES]
-        total = total + jnp.where(cls.astype(jnp.float32) == want, jnp.log(probs), 0.0)
+    x, core = me_ref[0], me_ref[1]
+    logits, wants = [], []
+    for i in range(NX * NC):
+        piece = lax.rem(x + NX - i // NC, NX) * NC + (core if i % NC == 0 else 1 - core)
+        here = pl.ds(pl.multiple_of(piece * LANES, LANES), LANES)
+        copies[i].wait()
+        logits.append(jnp.dot(hidden, w_ref[i], preferred_element_type=jnp.float32))
+        wants.append(jnp.dot(picked_ref[...], var_ref[:, here], preferred_element_type=jnp.float32))
+    logits, wants = jnp.concatenate(logits, axis=0), jnp.concatenate(wants, axis=0)
+    powers = jnp.exp(logits - within(logits, jnp.maximum))
+    probs = 0.99 * (powers / within(powers, jnp.add)) + 0.01 / CLASSES
+    terms = jnp.where(cls.astype(jnp.float32) == wants, jnp.log(probs), 0.0)
+    total = terms[:rows]
+    for i in range(1, NX * NC):
+        total = total + terms[i * rows : (i + 1) * rows]
     summed = jnp.where(mask_ref[...] > 0, jnp.sum(total, axis=1, keepdims=True), 0.0)
     lanes = lax.broadcasted_iota(jnp.int32, (rows, LANES), 1)
     diagonal = lax.broadcasted_iota(jnp.int32, (rows, LANES), 0) == lanes
@@ -349,22 +336,24 @@
     log_ref[...] = jnp.broadcast_to(line[None], log_ref.shape)
 
 
-def tail_call(parts, w_out, picked, mask):
+def tail_call(place, parts, mine, other, picked, mask):
     tensor_n, rows = parts.shape[:2]
     lane = jnp.arange(LAT, dtype=jnp.int32)
     var_of = (jnp.arange(STOCH, dtype=jnp.int32)[:, None] == lane[None, :] // CLASSES).astype(jnp.bfloat16)
-    vmem = pl.BlockSpec(memory_space=pltpu.VMEM)
+    vmem, hbm = pl.BlockSpec(memory_space=pltpu.VMEM), pl.BlockSpec(memory_space=pltpu.HBM)
+    mine, other = [pltpu.with_memory_space_constraint(value, pltpu.HBM) for value in (mine, other)]
     return pl.pallas_call(
         tail_kernel,
-        in_specs=[vmem] * 5,
+        in_specs=[pl.BlockSpec(memory_space=pltpu.SMEM), vmem, hbm, hbm, vmem, vmem, vmem],
         out_specs=vmem,
         out_shape=jax.ShapeDtypeStruct((tensor_n, 8, LANES), jnp.float32),
+        scratch_shapes=[pltpu.VMEM((NX * NC,) + mine.shape[1:], jnp.bfloat16), pltpu.SemaphoreType.DMA((NX * NC,))],
         compiler_params=pltpu.CompilerParams(vmem_limit_bytes=32 * MIB),
         cost_estimate=pl.CostEstimate(
-            flops=2 * rows * UNITS * LAT, bytes_accessed=2 * w_out.size, transcendentals=4 * rows * LAT
+            flops=2 * rows * UNITS * LAT, bytes_accessed=8 * mine.size, transcendentals=4 * rows * LAT
         ),
         name="tail",
-    )(parts, w_out, picked, var_of, mask)
+    )(place, parts, mine, other, picked, var_of, mask)
 
 
 def body(
@@ -394,13 +383,13 @@
     gate = jnp.broadcast_to(held[None], (NEAR,) + held.shape)
     gate = lax.all_to_all(gate, "dp", 0, 0, axis_index_groups=near_groups(n_dp))
 
-    mine = diagonal_gather(prep_call(w_stoch, w_action, post_sample.T, samples.transpose(0, 2, 1), actions), n_dp)
+    mine = ring_gather(prep_call(w_stoch, w_action, post_sample.T, samples.transpose(0, 2, 1), actions), n_dp, 1)
     other = core_swap(mine)
     features = features_call(rows, place, mine, other)
     sums = lax.all_to_all(gate_call(features, gate, n_far), "dp", 0, 0, axis_index_groups=y_groups(n_dp))
 
     w_out_late, _ = lax.optimization_barrier((w_prior_out, features))
-    out_mine = x_gather(w_out_late)
+    out_mine = ring_gather(w_out_late, n_dp, 0)
     out_other = core_swap(out_mine)
 
     positions = jnp.arange(STEPS, dtype=jnp.int32)
@@ -412,7 +401,7 @@
 
     deter, partial = gru_call(post_deter, w_rec[0], w_prior_in, sums, tensor_n)
     parts = lax.all_to_all(partial.reshape(tensor_n, IMAG * share, UNITS), "tensor", 0, 0)
-    logs = tail_call(parts, assemble_call(place, out_mine, out_other), picked, my_mask)
+    logs = tail_call(place, parts, out_mine, out_other, picked, my_mask)
     logs = lax.all_to_all(logs, "tensor", 0, 0)[:, 0, : IMAG * share]
     log_prob = logs.reshape(tensor_n, IMAG, share).transpose(1, 0, 2).reshape(IMAG, rows)
     deter_out = jnp.where(valid_mask[:, None], deter, jnp.zeros_like(deter))

time: 145 us -> 149 us (1.028)
  starting transfers between devices: 67.1 us -> 72.6 us
  waiting for transfers between devices: 37.5 us -> 40.2 us
  local copies, waits for them, and re-layouts: 6.48 us -> 4.27 us
  Pallas kernels: 30.6 us -> 28.6 us
    ppermute x6, waiting for transfers between devices: 19.2 us -> 12.2 us  [the longest x2 5.19 us: ring_gather(): across = lax.ppermute(passed, axes, step_perm(n_dp, along_y, (1, -1)))]
    all_to_all x1, waiting for transfers between devices: 0.59 us -> 7.13 us  [body(): lax.all_to_all(sent, 'dp', 0, 0, axis_index_groups=far_groups(n_dp))]
    ppermute x2, starting transfers between devices: 6.04 us -> 12 us  [core_swap(): return lax.ppermute(value, 'tensor', perm)]
    ppermute x6, starting transfers between devices: 23.2 us -> 27 us  [the longest x2 13.3 us: ring_gather(): ahead = lax.ppermute(value, axes, step_perm(n_dp, along_y, (-1, -1)))]
    all_to_all x1, waiting for transfers between devices: 11.2 us -> 14.4 us  [body(): lax.all_to_all(partial.reshape(tensor_n, IMAG * share, UNITS), 'tensor',...]
    all_to_all x1, starting transfers between devices: 18.4 us -> 16 us  [body(): lax.all_to_all(sent, 'dp', 0, 0, axis_index_groups=far_groups(n_dp))]
    unnamed x16 -> x12, local copies, waits for them, and re-layouts: 4.41 us -> 2.21 us
    pallas_call x3 -> x2, Pallas kernels: 11 us -> 9.79 us  [the longest x1 5.27 us: tail_call(): pl.pallas_call(tail_kernel, in_specs=[pl.BlockSpec(memory_space=pltpu.SME...]
  transfers between devices with their start and end apart: 13 -> 13, of which waited for: 9 -> 8; matrix products, arithmetic and copies ran while one was open for 2% -> 2% of each run, Pallas kernels for 15% -> 12%
where the time goes in v8:
time: 149 us; the launch traced here: 148 us
  starting transfers between devices  72.6 us (49%)
  waiting for transfers between devices  40.2 us (27%)
  Pallas kernels  28.6 us (19%)
  local copies, waits for them, and re-layouts  4.27 us (3%)
  other arithmetic  1.6 us (1%)
    all_to_all x1, starting transfers between devices, body(): lax.all_to_all(sent, 'dp', 0, 0, axis_index_groups=far_groups(n_dp))  16 us
    all_to_all x1, waiting for transfers between devices, body(): lax.all_to_all(partial.reshape(tensor_n, IMAG * share, UNITS), 'tensor',...  14.4 us
    ppermute x2, starting transfers between devices, ring_gather(): ahead = lax.ppermute(value, axes, step_perm(n_dp, along_y, (-1, -1)))  13.3 us
    ppermute x2, starting transfers between devices, core_swap(): return lax.ppermute(value, 'tensor', perm)  12 us
    pallas_call x1, Pallas kernels, features_call(): pl.pallas_call(features_kernel, grid=(NY,), in_specs=[pl.BlockSpec(memory...  11.6 us
    ppermute x2, starting transfers between devices, ring_gather(): across = lax.ppermute(passed, axes, step_perm(n_dp, along_y, (1, -1)))  9.92 us
    all_to_all x1, waiting for transfers between devices, body(): lax.all_to_all(sent, 'dp', 0, 0, axis_index_groups=far_groups(n_dp))  7.13 us
    all_to_all x1, starting transfers between devices, body(): gate = lax.all_to_all(gate, 'dp', 0, 0, axis_index_groups=near_groups(n_dp))  6.08 us
  transfers between devices with their start and end apart: 13, of which 8 were waited for; matrix products, arithmetic and copies ran while one was open for 2% of the time, Pallas kernels for 12%

profile of v8, /device:TPU:1, one launch (start us, length us, event | category | flops | bytes accessed | tf_op | source)
XLA Modules:
  0.0 148.2 jit_solution(13818833805011332371)
XLA Ops:
  0.6 1.8 %prep.1 = bf16[1312,128]{1,0:T(8,128)(2,1)} custom-call(bf16[1024,128]{1,0:T(8,128)(2,1)} %w_stoch_ref.1, bf16[18,128]{1,0:T(8,128)(2,1)} %w_action_ref.1, s32[32,256]{1,0:T(8,128)} %bitcast.34, s32[2,32,256]{2,1,0:T(8,128)} %bitcast.33, s32[2,256]{1,0:T(2,128)} %actions_ref.1), custom_call_target="tpu_custom_call" | custom-call | bytes 589824 | tf_op jit(solution)/shard_map/prep/pallas_call | solution.py:120
  2.4 7.7 %collective-permute-start.1 = (bf16[1312,128]{1,0:T(8,128)(2,1)}, bf16[1312,128]{1,0:T(8,128)(2,1)S(1)}, u32[]{:S(2)}, u32[]{:S(2)}) collective-permute-start(bf16[1312,128]{1,0:T(8,128)(2,1)} %prep.1), channel_id=1, source_target_pairs={{0,30},{1,31},{2,24},{3,25},{4,26},{5,27},{6,28},{7,29},{8,6},{9,7... | collective-permute-start | bytes 1007624 | tf_op jit(solution)/shard_map/ppermute | solution.py:59
  10.0 1.9 %collective-permute-start = (bf16[1312,128]{1,0:T(8,128)(2,1)}, bf16[1312,128]{1,0:T(8,128)(2,1)S(1)}, u32[]{:S(2)}, u32[]{:S(2)}) collective-permute-start(bf16[1312,128]{1,0:T(8,128)(2,1)} %prep.1), channel_id=1, source_target_pairs={{0,10},{1,11},{2,12},{3,13},{4,14},{5,15},{6,8},{7,9},{8,18},{9,19... | collective-permute-start | bytes 1007624 | tf_op jit(solution)/shard_map/ppermute | solution.py:58
  12.0 1.5 %split.1 = bf16[4,4,16,384]{3,2,1,0:T(8,128)(2,1)} custom-call(bf16[16,1536]{1,0:T(8,128)(2,1)} %w_ref.1), custom_call_target="tpu_custom_call" | custom-call | bytes 196608 | tf_op jit(solution)/shard_map/split/pallas_call | solution.py:91
  13.5 16.0 %all-to-all-start = ((bf16[16,16,384]{2,1,0:T(8,128)(2,1)}), bf16[16,16,384]{2,1,0:T(8,128)(2,1)S(1)}, u32[]{:S(2)}, u32[]{:S(2)}) async-start(bf16[16,16,384]{2,1,0:T(8,128)(2,1)} %bitcast.28), calls=%async_computation | async-start | bytes 393216 | tf_op jit(solution)/shard_map/all_to_all | solution.py:382
  29.6 8.0 %collective-permute-start.2 = (bf16[1312,128]{1,0:T(8,128)(2,1)S(1)}, bf16[1312,128]{1,0:T(8,128)(2,1)S(1)}, u32[]{:S(2)}, u32[]{:S(2)}) collective-permute-start(bf16[1312,128]{1,0:T(8,128)(2,1)S(1)} %broadcast_select_fusion), channel_id=1, source_target_pairs={{0,10},{1,31},{2,12},{3,25},{4,14},{5,27},{6,8},{7,29},{8,18},{9,7... | collective-permute-start | bytes 1007624 | tf_op jit(solution)/shard_map/ppermute | solution.py:61
  37.6 7.1 %all-to-all-done = bf16[16,16,384]{2,1,0:T(8,128)(2,1)S(1)} async-done(((bf16[16,16,384]{2,1,0:T(8,128)(2,1)}), bf16[16,16,384]{2,1,0:T(8,128)(2,1)S(1)}, u32[]{:S(2)}, u32[]{:S(2)}) %all-to-all-start) | async-done | bytes 196640 | tf_op jit(solution)/shard_map/all_to_all | solution.py:382
  44.7 0.9 broadcast_in_dim.41
  45.7 6.1 %all-to-all-start.1 = ((bf16[4,256,384]{2,1,0:T(8,128)(2,1)}), bf16[4,256,384]{2,1,0:T(8,128)(2,1)S(1)}, u32[]{:S(2)}, u32[]{:S(2)}) async-start(bf16[4,256,384]{2,1,0:T(8,128)(2,1)} %broadcast_in_dim.41), calls=%async_computation.1 | async-start | bytes 1572864 | tf_op jit(solution)/shard_map/all_to_all | solution.py:384
  51.8 0.2 pad_maximum_fusion.mine_ref
  51.9 4.8 %collective-permute-start.3 = (bf16[4,1312,128]{2,1,0:T(8,128)(2,1)S(1)}, bf16[4,1312,128]{2,1,0:T(8,128)(2,1)S(1)}, u32[]{:S(2)}, u32[]{:S(2)}) collective-permute-start(bf16[4,1312,128]{2,1,0:T(8,128)(2,1)S(1)} %pad_maximum_fusion.mine_ref), channel_id=1, source_target_pairs={{0,1},{1,0},{2,3},{3,2},{4,5},{5,4},{6,7},{7,6},{8,9},{9,8},{10,11... | collective-permute-start | bytes 4030472 | tf_op jit(solution)/shard_map/ppermute | solution.py:67
  57.0 2.5 %collective-permute-done.3.other_ref = bf16[4,1312,128]{2,1,0:T(8,128)(2,1)S(1)} collective-permute-done((bf16[4,1312,128]{2,1,0:T(8,128)(2,1)S(1)}, bf16[4,1312,128]{2,1,0:T(8,128)(2,1)S(1)}, u32[]{:S(2)}, u32[]{:S(2)}) %collective-permute-start.3) | collective-permute-done | bytes 1343520 | tf_op jit(solution)/shard_map/ppermute | solution.py:67
  59.5 11.6 %features.1.features_ref = bf16[2,4,256,1024]{3,2,1,0:T(8,128)(2,1)} custom-call(s32[3]{0:T(128)S(1)} %pad_add_fusion.1.place_ref.me_ref, bf16[80,2304]{1,0:T(8,128)(2,1)S(1)} %fusion.spread_ref, f32[1,1152]{1,0:T(1,128)S(1)} %fusion.8.target_ref, bf16[4,1312,128]{2,1,0:T(8,128)(2,1)S(1)} %pad_maximum_fusion.mine_ref, ...), custom_call_target="tpu_custom_call" | custom-call | flops 6522981376 | bytes 6553600 | tf_op jit(solution)/shard_map/features/pallas_call | solution.py:167
  71.1 2.2 %copy-done = bf16[2,4,256,1024]{3,2,1,0:T(8,128)(2,1)S(1)} copy-done((bf16[2,4,256,1024]{3,2,1,0:T(8,128)(2,1)S(1)}, bf16[2,4,256,1024]{3,2,1,0:T(8,128)(2,1)}, u32[]{:S(2)}) %copy-start) | copy-done | bytes 4194328
  73.3 4.0 %gate.1 = bf16[4,2,256,384]{3,2,1,0:T(8,128)(2,1)} custom-call(bf16[2,4,256,1024]{3,2,1,0:T(8,128)(2,1)S(1)} %copy-done, bf16[4,256,384]{2,1,0:T(8,128)(2,1)S(1)} %all-to-all-done.1.gate_ref), custom_call_target="tpu_custom_call" | custom-call | flops 1610612736 | bytes 6553600 | tf_op jit(solution)/shard_map/gate/pallas_call | solution.py:207
  77.2 3.7 %all-to-all-start.2 = ((bf16[4,2,256,384]{3,2,1,0:T(8,128)(2,1)}), bf16[4,2,256,384]{3,2,1,0:T(8,128)(2,1)S(1)}, u32[]{:S(2)}, u32[]{:S(2)}) async-start(bf16[4,2,256,384]{3,2,1,0:T(8,128)(2,1)} %gate.1), calls=%async_computation.2 | async-start | bytes 3145728 | tf_op jit(solution)/shard_map/all_to_all | solution.py:389
  80.9 5.6 %collective-permute-start.5 = (bf16[1024,128]{1,0:T(8,128)(2,1)S(1)}, bf16[1024,128]{1,0:T(8,128)(2,1)S(1)}, u32[]{:S(2)}, u32[]{:S(2)}) collective-permute-start(bf16[1024,128]{1,0:T(8,128)(2,1)S(1)} %copy-done.3), channel_id=1, source_target_pairs={{0,6},{1,7},{2,0},{3,1},{4,2},{5,3},{6,4},{7,5},{8,14},{9,15},{10,... | collective-permute-start | bytes 786440 | tf_op jit(solution)/shard_map/ppermute | solution.py:59
  86.6 1.9 %collective-permute-start.4 = (bf16[1024,128]{1,0:T(8,128)(2,1)S(1)}, bf16[1024,128]{1,0:T(8,128)(2,1)S(1)}, u32[]{:S(2)}, u32[]{:S(2)}) collective-permute-start(bf16[1024,128]{1,0:T(8,128)(2,1)S(1)} %copy-done.3), channel_id=1, source_target_pairs={{0,2},{1,3},{2,4},{3,5},{4,6},{5,7},{6,0},{7,1},{8,10},{9,11},{10,... | collective-permute-start | bytes 786440 | tf_op jit(solution)/shard_map/ppermute | solution.py:58
  88.5 1.9 %collective-permute-done.5 = bf16[1024,128]{1,0:T(8,128)(2,1)S(1)} collective-permute-done((bf16[1024,128]{1,0:T(8,128)(2,1)S(1)}, bf16[1024,128]{1,0:T(8,128)(2,1)S(1)}, u32[]{:S(2)}, u32[]{:S(2)}) %collective-permute-start.5) | collective-permute-done | bytes 262176 | tf_op jit(solution)/shard_map/ppermute | solution.py:59
  90.4 5.0 %collective-permute-done.4 = bf16[1024,128]{1,0:T(8,128)(2,1)S(1)} collective-permute-done((bf16[1024,128]{1,0:T(8,128)(2,1)S(1)}, bf16[1024,128]{1,0:T(8,128)(2,1)S(1)}, u32[]{:S(2)}, u32[]{:S(2)}) %collective-permute-start.4) | collective-permute-done | bytes 262176 | tf_op jit(solution)/shard_map/ppermute | solution.py:58
  95.5 1.9 %collective-permute-start.6 = (bf16[1024,128]{1,0:T(8,128)(2,1)S(1)}, bf16[1024,128]{1,0:T(8,128)(2,1)S(1)}, u32[]{:S(2)}, u32[]{:S(2)}) collective-permute-start(bf16[1024,128]{1,0:T(8,128)(2,1)S(1)} %broadcast_select_fusion.2), channel_id=1, source_target_pairs={{0,2},{1,7},{2,4},{3,1},{4,6},{5,3},{6,0},{7,5},{8,10},{9,15},{10,... | collective-permute-start | bytes 786440 | tf_op jit(solution)/shard_map/ppermute | solution.py:61
  97.4 5.2 %collective-permute-done.6 = bf16[1024,128]{1,0:T(8,128)(2,1)S(1)} collective-permute-done((bf16[1024,128]{1,0:T(8,128)(2,1)S(1)}, bf16[1024,128]{1,0:T(8,128)(2,1)S(1)}, u32[]{:S(2)}, u32[]{:S(2)}) %collective-permute-start.6) | collective-permute-done | bytes 262176 | tf_op jit(solution)/shard_map/ppermute | solution.py:61
  102.6 0.1 pad_maximum_fusion.1.mine_hbm
  102.7 7.2 %collective-permute-start.7 = (bf16[4,1024,128]{2,1,0:T(8,128)(2,1)S(1)}, bf16[4,1024,128]{2,1,0:T(8,128)(2,1)}, u32[]{:S(2)}, u32[]{:S(2)}) collective-permute-start(bf16[4,1024,128]{2,1,0:T(8,128)(2,1)S(1)} %pad_maximum_fusion.1.mine_hbm), channel_id=1, source_target_pairs={{0,1},{1,0},{2,3},{3,2},{4,5},{5,4},{6,7},{7,6},{8,9},{9,8},{10,11... | collective-permute-start | bytes 3145736 | tf_op jit(solution)/shard_map/ppermute | solution.py:67
  110.0 4.5 %gru.1 = (bf16[256,512]{1,0:T(8,128)(2,1)S(1)}, bf16[8,2,32,1024]{3,2,1,0:T(8,128)(2,1)}) custom-call(bf16[256,512]{1,0:T(8,128)(2,1)} %deter_hbm.1, bf16[512,1536]{1,0:T(8,128)(2,1)} %bitcast.36, bf16[512,1024]{1,0:T(8,128)(2,1)} %w_in_hbm.1, bf16[4,2,256,384]{3,2,1,0:T(8,128)(2,1)S(1)} %all-to-all-done.2.f_ref), custom_call_target="tpu_custom_call" | custom-call | flops 1342177280 | bytes 5767168 | tf_op jit(solution)/shard_map/gru/pallas_call | solution.py:271
  114.5 3.7 %all-to-all-start.3 = ((bf16[8,64,1024]{2,1,0:T(8,128)(2,1)}), bf16[8,64,1024]{2,1,0:T(8,128)(2,1)S(1)}, u32[]{:S(2)}, u32[]{:S(2)}) async-start(bf16[8,64,1024]{2,1,0:T(8,128)(2,1)} %bitcast.25), calls=%async_computation.3 | async-start | bytes 2097152 | tf_op jit(solution)/shard_map/all_to_all | solution.py:403
  118.8 14.4 %all-to-all-done.3.parts_ref = bf16[8,64,1024]{2,1,0:T(8,128)(2,1)S(1)} async-done(((bf16[8,64,1024]{2,1,0:T(8,128)(2,1)}), bf16[8,64,1024]{2,1,0:T(8,128)(2,1)S(1)}, u32[]{:S(2)}, u32[]{:S(2)}) %all-to-all-start.3) | async-done | bytes 1048608 | tf_op jit(solution)/shard_map/all_to_all | solution.py:403
  133.3 5.3 %tail.1 = f32[8,8,128]{2,1,0:T(8,128)} custom-call(s32[3]{0:T(128)S(1)} %pad_add_fusion.1.place_ref.me_ref, bf16[8,64,1024]{2,1,0:T(8,128)(2,1)S(1)} %all-to-all-done.3.parts_ref, bf16[4,1024,128]{2,1,0:T(8,128)(2,1)} %copy-done.1, bf16[4,1024,128]{2,1,0:T(8,128)(2,1)} %collective-permute-done.7.other_hbm, bf16[64,32]{1,0:T(8,128)(2,1)S(1)} %bitcast.21, ...), custom_call_target="tpu_custom_call" | custom-call | flops 134217728 | bytes 4194304 | tf_op jit(solution)/shard_map/tail/pallas_call | solution.py:345
  138.5 4.1 %all-to-all-start.4 = ((f32[8,8,128]{2,1,0:T(8,128)}), f32[8,8,128]{2,1,0:T(8,128)S(1)}, u32[]{:S(2)}, u32[]{:S(2)}) async-start(f32[8,8,128]{2,1,0:T(8,128)} %tail.1), calls=%async_computation.4 | async-start | bytes 65536 | tf_op jit(solution)/shard_map/all_to_all | solution.py:405
  142.7 0.8 broadcast_select_fusion.1
  143.5 3.9 %all-to-all-done.4 = f32[8,8,128]{2,1,0:T(8,128)S(1)} async-done(((f32[8,8,128]{2,1,0:T(8,128)}), f32[8,8,128]{2,1,0:T(8,128)S(1)}, u32[]{:S(2)}, u32[]{:S(2)}) %all-to-all-start.4) | async-done | bytes 32800 | tf_op jit(solution)/shard_map/all_to_all | solution.py:405
  147.5 0.7 reshape.114
  (36 shorter events, 1.0 us)
Async XLA Ops:
  2.4 27.1 %collective-permute-start.1 = (bf16[1312,128]{1,0:T(8,128)(2,1)}, bf16[1312,128]{1,0:T(8,128)(2,1)S(1)}, u32[]{:S(2)}, u32[]{:S(2)}) collective-permute-start(bf16[1312,128]{1,0:T(8,128)(2,1)} %prep.1), channel_id=1, source_target_pairs={{0,30},{1,31},{2,24},{3,25},{4,26},{5,27},{6,28},{7,29},{8,6},{9,7... | collective-permute-start | bytes 1007624 | tf_op jit(solution)/shard_map/ppermute | solution.py:59
  10.0 19.5 %collective-permute-start = (bf16[1312,128]{1,0:T(8,128)(2,1)}, bf16[1312,128]{1,0:T(8,128)(2,1)S(1)}, u32[]{:S(2)}, u32[]{:S(2)}) collective-permute-start(bf16[1312,128]{1,0:T(8,128)(2,1)} %prep.1), channel_id=1, source_target_pairs={{0,10},{1,11},{2,12},{3,13},{4,14},{5,15},{6,8},{7,9},{8,18},{9,19... | collective-permute-start | bytes 1007624 | tf_op jit(solution)/shard_map/ppermute | solution.py:58
  13.5 31.2 %all-to-all-start = ((bf16[16,16,384]{2,1,0:T(8,128)(2,1)}), bf16[16,16,384]{2,1,0:T(8,128)(2,1)S(1)}, u32[]{:S(2)}, u32[]{:S(2)}) async-start(bf16[16,16,384]{2,1,0:T(8,128)(2,1)} %bitcast.28), calls=%async_computation | async-start | bytes 393216 | tf_op jit(solution)/shard_map/all_to_all | solution.py:382
  29.6 22.2 %copy-start.2 = (bf16[1312,128]{1,0:T(8,128)(2,1)S(1)}, bf16[1312,128]{1,0:T(8,128)(2,1)}, u32[]{:S(2)}) copy-start(bf16[1312,128]{1,0:T(8,128)(2,1)} %prep.1) | copy-start | bytes 1007620
  29.6 22.2 %collective-permute-start.2 = (bf16[1312,128]{1,0:T(8,128)(2,1)S(1)}, bf16[1312,128]{1,0:T(8,128)(2,1)S(1)}, u32[]{:S(2)}, u32[]{:S(2)}) collective-permute-start(bf16[1312,128]{1,0:T(8,128)(2,1)S(1)} %broadcast_select_fusion), channel_id=1, source_target_pairs={{0,10},{1,31},{2,12},{3,25},{4,14},{5,27},{6,8},{7,29},{8,18},{9,7... | collective-permute-start | bytes 1007624 | tf_op jit(solution)/shard_map/ppermute | solution.py:61
  45.7 25.4 %all-to-all-start.1 = ((bf16[4,256,384]{2,1,0:T(8,128)(2,1)}), bf16[4,256,384]{2,1,0:T(8,128)(2,1)S(1)}, u32[]{:S(2)}, u32[]{:S(2)}) async-start(bf16[4,256,384]{2,1,0:T(8,128)(2,1)} %broadcast_in_dim.41), calls=%async_computation.1 | async-start | bytes 1572864 | tf_op jit(solution)/shard_map/all_to_all | solution.py:384
  51.9 7.5 %collective-permute-start.3 = (bf16[4,1312,128]{2,1,0:T(8,128)(2,1)S(1)}, bf16[4,1312,128]{2,1,0:T(8,128)(2,1)S(1)}, u32[]{:S(2)}, u32[]{:S(2)}) collective-permute-start(bf16[4,1312,128]{2,1,0:T(8,128)(2,1)S(1)} %pad_maximum_fusion.mine_ref), channel_id=1, source_target_pairs={{0,1},{1,0},{2,3},{3,2},{4,5},{5,4},{6,7},{7,6},{8,9},{9,8},{10,11... | collective-permute-start | bytes 4030472 | tf_op jit(solution)/shard_map/ppermute | solution.py:67
  71.1 2.2 %copy-start = (bf16[2,4,256,1024]{3,2,1,0:T(8,128)(2,1)S(1)}, bf16[2,4,256,1024]{3,2,1,0:T(8,128)(2,1)}, u32[]{:S(2)}) copy-start(bf16[2,4,256,1024]{3,2,1,0:T(8,128)(2,1)} %features.1.features_ref) | copy-start | bytes 12582916
  77.2 3.7 %copy-start.3 = (bf16[1024,128]{1,0:T(8,128)(2,1)S(1)}, bf16[1024,128]{1,0:T(8,128)(2,1)}, u32[]{:S(2)}) copy-start(bf16[1024,128]{1,0:T(8,128)(2,1)} %param.21) | copy-start | bytes 786436
  77.2 32.7 %all-to-all-start.2 = ((bf16[4,2,256,384]{3,2,1,0:T(8,128)(2,1)}), bf16[4,2,256,384]{3,2,1,0:T(8,128)(2,1)S(1)}, u32[]{:S(2)}, u32[]{:S(2)}) async-start(bf16[4,2,256,384]{3,2,1,0:T(8,128)(2,1)} %gate.1), calls=%async_computation.2 | async-start | bytes 3145728 | tf_op jit(solution)/shard_map/all_to_all | solution.py:389
  80.9 9.4 %collective-permute-start.5 = (bf16[1024,128]{1,0:T(8,128)(2,1)S(1)}, bf16[1024,128]{1,0:T(8,128)(2,1)S(1)}, u32[]{:S(2)}, u32[]{:S(2)}) collective-permute-start(bf16[1024,128]{1,0:T(8,128)(2,1)S(1)} %copy-done.3), channel_id=1, source_target_pairs={{0,6},{1,7},{2,0},{3,1},{4,2},{5,3},{6,4},{7,5},{8,14},{9,15},{10,... | collective-permute-start | bytes 786440 | tf_op jit(solution)/shard_map/ppermute | solution.py:59
  86.6 8.9 %collective-permute-start.4 = (bf16[1024,128]{1,0:T(8,128)(2,1)S(1)}, bf16[1024,128]{1,0:T(8,128)(2,1)S(1)}, u32[]{:S(2)}, u32[]{:S(2)}) collective-permute-start(bf16[1024,128]{1,0:T(8,128)(2,1)S(1)} %copy-done.3), channel_id=1, source_target_pairs={{0,2},{1,3},{2,4},{3,5},{4,6},{5,7},{6,0},{7,1},{8,10},{9,11},{10,... | collective-permute-start | bytes 786440 | tf_op jit(solution)/shard_map/ppermute | solution.py:58
  95.5 7.1 %collective-permute-start.6 = (bf16[1024,128]{1,0:T(8,128)(2,1)S(1)}, bf16[1024,128]{1,0:T(8,128)(2,1)S(1)}, u32[]{:S(2)}, u32[]{:S(2)}) collective-permute-start(bf16[1024,128]{1,0:T(8,128)(2,1)S(1)} %broadcast_select_fusion.2), channel_id=1, source_target_pairs={{0,2},{1,7},{2,4},{3,1},{4,6},{5,3},{6,0},{7,5},{8,10},{9,15},{10,... | collective-permute-start | bytes 786440 | tf_op jit(solution)/shard_map/ppermute | solution.py:61
  102.7 11.8 %copy-start.1 = (bf16[4,1024,128]{2,1,0:T(8,128)(2,1)}, bf16[4,1024,128]{2,1,0:T(8,128)(2,1)S(1)}, u32[]{:S(2)}) copy-start(bf16[4,1024,128]{2,1,0:T(8,128)(2,1)S(1)} %pad_maximum_fusion.1.mine_hbm) | copy-start | bytes 3145732
  102.7 16.1 %collective-permute-start.7 = (bf16[4,1024,128]{2,1,0:T(8,128)(2,1)S(1)}, bf16[4,1024,128]{2,1,0:T(8,128)(2,1)}, u32[]{:S(2)}, u32[]{:S(2)}) collective-permute-start(bf16[4,1024,128]{2,1,0:T(8,128)(2,1)S(1)} %pad_maximum_fusion.1.mine_hbm), channel_id=1, source_target_pairs={{0,1},{1,0},{2,3},{3,2},{4,5},{5,4},{6,7},{7,6},{8,9},{9,8},{10,11... | collective-permute-start | bytes 3145736 | tf_op jit(solution)/shard_map/ppermute | solution.py:67
  114.5 3.7 %copy-start.5 = (s32[4]{0:T(128)S(1)}, s32[4]{0:T(128)}, u32[]{:S(2)}) copy-start(s32[4]{0:T(128)} %param.15) | copy-start | bytes 52
  114.5 3.8 %copy-start.4 = (s32[2,256,32]{1,2,0:T(8,128)S(1)}, s32[2,256,32]{1,2,0:T(8,128)}, u32[]{:S(2)}) copy-start(s32[2,256,32]{1,2,0:T(8,128)} %param.13) | copy-start | bytes 196612
  114.5 18.7 %all-to-all-start.3 = ((bf16[8,64,1024]{2,1,0:T(8,128)(2,1)}), bf16[8,64,1024]{2,1,0:T(8,128)(2,1)S(1)}, u32[]{:S(2)}, u32[]{:S(2)}) async-start(bf16[8,64,1024]{2,1,0:T(8,128)(2,1)} %bitcast.25), calls=%async_computation.3 | async-start | bytes 2097152 | tf_op jit(solution)/shard_map/all_to_all | solution.py:403
  138.5 8.9 %all-to-all-start.4 = ((f32[8,8,128]{2,1,0:T(8,128)}), f32[8,8,128]{2,1,0:T(8,128)S(1)}, u32[]{:S(2)}, u32[]{:S(2)}) async-start(f32[8,8,128]{2,1,0:T(8,128)} %tail.1), calls=%async_computation.4 | async-start | bytes 65536 | tf_op jit(solution)/shard_map/all_to_all | solution.py:405

commit v9 on v7

--- a/solution.py
+++ b/solution.py
@@ -18,17 +18,25 @@
 NX = 4
 NC = 2
 LANES = 128
+NEAR = 4
 CODES = 80
 EPS = 1e-06
 MIB = 1024 * 1024
+FEATURES_WEIGHT = 12
 
 
 def y_groups(n_dp):
     return [[start + y for y in range(NY)] for start in range(0, n_dp, NY)]
 
 
-def z_groups(n_dp):
-    return [list(range(y, n_dp, NY)) for y in range(NY)]
+def far_groups(n_dp):
+    n_far = n_dp // NY // NEAR
+    return [[(far * NEAR + near) * NY + y for far in range(n_far)] for near in range(NEAR) for y in range(NY)]
+
+
+def near_groups(n_dp):
+    n_far = n_dp // NY // NEAR
+    return [[(far * NEAR + near) * NY + y for near in range(NEAR)] for far in range(n_far) for y in range(NY)]
 
 
 def x_shift(value, step):
@@ -159,17 +167,54 @@
             pl.BlockSpec((NX, width, LANES), lambda b: (0, 0, 0)),
             pl.BlockSpec((NX, width, LANES), lambda b: (0, 0, 0)),
         ],
-        out_specs=pl.BlockSpec((None, IMAG, rows, UNITS), lambda b: (b, 0, 0, 0)),
-        out_shape=pltpu.HBM((NY, IMAG, rows, UNITS), jnp.bfloat16),
+        out_specs=pl.BlockSpec((IMAG, None, rows, UNITS), lambda b: (0, b, 0, 0)),
+        out_shape=pltpu.HBM((IMAG, NY, rows, UNITS), jnp.bfloat16),
         scratch_shapes=[pltpu.VMEM((width, UNITS), jnp.bfloat16)],
         compiler_params=pltpu.CompilerParams(vmem_limit_bytes=32 * MIB),
         cost_estimate=pl.CostEstimate(
-            flops=2 * IMAG * NY * rows * width * (UNITS + LANES),
+            flops=FEATURES_WEIGHT * IMAG * NY * rows * width * (UNITS + LANES) // 5,
             bytes_accessed=IMAG * NY * rows * UNITS * 2 + width * UNITS * 2,
             transcendentals=IMAG * NY * rows * UNITS,
         ),
         name="features",
     )(place, came, spread, target, mine, other)
+
+
+def gate_kernel(n_far, features_ref, gate_ref, out_ref, w_ref):
+    near, held = gate_ref.shape[:2]
+    depth = held // n_far
+
+    @pl.when(pl.program_id(0) == 0)
+    def _():
+        for i in range(near):
+            for far in range(n_far):
+                w_ref[(far * near + i) * depth : (far * near + i + 1) * depth] = gate_ref[i, far * depth : (far + 1) * depth]
+
+    for k in range(IMAG):
+        out_ref[k] = jnp.dot(features_ref[k], w_ref[...], preferred_element_type=jnp.float32).astype(jnp.bfloat16)
+
+
+def gate_call(features, gate, n_far):
+    rows = features.shape[2]
+    width = gate.shape[2]
+    return pl.pallas_call(
+        functools.partial(gate_kernel, n_far),
+        grid=(NY,),
+        in_specs=[
+            pl.BlockSpec((IMAG, None, rows, UNITS), lambda b: (0, b, 0, 0)),
+            pl.BlockSpec(gate.shape, lambda b: (0, 0, 0)),
+        ],
+        out_specs=pl.BlockSpec((None, IMAG, rows, width), lambda b: (b, 0, 0, 0)),
+        out_shape=jax.ShapeDtypeStruct((NY, IMAG, rows, width), jnp.bfloat16),
+        scratch_shapes=[pltpu.VMEM((UNITS, width), jnp.bfloat16)],
+        compiler_params=pltpu.CompilerParams(vmem_limit_bytes=32 * MIB),
+        cost_estimate=pl.CostEstimate(
+            flops=2 * IMAG * NY * rows * UNITS * width,
+            bytes_accessed=IMAG * NY * rows * (UNITS + width) * 2 + UNITS * width * 2,
+            transcendentals=0,
+        ),
+        name="gate",
+    )(features, gate)
 
 
 def gru_kernel(
@@ -320,16 +365,17 @@
 
     sent = prep_call(w_gate, post_sample.T, samples.transpose(0, 2, 1), actions)
     came = lax.all_to_all(sent, "dp", 0, 0, axis_index_groups=y_groups(n_dp))
-    held = copies_call(came, n_dp // NY, depth, w_gate.shape[1] // NY)
-    gate = lax.all_to_all(held, "dp", 0, 0, axis_index_groups=z_groups(n_dp)).reshape(n_dp * depth, -1)
+    n_far = n_dp // NY // NEAR
+    held = copies_call(came, n_far, depth, w_gate.shape[1] // NY)
+    held = lax.all_to_all(held, "dp", 0, 0, axis_index_groups=far_groups(n_dp)).reshape(n_far * NY * depth, -1)
+    gate = jnp.broadcast_to(held[None], (NEAR,) + held.shape)
+    gate = lax.all_to_all(gate, "dp", 0, 0, axis_index_groups=near_groups(n_dp))
 
     action_rows = jnp.pad(w_action, ((0, LANES - ACTIONS), (0, 0)))
     mine, other = tensor_gather(jnp.concatenate([w_stoch, action_rows], axis=0))
 
     features = features_call(place, came, mine, other)
-    total = jnp.dot(features.reshape(-1, UNITS), gate, preferred_element_type=jnp.float32).astype(jnp.bfloat16)
-    total = total.reshape(NY, IMAG, rows, -1)
-    sums = lax.all_to_all(total, "dp", 0, 0, axis_index_groups=y_groups(n_dp))
+    sums = lax.all_to_all(gate_call(features, gate, n_far), "dp", 0, 0, axis_index_groups=y_groups(n_dp))
 
     w_out_late, _ = lax.optimization_barrier((w_prior_out, features))
     out_mine, out_other = tensor_gather(w_out_late)

time: 137 us -> 139 us (1.015)
  matrix products: 5.74 us -> 0 us
  starting transfers between devices: 49.7 us -> 54.4 us
  waiting for transfers between devices: 44.5 us -> 40.5 us
  Pallas kernels: 22.6 us -> 26.3 us
  local copies, waits for them, and re-layouts: 1.14 us -> 4.27 us
    ppermute x6, waiting for transfers between devices: 23.9 us -> 16.6 us  [x_shift(): return lax.ppermute(value, 'tensor', perm)]
    dot_general x1 -> x0, matrix products: 5.74 us -> none  [body(): jnp.dot(features.reshape(-1, UNITS), gate, preferred_element_type=jnp.flo...]
    pallas_call x0 -> x1, Pallas kernels: none -> 3.97 us  [gate_call(): pl.pallas_call(functools.partial(gate_kernel, n_far), grid=(NY,), in_spec...]
    all_to_all x2 -> x3, starting transfers between devices: 18.6 us -> 22.5 us  [the longest x1 14.8 us: body(): lax.all_to_all(held, 'dp', 0, 0, axis_index_groups=far_groups(n_dp))]
    all_to_all x2 -> x3, waiting for transfers between devices: 0.01 us -> 3.25 us  [the longest x1 3.24 us: body(): lax.all_to_all(held, 'dp', 0, 0, axis_index_groups=far_groups(n_dp))]
    unnamed x10 -> x12, local copies, waits for them, and re-layouts: 0.02 us -> 2.21 us
    ppermute x6, starting transfers between devices: 16.5 us -> 18.2 us  [x_shift(): return lax.ppermute(value, 'tensor', perm)]
  transfers between devices with their start and end apart: 12 -> 13, of which waited for: 8 -> 8; matrix products, arithmetic and copies ran while one was open for 1% -> 2% of each run, Pallas kernels for 12% -> 12%
where the time goes in v9:
time: 139 us; the launch traced here: 138 us
  starting transfers between devices  54.4 us (39%)
  waiting for transfers between devices  40.5 us (29%)
  Pallas kernels  26.3 us (19%)
  blocking collectives  10.4 us (7%)
  local copies, waits for them, and re-layouts  4.27 us (3%)
  other arithmetic  1.54 us (1%)
    ppermute x6, starting transfers between devices, x_shift(): return lax.ppermute(value, 'tensor', perm)  18.2 us
    ppermute x6, waiting for transfers between devices, x_shift(): return lax.ppermute(value, 'tensor', perm)  16.6 us
    all_to_all x1, starting transfers between devices, body(): lax.all_to_all(held, 'dp', 0, 0, axis_index_groups=far_groups(n_dp))  14.8 us
    all_to_all x1, waiting for transfers between devices, body(): lax.all_to_all(partial.reshape(tensor_n, IMAG * share, UNITS), 'tensor',...  14.4 us
    pallas_call x1, Pallas kernels, features_call(): pl.pallas_call(features_kernel, grid=(NY,), in_specs=[pl.BlockSpec(memory...  11.5 us
    all_to_all x1, blocking collectives, body(): came = lax.all_to_all(sent, 'dp', 0, 0, axis_index_groups=y_groups(n_dp))  10.4 us
    ppermute x2, starting transfers between devices, core_swap(): return lax.ppermute(value, 'tensor', perm)  5.98 us
    pallas_call x1, Pallas kernels, gru_call(): pl.pallas_call(gru_kernel, in_specs=[hbm] * 3 + [vmem], out_specs=[vmem,...  4.59 us
  transfers between devices with their start and end apart: 13, of which 8 were waited for; matrix products, arithmetic and copies ran while one was open for 2% of the time, Pallas kernels for 12%

profile of v9, /device:TPU:1, one launch (start us, length us, event | category | flops | bytes accessed | tf_op | source)
XLA Modules:
  0.0 138.3 jit_solution(11112560352444683793)
XLA Ops:
  0.7 1.6 %prep.1 = bf16[4,112,256]{2,1,0:T(8,128)(2,1)} custom-call(bf16[16,1536]{1,0:T(8,128)(2,1)} %w_ref.1, s32[32,256]{1,0:T(8,128)} %bitcast.31, s32[2,32,256]{2,1,0:T(8,128)} %bitcast.30, s32[2,256]{1,0:T(2,128)} %actions_ref.1), custom_call_target="tpu_custom_call" | custom-call | bytes 524288 | tf_op jit(solution)/shard_map/prep/pallas_call | solution.py:89
  2.3 10.4 %all_to_all.30.came_ref = bf16[4,112,256]{2,1,0:T(8,128)(2,1)S(1)} all-to-all(bf16[4,112,256]{2,1,0:T(8,128)(2,1)} %prep.1), channel_id=1, replica_groups={{0,8,16,24},{32,40,48,56},{64,72,80,88},{96,104,112,120},{128,136,144,1..., dimensions={0} | all-to-all | bytes 458752 | tf_op jit(solution)/shard_map/all_to_all | solution.py:367
  12.7 0.7 copies.1
  13.4 14.8 %all-to-all-start.1 = ((bf16[4,64,384]{2,1,0:T(8,128)(2,1)}), bf16[4,64,384]{2,1,0:T(8,128)(2,1)S(1)}, u32[]{:S(2)}, u32[]{:S(2)}) async-start(bf16[4,64,384]{2,1,0:T(8,128)(2,1)} %copies.1), calls=%async_computation.1 | async-start | bytes 393216 | tf_op jit(solution)/shard_map/all_to_all | solution.py:370
  28.2 4.4 %collective-permute-start.2 = (bf16[1152,128]{1,0:T(8,128)(2,1)S(1)}, bf16[1152,128]{1,0:T(8,128)(2,1)S(1)}, u32[]{:S(2)}, u32[]{:S(2)}) collective-permute-start(bf16[1152,128]{1,0:T(8,128)(2,1)S(1)} %get-tuple-element.9), channel_id=1, source_target_pairs={{0,6},{1,7},{2,0},{3,1},{4,2},{5,3},{6,4},{7,5},{8,14},{9,15},{10,... | collective-permute-start | bytes 884744 | tf_op jit(solution)/shard_map/ppermute | solution.py:45
  32.6 2.4 %collective-permute-start.1 = (bf16[1152,128]{1,0:T(8,128)(2,1)S(1)}, bf16[1152,128]{1,0:T(8,128)(2,1)S(1)}, u32[]{:S(2)}, u32[]{:S(2)}) collective-permute-start(bf16[1152,128]{1,0:T(8,128)(2,1)S(1)} %get-tuple-element.9), channel_id=1, source_target_pairs={{0,4},{1,5},{2,6},{3,7},{4,0},{5,1},{6,2},{7,3},{8,12},{9,13},{10,... | collective-permute-start | bytes 884744 | tf_op jit(solution)/shard_map/ppermute | solution.py:45
  35.1 2.5 %collective-permute-start = (bf16[1152,128]{1,0:T(8,128)(2,1)S(1)}, bf16[1152,128]{1,0:T(8,128)(2,1)S(1)}, u32[]{:S(2)}, u32[]{:S(2)}) collective-permute-start(bf16[1152,128]{1,0:T(8,128)(2,1)S(1)} %get-tuple-element.9), channel_id=1, source_target_pairs={{0,2},{1,3},{2,4},{3,5},{4,6},{5,7},{6,0},{7,1},{8,10},{9,11},{10,... | collective-permute-start | bytes 884744 | tf_op jit(solution)/shard_map/ppermute | solution.py:45
  37.6 3.2 %all-to-all-done.1 = bf16[4,64,384]{2,1,0:T(8,128)(2,1)S(1)} async-done(((bf16[4,64,384]{2,1,0:T(8,128)(2,1)}), bf16[4,64,384]{2,1,0:T(8,128)(2,1)S(1)}, u32[]{:S(2)}, u32[]{:S(2)}) %all-to-all-start.1) | async-done | bytes 196640 | tf_op jit(solution)/shard_map/all_to_all | solution.py:370
  40.8 0.9 broadcast_in_dim.41
  41.8 4.0 %all-to-all-start.2 = ((bf16[4,256,384]{2,1,0:T(8,128)(2,1)}), bf16[4,256,384]{2,1,0:T(8,128)(2,1)S(1)}, u32[]{:S(2)}, u32[]{:S(2)}) async-start(bf16[4,256,384]{2,1,0:T(8,128)(2,1)} %broadcast_in_dim.41), calls=%async_computation.2 | async-start | bytes 1572864 | tf_op jit(solution)/shard_map/all_to_all | solution.py:372
  45.8 4.4 %collective-permute-done = bf16[1152,128]{1,0:T(8,128)(2,1)S(1)} collective-permute-done((bf16[1152,128]{1,0:T(8,128)(2,1)S(1)}, bf16[1152,128]{1,0:T(8,128)(2,1)S(1)}, u32[]{:S(2)}, u32[]{:S(2)}) %collective-permute-start) | collective-permute-done | bytes 294944 | tf_op jit(solution)/shard_map/ppermute | solution.py:45
  50.3 3.6 %collective-permute-start.3 = (bf16[4,1152,128]{2,1,0:T(8,128)(2,1)S(1)}, bf16[4,1152,128]{2,1,0:T(8,128)(2,1)S(1)}, u32[]{:S(2)}, u32[]{:S(2)}) collective-permute-start(bf16[4,1152,128]{2,1,0:T(8,128)(2,1)S(1)} %pad_maximum_fusion.mine_ref), channel_id=1, source_target_pairs={{0,1},{1,0},{2,3},{3,2},{4,5},{5,4},{6,7},{7,6},{8,9},{9,8},{10,11... | collective-permute-start | bytes 3538952 | tf_op jit(solution)/shard_map/ppermute | solution.py:50
  54.0 2.3 %collective-permute-done.3.other_ref = bf16[4,1152,128]{2,1,0:T(8,128)(2,1)S(1)} collective-permute-done((bf16[4,1152,128]{2,1,0:T(8,128)(2,1)S(1)}, bf16[4,1152,128]{2,1,0:T(8,128)(2,1)S(1)}, u32[]{:S(2)}, u32[]{:S(2)}) %collective-permute-start.3) | collective-permute-done | bytes 1179680 | tf_op jit(solution)/shard_map/ppermute | solution.py:50
  56.3 11.5 %features.1.features_ref = bf16[2,4,256,1024]{3,2,1,0:T(8,128)(2,1)} custom-call(s32[2]{0:T(128)S(1)} %pad_add_fusion.1.place_ref.me_ref, bf16[4,112,256]{2,1,0:T(8,128)(2,1)S(1)} %all_to_all.30.came_ref, bf16[80,2304]{1,0:T(8,128)(2,1)S(1)} %fusion.spread_ref, f32[1,1152]{1,0:T(1,128)S(1)} %fusion.10.target_ref, ...), custom_call_target="tpu_custom_call" | custom-call | flops 6522981376 | bytes 6553600 | tf_op jit(solution)/shard_map/features/pallas_call | solution.py:159
  67.8 2.2 %copy-done = bf16[2,4,256,1024]{3,2,1,0:T(8,128)(2,1)S(1)} copy-done((bf16[2,4,256,1024]{3,2,1,0:T(8,128)(2,1)S(1)}, bf16[2,4,256,1024]{3,2,1,0:T(8,128)(2,1)}, u32[]{:S(2)}) %copy-start) | copy-done | bytes 4194328
  70.0 4.0 %gate.1 = bf16[4,2,256,384]{3,2,1,0:T(8,128)(2,1)} custom-call(bf16[2,4,256,1024]{3,2,1,0:T(8,128)(2,1)S(1)} %copy-done, bf16[4,256,384]{2,1,0:T(8,128)(2,1)S(1)} %all-to-all-done.2.gate_ref), custom_call_target="tpu_custom_call" | custom-call | flops 1610612736 | bytes 6553600 | tf_op jit(solution)/shard_map/gate/pallas_call | solution.py:200
  73.9 3.7 %all-to-all-start.3 = ((bf16[4,2,256,384]{3,2,1,0:T(8,128)(2,1)}), bf16[4,2,256,384]{3,2,1,0:T(8,128)(2,1)S(1)}, u32[]{:S(2)}, u32[]{:S(2)}) async-start(bf16[4,2,256,384]{3,2,1,0:T(8,128)(2,1)} %gate.1), calls=%async_computation.3 | async-start | bytes 3145728 | tf_op jit(solution)/shard_map/all_to_all | solution.py:378
  77.7 3.9 %collective-permute-start.6 = (bf16[1024,128]{1,0:T(8,128)(2,1)S(1)}, bf16[1024,128]{1,0:T(8,128)(2,1)S(1)}, u32[]{:S(2)}, u32[]{:S(2)}) collective-permute-start(bf16[1024,128]{1,0:T(8,128)(2,1)S(1)} %copy-done.2), channel_id=1, source_target_pairs={{0,6},{1,7},{2,0},{3,1},{4,2},{5,3},{6,4},{7,5},{8,14},{9,15},{10,... | collective-permute-start | bytes 786440 | tf_op jit(solution)/shard_map/ppermute | solution.py:45
  81.6 2.4 %collective-permute-start.5 = (bf16[1024,128]{1,0:T(8,128)(2,1)S(1)}, bf16[1024,128]{1,0:T(8,128)(2,1)S(1)}, u32[]{:S(2)}, u32[]{:S(2)}) collective-permute-start(bf16[1024,128]{1,0:T(8,128)(2,1)S(1)} %copy-done.2), channel_id=1, source_target_pairs={{0,4},{1,5},{2,6},{3,7},{4,0},{5,1},{6,2},{7,3},{8,12},{9,13},{10,... | collective-permute-start | bytes 786440 | tf_op jit(solution)/shard_map/ppermute | solution.py:45
  84.0 2.5 %collective-permute-start.4 = (bf16[1024,128]{1,0:T(8,128)(2,1)S(1)}, bf16[1024,128]{1,0:T(8,128)(2,1)S(1)}, u32[]{:S(2)}, u32[]{:S(2)}) collective-permute-start(bf16[1024,128]{1,0:T(8,128)(2,1)S(1)} %copy-done.2), channel_id=1, source_target_pairs={{0,2},{1,3},{2,4},{3,5},{4,6},{5,7},{6,0},{7,1},{8,10},{9,11},{10,... | collective-permute-start | bytes 786440 | tf_op jit(solution)/shard_map/ppermute | solution.py:45
  86.6 0.7 collective-permute-done.6
  87.2 5.0 %collective-permute-done.5 = bf16[1024,128]{1,0:T(8,128)(2,1)S(1)} collective-permute-done((bf16[1024,128]{1,0:T(8,128)(2,1)S(1)}, bf16[1024,128]{1,0:T(8,128)(2,1)S(1)}, u32[]{:S(2)}, u32[]{:S(2)}) %collective-permute-start.5) | collective-permute-done | bytes 262176 | tf_op jit(solution)/shard_map/ppermute | solution.py:45
  92.2 6.6 %collective-permute-done.4 = bf16[1024,128]{1,0:T(8,128)(2,1)S(1)} collective-permute-done((bf16[1024,128]{1,0:T(8,128)(2,1)S(1)}, bf16[1024,128]{1,0:T(8,128)(2,1)S(1)}, u32[]{:S(2)}, u32[]{:S(2)}) %collective-permute-start.4) | collective-permute-done | bytes 262176 | tf_op jit(solution)/shard_map/ppermute | solution.py:45
  99.0 2.4 %collective-permute-start.7 = (bf16[4,1024,128]{2,1,0:T(8,128)(2,1)S(1)}, bf16[4,1024,128]{2,1,0:T(8,128)(2,1)}, u32[]{:S(2)}, u32[]{:S(2)}) collective-permute-start(bf16[4,1024,128]{2,1,0:T(8,128)(2,1)S(1)} %pad_maximum_fusion.1.mine_ref), channel_id=1, source_target_pairs={{0,1},{1,0},{2,3},{3,2},{4,5},{5,4},{6,7},{7,6},{8,9},{9,8},{10,11... | collective-permute-start | bytes 3145736 | tf_op jit(solution)/shard_map/ppermute | solution.py:50
  101.4 4.6 %gru.1 = (bf16[256,512]{1,0:T(8,128)(2,1)S(1)}, bf16[8,2,32,1024]{3,2,1,0:T(8,128)(2,1)}) custom-call(bf16[256,512]{1,0:T(8,128)(2,1)} %deter_hbm.1, bf16[512,1536]{1,0:T(8,128)(2,1)} %bitcast.33, bf16[512,1024]{1,0:T(8,128)(2,1)} %w_in_hbm.1, bf16[4,2,256,384]{3,2,1,0:T(8,128)(2,1)S(1)} %all-to-all-done.3.f_ref), custom_call_target="tpu_custom_call" | custom-call | flops 1342177280 | bytes 5767168 | tf_op jit(solution)/shard_map/gru/pallas_call | solution.py:264
  106.0 3.7 %all-to-all-start.4 = ((bf16[8,64,1024]{2,1,0:T(8,128)(2,1)}), bf16[8,64,1024]{2,1,0:T(8,128)(2,1)S(1)}, u32[]{:S(2)}, u32[]{:S(2)}) async-start(bf16[8,64,1024]{2,1,0:T(8,128)(2,1)} %bitcast.21), calls=%async_computation.4 | async-start | bytes 2097152 | tf_op jit(solution)/shard_map/all_to_all | solution.py:391
  110.3 14.4 %all-to-all-done.4.parts_ref = bf16[8,64,1024]{2,1,0:T(8,128)(2,1)S(1)} async-done(((bf16[8,64,1024]{2,1,0:T(8,128)(2,1)}), bf16[8,64,1024]{2,1,0:T(8,128)(2,1)S(1)}, u32[]{:S(2)}, u32[]{:S(2)}) %all-to-all-start.4) | async-done | bytes 1048608 | tf_op jit(solution)/shard_map/all_to_all | solution.py:391
  124.8 3.9 %tail.1 = f32[8,8,128]{2,1,0:T(8,128)} custom-call(s32[2]{0:T(128)S(1)} %pad_add_fusion.1.place_ref.me_ref, bf16[8,64,1024]{2,1,0:T(8,128)(2,1)S(1)} %all-to-all-done.4.parts_ref, bf16[4,1024,128]{2,1,0:T(8,128)(2,1)S(1)} %pad_maximum_fusion.1.mine_ref, bf16[4,1024,128]{2,1,0:T(8,128)(2,1)} %collective-permute-done.7.other_ref, bf16[64,32]{1,0:T(8,128)(2,1)S(1)} %bitcast.20, ...), custom_call_target="tpu_custom_call" | custom-call | flops 134217728 | bytes 4194304 | tf_op jit(solution)/shard_map/tail/pallas_call | solution.py:332
  128.7 4.1 %all-to-all-start.5 = ((f32[8,8,128]{2,1,0:T(8,128)}), f32[8,8,128]{2,1,0:T(8,128)S(1)}, u32[]{:S(2)}, u32[]{:S(2)}) async-start(f32[8,8,128]{2,1,0:T(8,128)} %tail.1), calls=%async_computation.5 | async-start | bytes 65536 | tf_op jit(solution)/shard_map/all_to_all | solution.py:393
  132.8 0.8 broadcast_select_fusion
  133.6 3.9 %all-to-all-done.5 = f32[8,8,128]{2,1,0:T(8,128)S(1)} async-done(((f32[8,8,128]{2,1,0:T(8,128)}), f32[8,8,128]{2,1,0:T(8,128)S(1)}, u32[]{:S(2)}, u32[]{:S(2)}) %all-to-all-start.5) | async-done | bytes 32800 | tf_op jit(solution)/shard_map/all_to_all | solution.py:393
  137.6 0.7 reshape.110
  (36 shorter events, 1.2 us)
Async XLA Ops:
  0.6 27.6 %copy-start.4 = (bf16[18,128]{1,0:T(8,128)(2,1)S(1)}, bf16[18,128]{1,0:T(8,128)(2,1)}, u32[]{:S(2)}) copy-start(bf16[18,128]{1,0:T(8,128)(2,1)} %param.17) | copy-start | bytes 13828
  0.6 27.6 %copy-start.1 = (bf16[1024,128]{1,0:T(8,128)(2,1)S(1)}, bf16[1024,128]{1,0:T(8,128)(2,1)}, u32[]{:S(2)}) copy-start(bf16[1024,128]{1,0:T(8,128)(2,1)} %param.16) | copy-start | bytes 786436
  13.4 27.5 %all-to-all-start.1 = ((bf16[4,64,384]{2,1,0:T(8,128)(2,1)}), bf16[4,64,384]{2,1,0:T(8,128)(2,1)S(1)}, u32[]{:S(2)}, u32[]{:S(2)}) async-start(bf16[4,64,384]{2,1,0:T(8,128)(2,1)} %copies.1), calls=%async_computation.1 | async-start | bytes 393216 | tf_op jit(solution)/shard_map/all_to_all | solution.py:370
  28.2 17.5 %collective-permute-start.2 = (bf16[1152,128]{1,0:T(8,128)(2,1)S(1)}, bf16[1152,128]{1,0:T(8,128)(2,1)S(1)}, u32[]{:S(2)}, u32[]{:S(2)}) collective-permute-start(bf16[1152,128]{1,0:T(8,128)(2,1)S(1)} %get-tuple-element.9), channel_id=1, source_target_pairs={{0,6},{1,7},{2,0},{3,1},{4,2},{5,3},{6,4},{7,5},{8,14},{9,15},{10,... | collective-permute-start | bytes 884744 | tf_op jit(solution)/shard_map/ppermute | solution.py:45
  32.6 13.1 %collective-permute-start.1 = (bf16[1152,128]{1,0:T(8,128)(2,1)S(1)}, bf16[1152,128]{1,0:T(8,128)(2,1)S(1)}, u32[]{:S(2)}, u32[]{:S(2)}) collective-permute-start(bf16[1152,128]{1,0:T(8,128)(2,1)S(1)} %get-tuple-element.9), channel_id=1, source_target_pairs={{0,4},{1,5},{2,6},{3,7},{4,0},{5,1},{6,2},{7,3},{8,12},{9,13},{10,... | collective-permute-start | bytes 884744 | tf_op jit(solution)/shard_map/ppermute | solution.py:45
  35.1 15.0 %collective-permute-start = (bf16[1152,128]{1,0:T(8,128)(2,1)S(1)}, bf16[1152,128]{1,0:T(8,128)(2,1)S(1)}, u32[]{:S(2)}, u32[]{:S(2)}) collective-permute-start(bf16[1152,128]{1,0:T(8,128)(2,1)S(1)} %get-tuple-element.9), channel_id=1, source_target_pairs={{0,2},{1,3},{2,4},{3,5},{4,6},{5,7},{6,0},{7,1},{8,10},{9,11},{10,... | collective-permute-start | bytes 884744 | tf_op jit(solution)/shard_map/ppermute | solution.py:45
  41.8 26.0 %all-to-all-start.2 = ((bf16[4,256,384]{2,1,0:T(8,128)(2,1)}), bf16[4,256,384]{2,1,0:T(8,128)(2,1)S(1)}, u32[]{:S(2)}, u32[]{:S(2)}) async-start(bf16[4,256,384]{2,1,0:T(8,128)(2,1)} %broadcast_in_dim.41), calls=%async_computation.2 | async-start | bytes 1572864 | tf_op jit(solution)/shard_map/all_to_all | solution.py:372
  50.3 6.0 %collective-permute-start.3 = (bf16[4,1152,128]{2,1,0:T(8,128)(2,1)S(1)}, bf16[4,1152,128]{2,1,0:T(8,128)(2,1)S(1)}, u32[]{:S(2)}, u32[]{:S(2)}) collective-permute-start(bf16[4,1152,128]{2,1,0:T(8,128)(2,1)S(1)} %pad_maximum_fusion.mine_ref), channel_id=1, source_target_pairs={{0,1},{1,0},{2,3},{3,2},{4,5},{5,4},{6,7},{7,6},{8,9},{9,8},{10,11... | collective-permute-start | bytes 3538952 | tf_op jit(solution)/shard_map/ppermute | solution.py:50
  67.8 2.2 %copy-start = (bf16[2,4,256,1024]{3,2,1,0:T(8,128)(2,1)S(1)}, bf16[2,4,256,1024]{3,2,1,0:T(8,128)(2,1)}, u32[]{:S(2)}) copy-start(bf16[2,4,256,1024]{3,2,1,0:T(8,128)(2,1)} %features.1.features_ref) | copy-start | bytes 12582916
  73.9 3.7 %copy-start.2 = (bf16[1024,128]{1,0:T(8,128)(2,1)S(1)}, bf16[1024,128]{1,0:T(8,128)(2,1)}, u32[]{:S(2)}) copy-start(bf16[1024,128]{1,0:T(8,128)(2,1)} %param.21) | copy-start | bytes 786436
  73.9 27.4 %all-to-all-start.3 = ((bf16[4,2,256,384]{3,2,1,0:T(8,128)(2,1)}), bf16[4,2,256,384]{3,2,1,0:T(8,128)(2,1)S(1)}, u32[]{:S(2)}, u32[]{:S(2)}) async-start(bf16[4,2,256,384]{3,2,1,0:T(8,128)(2,1)} %gate.1), calls=%async_computation.3 | async-start | bytes 3145728 | tf_op jit(solution)/shard_map/all_to_all | solution.py:378
  77.7 9.6 %collective-permute-start.6 = (bf16[1024,128]{1,0:T(8,128)(2,1)S(1)}, bf16[1024,128]{1,0:T(8,128)(2,1)S(1)}, u32[]{:S(2)}, u32[]{:S(2)}) collective-permute-start(bf16[1024,128]{1,0:T(8,128)(2,1)S(1)} %copy-done.2), channel_id=1, source_target_pairs={{0,6},{1,7},{2,0},{3,1},{4,2},{5,3},{6,4},{7,5},{8,14},{9,15},{10,... | collective-permute-start | bytes 786440 | tf_op jit(solution)/shard_map/ppermute | solution.py:45
  81.6 10.6 %collective-permute-start.5 = (bf16[1024,128]{1,0:T(8,128)(2,1)S(1)}, bf16[1024,128]{1,0:T(8,128)(2,1)S(1)}, u32[]{:S(2)}, u32[]{:S(2)}) collective-permute-start(bf16[1024,128]{1,0:T(8,128)(2,1)S(1)} %copy-done.2), channel_id=1, source_target_pairs={{0,4},{1,5},{2,6},{3,7},{4,0},{5,1},{6,2},{7,3},{8,12},{9,13},{10,... | collective-permute-start | bytes 786440 | tf_op jit(solution)/shard_map/ppermute | solution.py:45
  84.0 14.8 %collective-permute-start.4 = (bf16[1024,128]{1,0:T(8,128)(2,1)S(1)}, bf16[1024,128]{1,0:T(8,128)(2,1)S(1)}, u32[]{:S(2)}, u32[]{:S(2)}) collective-permute-start(bf16[1024,128]{1,0:T(8,128)(2,1)S(1)} %copy-done.2), channel_id=1, source_target_pairs={{0,2},{1,3},{2,4},{3,5},{4,6},{5,7},{6,0},{7,1},{8,10},{9,11},{10,... | collective-permute-start | bytes 786440 | tf_op jit(solution)/shard_map/ppermute | solution.py:45
  99.0 11.3 %collective-permute-start.7 = (bf16[4,1024,128]{2,1,0:T(8,128)(2,1)S(1)}, bf16[4,1024,128]{2,1,0:T(8,128)(2,1)}, u32[]{:S(2)}, u32[]{:S(2)}) collective-permute-start(bf16[4,1024,128]{2,1,0:T(8,128)(2,1)S(1)} %pad_maximum_fusion.1.mine_ref), channel_id=1, source_target_pairs={{0,1},{1,0},{2,3},{3,2},{4,5},{5,4},{6,7},{7,6},{8,9},{9,8},{10,11... | collective-permute-start | bytes 3145736 | tf_op jit(solution)/shard_map/ppermute | solution.py:50
  106.0 3.7 %copy-start.5 = (s32[4]{0:T(128)S(1)}, s32[4]{0:T(128)}, u32[]{:S(2)}) copy-start(s32[4]{0:T(128)} %param.15) | copy-start | bytes 52
  106.0 3.8 %copy-start.3 = (s32[2,256,32]{1,2,0:T(8,128)S(1)}, s32[2,256,32]{1,2,0:T(8,128)}, u32[]{:S(2)}) copy-start(s32[2,256,32]{1,2,0:T(8,128)} %param.13) | copy-start | bytes 196612
  106.0 18.7 %all-to-all-start.4 = ((bf16[8,64,1024]{2,1,0:T(8,128)(2,1)}), bf16[8,64,1024]{2,1,0:T(8,128)(2,1)S(1)}, u32[]{:S(2)}, u32[]{:S(2)}) async-start(bf16[8,64,1024]{2,1,0:T(8,128)(2,1)} %bitcast.21), calls=%async_computation.4 | async-start | bytes 2097152 | tf_op jit(solution)/shard_map/all_to_all | solution.py:391
  128.7 8.8 %all-to-all-start.5 = ((f32[8,8,128]{2,1,0:T(8,128)}), f32[8,8,128]{2,1,0:T(8,128)S(1)}, u32[]{:S(2)}, u32[]{:S(2)}) async-start(f32[8,8,128]{2,1,0:T(8,128)} %tail.1), calls=%async_computation.5 | async-start | bytes 65536 | tf_op jit(solution)/shard_map/all_to_all | solution.py:393

commit v10 on v7

--- a/solution.py
+++ b/solution.py
@@ -177,18 +177,26 @@
 ):
     rows, bw = deter_ref.shape
     part = bw // NY
-    pairs = [(deter_hbm, deter_ref), (w_rec_hbm, w_rec_ref), (w_in_hbm, w_in_ref)]
+    half = bw // 2
+    pairs = [(deter_hbm, deter_ref)]
+    pairs += [(w_rec_hbm.at[pl.ds(i * half, half)], w_rec_ref.at[pl.ds(i * half, half)]) for i in range(2)]
+    pairs += [(w_in_hbm, w_in_ref)]
     pairs += [(prior_ref.at[:, k], prior_hbm.at[:, k]) for k in range(IMAG)]
     copies = [pltpu.make_async_copy(src, dst, sems.at[i]) for i, (src, dst) in enumerate(pairs)]
-    for copy in copies[:3]:
+    for copy in copies[:4]:
         copy.start()
     copies[0].wait()
-    copies[1].wait()
     for k in range(IMAG):
         old_ref = deter_ref if k == 0 else mid_ref
         next_ref = new_ref if k == IMAG - 1 else mid_ref
         old = old_ref[...]
-        rec = jnp.dot(old, w_rec_ref[...], preferred_element_type=jnp.float32)
+        if k == 0:
+            copies[1].wait()
+            rec = jnp.dot(old[:, :half], w_rec_ref[:half], preferred_element_type=jnp.float32)
+            copies[2].wait()
+            rec = rec + jnp.dot(old[:, half:], w_rec_ref[half:], preferred_element_type=jnp.float32)
+        else:
+            rec = jnp.dot(old, w_rec_ref[...], preferred_element_type=jnp.float32)
         for q in range(NY):
 
             def gate(which):
@@ -202,14 +210,14 @@
             fresh = update * candidate + (1.0 - update) * before
             next_ref[:, q * part : (q + 1) * part] = fresh.astype(jnp.bfloat16)
         if k == 0:
-            copies[2].wait()
+            copies[3].wait()
         prior = jnp.dot(next_ref[...], w_in_ref[...], preferred_element_type=jnp.float32).astype(jnp.bfloat16)
         share = prior_ref.shape[2]
         for j in range(prior_ref.shape[0]):
             prior_ref[j, k] = prior[j * share : (j + 1) * share]
-        copies[3 + k].start()
+        copies[4 + k].start()
     for k in range(IMAG):
-        copies[3 + k].wait()
+        copies[4 + k].wait()
 
 
 def gru_call(deter, w_rec, w_in, sums, tensor_n):
@@ -227,7 +235,7 @@
             pltpu.VMEM(w_in.shape, jnp.bfloat16),
             pltpu.VMEM((rows, bw), jnp.bfloat16),
             pltpu.VMEM(prior, jnp.bfloat16),
-            pltpu.SemaphoreType.DMA((3 + IMAG,)),
+            pltpu.SemaphoreType.DMA((4 + IMAG,)),
         ],
         compiler_params=pltpu.CompilerParams(vmem_limit_bytes=24 * MIB),
         cost_estimate=pl.CostEstimate(
@@ -259,12 +267,14 @@
 
     x, core = me_ref[0], me_ref[1]
     logits, wants = [], []
-    for i in range(NX * NC):
-        w_ref = mine_ref if i % NC == 0 else other_ref
-        piece = lax.rem(x + NX - i // NC, NX) * NC + (core if i % NC == 0 else 1 - core)
-        here = pl.ds(pl.multiple_of(piece * LANES, LANES), LANES)
-        logits.append(jnp.dot(hidden, w_ref[i // NC], preferred_element_type=jnp.float32))
-        wants.append(jnp.dot(picked_ref[...], var_ref[:, here], preferred_element_type=jnp.float32))
+    for i in range(NX):
+        w_pair = jnp.concatenate([mine_ref[i], other_ref[i]], axis=1)
+        pair = jnp.dot(hidden, w_pair, preferred_element_type=jnp.float32)
+        base = lax.rem(x + NX - i, NX) * NC
+        for half, piece in enumerate((base + core, base + 1 - core)):
+            here = pl.ds(pl.multiple_of(piece * LANES, LANES), LANES)
+            logits.append(pair[:, half * LANES : (half + 1) * LANES])
+            wants.append(jnp.dot(picked_ref[...], var_ref[:, here], preferred_element_type=jnp.float32))
     logits, wants = jnp.concatenate(logits, axis=0), jnp.concatenate(wants, axis=0)
     powers = jnp.exp(logits - within(logits, jnp.maximum))
     probs = 0.99 * (powers / within(powers, jnp.add)) + 0.01 / CLASSES

time: 137 us -> 138 us (level)
  no operation moved by 1% of the time
where the time goes in v10:
time: 138 us; the launch traced here: 137 us
  starting transfers between devices  49.7 us (36%)
  waiting for transfers between devices  44.5 us (32%)
  Pallas kernels  22.6 us (16%)
  blocking collectives  10.5 us (8%)
  matrix products  5.74 us (4%)
  other arithmetic  1.54 us (1%)
    ppermute x6, waiting for transfers between devices, x_shift(): return lax.ppermute(value, 'tensor', perm)  23.9 us
    ppermute x6, starting transfers between devices, x_shift(): return lax.ppermute(value, 'tensor', perm)  16.5 us
    all_to_all x1, starting transfers between devices, body(): lax.all_to_all(held, 'dp', 0, 0, axis_index_groups=z_groups(n_dp))  14.9 us
    all_to_all x1, waiting for transfers between devices, body(): lax.all_to_all(partial.reshape(tensor_n, IMAG * share, UNITS), 'tensor',...  14.4 us
    pallas_call x1, Pallas kernels, features_call(): pl.pallas_call(features_kernel, grid=(NY,), in_specs=[pl.BlockSpec(memory...  11.5 us
    all_to_all x1, blocking collectives, body(): came = lax.all_to_all(sent, 'dp', 0, 0, axis_index_groups=y_groups(n_dp))  10.5 us
    ppermute x2, starting transfers between devices, core_swap(): return lax.ppermute(value, 'tensor', perm)  6.79 us
    dot_general x1, matrix products, body(): jnp.dot(features.reshape(-1, UNITS), gate, preferred_element_type=jnp.flo...  5.74 us
  transfers between devices with their start and end apart: 12, of which 8 were waited for; matrix products, arithmetic and copies ran while one was open for 1% of the time, Pallas kernels for 12%

profile of v10, /device:TPU:1, one launch (start us, length us, event | category | flops | bytes accessed | tf_op | source)
XLA Modules:
  0.0 136.7 jit_solution(17135916624246357927)
XLA Ops:
  0.6 1.6 %prep.1 = bf16[4,112,256]{2,1,0:T(8,128)(2,1)} custom-call(bf16[16,1536]{1,0:T(8,128)(2,1)} %w_ref.1, s32[32,256]{1,0:T(8,128)} %bitcast.36, s32[2,32,256]{2,1,0:T(8,128)} %bitcast.35, s32[2,256]{1,0:T(2,128)} %actions_ref.1), custom_call_target="tpu_custom_call" | custom-call | bytes 524288 | tf_op jit(solution)/shard_map/prep/pallas_call | solution.py:81
  2.2 10.5 %all_to_all.25.came_ref = bf16[4,112,256]{2,1,0:T(8,128)(2,1)S(1)} all-to-all(bf16[4,112,256]{2,1,0:T(8,128)(2,1)} %prep.1), channel_id=1, replica_groups={{0,8,16,24},{32,40,48,56},{64,72,80,88},{96,104,112,120},{128,136,144,1..., dimensions={0} | all-to-all | bytes 458752 | tf_op jit(solution)/shard_map/all_to_all | solution.py:332
  12.7 1.0 copies.1
  13.8 14.9 %all-to-all-start.1 = ((bf16[16,64,384]{2,1,0:T(8,128)(2,1)}), bf16[16,64,384]{2,1,0:T(8,128)(2,1)S(1)}, u32[]{:S(2)}, u32[]{:S(2)}) async-start(bf16[16,64,384]{2,1,0:T(8,128)(2,1)} %copies.1), calls=%async_computation.1 | async-start | bytes 1572864 | tf_op jit(solution)/shard_map/all_to_all | solution.py:334
  28.8 4.4 %collective-permute-start.2 = (bf16[1152,128]{1,0:T(8,128)(2,1)S(1)}, bf16[1152,128]{1,0:T(8,128)(2,1)S(1)}, u32[]{:S(2)}, u32[]{:S(2)}) collective-permute-start(bf16[1152,128]{1,0:T(8,128)(2,1)S(1)} %get-tuple-element.9), channel_id=1, source_target_pairs={{0,6},{1,7},{2,0},{3,1},{4,2},{5,3},{6,4},{7,5},{8,14},{9,15},{10,... | collective-permute-start | bytes 884744 | tf_op jit(solution)/shard_map/ppermute | solution.py:37
  33.2 2.4 %collective-permute-start.1 = (bf16[1152,128]{1,0:T(8,128)(2,1)S(1)}, bf16[1152,128]{1,0:T(8,128)(2,1)S(1)}, u32[]{:S(2)}, u32[]{:S(2)}) collective-permute-start(bf16[1152,128]{1,0:T(8,128)(2,1)S(1)} %get-tuple-element.9), channel_id=1, source_target_pairs={{0,4},{1,5},{2,6},{3,7},{4,0},{5,1},{6,2},{7,3},{8,12},{9,13},{10,... | collective-permute-start | bytes 884744 | tf_op jit(solution)/shard_map/ppermute | solution.py:37
  35.6 2.5 %collective-permute-start = (bf16[1152,128]{1,0:T(8,128)(2,1)S(1)}, bf16[1152,128]{1,0:T(8,128)(2,1)S(1)}, u32[]{:S(2)}, u32[]{:S(2)}) collective-permute-start(bf16[1152,128]{1,0:T(8,128)(2,1)S(1)} %get-tuple-element.9), channel_id=1, source_target_pairs={{0,2},{1,3},{2,4},{3,5},{4,6},{5,7},{6,0},{7,1},{8,10},{9,11},{10,... | collective-permute-start | bytes 884744 | tf_op jit(solution)/shard_map/ppermute | solution.py:37
  38.2 4.3 %collective-permute-done.1 = bf16[1152,128]{1,0:T(8,128)(2,1)S(1)} collective-permute-done((bf16[1152,128]{1,0:T(8,128)(2,1)S(1)}, bf16[1152,128]{1,0:T(8,128)(2,1)S(1)}, u32[]{:S(2)}, u32[]{:S(2)}) %collective-permute-start.1) | collective-permute-done | bytes 294944 | tf_op jit(solution)/shard_map/ppermute | solution.py:37
  42.4 8.2 %collective-permute-done = bf16[1152,128]{1,0:T(8,128)(2,1)S(1)} collective-permute-done((bf16[1152,128]{1,0:T(8,128)(2,1)S(1)}, bf16[1152,128]{1,0:T(8,128)(2,1)S(1)}, u32[]{:S(2)}, u32[]{:S(2)}) %collective-permute-start) | collective-permute-done | bytes 294944 | tf_op jit(solution)/shard_map/ppermute | solution.py:37
  50.7 0.1 pad_maximum_fusion.mine_ref
  50.8 3.6 %collective-permute-start.3 = (bf16[4,1152,128]{2,1,0:T(8,128)(2,1)S(1)}, bf16[4,1152,128]{2,1,0:T(8,128)(2,1)S(1)}, u32[]{:S(2)}, u32[]{:S(2)}) collective-permute-start(bf16[4,1152,128]{2,1,0:T(8,128)(2,1)S(1)} %pad_maximum_fusion.mine_ref), channel_id=1, source_target_pairs={{0,1},{1,0},{2,3},{3,2},{4,5},{5,4},{6,7},{7,6},{8,9},{9,8},{10,11... | collective-permute-start | bytes 3538952 | tf_op jit(solution)/shard_map/ppermute | solution.py:42
  54.6 2.3 %collective-permute-done.3.other_ref = bf16[4,1152,128]{2,1,0:T(8,128)(2,1)S(1)} collective-permute-done((bf16[4,1152,128]{2,1,0:T(8,128)(2,1)S(1)}, bf16[4,1152,128]{2,1,0:T(8,128)(2,1)S(1)}, u32[]{:S(2)}, u32[]{:S(2)}) %collective-permute-start.3) | collective-permute-done | bytes 1179680 | tf_op jit(solution)/shard_map/ppermute | solution.py:42
  56.8 11.5 %features.1 = bf16[4,2,256,1024]{3,2,1,0:T(8,128)(2,1)} custom-call(s32[2]{0:T(128)S(1)} %pad_add_fusion.1.place_ref.me_ref, bf16[4,112,256]{2,1,0:T(8,128)(2,1)S(1)} %all_to_all.25.came_ref, bf16[80,2304]{1,0:T(8,128)(2,1)S(1)} %fusion.spread_ref, f32[1,1152]{1,0:T(1,128)S(1)} %fusion.10.target_ref, bf16[4,1152,128]{2,1,0:T(8,128)(2,1)S(1)} %pad_maximum_fusion.mine_ref, ...), custom_call_target="tpu_custom_call" | custom-call | flops 5435817984 | bytes 6553600 | tf_op jit(solution)/shard_map/features/pallas_call | solution.py:151
  68.3 5.7 %convolution_convert_fusion = bf16[2048,384]{1,0:T(8,128)(2,1)} fusion(bf16[2048,1024]{1,0:T(8,128)(2,1)} %bitcast.39, bf16[1024,384]{1,0:T(8,128)(2,1)S(1)} %bitcast.27), kind=kOutput, calls=%fused_computation | convolution fusion | flops 1611399168 | bytes 6553600 | tf_op jit(solution)/shard_map/dot_general | solution.py:340
  74.1 3.7 %all-to-all-start.2 = ((bf16[4,2,256,384]{3,2,1,0:T(8,128)(2,1)}), bf16[4,2,256,384]{3,2,1,0:T(8,128)(2,1)S(1)}, u32[]{:S(2)}, u32[]{:S(2)}) async-start(bf16[4,2,256,384]{3,2,1,0:T(8,128)(2,1)} %bitcast.25), calls=%async_computation.2 | async-start | bytes 3145728 | tf_op jit(solution)/shard_map/all_to_all | solution.py:342
  77.8 2.2 %collective-permute-start.6 = (bf16[1024,128]{1,0:T(8,128)(2,1)S(1)}, bf16[1024,128]{1,0:T(8,128)(2,1)S(1)}, u32[]{:S(2)}, u32[]{:S(2)}) collective-permute-start(bf16[1024,128]{1,0:T(8,128)(2,1)S(1)} %copy-done.1), channel_id=1, source_target_pairs={{0,6},{1,7},{2,0},{3,1},{4,2},{5,3},{6,4},{7,5},{8,14},{9,15},{10,... | collective-permute-start | bytes 786440 | tf_op jit(solution)/shard_map/ppermute | solution.py:37
  80.0 2.4 %collective-permute-start.5 = (bf16[1024,128]{1,0:T(8,128)(2,1)S(1)}, bf16[1024,128]{1,0:T(8,128)(2,1)S(1)}, u32[]{:S(2)}, u32[]{:S(2)}) collective-permute-start(bf16[1024,128]{1,0:T(8,128)(2,1)S(1)} %copy-done.1), channel_id=1, source_target_pairs={{0,4},{1,5},{2,6},{3,7},{4,0},{5,1},{6,2},{7,3},{8,12},{9,13},{10,... | collective-permute-start | bytes 786440 | tf_op jit(solution)/shard_map/ppermute | solution.py:37
  82.4 2.6 %collective-permute-start.4 = (bf16[1024,128]{1,0:T(8,128)(2,1)S(1)}, bf16[1024,128]{1,0:T(8,128)(2,1)S(1)}, u32[]{:S(2)}, u32[]{:S(2)}) collective-permute-start(bf16[1024,128]{1,0:T(8,128)(2,1)S(1)} %copy-done.1), channel_id=1, source_target_pairs={{0,2},{1,3},{2,4},{3,5},{4,6},{5,7},{6,0},{7,1},{8,10},{9,11},{10,... | collective-permute-start | bytes 786440 | tf_op jit(solution)/shard_map/ppermute | solution.py:37
  85.0 2.2 %collective-permute-done.6 = bf16[1024,128]{1,0:T(8,128)(2,1)S(1)} collective-permute-done((bf16[1024,128]{1,0:T(8,128)(2,1)S(1)}, bf16[1024,128]{1,0:T(8,128)(2,1)S(1)}, u32[]{:S(2)}, u32[]{:S(2)}) %collective-permute-start.6) | collective-permute-done | bytes 262176 | tf_op jit(solution)/shard_map/ppermute | solution.py:37
  87.2 1.4 %collective-permute-done.5 = bf16[1024,128]{1,0:T(8,128)(2,1)S(1)} collective-permute-done((bf16[1024,128]{1,0:T(8,128)(2,1)S(1)}, bf16[1024,128]{1,0:T(8,128)(2,1)S(1)}, u32[]{:S(2)}, u32[]{:S(2)}) %collective-permute-start.5) | collective-permute-done | bytes 262176 | tf_op jit(solution)/shard_map/ppermute | solution.py:37
  88.6 7.8 %collective-permute-done.4 = bf16[1024,128]{1,0:T(8,128)(2,1)S(1)} collective-permute-done((bf16[1024,128]{1,0:T(8,128)(2,1)S(1)}, bf16[1024,128]{1,0:T(8,128)(2,1)S(1)}, u32[]{:S(2)}, u32[]{:S(2)}) %collective-permute-start.4) | collective-permute-done | bytes 262176 | tf_op jit(solution)/shard_map/ppermute | solution.py:37
  96.4 0.1 pad_maximum_fusion.1.mine_ref
  96.5 3.2 %collective-permute-start.7 = (bf16[4,1024,128]{2,1,0:T(8,128)(2,1)S(1)}, bf16[4,1024,128]{2,1,0:T(8,128)(2,1)}, u32[]{:S(2)}, u32[]{:S(2)}) collective-permute-start(bf16[4,1024,128]{2,1,0:T(8,128)(2,1)S(1)} %pad_maximum_fusion.1.mine_ref), channel_id=1, source_target_pairs={{0,1},{1,0},{2,3},{3,2},{4,5},{5,4},{6,7},{7,6},{8,9},{9,8},{10,11... | collective-permute-start | bytes 3145736 | tf_op jit(solution)/shard_map/ppermute | solution.py:42
  99.8 4.5 %gru.1 = (bf16[256,512]{1,0:T(8,128)(2,1)S(1)}, bf16[8,2,32,1024]{3,2,1,0:T(8,128)(2,1)}) custom-call(bf16[256,512]{1,0:T(8,128)(2,1)} %deter_hbm.1, bf16[512,1536]{1,0:T(8,128)(2,1)} %bitcast.38, bf16[512,1024]{1,0:T(8,128)(2,1)} %w_in_hbm.1, bf16[4,2,256,384]{3,2,1,0:T(8,128)(2,1)S(1)} %all-to-all-done.2.f_ref), custom_call_target="tpu_custom_call" | custom-call | flops 1342177280 | bytes 5767168 | tf_op jit(solution)/shard_map/gru/pallas_call | solution.py:227
  104.3 3.7 %all-to-all-start.3 = ((bf16[8,64,1024]{2,1,0:T(8,128)(2,1)}), bf16[8,64,1024]{2,1,0:T(8,128)(2,1)S(1)}, u32[]{:S(2)}, u32[]{:S(2)}) async-start(bf16[8,64,1024]{2,1,0:T(8,128)(2,1)} %bitcast.26), calls=%async_computation.3 | async-start | bytes 2097152 | tf_op jit(solution)/shard_map/all_to_all | solution.py:355
  108.5 0.1 copy.14.mask_ref
  108.6 14.4 %all-to-all-done.3.parts_ref = bf16[8,64,1024]{2,1,0:T(8,128)(2,1)S(1)} async-done(((bf16[8,64,1024]{2,1,0:T(8,128)(2,1)}), bf16[8,64,1024]{2,1,0:T(8,128)(2,1)S(1)}, u32[]{:S(2)}, u32[]{:S(2)}) %all-to-all-start.3) | async-done | bytes 1048608 | tf_op jit(solution)/shard_map/all_to_all | solution.py:355
  123.1 4.0 %tail.1 = f32[8,8,128]{2,1,0:T(8,128)} custom-call(s32[2]{0:T(128)S(1)} %pad_add_fusion.1.place_ref.me_ref, bf16[8,64,1024]{2,1,0:T(8,128)(2,1)S(1)} %all-to-all-done.3.parts_ref, bf16[4,1024,128]{2,1,0:T(8,128)(2,1)S(1)} %pad_maximum_fusion.1.mine_ref, bf16[4,1024,128]{2,1,0:T(8,128)(2,1)} %collective-permute-done.7.other_ref, bf16[64,32]{1,0:T(8,128)(2,1)S(1)} %bitcast.24, ...), custom_call_target="tpu_custom_call" | custom-call | flops 134217728 | bytes 4194304 | tf_op jit(solution)/shard_map/tail/pallas_call | solution.py:297
  127.0 4.1 %all-to-all-start.4 = ((f32[8,8,128]{2,1,0:T(8,128)}), f32[8,8,128]{2,1,0:T(8,128)S(1)}, u32[]{:S(2)}, u32[]{:S(2)}) async-start(f32[8,8,128]{2,1,0:T(8,128)} %tail.1), calls=%async_computation.4 | async-start | bytes 65536 | tf_op jit(solution)/shard_map/all_to_all | solution.py:357
  131.2 0.8 broadcast_select_fusion
  132.0 3.9 %all-to-all-done.4 = f32[8,8,128]{2,1,0:T(8,128)S(1)} async-done(((f32[8,8,128]{2,1,0:T(8,128)}), f32[8,8,128]{2,1,0:T(8,128)S(1)}, u32[]{:S(2)}, u32[]{:S(2)}) %all-to-all-start.4) | async-done | bytes 32800 | tf_op jit(solution)/shard_map/all_to_all | solution.py:357
  136.0 0.7 reshape.121
  (31 shorter events, 0.8 us)
Async XLA Ops:
  2.2 26.5 %copy-start = (bf16[1024,128]{1,0:T(8,128)(2,1)S(1)}, bf16[1024,128]{1,0:T(8,128)(2,1)}, u32[]{:S(2)}) copy-start(bf16[1024,128]{1,0:T(8,128)(2,1)} %param.16) | copy-start | bytes 786436
  2.2 26.5 %copy-start.3 = (bf16[18,128]{1,0:T(8,128)(2,1)S(1)}, bf16[18,128]{1,0:T(8,128)(2,1)}, u32[]{:S(2)}) copy-start(bf16[18,128]{1,0:T(8,128)(2,1)} %param.17) | copy-start | bytes 13828
  13.8 54.5 %all-to-all-start.1 = ((bf16[16,64,384]{2,1,0:T(8,128)(2,1)}), bf16[16,64,384]{2,1,0:T(8,128)(2,1)S(1)}, u32[]{:S(2)}, u32[]{:S(2)}) async-start(bf16[16,64,384]{2,1,0:T(8,128)(2,1)} %copies.1), calls=%async_computation.1 | async-start | bytes 1572864 | tf_op jit(solution)/shard_map/all_to_all | solution.py:334
  28.8 9.4 %collective-permute-start.2 = (bf16[1152,128]{1,0:T(8,128)(2,1)S(1)}, bf16[1152,128]{1,0:T(8,128)(2,1)S(1)}, u32[]{:S(2)}, u32[]{:S(2)}) collective-permute-start(bf16[1152,128]{1,0:T(8,128)(2,1)S(1)} %get-tuple-element.9), channel_id=1, source_target_pairs={{0,6},{1,7},{2,0},{3,1},{4,2},{5,3},{6,4},{7,5},{8,14},{9,15},{10,... | collective-permute-start | bytes 884744 | tf_op jit(solution)/shard_map/ppermute | solution.py:37
  33.2 9.3 %collective-permute-start.1 = (bf16[1152,128]{1,0:T(8,128)(2,1)S(1)}, bf16[1152,128]{1,0:T(8,128)(2,1)S(1)}, u32[]{:S(2)}, u32[]{:S(2)}) collective-permute-start(bf16[1152,128]{1,0:T(8,128)(2,1)S(1)} %get-tuple-element.9), channel_id=1, source_target_pairs={{0,4},{1,5},{2,6},{3,7},{4,0},{5,1},{6,2},{7,3},{8,12},{9,13},{10,... | collective-permute-start | bytes 884744 | tf_op jit(solution)/shard_map/ppermute | solution.py:37
  35.6 15.0 %collective-permute-start = (bf16[1152,128]{1,0:T(8,128)(2,1)S(1)}, bf16[1152,128]{1,0:T(8,128)(2,1)S(1)}, u32[]{:S(2)}, u32[]{:S(2)}) collective-permute-start(bf16[1152,128]{1,0:T(8,128)(2,1)S(1)} %get-tuple-element.9), channel_id=1, source_target_pairs={{0,2},{1,3},{2,4},{3,5},{4,6},{5,7},{6,0},{7,1},{8,10},{9,11},{10,... | collective-permute-start | bytes 884744 | tf_op jit(solution)/shard_map/ppermute | solution.py:37
  50.8 6.0 %collective-permute-start.3 = (bf16[4,1152,128]{2,1,0:T(8,128)(2,1)S(1)}, bf16[4,1152,128]{2,1,0:T(8,128)(2,1)S(1)}, u32[]{:S(2)}, u32[]{:S(2)}) collective-permute-start(bf16[4,1152,128]{2,1,0:T(8,128)(2,1)S(1)} %pad_maximum_fusion.mine_ref), channel_id=1, source_target_pairs={{0,1},{1,0},{2,3},{3,2},{4,5},{5,4},{6,7},{7,6},{8,9},{9,8},{10,11... | collective-permute-start | bytes 3538952 | tf_op jit(solution)/shard_map/ppermute | solution.py:42
  74.1 3.7 %copy-start.1 = (bf16[1024,128]{1,0:T(8,128)(2,1)S(1)}, bf16[1024,128]{1,0:T(8,128)(2,1)}, u32[]{:S(2)}) copy-start(bf16[1024,128]{1,0:T(8,128)(2,1)} %param.21) | copy-start | bytes 786436
  74.1 25.7 %all-to-all-start.2 = ((bf16[4,2,256,384]{3,2,1,0:T(8,128)(2,1)}), bf16[4,2,256,384]{3,2,1,0:T(8,128)(2,1)S(1)}, u32[]{:S(2)}, u32[]{:S(2)}) async-start(bf16[4,2,256,384]{3,2,1,0:T(8,128)(2,1)} %bitcast.25), calls=%async_computation.2 | async-start | bytes 3145728 | tf_op jit(solution)/shard_map/all_to_all | solution.py:342
  77.8 9.4 %collective-permute-start.6 = (bf16[1024,128]{1,0:T(8,128)(2,1)S(1)}, bf16[1024,128]{1,0:T(8,128)(2,1)S(1)}, u32[]{:S(2)}, u32[]{:S(2)}) collective-permute-start(bf16[1024,128]{1,0:T(8,128)(2,1)S(1)} %copy-done.1), channel_id=1, source_target_pairs={{0,6},{1,7},{2,0},{3,1},{4,2},{5,3},{6,4},{7,5},{8,14},{9,15},{10,... | collective-permute-start | bytes 786440 | tf_op jit(solution)/shard_map/ppermute | solution.py:37
  80.0 8.6 %collective-permute-start.5 = (bf16[1024,128]{1,0:T(8,128)(2,1)S(1)}, bf16[1024,128]{1,0:T(8,128)(2,1)S(1)}, u32[]{:S(2)}, u32[]{:S(2)}) collective-permute-start(bf16[1024,128]{1,0:T(8,128)(2,1)S(1)} %copy-done.1), channel_id=1, source_target_pairs={{0,4},{1,5},{2,6},{3,7},{4,0},{5,1},{6,2},{7,3},{8,12},{9,13},{10,... | collective-permute-start | bytes 786440 | tf_op jit(solution)/shard_map/ppermute | solution.py:37
  82.4 14.0 %collective-permute-start.4 = (bf16[1024,128]{1,0:T(8,128)(2,1)S(1)}, bf16[1024,128]{1,0:T(8,128)(2,1)S(1)}, u32[]{:S(2)}, u32[]{:S(2)}) collective-permute-start(bf16[1024,128]{1,0:T(8,128)(2,1)S(1)} %copy-done.1), channel_id=1, source_target_pairs={{0,2},{1,3},{2,4},{3,5},{4,6},{5,7},{6,0},{7,1},{8,10},{9,11},{10,... | collective-permute-start | bytes 786440 | tf_op jit(solution)/shard_map/ppermute | solution.py:37
  96.5 12.1 %collective-permute-start.7 = (bf16[4,1024,128]{2,1,0:T(8,128)(2,1)S(1)}, bf16[4,1024,128]{2,1,0:T(8,128)(2,1)}, u32[]{:S(2)}, u32[]{:S(2)}) collective-permute-start(bf16[4,1024,128]{2,1,0:T(8,128)(2,1)S(1)} %pad_maximum_fusion.1.mine_ref), channel_id=1, source_target_pairs={{0,1},{1,0},{2,3},{3,2},{4,5},{5,4},{6,7},{7,6},{8,9},{9,8},{10,11... | collective-permute-start | bytes 3145736 | tf_op jit(solution)/shard_map/ppermute | solution.py:42
  104.3 3.7 %copy-start.4 = (s32[4]{0:T(128)S(1)}, s32[4]{0:T(128)}, u32[]{:S(2)}) copy-start(s32[4]{0:T(128)} %param.15) | copy-start | bytes 52
  104.3 3.8 %copy-start.2 = (s32[2,256,32]{1,2,0:T(8,128)S(1)}, s32[2,256,32]{1,2,0:T(8,128)}, u32[]{:S(2)}) copy-start(s32[2,256,32]{1,2,0:T(8,128)} %param.13) | copy-start | bytes 196612
  104.3 18.7 %all-to-all-start.3 = ((bf16[8,64,1024]{2,1,0:T(8,128)(2,1)}), bf16[8,64,1024]{2,1,0:T(8,128)(2,1)S(1)}, u32[]{:S(2)}, u32[]{:S(2)}) async-start(bf16[8,64,1024]{2,1,0:T(8,128)(2,1)} %bitcast.26), calls=%async_computation.3 | async-start | bytes 2097152 | tf_op jit(solution)/shard_map/all_to_all | solution.py:355
  127.0 8.8 %all-to-all-start.4 = ((f32[8,8,128]{2,1,0:T(8,128)}), f32[8,8,128]{2,1,0:T(8,128)S(1)}, u32[]{:S(2)}, u32[]{:S(2)}) async-start(f32[8,8,128]{2,1,0:T(8,128)} %tail.1), calls=%async_computation.4 | async-start | bytes 65536 | tf_op jit(solution)/shard_map/all_to_all | solution.py:357

commit v11 on v9

--- a/solution.py
+++ b/solution.py
@@ -51,8 +51,9 @@
 
 
 def tensor_gather(value):
-    mine = jnp.stack([value] + [x_shift(value, step) for step in range(1, NX)])
-    return mine, core_swap(mine)
+    pieces = [value] + [x_shift(value, step) for step in range(1, NX)]
+    mine = jnp.stack(pieces)
+    return mine, core_swap(mine), pieces[1]
 
 
 def silu(value):
@@ -97,7 +98,7 @@
     )(w_gate, latent, samples, actions)
 
 
-def copies_kernel(came_ref, out_hbm, one_ref, sems):
+def copies_kernel(came_ref, _, out_hbm, one_ref, sems):
     depth = one_ref.shape[0] // NY
     part = one_ref.shape[1] // 3
     for y in range(NY):
@@ -111,17 +112,17 @@
         copy.wait()
 
 
-def copies_call(came, n_z, depth, width):
+def copies_call(came, early, n_z, depth, width):
     return pl.pallas_call(
         copies_kernel,
-        in_specs=[pl.BlockSpec(memory_space=pltpu.VMEM)],
+        in_specs=[pl.BlockSpec(memory_space=pltpu.VMEM), pl.BlockSpec(memory_space=pl.ANY)],
         out_specs=pl.BlockSpec(memory_space=pltpu.HBM),
         out_shape=pltpu.HBM((n_z, NY * depth, width), jnp.bfloat16),
         scratch_shapes=[pltpu.VMEM((NY * depth, width), jnp.bfloat16), pltpu.SemaphoreType.DMA((n_z,))],
         compiler_params=pltpu.CompilerParams(vmem_limit_bytes=16 * MIB),
         cost_estimate=pl.CostEstimate(flops=0, bytes_accessed=4 * n_z * depth * width, transcendentals=0),
         name="copies",
-    )(came)
+    )(came, early)
 
 
 def features_kernel(place_ref, came_ref, spread_ref, target_ref, mine_ref, other_ref, out_ref, w_ref):
@@ -365,20 +366,20 @@
 
     sent = prep_call(w_gate, post_sample.T, samples.transpose(0, 2, 1), actions)
     came = lax.all_to_all(sent, "dp", 0, 0, axis_index_groups=y_groups(n_dp))
+    action_rows = jnp.pad(w_action, ((0, LANES - ACTIONS), (0, 0)))
+    mine, other, early = tensor_gather(jnp.concatenate([w_stoch, action_rows], axis=0))
+
     n_far = n_dp // NY // NEAR
-    held = copies_call(came, n_far, depth, w_gate.shape[1] // NY)
+    held = copies_call(came, early, n_far, depth, w_gate.shape[1] // NY)
     held = lax.all_to_all(held, "dp", 0, 0, axis_index_groups=far_groups(n_dp)).reshape(n_far * NY * depth, -1)
     gate = jnp.broadcast_to(held[None], (NEAR,) + held.shape)
     gate = lax.all_to_all(gate, "dp", 0, 0, axis_index_groups=near_groups(n_dp))
 
-    action_rows = jnp.pad(w_action, ((0, LANES - ACTIONS), (0, 0)))
-    mine, other = tensor_gather(jnp.concatenate([w_stoch, action_rows], axis=0))
-
     features = features_call(place, came, mine, other)
     sums = lax.all_to_all(gate_call(features, gate, n_far), "dp", 0, 0, axis_index_groups=y_groups(n_dp))
 
     w_out_late, _ = lax.optimization_barrier((w_prior_out, features))
-    out_mine, out_other = tensor_gather(w_out_late)
+    out_mine, out_other, _ = tensor_gather(w_out_late)
 
     positions = jnp.arange(STEPS, dtype=jnp.int32)
     valid_mask = (positions[None, :] < counts[:, None]).reshape(rows)

time: 139 us -> 142 us (1.022)
  starting transfers between devices: 54.4 us -> 59.9 us
  waiting for transfers between devices: 40.5 us -> 38 us
    ppermute x6, waiting for transfers between devices: 16.6 us -> 11.6 us  [x_shift(): return lax.ppermute(value, 'tensor', perm)]
    ppermute x2, starting transfers between devices: 5.98 us -> 9.84 us  [core_swap(): return lax.ppermute(value, 'tensor', perm)]
    all_to_all x1, waiting for transfers between devices: 3.24 us -> 5.83 us  [body(): lax.all_to_all(held, 'dp', 0, 0, axis_index_groups=far_groups(n_dp))]
    ppermute x6, starting transfers between devices: 18.2 us -> 19.8 us  [x_shift(): return lax.ppermute(value, 'tensor', perm)]
  transfers between devices with their start and end apart: 13 -> 13, of which waited for: 8 -> 7; matrix products, arithmetic and copies ran while one was open for 2% -> 2% of each run, Pallas kernels for 12% -> 13%
where the time goes in v11:
time: 142 us; the launch traced here: 141 us
  starting transfers between devices  59.9 us (42%)
  waiting for transfers between devices  38 us (27%)
  Pallas kernels  26.3 us (19%)
  blocking collectives  9.54 us (7%)
  local copies, waits for them, and re-layouts  4.27 us (3%)
  other arithmetic  2.54 us (2%)
    ppermute x6, starting transfers between devices, x_shift(): return lax.ppermute(value, 'tensor', perm)  19.8 us
    all_to_all x1, starting transfers between devices, body(): lax.all_to_all(held, 'dp', 0, 0, axis_index_groups=far_groups(n_dp))  14.8 us
    all_to_all x1, waiting for transfers between devices, body(): lax.all_to_all(partial.reshape(tensor_n, IMAG * share, UNITS), 'tensor',...  14.4 us
    ppermute x6, waiting for transfers between devices, x_shift(): return lax.ppermute(value, 'tensor', perm)  11.6 us
    pallas_call x1, Pallas kernels, features_call(): pl.pallas_call(features_kernel, grid=(NY,), in_specs=[pl.BlockSpec(memory...  11.5 us
    ppermute x2, starting transfers between devices, core_swap(): return lax.ppermute(value, 'tensor', perm)  9.84 us
    all_to_all x1, blocking collectives, body(): came = lax.all_to_all(sent, 'dp', 0, 0, axis_index_groups=y_groups(n_dp))  9.54 us
    all_to_all x1, waiting for transfers between devices, body(): lax.all_to_all(held, 'dp', 0, 0, axis_index_groups=far_groups(n_dp))  5.83 us
  transfers between devices with their start and end apart: 13, of which 7 were waited for; matrix products, arithmetic and copies ran while one was open for 2% of the time, Pallas kernels for 13%

profile of v11, /device:TPU:1, one launch (start us, length us, event | category | flops | bytes accessed | tf_op | source)
XLA Modules:
  0.0 141.3 jit_solution(2707772383365409032)
XLA Ops:
  0.6 1.0 fusion.15
  1.7 3.9 %collective-permute-start = (bf16[1152,128]{1,0:T(8,128)(2,1)S(1)}, bf16[1152,128]{1,0:T(8,128)(2,1)S(1)}, u32[]{:S(2)}, u32[]{:S(2)}) collective-permute-start(bf16[1152,128]{1,0:T(8,128)(2,1)S(1)} %get-tuple-element.9), channel_id=1, source_target_pairs={{0,2},{1,3},{2,4},{3,5},{4,6},{5,7},{6,0},{7,1},{8,10},{9,11},{10,... | collective-permute-start | bytes 884744 | tf_op jit(solution)/shard_map/ppermute | solution.py:45
  5.6 1.6 %prep.1 = bf16[4,112,256]{2,1,0:T(8,128)(2,1)} custom-call(bf16[16,1536]{1,0:T(8,128)(2,1)} %w_ref.1, s32[32,256]{1,0:T(8,128)} %bitcast.31, s32[2,32,256]{2,1,0:T(8,128)} %bitcast.30, s32[2,256]{1,0:T(2,128)} %actions_ref.1), custom_call_target="tpu_custom_call" | custom-call | bytes 524288 | tf_op jit(solution)/shard_map/prep/pallas_call | solution.py:90
  7.2 9.5 %all_to_all.30.came_ref = bf16[4,112,256]{2,1,0:T(8,128)(2,1)S(1)} all-to-all(bf16[4,112,256]{2,1,0:T(8,128)(2,1)} %prep.1), channel_id=1, replica_groups={{0,8,16,24},{32,40,48,56},{64,72,80,88},{96,104,112,120},{128,136,144,1..., dimensions={0} | all-to-all | bytes 458752 | tf_op jit(solution)/shard_map/all_to_all | solution.py:368
  16.8 0.7 copies.1
  17.5 14.8 %all-to-all-start.1 = ((bf16[4,64,384]{2,1,0:T(8,128)(2,1)}), bf16[4,64,384]{2,1,0:T(8,128)(2,1)S(1)}, u32[]{:S(2)}, u32[]{:S(2)}) async-start(bf16[4,64,384]{2,1,0:T(8,128)(2,1)} %copies.1), calls=%async_computation.1 | async-start | bytes 393216 | tf_op jit(solution)/shard_map/all_to_all | solution.py:374
  32.3 3.4 %collective-permute-start.2 = (bf16[1152,128]{1,0:T(8,128)(2,1)S(1)}, bf16[1152,128]{1,0:T(8,128)(2,1)S(1)}, u32[]{:S(2)}, u32[]{:S(2)}) collective-permute-start(bf16[1152,128]{1,0:T(8,128)(2,1)S(1)} %get-tuple-element.9), channel_id=1, source_target_pairs={{0,6},{1,7},{2,0},{3,1},{4,2},{5,3},{6,4},{7,5},{8,14},{9,15},{10,... | collective-permute-start | bytes 884744 | tf_op jit(solution)/shard_map/ppermute | solution.py:45
  35.7 3.4 %collective-permute-start.1 = (bf16[1152,128]{1,0:T(8,128)(2,1)S(1)}, bf16[1152,128]{1,0:T(8,128)(2,1)S(1)}, u32[]{:S(2)}, u32[]{:S(2)}) collective-permute-start(bf16[1152,128]{1,0:T(8,128)(2,1)S(1)} %get-tuple-element.9), channel_id=1, source_target_pairs={{0,4},{1,5},{2,6},{3,7},{4,0},{5,1},{6,2},{7,3},{8,12},{9,13},{10,... | collective-permute-start | bytes 884744 | tf_op jit(solution)/shard_map/ppermute | solution.py:45
  39.1 5.8 %all-to-all-done.1 = bf16[4,64,384]{2,1,0:T(8,128)(2,1)S(1)} async-done(((bf16[4,64,384]{2,1,0:T(8,128)(2,1)}), bf16[4,64,384]{2,1,0:T(8,128)(2,1)S(1)}, u32[]{:S(2)}, u32[]{:S(2)}) %all-to-all-start.1) | async-done | bytes 196640 | tf_op jit(solution)/shard_map/all_to_all | solution.py:374
  45.0 0.9 broadcast_in_dim.41
  45.9 4.0 %all-to-all-start.2 = ((bf16[4,256,384]{2,1,0:T(8,128)(2,1)}), bf16[4,256,384]{2,1,0:T(8,128)(2,1)S(1)}, u32[]{:S(2)}, u32[]{:S(2)}) async-start(bf16[4,256,384]{2,1,0:T(8,128)(2,1)} %broadcast_in_dim.41), calls=%async_computation.2 | async-start | bytes 1572864 | tf_op jit(solution)/shard_map/all_to_all | solution.py:376
  50.0 7.4 %collective-permute-start.3 = (bf16[4,1152,128]{2,1,0:T(8,128)(2,1)S(1)}, bf16[4,1152,128]{2,1,0:T(8,128)(2,1)S(1)}, u32[]{:S(2)}, u32[]{:S(2)}) collective-permute-start(bf16[4,1152,128]{2,1,0:T(8,128)(2,1)S(1)} %pad_maximum_fusion.mine_ref), channel_id=1, source_target_pairs={{0,1},{1,0},{2,3},{3,2},{4,5},{5,4},{6,7},{7,6},{8,9},{9,8},{10,11... | collective-permute-start | bytes 3538952 | tf_op jit(solution)/shard_map/ppermute | solution.py:50
  57.7 2.3 %collective-permute-done.3.other_ref = bf16[4,1152,128]{2,1,0:T(8,128)(2,1)S(1)} collective-permute-done((bf16[4,1152,128]{2,1,0:T(8,128)(2,1)S(1)}, bf16[4,1152,128]{2,1,0:T(8,128)(2,1)S(1)}, u32[]{:S(2)}, u32[]{:S(2)}) %collective-permute-start.3) | collective-permute-done | bytes 1179680 | tf_op jit(solution)/shard_map/ppermute | solution.py:50
  59.9 11.5 %features.1.features_ref = bf16[2,4,256,1024]{3,2,1,0:T(8,128)(2,1)} custom-call(s32[2]{0:T(128)S(1)} %pad_add_fusion.1.place_ref.me_ref, bf16[4,112,256]{2,1,0:T(8,128)(2,1)S(1)} %all_to_all.30.came_ref, bf16[80,2304]{1,0:T(8,128)(2,1)S(1)} %fusion.spread_ref, f32[1,1152]{1,0:T(1,128)S(1)} %fusion.10.target_ref, ...), custom_call_target="tpu_custom_call" | custom-call | flops 6522981376 | bytes 6553600 | tf_op jit(solution)/shard_map/features/pallas_call | solution.py:160
  71.4 2.2 %copy-done = bf16[2,4,256,1024]{3,2,1,0:T(8,128)(2,1)S(1)} copy-done((bf16[2,4,256,1024]{3,2,1,0:T(8,128)(2,1)S(1)}, bf16[2,4,256,1024]{3,2,1,0:T(8,128)(2,1)}, u32[]{:S(2)}) %copy-start) | copy-done | bytes 4194328
  73.6 4.0 %gate.1 = bf16[4,2,256,384]{3,2,1,0:T(8,128)(2,1)} custom-call(bf16[2,4,256,1024]{3,2,1,0:T(8,128)(2,1)S(1)} %copy-done, bf16[4,256,384]{2,1,0:T(8,128)(2,1)S(1)} %all-to-all-done.2.gate_ref), custom_call_target="tpu_custom_call" | custom-call | flops 1610612736 | bytes 6553600 | tf_op jit(solution)/shard_map/gate/pallas_call | solution.py:201
  77.6 3.7 %all-to-all-start.3 = ((bf16[4,2,256,384]{3,2,1,0:T(8,128)(2,1)}), bf16[4,2,256,384]{3,2,1,0:T(8,128)(2,1)S(1)}, u32[]{:S(2)}, u32[]{:S(2)}) async-start(bf16[4,2,256,384]{3,2,1,0:T(8,128)(2,1)} %gate.1), calls=%async_computation.3 | async-start | bytes 3145728 | tf_op jit(solution)/shard_map/all_to_all | solution.py:379
  81.3 3.4 %collective-permute-start.6 = (bf16[1024,128]{1,0:T(8,128)(2,1)S(1)}, bf16[1024,128]{1,0:T(8,128)(2,1)S(1)}, u32[]{:S(2)}, u32[]{:S(2)}) collective-permute-start(bf16[1024,128]{1,0:T(8,128)(2,1)S(1)} %copy-done.1), channel_id=1, source_target_pairs={{0,6},{1,7},{2,0},{3,1},{4,2},{5,3},{6,4},{7,5},{8,14},{9,15},{10,... | collective-permute-start | bytes 786440 | tf_op jit(solution)/shard_map/ppermute | solution.py:45
  84.7 3.4 %collective-permute-start.5 = (bf16[1024,128]{1,0:T(8,128)(2,1)S(1)}, bf16[1024,128]{1,0:T(8,128)(2,1)S(1)}, u32[]{:S(2)}, u32[]{:S(2)}) collective-permute-start(bf16[1024,128]{1,0:T(8,128)(2,1)S(1)} %copy-done.1), channel_id=1, source_target_pairs={{0,4},{1,5},{2,6},{3,7},{4,0},{5,1},{6,2},{7,3},{8,12},{9,13},{10,... | collective-permute-start | bytes 786440 | tf_op jit(solution)/shard_map/ppermute | solution.py:45
  88.1 2.2 %collective-permute-start.4 = (bf16[1024,128]{1,0:T(8,128)(2,1)S(1)}, bf16[1024,128]{1,0:T(8,128)(2,1)S(1)}, u32[]{:S(2)}, u32[]{:S(2)}) collective-permute-start(bf16[1024,128]{1,0:T(8,128)(2,1)S(1)} %copy-done.1), channel_id=1, source_target_pairs={{0,2},{1,3},{2,4},{3,5},{4,6},{5,7},{6,0},{7,1},{8,10},{9,11},{10,... | collective-permute-start | bytes 786440 | tf_op jit(solution)/shard_map/ppermute | solution.py:45
  90.3 0.3 collective-permute-done.6
  90.7 4.6 %collective-permute-done.5 = bf16[1024,128]{1,0:T(8,128)(2,1)S(1)} collective-permute-done((bf16[1024,128]{1,0:T(8,128)(2,1)S(1)}, bf16[1024,128]{1,0:T(8,128)(2,1)S(1)}, u32[]{:S(2)}, u32[]{:S(2)}) %collective-permute-start.5) | collective-permute-done | bytes 262176 | tf_op jit(solution)/shard_map/ppermute | solution.py:45
  95.3 6.6 %collective-permute-done.4 = bf16[1024,128]{1,0:T(8,128)(2,1)S(1)} collective-permute-done((bf16[1024,128]{1,0:T(8,128)(2,1)S(1)}, bf16[1024,128]{1,0:T(8,128)(2,1)S(1)}, u32[]{:S(2)}, u32[]{:S(2)}) %collective-permute-start.4) | collective-permute-done | bytes 262176 | tf_op jit(solution)/shard_map/ppermute | solution.py:45
  102.0 2.4 %collective-permute-start.7 = (bf16[4,1024,128]{2,1,0:T(8,128)(2,1)S(1)}, bf16[4,1024,128]{2,1,0:T(8,128)(2,1)}, u32[]{:S(2)}, u32[]{:S(2)}) collective-permute-start(bf16[4,1024,128]{2,1,0:T(8,128)(2,1)S(1)} %pad_maximum_fusion.1.mine_ref), channel_id=1, source_target_pairs={{0,1},{1,0},{2,3},{3,2},{4,5},{5,4},{6,7},{7,6},{8,9},{9,8},{10,11... | collective-permute-start | bytes 3145736 | tf_op jit(solution)/shard_map/ppermute | solution.py:50
  104.5 4.6 %gru.1 = (bf16[256,512]{1,0:T(8,128)(2,1)S(1)}, bf16[8,2,32,1024]{3,2,1,0:T(8,128)(2,1)}) custom-call(bf16[256,512]{1,0:T(8,128)(2,1)} %deter_hbm.1, bf16[512,1536]{1,0:T(8,128)(2,1)} %bitcast.33, bf16[512,1024]{1,0:T(8,128)(2,1)} %w_in_hbm.1, bf16[4,2,256,384]{3,2,1,0:T(8,128)(2,1)S(1)} %all-to-all-done.3.f_ref), custom_call_target="tpu_custom_call" | custom-call | flops 1342177280 | bytes 5767168 | tf_op jit(solution)/shard_map/gru/pallas_call | solution.py:265
  109.1 3.7 %all-to-all-start.4 = ((bf16[8,64,1024]{2,1,0:T(8,128)(2,1)}), bf16[8,64,1024]{2,1,0:T(8,128)(2,1)S(1)}, u32[]{:S(2)}, u32[]{:S(2)}) async-start(bf16[8,64,1024]{2,1,0:T(8,128)(2,1)} %bitcast.22), calls=%async_computation.4 | async-start | bytes 2097152 | tf_op jit(solution)/shard_map/all_to_all | solution.py:392
  113.4 14.4 %all-to-all-done.4.parts_ref = bf16[8,64,1024]{2,1,0:T(8,128)(2,1)S(1)} async-done(((bf16[8,64,1024]{2,1,0:T(8,128)(2,1)}), bf16[8,64,1024]{2,1,0:T(8,128)(2,1)S(1)}, u32[]{:S(2)}, u32[]{:S(2)}) %all-to-all-start.4) | async-done | bytes 1048608 | tf_op jit(solution)/shard_map/all_to_all | solution.py:392
  127.8 3.9 %tail.1 = f32[8,8,128]{2,1,0:T(8,128)} custom-call(s32[2]{0:T(128)S(1)} %pad_add_fusion.1.place_ref.me_ref, bf16[8,64,1024]{2,1,0:T(8,128)(2,1)S(1)} %all-to-all-done.4.parts_ref, bf16[4,1024,128]{2,1,0:T(8,128)(2,1)S(1)} %pad_maximum_fusion.1.mine_ref, bf16[4,1024,128]{2,1,0:T(8,128)(2,1)} %collective-permute-done.7.other_ref, bf16[64,32]{1,0:T(8,128)(2,1)S(1)} %bitcast.21, ...), custom_call_target="tpu_custom_call" | custom-call | flops 134217728 | bytes 4194304 | tf_op jit(solution)/shard_map/tail/pallas_call | solution.py:333
  131.7 4.1 %all-to-all-start.5 = ((f32[8,8,128]{2,1,0:T(8,128)}), f32[8,8,128]{2,1,0:T(8,128)S(1)}, u32[]{:S(2)}, u32[]{:S(2)}) async-start(f32[8,8,128]{2,1,0:T(8,128)} %tail.1), calls=%async_computation.5 | async-start | bytes 65536 | tf_op jit(solution)/shard_map/all_to_all | solution.py:394
  135.8 0.8 broadcast_select_fusion
  136.6 3.9 %all-to-all-done.5 = f32[8,8,128]{2,1,0:T(8,128)S(1)} async-done(((f32[8,8,128]{2,1,0:T(8,128)}), f32[8,8,128]{2,1,0:T(8,128)S(1)}, u32[]{:S(2)}, u32[]{:S(2)}) %all-to-all-start.5) | async-done | bytes 32800 | tf_op jit(solution)/shard_map/all_to_all | solution.py:394
  140.7 0.7 reshape.110
  (32 shorter events, 1.2 us)
Async XLA Ops:
  1.7 15.1 %collective-permute-start = (bf16[1152,128]{1,0:T(8,128)(2,1)S(1)}, bf16[1152,128]{1,0:T(8,128)(2,1)S(1)}, u32[]{:S(2)}, u32[]{:S(2)}) collective-permute-start(bf16[1152,128]{1,0:T(8,128)(2,1)S(1)} %get-tuple-element.9), channel_id=1, source_target_pairs={{0,2},{1,3},{2,4},{3,5},{4,6},{5,7},{6,0},{7,1},{8,10},{9,11},{10,... | collective-permute-start | bytes 884744 | tf_op jit(solution)/shard_map/ppermute | solution.py:45
  17.5 27.5 %all-to-all-start.1 = ((bf16[4,64,384]{2,1,0:T(8,128)(2,1)}), bf16[4,64,384]{2,1,0:T(8,128)(2,1)S(1)}, u32[]{:S(2)}, u32[]{:S(2)}) async-start(bf16[4,64,384]{2,1,0:T(8,128)(2,1)} %copies.1), calls=%async_computation.1 | async-start | bytes 393216 | tf_op jit(solution)/shard_map/all_to_all | solution.py:374
  32.3 17.6 %collective-permute-start.2 = (bf16[1152,128]{1,0:T(8,128)(2,1)S(1)}, bf16[1152,128]{1,0:T(8,128)(2,1)S(1)}, u32[]{:S(2)}, u32[]{:S(2)}) collective-permute-start(bf16[1152,128]{1,0:T(8,128)(2,1)S(1)} %get-tuple-element.9), channel_id=1, source_target_pairs={{0,6},{1,7},{2,0},{3,1},{4,2},{5,3},{6,4},{7,5},{8,14},{9,15},{10,... | collective-permute-start | bytes 884744 | tf_op jit(solution)/shard_map/ppermute | solution.py:45
  35.7 14.2 %collective-permute-start.1 = (bf16[1152,128]{1,0:T(8,128)(2,1)S(1)}, bf16[1152,128]{1,0:T(8,128)(2,1)S(1)}, u32[]{:S(2)}, u32[]{:S(2)}) collective-permute-start(bf16[1152,128]{1,0:T(8,128)(2,1)S(1)} %get-tuple-element.9), channel_id=1, source_target_pairs={{0,4},{1,5},{2,6},{3,7},{4,0},{5,1},{6,2},{7,3},{8,12},{9,13},{10,... | collective-permute-start | bytes 884744 | tf_op jit(solution)/shard_map/ppermute | solution.py:45
  45.9 25.5 %all-to-all-start.2 = ((bf16[4,256,384]{2,1,0:T(8,128)(2,1)}), bf16[4,256,384]{2,1,0:T(8,128)(2,1)S(1)}, u32[]{:S(2)}, u32[]{:S(2)}) async-start(bf16[4,256,384]{2,1,0:T(8,128)(2,1)} %broadcast_in_dim.41), calls=%async_computation.2 | async-start | bytes 1572864 | tf_op jit(solution)/shard_map/all_to_all | solution.py:376
  50.0 9.9 %collective-permute-start.3 = (bf16[4,1152,128]{2,1,0:T(8,128)(2,1)S(1)}, bf16[4,1152,128]{2,1,0:T(8,128)(2,1)S(1)}, u32[]{:S(2)}, u32[]{:S(2)}) collective-permute-start(bf16[4,1152,128]{2,1,0:T(8,128)(2,1)S(1)} %pad_maximum_fusion.mine_ref), channel_id=1, source_target_pairs={{0,1},{1,0},{2,3},{3,2},{4,5},{5,4},{6,7},{7,6},{8,9},{9,8},{10,11... | collective-permute-start | bytes 3538952 | tf_op jit(solution)/shard_map/ppermute | solution.py:50
  71.4 2.2 %copy-start = (bf16[2,4,256,1024]{3,2,1,0:T(8,128)(2,1)S(1)}, bf16[2,4,256,1024]{3,2,1,0:T(8,128)(2,1)}, u32[]{:S(2)}) copy-start(bf16[2,4,256,1024]{3,2,1,0:T(8,128)(2,1)} %features.1.features_ref) | copy-start | bytes 12582916
  77.6 3.7 %copy-start.1 = (bf16[1024,128]{1,0:T(8,128)(2,1)S(1)}, bf16[1024,128]{1,0:T(8,128)(2,1)}, u32[]{:S(2)}) copy-start(bf16[1024,128]{1,0:T(8,128)(2,1)} %param.21) | copy-start | bytes 786436
  77.6 26.9 %all-to-all-start.3 = ((bf16[4,2,256,384]{3,2,1,0:T(8,128)(2,1)}), bf16[4,2,256,384]{3,2,1,0:T(8,128)(2,1)S(1)}, u32[]{:S(2)}, u32[]{:S(2)}) async-start(bf16[4,2,256,384]{3,2,1,0:T(8,128)(2,1)} %gate.1), calls=%async_computation.3 | async-start | bytes 3145728 | tf_op jit(solution)/shard_map/all_to_all | solution.py:379
  81.3 9.4 %collective-permute-start.6 = (bf16[1024,128]{1,0:T(8,128)(2,1)S(1)}, bf16[1024,128]{1,0:T(8,128)(2,1)S(1)}, u32[]{:S(2)}, u32[]{:S(2)}) collective-permute-start(bf16[1024,128]{1,0:T(8,128)(2,1)S(1)} %copy-done.1), channel_id=1, source_target_pairs={{0,6},{1,7},{2,0},{3,1},{4,2},{5,3},{6,4},{7,5},{8,14},{9,15},{10,... | collective-permute-start | bytes 786440 | tf_op jit(solution)/shard_map/ppermute | solution.py:45
  84.7 10.6 %collective-permute-start.5 = (bf16[1024,128]{1,0:T(8,128)(2,1)S(1)}, bf16[1024,128]{1,0:T(8,128)(2,1)S(1)}, u32[]{:S(2)}, u32[]{:S(2)}) collective-permute-start(bf16[1024,128]{1,0:T(8,128)(2,1)S(1)} %copy-done.1), channel_id=1, source_target_pairs={{0,4},{1,5},{2,6},{3,7},{4,0},{5,1},{6,2},{7,3},{8,12},{9,13},{10,... | collective-permute-start | bytes 786440 | tf_op jit(solution)/shard_map/ppermute | solution.py:45
  88.1 13.8 %collective-permute-start.4 = (bf16[1024,128]{1,0:T(8,128)(2,1)S(1)}, bf16[1024,128]{1,0:T(8,128)(2,1)S(1)}, u32[]{:S(2)}, u32[]{:S(2)}) collective-permute-start(bf16[1024,128]{1,0:T(8,128)(2,1)S(1)} %copy-done.1), channel_id=1, source_target_pairs={{0,2},{1,3},{2,4},{3,5},{4,6},{5,7},{6,0},{7,1},{8,10},{9,11},{10,... | collective-permute-start | bytes 786440 | tf_op jit(solution)/shard_map/ppermute | solution.py:45
  102.0 11.3 %collective-permute-start.7 = (bf16[4,1024,128]{2,1,0:T(8,128)(2,1)S(1)}, bf16[4,1024,128]{2,1,0:T(8,128)(2,1)}, u32[]{:S(2)}, u32[]{:S(2)}) collective-permute-start(bf16[4,1024,128]{2,1,0:T(8,128)(2,1)S(1)} %pad_maximum_fusion.1.mine_ref), channel_id=1, source_target_pairs={{0,1},{1,0},{2,3},{3,2},{4,5},{5,4},{6,7},{7,6},{8,9},{9,8},{10,11... | collective-permute-start | bytes 3145736 | tf_op jit(solution)/shard_map/ppermute | solution.py:50
  109.1 3.7 %copy-start.3 = (s32[4]{0:T(128)S(1)}, s32[4]{0:T(128)}, u32[]{:S(2)}) copy-start(s32[4]{0:T(128)} %param.15) | copy-start | bytes 52
  109.1 3.8 %copy-start.2 = (s32[2,256,32]{1,2,0:T(8,128)S(1)}, s32[2,256,32]{1,2,0:T(8,128)}, u32[]{:S(2)}) copy-start(s32[2,256,32]{1,2,0:T(8,128)} %param.13) | copy-start | bytes 196612
  109.1 18.7 %all-to-all-start.4 = ((bf16[8,64,1024]{2,1,0:T(8,128)(2,1)}), bf16[8,64,1024]{2,1,0:T(8,128)(2,1)S(1)}, u32[]{:S(2)}, u32[]{:S(2)}) async-start(bf16[8,64,1024]{2,1,0:T(8,128)(2,1)} %bitcast.22), calls=%async_computation.4 | async-start | bytes 2097152 | tf_op jit(solution)/shard_map/all_to_all | solution.py:392
  131.7 8.8 %all-to-all-start.5 = ((f32[8,8,128]{2,1,0:T(8,128)}), f32[8,8,128]{2,1,0:T(8,128)S(1)}, u32[]{:S(2)}, u32[]{:S(2)}) async-start(f32[8,8,128]{2,1,0:T(8,128)} %tail.1), calls=%async_computation.5 | async-start | bytes 65536 | tf_op jit(solution)/shard_map/all_to_all | solution.py:394

commit v12 on v7

--- a/solution.py
+++ b/solution.py
@@ -173,12 +173,12 @@
 
 
 def gru_kernel(
-    deter_hbm, w_rec_hbm, w_in_hbm, f_ref, new_ref, prior_hbm, deter_ref, w_rec_ref, w_in_ref, mid_ref, prior_ref, sems
+    me_ref, deter_hbm, w_rec_hbm, w_in_hbm, f_ref, new_ref, keep_hbm, send_hbm, deter_ref, w_rec_ref, w_in_ref, mid_ref, prior_ref, sems
 ):
     rows, bw = deter_ref.shape
     part = bw // NY
     pairs = [(deter_hbm, deter_ref), (w_rec_hbm, w_rec_ref), (w_in_hbm, w_in_ref)]
-    pairs += [(prior_ref.at[:, k], prior_hbm.at[:, k]) for k in range(IMAG)]
+    pairs += [(prior_ref.at[i, :, k], out.at[:, k]) for k in range(IMAG) for i, out in enumerate((keep_hbm, send_hbm))]
     copies = [pltpu.make_async_copy(src, dst, sems.at[i]) for i, (src, dst) in enumerate(pairs)]
     for copy in copies[:3]:
         copy.start()
@@ -204,30 +204,32 @@
         if k == 0:
             copies[2].wait()
         prior = jnp.dot(next_ref[...], w_in_ref[...], preferred_element_type=jnp.float32).astype(jnp.bfloat16)
-        share = prior_ref.shape[2]
-        for j in range(prior_ref.shape[0]):
-            prior_ref[j, k] = prior[j * share : (j + 1) * share]
-        copies[3 + k].start()
-    for k in range(IMAG):
-        copies[3 + k].wait()
-
-
-def gru_call(deter, w_rec, w_in, sums, tensor_n):
+        share = prior_ref.shape[3]
+        for j in range(NX * NC):
+            other = lax.rem(me_ref[1] + j % NC, NC)
+            prior_ref[other, j // NC, k] = prior[j * share : (j + 1) * share]
+        for i in range(NC):
+            copies[3 + NC * k + i].start()
+    for copy in copies[3:]:
+        copy.wait()
+
+
+def gru_call(place, deter, w_rec, w_in, sums):
     rows, bw = deter.shape
     hbm, vmem = pl.BlockSpec(memory_space=pltpu.HBM), pl.BlockSpec(memory_space=pltpu.VMEM)
-    prior = (tensor_n, IMAG, rows // tensor_n, w_in.shape[1])
+    prior = (NX, IMAG, rows // (NX * NC), w_in.shape[1])
     return pl.pallas_call(
         gru_kernel,
-        in_specs=[hbm] * 3 + [vmem],
-        out_specs=[vmem, hbm],
-        out_shape=[jax.ShapeDtypeStruct((rows, bw), jnp.bfloat16), pltpu.HBM(prior, jnp.bfloat16)],
+        in_specs=[pl.BlockSpec(memory_space=pltpu.SMEM)] + [hbm] * 3 + [vmem],
+        out_specs=[vmem, hbm, hbm],
+        out_shape=[jax.ShapeDtypeStruct((rows, bw), jnp.bfloat16), pltpu.HBM(prior, jnp.bfloat16), pltpu.HBM(prior, jnp.bfloat16)],
         scratch_shapes=[
             pltpu.VMEM(deter.shape, jnp.bfloat16),
             pltpu.VMEM(w_rec.shape, jnp.bfloat16),
             pltpu.VMEM(w_in.shape, jnp.bfloat16),
             pltpu.VMEM((rows, bw), jnp.bfloat16),
-            pltpu.VMEM(prior, jnp.bfloat16),
-            pltpu.SemaphoreType.DMA((3 + IMAG,)),
+            pltpu.VMEM((NC,) + prior, jnp.bfloat16),
+            pltpu.SemaphoreType.DMA((3 + NC * IMAG,)),
         ],
         compiler_params=pltpu.CompilerParams(vmem_limit_bytes=24 * MIB),
         cost_estimate=pl.CostEstimate(
@@ -236,7 +238,7 @@
             transcendentals=6 * rows * bw,
         ),
         name="gru",
-    )(*[pltpu.with_memory_space_constraint(value, pltpu.HBM) for value in (deter, w_rec, w_in)], sums)
+    )(place, *[pltpu.with_memory_space_constraint(value, pltpu.HBM) for value in (deter, w_rec, w_in)], sums)
 
 
 def tail_kernel(me_ref, parts_ref, mine_ref, other_ref, picked_ref, var_ref, mask_ref, log_ref):
@@ -280,7 +282,7 @@
 
 
 def tail_call(place, parts, mine, other, picked, mask):
-    tensor_n, rows = parts.shape[:2]
+    rows = parts.shape[1]
     lane = jnp.arange(LAT, dtype=jnp.int32)
     var_of = (jnp.arange(STOCH, dtype=jnp.int32)[:, None] == lane[None, :] // CLASSES).astype(jnp.bfloat16)
     vmem = pl.BlockSpec(memory_space=pltpu.VMEM)
@@ -288,7 +290,7 @@
         tail_kernel,
         in_specs=[pl.BlockSpec(memory_space=pltpu.SMEM)] + [vmem] * 6,
         out_specs=vmem,
-        out_shape=jax.ShapeDtypeStruct((tensor_n, 8, LANES), jnp.float32),
+        out_shape=jax.ShapeDtypeStruct((NX * NC, 8, LANES), jnp.float32),
         compiler_params=pltpu.CompilerParams(vmem_limit_bytes=32 * MIB),
         cost_estimate=pl.CostEstimate(
             flops=2 * rows * UNITS * LAT, bytes_accessed=8 * mine.size, transcendentals=4 * rows * LAT
@@ -341,8 +343,10 @@
     picked = lax.dynamic_slice_in_dim(samples, me * share, share, 1)
     picked = picked.reshape(IMAG * share, STOCH).astype(jnp.bfloat16)
 
-    deter, partial = gru_call(post_deter, w_rec[0], w_prior_in, sums, tensor_n)
-    parts = lax.all_to_all(partial.reshape(tensor_n, IMAG * share, UNITS), "tensor", 0, 0)
+    deter, keep, send = gru_call(place, post_deter, w_rec[0], w_prior_in, sums)
+    pair = (keep.astype(jnp.float32) + core_swap(send).astype(jnp.float32)).astype(jnp.bfloat16)
+    x_groups = [list(range(core, tensor_n, NC)) for core in range(NC)]
+    parts = lax.all_to_all(pair.reshape(NX, IMAG * share, UNITS), "tensor", 0, 0, axis_index_groups=x_groups)
     logs = tail_call(place, parts, out_mine, out_other, picked, my_mask)
     logs = lax.all_to_all(logs, "tensor", 0, 0)[:, 0, : IMAG * share]
     log_prob = logs.reshape(tensor_n, IMAG, share).transpose(1, 0, 2).reshape(IMAG, rows)

time: 137 us -> 138 us (level)
  waiting for transfers between devices: 44.5 us -> 40.6 us
  starting transfers between devices: 49.7 us -> 51.9 us
  other arithmetic: 1.54 us -> 3.57 us
    all_to_all x1, waiting for transfers between devices: 0.01 us -> 13.2 us  [body(): sums = lax.all_to_all(total, 'dp', 0, 0, axis_index_groups=y_groups(n_dp))]
    ppermute x6, waiting for transfers between devices: 23.9 us -> 12.5 us  [x_shift(): return lax.ppermute(value, 'tensor', perm)]
    all_to_all x1, waiting for transfers between devices: 14.4 us -> 8.74 us  [body(): lax.all_to_all(pair.reshape(NX, IMAG * share, UNITS), 'tensor', 0, 0, axi...]
    ppermute x2 -> x3, starting transfers between devices: 6.79 us -> 8.74 us  [core_swap(): return lax.ppermute(value, 'tensor', perm)]
  transfers between devices with their start and end apart: 12 -> 13, of which waited for: 8 -> 6; matrix products, arithmetic and copies ran while one was open for 1% -> 3% of each run, Pallas kernels for 12% -> 12%
where the time goes in v12:
time: 138 us; the launch traced here: 137 us
  starting transfers between devices  51.9 us (38%)
  waiting for transfers between devices  40.6 us (29%)
  Pallas kernels  22.3 us (16%)
  blocking collectives  10.5 us (8%)
  matrix products  5.72 us (4%)
  other arithmetic  3.57 us (3%)
    ppermute x6, starting transfers between devices, x_shift(): return lax.ppermute(value, 'tensor', perm)  16.5 us
    all_to_all x1, starting transfers between devices, body(): lax.all_to_all(held, 'dp', 0, 0, axis_index_groups=z_groups(n_dp))  14.9 us
    all_to_all x1, waiting for transfers between devices, body(): sums = lax.all_to_all(total, 'dp', 0, 0, axis_index_groups=y_groups(n_dp))  13.2 us
    ppermute x6, waiting for transfers between devices, x_shift(): return lax.ppermute(value, 'tensor', perm)  12.5 us
    pallas_call x1, Pallas kernels, features_call(): pl.pallas_call(features_kernel, grid=(NY,), in_specs=[pl.BlockSpec(memory...  11.5 us
    all_to_all x1, blocking collectives, body(): came = lax.all_to_all(sent, 'dp', 0, 0, axis_index_groups=y_groups(n_dp))  10.5 us
    all_to_all x1, waiting for transfers between devices, body(): lax.all_to_all(pair.reshape(NX, IMAG * share, UNITS), 'tensor', 0, 0, axi...  8.74 us
    ppermute x3, starting transfers between devices, core_swap(): return lax.ppermute(value, 'tensor', perm)  8.74 us
  transfers between devices with their start and end apart: 13, of which 6 were waited for; matrix products, arithmetic and copies ran while one was open for 3% of the time, Pallas kernels for 12%

profile of v12, /device:TPU:1, one launch (start us, length us, event | category | flops | bytes accessed | tf_op | source)
XLA Modules:
  0.0 136.8 jit_solution(12040743404748564879)
XLA Ops:
  0.6 1.6 %prep.1 = bf16[4,112,256]{2,1,0:T(8,128)(2,1)} custom-call(bf16[16,1536]{1,0:T(8,128)(2,1)} %w_ref.1, s32[32,256]{1,0:T(8,128)} %bitcast.32, s32[2,32,256]{2,1,0:T(8,128)} %bitcast.31, s32[2,256]{1,0:T(2,128)} %actions_ref.1), custom_call_target="tpu_custom_call" | custom-call | bytes 524288 | tf_op jit(solution)/shard_map/prep/pallas_call | solution.py:81
  2.2 10.5 %all_to_all.25.came_ref = bf16[4,112,256]{2,1,0:T(8,128)(2,1)S(1)} all-to-all(bf16[4,112,256]{2,1,0:T(8,128)(2,1)} %prep.1), channel_id=1, replica_groups={{0,8,16,24},{32,40,48,56},{64,72,80,88},{96,104,112,120},{128,136,144,1..., dimensions={0} | all-to-all | bytes 458752 | tf_op jit(solution)/shard_map/all_to_all | solution.py:324
  12.7 1.0 copies.1
  13.8 14.9 %all-to-all-start.1 = ((bf16[16,64,384]{2,1,0:T(8,128)(2,1)}), bf16[16,64,384]{2,1,0:T(8,128)(2,1)S(1)}, u32[]{:S(2)}, u32[]{:S(2)}) async-start(bf16[16,64,384]{2,1,0:T(8,128)(2,1)} %copies.1), calls=%async_computation.1 | async-start | bytes 1572864 | tf_op jit(solution)/shard_map/all_to_all | solution.py:326
  28.8 4.4 %collective-permute-start.2 = (bf16[1152,128]{1,0:T(8,128)(2,1)S(1)}, bf16[1152,128]{1,0:T(8,128)(2,1)S(1)}, u32[]{:S(2)}, u32[]{:S(2)}) collective-permute-start(bf16[1152,128]{1,0:T(8,128)(2,1)S(1)} %get-tuple-element.11), channel_id=1, source_target_pairs={{0,6},{1,7},{2,0},{3,1},{4,2},{5,3},{6,4},{7,5},{8,14},{9,15},{10,... | collective-permute-start | bytes 884744 | tf_op jit(solution)/shard_map/ppermute | solution.py:37
  33.2 2.4 %collective-permute-start.1 = (bf16[1152,128]{1,0:T(8,128)(2,1)S(1)}, bf16[1152,128]{1,0:T(8,128)(2,1)S(1)}, u32[]{:S(2)}, u32[]{:S(2)}) collective-permute-start(bf16[1152,128]{1,0:T(8,128)(2,1)S(1)} %get-tuple-element.11), channel_id=1, source_target_pairs={{0,4},{1,5},{2,6},{3,7},{4,0},{5,1},{6,2},{7,3},{8,12},{9,13},{10,... | collective-permute-start | bytes 884744 | tf_op jit(solution)/shard_map/ppermute | solution.py:37
  35.6 2.5 %collective-permute-start = (bf16[1152,128]{1,0:T(8,128)(2,1)S(1)}, bf16[1152,128]{1,0:T(8,128)(2,1)S(1)}, u32[]{:S(2)}, u32[]{:S(2)}) collective-permute-start(bf16[1152,128]{1,0:T(8,128)(2,1)S(1)} %get-tuple-element.11), channel_id=1, source_target_pairs={{0,2},{1,3},{2,4},{3,5},{4,6},{5,7},{6,0},{7,1},{8,10},{9,11},{10,... | collective-permute-start | bytes 884744 | tf_op jit(solution)/shard_map/ppermute | solution.py:37
  38.2 4.3 %collective-permute-done.1 = bf16[1152,128]{1,0:T(8,128)(2,1)S(1)} collective-permute-done((bf16[1152,128]{1,0:T(8,128)(2,1)S(1)}, bf16[1152,128]{1,0:T(8,128)(2,1)S(1)}, u32[]{:S(2)}, u32[]{:S(2)}) %collective-permute-start.1) | collective-permute-done | bytes 294944 | tf_op jit(solution)/shard_map/ppermute | solution.py:37
  42.4 8.2 %collective-permute-done = bf16[1152,128]{1,0:T(8,128)(2,1)S(1)} collective-permute-done((bf16[1152,128]{1,0:T(8,128)(2,1)S(1)}, bf16[1152,128]{1,0:T(8,128)(2,1)S(1)}, u32[]{:S(2)}, u32[]{:S(2)}) %collective-permute-start) | collective-permute-done | bytes 294944 | tf_op jit(solution)/shard_map/ppermute | solution.py:37
  50.6 0.1 pad_maximum_fusion.mine_ref
  50.8 3.6 %collective-permute-start.3 = (bf16[4,1152,128]{2,1,0:T(8,128)(2,1)S(1)}, bf16[4,1152,128]{2,1,0:T(8,128)(2,1)S(1)}, u32[]{:S(2)}, u32[]{:S(2)}) collective-permute-start(bf16[4,1152,128]{2,1,0:T(8,128)(2,1)S(1)} %pad_maximum_fusion.mine_ref), channel_id=1, source_target_pairs={{0,1},{1,0},{2,3},{3,2},{4,5},{5,4},{6,7},{7,6},{8,9},{9,8},{10,11... | collective-permute-start | bytes 3538952 | tf_op jit(solution)/shard_map/ppermute | solution.py:42
  54.6 2.3 %collective-permute-done.3.other_ref = bf16[4,1152,128]{2,1,0:T(8,128)(2,1)S(1)} collective-permute-done((bf16[4,1152,128]{2,1,0:T(8,128)(2,1)S(1)}, bf16[4,1152,128]{2,1,0:T(8,128)(2,1)S(1)}, u32[]{:S(2)}, u32[]{:S(2)}) %collective-permute-start.3) | collective-permute-done | bytes 1179680 | tf_op jit(solution)/shard_map/ppermute | solution.py:42
  56.8 11.5 %features.1 = bf16[4,2,256,1024]{3,2,1,0:T(8,128)(2,1)} custom-call(s32[2]{0:T(128)S(1)} %pad_add_fusion.1.place_ref.me_ref, bf16[4,112,256]{2,1,0:T(8,128)(2,1)S(1)} %all_to_all.25.came_ref, bf16[80,2304]{1,0:T(8,128)(2,1)S(1)} %fusion.spread_ref, f32[1,1152]{1,0:T(1,128)S(1)} %fusion.10.target_ref, bf16[4,1152,128]{2,1,0:T(8,128)(2,1)S(1)} %pad_maximum_fusion.mine_ref, ...), custom_call_target="tpu_custom_call" | custom-call | flops 5435817984 | bytes 6553600 | tf_op jit(solution)/shard_map/features/pallas_call | solution.py:151
  68.3 5.7 %convolution_convert_fusion = bf16[2048,384]{1,0:T(8,128)(2,1)} fusion(bf16[2048,1024]{1,0:T(8,128)(2,1)} %bitcast.35, bf16[1024,384]{1,0:T(8,128)(2,1)S(1)} %bitcast.25), kind=kOutput, calls=%fused_computation | convolution fusion | flops 1611399168 | bytes 6553600 | tf_op jit(solution)/shard_map/dot_general | solution.py:332
  74.0 3.7 %all-to-all-start.2 = ((bf16[4,2,256,384]{3,2,1,0:T(8,128)(2,1)}), bf16[4,2,256,384]{3,2,1,0:T(8,128)(2,1)S(1)}, u32[]{:S(2)}, u32[]{:S(2)}) async-start(bf16[4,2,256,384]{3,2,1,0:T(8,128)(2,1)} %bitcast.11), calls=%async_computation.2 | async-start | bytes 3145728 | tf_op jit(solution)/shard_map/all_to_all | solution.py:334
  77.7 2.2 %collective-permute-start.7 = (bf16[1024,128]{1,0:T(8,128)(2,1)S(1)}, bf16[1024,128]{1,0:T(8,128)(2,1)S(1)}, u32[]{:S(2)}, u32[]{:S(2)}) collective-permute-start(bf16[1024,128]{1,0:T(8,128)(2,1)S(1)} %copy-done.2), channel_id=1, source_target_pairs={{0,6},{1,7},{2,0},{3,1},{4,2},{5,3},{6,4},{7,5},{8,14},{9,15},{10,... | collective-permute-start | bytes 786440 | tf_op jit(solution)/shard_map/ppermute | solution.py:37
  79.9 2.4 %collective-permute-start.6 = (bf16[1024,128]{1,0:T(8,128)(2,1)S(1)}, bf16[1024,128]{1,0:T(8,128)(2,1)}, u32[]{:S(2)}, u32[]{:S(2)}) collective-permute-start(bf16[1024,128]{1,0:T(8,128)(2,1)S(1)} %copy-done.2), channel_id=1, source_target_pairs={{0,4},{1,5},{2,6},{3,7},{4,0},{5,1},{6,2},{7,3},{8,12},{9,13},{10,... | collective-permute-start | bytes 786440 | tf_op jit(solution)/shard_map/ppermute | solution.py:37
  82.4 2.6 %collective-permute-start.5 = (bf16[1024,128]{1,0:T(8,128)(2,1)S(1)}, bf16[1024,128]{1,0:T(8,128)(2,1)}, u32[]{:S(2)}, u32[]{:S(2)}) collective-permute-start(bf16[1024,128]{1,0:T(8,128)(2,1)S(1)} %copy-done.2), channel_id=1, source_target_pairs={{0,2},{1,3},{2,4},{3,5},{4,6},{5,7},{6,0},{7,1},{8,10},{9,11},{10,... | collective-permute-start | bytes 786440 | tf_op jit(solution)/shard_map/ppermute | solution.py:37
  85.0 13.2 %all-to-all-done.2.f_ref = bf16[4,2,256,384]{3,2,1,0:T(8,128)(2,1)S(1)} async-done(((bf16[4,2,256,384]{3,2,1,0:T(8,128)(2,1)}), bf16[4,2,256,384]{3,2,1,0:T(8,128)(2,1)S(1)}, u32[]{:S(2)}, u32[]{:S(2)}) %all-to-all-start.2) | async-done | bytes 1572896 | tf_op jit(solution)/shard_map/all_to_all | solution.py:334
  98.2 5.1 %gru.1 = (bf16[256,512]{1,0:T(8,128)(2,1)S(1)}, bf16[4,2,32,1024]{3,2,1,0:T(8,128)(2,1)}, bf16[4,2,32,1024]{3,2,1,0:T(8,128)(2,1)}) custom-call(s32[2]{0:T(128)S(1)} %pad_add_fusion.1.place_ref.me_ref, bf16[256,512]{1,0:T(8,128)(2,1)} %deter_hbm.1, bf16[512,1536]{1,0:T(8,128)(2,1)} %bitcast.34, bf16[512,1024]{1,0:T(8,128)(2,1)} %w_in_hbm.1, ...), custom_call_target="tpu_custom_call" | custom-call | flops 1342177280 | bytes 5767168 | tf_op jit(solution)/shard_map/gru/pallas_call | solution.py:221
  103.3 3.2 %collective-permute-start.4 = (bf16[4,2,32,1024]{3,2,1,0:T(8,128)(2,1)}, bf16[4,2,32,1024]{3,2,1,0:T(8,128)(2,1)S(1)}, u32[]{:S(2)}, u32[]{:S(2)}) collective-permute-start(bf16[4,2,32,1024]{3,2,1,0:T(8,128)(2,1)} %get-tuple-element.8), channel_id=1, source_target_pairs={{0,1},{1,0},{2,3},{3,2},{4,5},{5,4},{6,7},{7,6},{8,9},{9,8},{10,11... | collective-permute-start | bytes 1572872 | tf_op jit(solution)/shard_map/ppermute | solution.py:42
  106.6 1.2 pad_maximum_fusion.1.mine_ref
  107.7 1.9 %collective-permute-start.8 = (bf16[4,1024,128]{2,1,0:T(8,128)(2,1)S(1)}, bf16[4,1024,128]{2,1,0:T(8,128)(2,1)S(1)}, u32[]{:S(2)}, u32[]{:S(2)}) collective-permute-start(bf16[4,1024,128]{2,1,0:T(8,128)(2,1)S(1)} %pad_maximum_fusion.1.mine_ref), channel_id=1, source_target_pairs={{0,1},{1,0},{2,3},{3,2},{4,5},{5,4},{6,7},{7,6},{8,9},{9,8},{10,11... | collective-permute-start | bytes 3145736 | tf_op jit(solution)/shard_map/ppermute | solution.py:42
  110.0 1.0 add_convert_fusion
  111.0 3.5 %all-to-all-start.3 = ((bf16[4,64,1024]{2,1,0:T(8,128)(2,1)}), bf16[4,64,1024]{2,1,0:T(8,128)(2,1)S(1)}, u32[]{:S(2)}, u32[]{:S(2)}) async-start(bf16[4,64,1024]{2,1,0:T(8,128)(2,1)} %bitcast.12), calls=%async_computation.3 | async-start | bytes 1048576 | tf_op jit(solution)/shard_map/all_to_all | solution.py:349
  114.7 0.1 copy.14.mask_ref
  114.8 8.7 %all-to-all-done.3.parts_ref = bf16[4,64,1024]{2,1,0:T(8,128)(2,1)S(1)} async-done(((bf16[4,64,1024]{2,1,0:T(8,128)(2,1)}), bf16[4,64,1024]{2,1,0:T(8,128)(2,1)S(1)}, u32[]{:S(2)}, u32[]{:S(2)}) %all-to-all-start.3) | async-done | bytes 524320 | tf_op jit(solution)/shard_map/all_to_all | solution.py:349
  123.5 3.2 %tail.1 = f32[8,8,128]{2,1,0:T(8,128)} custom-call(s32[2]{0:T(128)S(1)} %pad_add_fusion.1.place_ref.me_ref, bf16[4,64,1024]{2,1,0:T(8,128)(2,1)S(1)} %all-to-all-done.3.parts_ref, bf16[4,1024,128]{2,1,0:T(8,128)(2,1)S(1)} %pad_maximum_fusion.1.mine_ref, bf16[4,1024,128]{2,1,0:T(8,128)(2,1)S(1)} %collective-permute-done.8.other_ref, ...), custom_call_target="tpu_custom_call" | custom-call | flops 134217728 | bytes 4194304 | tf_op jit(solution)/shard_map/tail/pallas_call | solution.py:289
  126.7 4.6 %all-to-all-start.4 = ((f32[8,8,128]{2,1,0:T(8,128)}), f32[8,8,128]{2,1,0:T(8,128)S(1)}, u32[]{:S(2)}, u32[]{:S(2)}) async-start(f32[8,8,128]{2,1,0:T(8,128)} %tail.1), calls=%async_computation.4 | async-start | bytes 65536 | tf_op jit(solution)/shard_map/all_to_all | solution.py:351
  131.3 0.8 broadcast_select_fusion
  132.1 3.9 %all-to-all-done.4 = f32[8,8,128]{2,1,0:T(8,128)S(1)} async-done(((f32[8,8,128]{2,1,0:T(8,128)}), f32[8,8,128]{2,1,0:T(8,128)S(1)}, u32[]{:S(2)}, u32[]{:S(2)}) %all-to-all-start.4) | async-done | bytes 32800 | tf_op jit(solution)/shard_map/all_to_all | solution.py:351
  136.1 0.7 reshape.121
  (36 shorter events, 0.9 us)
Async XLA Ops:
  2.2 26.5 %copy-start.1 = (bf16[1024,128]{1,0:T(8,128)(2,1)S(1)}, bf16[1024,128]{1,0:T(8,128)(2,1)}, u32[]{:S(2)}) copy-start(bf16[1024,128]{1,0:T(8,128)(2,1)} %param.16) | copy-start | bytes 786436
  2.2 26.5 %copy-start.4 = (bf16[18,128]{1,0:T(8,128)(2,1)S(1)}, bf16[18,128]{1,0:T(8,128)(2,1)}, u32[]{:S(2)}) copy-start(bf16[18,128]{1,0:T(8,128)(2,1)} %param.17) | copy-start | bytes 13828
  13.8 54.5 %all-to-all-start.1 = ((bf16[16,64,384]{2,1,0:T(8,128)(2,1)}), bf16[16,64,384]{2,1,0:T(8,128)(2,1)S(1)}, u32[]{:S(2)}, u32[]{:S(2)}) async-start(bf16[16,64,384]{2,1,0:T(8,128)(2,1)} %copies.1), calls=%async_computation.1 | async-start | bytes 1572864 | tf_op jit(solution)/shard_map/all_to_all | solution.py:326
  28.8 9.4 %collective-permute-start.2 = (bf16[1152,128]{1,0:T(8,128)(2,1)S(1)}, bf16[1152,128]{1,0:T(8,128)(2,1)S(1)}, u32[]{:S(2)}, u32[]{:S(2)}) collective-permute-start(bf16[1152,128]{1,0:T(8,128)(2,1)S(1)} %get-tuple-element.11), channel_id=1, source_target_pairs={{0,6},{1,7},{2,0},{3,1},{4,2},{5,3},{6,4},{7,5},{8,14},{9,15},{10,... | collective-permute-start | bytes 884744 | tf_op jit(solution)/shard_map/ppermute | solution.py:37
  33.2 9.3 %collective-permute-start.1 = (bf16[1152,128]{1,0:T(8,128)(2,1)S(1)}, bf16[1152,128]{1,0:T(8,128)(2,1)S(1)}, u32[]{:S(2)}, u32[]{:S(2)}) collective-permute-start(bf16[1152,128]{1,0:T(8,128)(2,1)S(1)} %get-tuple-element.11), channel_id=1, source_target_pairs={{0,4},{1,5},{2,6},{3,7},{4,0},{5,1},{6,2},{7,3},{8,12},{9,13},{10,... | collective-permute-start | bytes 884744 | tf_op jit(solution)/shard_map/ppermute | solution.py:37
  35.6 15.0 %collective-permute-start = (bf16[1152,128]{1,0:T(8,128)(2,1)S(1)}, bf16[1152,128]{1,0:T(8,128)(2,1)S(1)}, u32[]{:S(2)}, u32[]{:S(2)}) collective-permute-start(bf16[1152,128]{1,0:T(8,128)(2,1)S(1)} %get-tuple-element.11), channel_id=1, source_target_pairs={{0,2},{1,3},{2,4},{3,5},{4,6},{5,7},{6,0},{7,1},{8,10},{9,11},{10,... | collective-permute-start | bytes 884744 | tf_op jit(solution)/shard_map/ppermute | solution.py:37
  50.8 6.0 %collective-permute-start.3 = (bf16[4,1152,128]{2,1,0:T(8,128)(2,1)S(1)}, bf16[4,1152,128]{2,1,0:T(8,128)(2,1)S(1)}, u32[]{:S(2)}, u32[]{:S(2)}) collective-permute-start(bf16[4,1152,128]{2,1,0:T(8,128)(2,1)S(1)} %pad_maximum_fusion.mine_ref), channel_id=1, source_target_pairs={{0,1},{1,0},{2,3},{3,2},{4,5},{5,4},{6,7},{7,6},{8,9},{9,8},{10,11... | collective-permute-start | bytes 3538952 | tf_op jit(solution)/shard_map/ppermute | solution.py:42
  74.0 3.7 %copy-start.2 = (bf16[1024,128]{1,0:T(8,128)(2,1)S(1)}, bf16[1024,128]{1,0:T(8,128)(2,1)}, u32[]{:S(2)}) copy-start(bf16[1024,128]{1,0:T(8,128)(2,1)} %param.21) | copy-start | bytes 786436
  74.0 24.1 %all-to-all-start.2 = ((bf16[4,2,256,384]{3,2,1,0:T(8,128)(2,1)}), bf16[4,2,256,384]{3,2,1,0:T(8,128)(2,1)S(1)}, u32[]{:S(2)}, u32[]{:S(2)}) async-start(bf16[4,2,256,384]{3,2,1,0:T(8,128)(2,1)} %bitcast.11), calls=%async_computation.2 | async-start | bytes 3145728 | tf_op jit(solution)/shard_map/all_to_all | solution.py:334
  77.7 28.8 %collective-permute-start.7 = (bf16[1024,128]{1,0:T(8,128)(2,1)S(1)}, bf16[1024,128]{1,0:T(8,128)(2,1)S(1)}, u32[]{:S(2)}, u32[]{:S(2)}) collective-permute-start(bf16[1024,128]{1,0:T(8,128)(2,1)S(1)} %copy-done.2), channel_id=1, source_target_pairs={{0,6},{1,7},{2,0},{3,1},{4,2},{5,3},{6,4},{7,5},{8,14},{9,15},{10,... | collective-permute-start | bytes 786440 | tf_op jit(solution)/shard_map/ppermute | solution.py:37
  79.9 26.6 %collective-permute-start.6 = (bf16[1024,128]{1,0:T(8,128)(2,1)S(1)}, bf16[1024,128]{1,0:T(8,128)(2,1)}, u32[]{:S(2)}, u32[]{:S(2)}) collective-permute-start(bf16[1024,128]{1,0:T(8,128)(2,1)S(1)} %copy-done.2), channel_id=1, source_target_pairs={{0,4},{1,5},{2,6},{3,7},{4,0},{5,1},{6,2},{7,3},{8,12},{9,13},{10,... | collective-permute-start | bytes 786440 | tf_op jit(solution)/shard_map/ppermute | solution.py:37
  82.4 24.2 %collective-permute-start.5 = (bf16[1024,128]{1,0:T(8,128)(2,1)S(1)}, bf16[1024,128]{1,0:T(8,128)(2,1)}, u32[]{:S(2)}, u32[]{:S(2)}) collective-permute-start(bf16[1024,128]{1,0:T(8,128)(2,1)S(1)} %copy-done.2), channel_id=1, source_target_pairs={{0,2},{1,3},{2,4},{3,5},{4,6},{5,7},{6,0},{7,1},{8,10},{9,11},{10,... | collective-permute-start | bytes 786440 | tf_op jit(solution)/shard_map/ppermute | solution.py:37
  103.3 6.4 %copy-start.5 = (s32[4]{0:T(128)S(1)}, s32[4]{0:T(128)}, u32[]{:S(2)}) copy-start(s32[4]{0:T(128)} %param.15) | copy-start | bytes 52
  103.3 6.7 %copy-start.3 = (s32[2,256,32]{1,2,0:T(8,128)S(1)}, s32[2,256,32]{1,2,0:T(8,128)}, u32[]{:S(2)}) copy-start(s32[2,256,32]{1,2,0:T(8,128)} %param.13) | copy-start | bytes 196612
  103.3 6.7 %copy-start = (bf16[4,2,32,1024]{3,2,1,0:T(8,128)(2,1)S(1)}, bf16[4,2,32,1024]{3,2,1,0:T(8,128)(2,1)}, u32[]{:S(2)}) copy-start(bf16[4,2,32,1024]{3,2,1,0:T(8,128)(2,1)} %get-tuple-element.7) | copy-start | bytes 1572868
  103.3 6.7 %collective-permute-start.4 = (bf16[4,2,32,1024]{3,2,1,0:T(8,128)(2,1)}, bf16[4,2,32,1024]{3,2,1,0:T(8,128)(2,1)S(1)}, u32[]{:S(2)}, u32[]{:S(2)}) collective-permute-start(bf16[4,2,32,1024]{3,2,1,0:T(8,128)(2,1)} %get-tuple-element.8), channel_id=1, source_target_pairs={{0,1},{1,0},{2,3},{3,2},{4,5},{5,4},{6,7},{7,6},{8,9},{9,8},{10,11... | collective-permute-start | bytes 1572872 | tf_op jit(solution)/shard_map/ppermute | solution.py:42
  107.7 7.1 %collective-permute-start.8 = (bf16[4,1024,128]{2,1,0:T(8,128)(2,1)S(1)}, bf16[4,1024,128]{2,1,0:T(8,128)(2,1)S(1)}, u32[]{:S(2)}, u32[]{:S(2)}) collective-permute-start(bf16[4,1024,128]{2,1,0:T(8,128)(2,1)S(1)} %pad_maximum_fusion.1.mine_ref), channel_id=1, source_target_pairs={{0,1},{1,0},{2,3},{3,2},{4,5},{5,4},{6,7},{7,6},{8,9},{9,8},{10,11... | collective-permute-start | bytes 3145736 | tf_op jit(solution)/shard_map/ppermute | solution.py:42
  111.0 12.5 %all-to-all-start.3 = ((bf16[4,64,1024]{2,1,0:T(8,128)(2,1)}), bf16[4,64,1024]{2,1,0:T(8,128)(2,1)S(1)}, u32[]{:S(2)}, u32[]{:S(2)}) async-start(bf16[4,64,1024]{2,1,0:T(8,128)(2,1)} %bitcast.12), calls=%async_computation.3 | async-start | bytes 1048576 | tf_op jit(solution)/shard_map/all_to_all | solution.py:349
  126.7 9.3 %all-to-all-start.4 = ((f32[8,8,128]{2,1,0:T(8,128)}), f32[8,8,128]{2,1,0:T(8,128)S(1)}, u32[]{:S(2)}, u32[]{:S(2)}) async-start(f32[8,8,128]{2,1,0:T(8,128)} %tail.1), calls=%async_computation.4 | async-start | bytes 65536 | tf_op jit(solution)/shard_map/all_to_all | solution.py:351
